TPU v7x, 32 devices: a whole 2x2x4 slice. The times are simulated.
32 devices in a mesh: pipe: 4 (over z), dp: 8 (over y, x, core).
Axes of the slice: x: 2, y: 2, z: 4, core: 2. Of those that a mesh axis runs over, the one named last changes fastest.
Arguments:
- acts: bfloat16 [4, 1024, 5120], P('pipe', 'dp'), may hold values from -6 to 6
- cotangent: bfloat16 [1024, 5120], P('dp'), may hold values from -0.59765625 to 0.59765625
- kv_grads: bfloat16 [4, 1024, 2048], P('pipe', 'dp'), may hold values from -6 to 6
- w_kv: bfloat16 [4, 5120, 2048], P('pipe'), may hold values from -0.0078125 to 0.0078125
- momentum: bfloat16 [4, 5120, 2048], P('pipe', 'dp'), may hold values from -0.119628906 to 0.119628906
Outputs:
- update: bfloat16 [4, 5120, 2048], P('pipe', 'dp')
- input_grads: bfloat16 [4, 1024, 5120], P('pipe', 'dp')
All inputs are finite; a program needn't handle non-finite values.
Results may differ from a plain program's by a relative error of at most 0.022.
Values may be sent and summed in bfloat16 or wider, within the bound.
No kernel may reach another device: no remote copies, remote signals or barrier semaphores. Data moves between devices by JAX's collectives and lax.ppermute only.
A program may use at most 128 MiB of HBM per device.

v0:
```python
import functools
import math

import jax
import jax.numpy as jnp
from jax import lax
from jax.experimental import pallas as pl
from jax.experimental.pallas import tpu as pltpu
from jax.sharding import PartitionSpec as P

HEAD = 128
ITERS = 5
CORES = 2
CHUNKS = 4
LAG = 2
PAD = 8

momentum_rate = 0.95
quintic_a = 3.4445
quintic_b = -4.775
quintic_c = 2.0315
epsilon = 1e-07

F32 = jnp.float32
BF16 = jnp.bfloat16
ANY = pl.BlockSpec(memory_space=pl.ANY)


def cost(flops, moved):
    return pl.CostEstimate(flops=int(flops), bytes_accessed=int(moved), transcendentals=0)


def params(mib):
    return pltpu.CompilerParams(vmem_limit_bytes=mib * 1024 * 1024)


def after(value, *others):
    return lax.optimization_barrier((value, *others))[0]


def swap(value, by):
    count = lax.axis_size("dp")
    return lax.ppermute(value, "dp", [(i ^ by[i % CORES], i) for i in range(count)])


def down(value):
    count = lax.axis_size("pipe")
    return lax.ppermute(value, "pipe", [(i, i - 1) for i in range(1, count)])


def by_core(pair):
    own = lax.axis_index("dp")
    if pair[0] == pair[1]:
        return pair[0]
    return jnp.where(own % CORES == 0, pair[0], pair[1])


def split_columns(inputs, relations):
    count = lax.axis_size("dp")
    tokens, width = inputs.shape
    block = width // count

    def kernel(in_ref, *out_refs):
        own = lax.axis_index("dp")
        for relation, out_ref in zip(relations, out_refs):
            flipped = relation if relation[0] % CORES == 0 else relation[::-1]
            owner = own ^ by_core(flipped)
            if block % 128 == 0:
                columns = pl.ds(pl.multiple_of(owner * block, 128), block)
                out_ref[...] = in_ref[:, columns].T
            else:
                for other in range(count):
                    @pl.when(owner == other)
                    def store():
                        out_ref[...] = in_ref[:, other * block : (other + 1) * block].T

    shape = jax.ShapeDtypeStruct((block, tokens), BF16)
    return pl.pallas_call(
        kernel,
        grid=(1,),
        out_shape=[shape] * len(relations),
        in_specs=[pl.BlockSpec((tokens, width), lambda i: (0, 0))],
        out_specs=[pl.BlockSpec((block, tokens), lambda i: (0, 0))] * len(relations),
        compiler_params=params(16),
        cost_estimate=cost(0, 4 * tokens * width),
        name="split_columns",
    )(inputs)


def triangle():
    row = lax.broadcasted_iota(jnp.int32, (HEAD, HEAD), 0)
    col = lax.broadcasted_iota(jnp.int32, (HEAD, HEAD), 1)
    return row, col


def pack(mats):
    if len(mats) % 2:
        return jnp.concatenate(mats, axis=0)
    row, col = triangle()
    rows = []
    for first, second in zip(mats[::2], mats[1::2]):
        diagonal = jnp.sum(jnp.where(row == col, second, 0.0), axis=0, keepdims=True)
        rows.append(jnp.where(col >= row, first, second))
        rows.append(jnp.broadcast_to(diagonal, (PAD, HEAD)))
    return jnp.concatenate(rows, axis=0)


def packed_rows(slots):
    return slots * HEAD if slots % 2 else slots // 2 * (HEAD + PAD)


def unpack(packed, slots):
    if slots % 2:
        return [packed[i * HEAD : (i + 1) * HEAD] for i in range(slots)]
    row, col = triangle()
    mats = []
    for pair in range(slots // 2):
        at = pair * (HEAD + PAD)
        square = packed[at : at + HEAD]
        diagonal = packed[at + HEAD : at + HEAD + 1]
        other = square.T
        mats.append(jnp.where(col >= row, square, other))
        mats.append(jnp.where(col == row, diagonal, jnp.where(col < row, square, other)))
    return mats


def gradient(left, right, moment, scale, slots):
    rows, width = moment.shape
    count = lax.axis_size("dp")
    mats = width // HEAD
    owners = mats // slots
    per_step = 2 if owners % 2 == 0 else 1
    block = per_step * slots * HEAD
    tokens = sum(piece.shape[0] for piece in right)
    n_left, n_right = len(left), len(right)
    packed = packed_rows(slots)
    steps = owners // per_step

    def kernel(*refs):
        left_refs = refs[:n_left]
        right_refs = refs[n_left : n_left + n_right]
        mom_ref, buf_ref = refs[n_left + n_right : n_left + n_right + 2]
        gram_refs = refs[n_left + n_right + 2 : -2]
        held, grams = refs[-2:]
        step = pl.program_id(0)
        own = lax.axis_index("dp")

        @pl.when(step == 0)
        def load():
            at = 0
            for ref in left_refs:
                held[:, at : at + ref.shape[1]] = ref[...]
                at += ref.shape[1]
            if owners < count:
                grams[...] = jnp.zeros_like(grams)

        kv_block = jnp.concatenate([ref[...] for ref in right_refs], axis=0)
        grad = jnp.dot(held[...], kv_block, preferred_element_type=F32)
        buffer = (momentum_rate * mom_ref[...].astype(F32) + grad * scale).astype(BF16)
        buf_ref[...] = buffer
        for which in range(per_step):
            first = which * slots * HEAD
            values = buffer[:, first : first + slots * HEAD]
            gram = lax.dot_general(values, values, (((0,), (0,)), ((), ())), preferred_element_type=F32)
            spans = [slice(slot * HEAD, (slot + 1) * HEAD) for slot in range(slots)]
            owner = step * per_step + which
            grams[owner ^ own] = pack([gram[span, span] for span in spans])

        @pl.when(step == steps - 1)
        def store():
            for distance, ref in enumerate(gram_refs):
                ref[...] = grams[distance]

    column = lambda height: pl.BlockSpec((height, block), lambda j: (0, j))
    return pl.pallas_call(
        kernel,
        grid=(steps,),
        out_shape=[jax.ShapeDtypeStruct((rows, width), BF16)]
        + [jax.ShapeDtypeStruct((packed, HEAD), F32)] * count,
        in_specs=[pl.BlockSpec(a.shape, lambda j: (0, 0)) for a in left]
        + [column(piece.shape[0]) for piece in right]
        + [column(rows)],
        out_specs=[column(rows)] + [pl.BlockSpec((packed, HEAD), lambda j: (0, 0))] * count,
        scratch_shapes=[pltpu.VMEM((rows, tokens), BF16), pltpu.VMEM((count, packed, HEAD), F32)],
        compiler_params=params(24),
        cost_estimate=cost(2 * rows * tokens * width, 2 * tokens * (rows + width) + 4 * rows * width),
        name="gradient",
    )(*left, *right, moment)


def mixing(grams, scale, slots):
    highest = lax.Precision.HIGHEST

    def product(left, right):
        return jnp.dot(left, right, precision=highest, preferred_element_type=F32)

    def kernel(*refs):
        gram_refs, out_ref = refs[:-1], refs[-1]
        row, col = triangle()
        eye = (row == col).astype(F32)
        total = gram_refs[0][...]
        for ref in gram_refs[1:]:
            total = total + ref[...]
        grams, inverses, mixes = [], [], []
        for gram in unpack(total, slots):
            squares = jnp.sum(gram * eye, keepdims=True)
            inverse = 1.0 / (jnp.sqrt(squares) + epsilon)
            grams.append(gram * inverse * inverse)
            inverses.append(inverse)
            mixes.append(None)
        for step in range(ITERS):
            square = [product(gram, gram) for gram in grams]
            factor = [
                quintic_a * eye + quintic_b * gram + quintic_c * sq for gram, sq in zip(grams, square)
            ]
            mixes = [f if mix is None else product(mix, f) for mix, f in zip(mixes, factor)]
            if step < ITERS - 1:
                half = [product(gram, f) for gram, f in zip(grams, factor)]
                grams = [product(h, f) for h, f in zip(half, factor)]
        out_ref[...] = pack([mix * (scale * inverse) for mix, inverse in zip(mixes, inverses)])

    packed = packed_rows(slots)
    spec = pl.BlockSpec((packed, HEAD), lambda i: (0, 0))
    return pl.pallas_call(
        kernel,
        grid=(1,),
        out_shape=jax.ShapeDtypeStruct((packed, HEAD), F32),
        in_specs=[spec] * len(grams),
        out_specs=spec,
        compiler_params=params(16),
        cost_estimate=cost(slots * 18 * 2 * 6 * HEAD**3, 4 * slots * HEAD * HEAD * 9),
        name="mixing",
    )(*grams)


def apply_mixing(buffer, mixes, slots):
    rows, width = buffer.shape
    count = lax.axis_size("dp")
    mats = width // HEAD
    owners = mats // slots
    per_step = 2 if owners % 2 == 0 else 1
    span = slots * HEAD
    block = per_step * span
    packed = packed_rows(slots)

    def kernel(*refs):
        mix_refs = refs[:count]
        buf_ref, out_ref, held = refs[count:]
        own = lax.axis_index("dp")
        step = pl.program_id(0)

        @pl.when(step == 0)
        def load():
            for distance, ref in enumerate(mix_refs):
                held[distance] = ref[...]

        for which in range(per_step):
            parts = unpack(held[(step * per_step + which) ^ own], slots)
            zero = jnp.zeros((HEAD, HEAD), F32)
            mix = jnp.concatenate(
                [
                    jnp.concatenate([part if j == i else zero for j in range(slots)], axis=1)
                    for i, part in enumerate(parts)
                ],
                axis=0,
            )
            columns = slice(which * span, (which + 1) * span)
            values = buf_ref[:, columns]
            total = None
            for part in range(3):
                piece = mix.astype(BF16)
                mix = mix - piece.astype(F32)
                term = jnp.dot(values, piece, preferred_element_type=F32)
                total = term if total is None else total + term
            out_ref[:, columns] = total.astype(BF16)

    column = pl.BlockSpec((rows, block), lambda j: (0, j))
    return pl.pallas_call(
        kernel,
        grid=(owners // per_step,),
        out_shape=jax.ShapeDtypeStruct((rows, width), BF16),
        in_specs=[pl.BlockSpec((packed, HEAD), lambda j: (0, 0))] * count + [column],
        out_specs=column,
        scratch_shapes=[pltpu.VMEM((count, packed, HEAD), F32)],
        compiler_params=params(16),
        cost_estimate=cost(6 * rows * width * HEAD, 4 * rows * width),
        name="apply_mixing",
    )(*mixes, buffer)


def weight_product(chunk, kv_rows, weights, cotangent):
    tokens, lat = kv_rows.shape
    width = weights.shape[0]
    span = width // CHUNKS
    block = 256 if span % 256 == 0 else span
    pieces = span // block

    def kernel(kv_ref, cot_ref, w_ref, out_ref, held, sems):
        copies = []
        for piece in range(pieces):
            source = w_ref.at[pl.ds(chunk * span + piece * block, block)]
            copies.append(
                pltpu.make_async_copy(source, held.at[pl.ds(piece * block, block)], sems.at[piece])
            )
            copies[-1].start()
        last = lax.axis_index("pipe") == lax.axis_size("pipe") - 1
        for piece in range(pieces):
            columns = slice(piece * block, (piece + 1) * block)
            copies[piece].wait()
            out = lax.dot_general(
                kv_ref[...], held[columns], (((1,), (1,)), ((), ())), preferred_element_type=F32
            )
            out_ref[:, columns] = out + jnp.where(last, cot_ref[:, columns].astype(F32), 0.0)

    return pl.pallas_call(
        kernel,
        grid=(1,),
        out_shape=jax.ShapeDtypeStruct((tokens, span), F32),
        in_specs=[
            pl.BlockSpec((tokens, lat), lambda i: (0, 0)),
            pl.BlockSpec((tokens, span), lambda i: (0, chunk)),
            ANY,
        ],
        out_specs=pl.BlockSpec((tokens, span), lambda i: (0, 0)),
        scratch_shapes=[pltpu.VMEM((span, lat), BF16), pltpu.SemaphoreType.DMA((pieces,))],
        compiler_params=params(16),
        cost_estimate=cost(2 * tokens * lat * span, 2 * lat * (tokens + span) + 4 * tokens * span),
        name="weight_product",
    )(kv_rows, cotangent, weights)


def relay_step(tick, received, products):
    tokens, span = products[0].shape
    sections = lax.axis_size("pipe")
    held = [(s, tick - LAG * (sections - 1 - s)) for s in range(sections)]
    held = [(s, c) for s, c in held if 0 <= c < CHUNKS]
    used = [products[c] for _, c in held]
    first = [] if received is None else [received]

    def kernel(*refs):
        prod_refs = refs[len(first) : len(first) + len(used)]
        out_ref, prod, sem = refs[-3:]
        stage = lax.axis_index("pipe")
        for (section, _), ref in zip(held, prod_refs):
            @pl.when(stage == section)
            def one():
                copy = pltpu.make_async_copy(ref, prod, sem)
                copy.start()
                copy.wait()
                if first and section < sections - 1:
                    out_ref[...] = (refs[0][...].astype(F32) + prod[...]).astype(BF16)
                else:
                    out_ref[...] = prod[...].astype(BF16)

    block = pl.BlockSpec((tokens, span), lambda i: (0, 0))
    return pl.pallas_call(
        kernel,
        grid=(1,),
        in_specs=[block] * len(first) + [ANY] * len(used),
        out_specs=block,
        out_shape=jax.ShapeDtypeStruct((tokens, span), BF16),
        scratch_shapes=[pltpu.VMEM((tokens, span), F32), pltpu.SemaphoreType.DMA],
        compiler_params=params(8),
        cost_estimate=cost(tokens * span, 8 * tokens * span),
        name="relay_step",
    )(*first, *used)


def collect(sent):
    tokens, span = sent[0].shape
    sections = lax.axis_size("pipe")

    def kernel(*refs):
        sent_refs = refs[: len(sent)]
        out_ref, sems = refs[len(sent) :]
        stage = lax.axis_index("pipe")
        for section in range(sections):
            @pl.when(stage == section)
            def one():
                copies = []
                for chunk in range(CHUNKS):
                    ref = sent_refs[chunk + LAG * (sections - 1 - section)]
                    target = out_ref.at[:, pl.ds(chunk * span, span)]
                    copies.append(pltpu.make_async_copy(ref, target, sems.at[chunk]))
                    copies[-1].start()
                for copy in copies:
                    copy.wait()

    return pl.pallas_call(
        kernel,
        in_specs=[ANY] * len(sent),
        out_specs=ANY,
        out_shape=jax.ShapeDtypeStruct((tokens, span * CHUNKS), BF16),
        scratch_shapes=[pltpu.SemaphoreType.DMA((CHUNKS,))],
        compiler_params=params(8),
        cost_estimate=cost(0, 4 * tokens * span * CHUNKS),
        name="collect",
    )(*sent)


def token_relations():
    count = lax.axis_size("dp")
    chips = count // CORES
    if chips == 4:
        base = [(0, 0), (CORES, 2 * CORES), (2 * CORES, CORES), (3 * CORES, 3 * CORES)]
    else:
        base = [(CORES * d, CORES * d) for d in range(chips)]
    return base, [(b ^ 1, a ^ 1) for a, b in base]


def shards(acts, cotangent, kv_grads, w_kv, momentum):
    inputs, kv_rows, weights, moment = acts[0], kv_grads[0], w_kv[0], momentum[0]
    tokens, width = inputs.shape
    groups = lax.axis_size("dp")
    sections = lax.axis_size("pipe")
    chips = groups // CORES
    mats = moment.shape[1] // HEAD
    slots = max(1, mats // groups)
    scale_grad = 1.0 / (tokens * groups)
    scale = 0.2 * math.sqrt(max(width, HEAD))
    other_core = (1, 1)

    same, crossed = token_relations()
    relations = same + crossed
    ticks = CHUNKS + LAG * (sections - 1)
    products, sent, moved = [], [], []

    def product(chunk, rows):
        products.append(weight_product(chunk, rows, weights, cotangent))

    def relay(*others):
        tick = len(sent)
        received = moved[tick - LAG] if tick >= LAG else None
        if received is not None:
            if others:
                received = after(received, *others)
            sent.append(relay_step(tick, received, products))
        else:
            sent.append(relay_step(tick, None, products))
        if tick < ticks - LAG:
            moved.append(down(sent[-1]))

    near = [kv_rows, swap(kv_rows, same[1])]
    if chips == 4:
        near.append(swap(kv_rows, same[2]))
        near.append(swap(near[1], same[2]))
    else:
        near.extend(swap(kv_rows, relation) for relation in same[2:])

    product(0, kv_rows)
    relay()
    columns = split_columns(after(inputs, sent[0]), relations)
    left = [columns[0]] + [swap(c, r) for c, r in zip(columns[1:], relations[1:])]
    product(1, after(kv_rows, columns[0]))
    relay()
    for chunk in range(2, CHUNKS):
        product(chunk, after(kv_rows, sent[-1]))
    far = [swap(piece, other_core) for piece in near]
    while len(sent) < 5:
        relay(*products[-1:])

    outs = gradient(left, near + far, after(moment, sent[-1]), scale_grad, slots)
    buffer, grams = outs[0], outs[1:]
    grams = [grams[0]] + [swap(g, (d, d)) for d, g in enumerate(grams) if d]
    while len(sent) < 7:
        relay(outs[1])
    mix = mixing([after(grams[0], sent[-1])] + grams[1:], scale, slots)
    mixes = [mix] + [swap(mix, (d, d)) for d in range(1, groups)]
    while len(sent) < ticks:
        relay(mix)
    update = apply_mixing(after(buffer, sent[-2]), mixes, slots)
    outgoing = collect(sent)
    return (update[None], outgoing[None])


def solution(mesh):
    in_specs = (
        P("pipe", "dp", None),
        P("dp", None),
        P("pipe", "dp", None),
        P("pipe", None, None),
        P("pipe", "dp", None),
    )
    out_specs = (P("pipe", "dp", None), P("pipe", "dp", None))
    return jax.shard_map(shards, mesh=mesh, in_specs=in_specs, out_specs=out_specs, check_vma=False)
```

profile of v0, /device:TPU:0, one launch (start us, length us, event | category | flops | bytes accessed | tf_op | source)
XLA Modules:
  0.0 129.6 jit_solution(15990400031205172126)
XLA Ops:
  0.6 3.0 %collective-permute-start.7 = (bf16[128,2048]{1,0:T(8,128)(2,1)}, bf16[128,2048]{1,0:T(8,128)(2,1)S(1)}, u32[]{:S(2)}, u32[]{:S(2)}) collective-permute-start(bf16[128,2048]{1,0:T(8,128)(2,1)} %bitcast.10), channel_id=1, source_target_pairs={{2,0},{5,1},{0,2},{7,3},{6,4},{1,5},{4,6},{3,7},{10,8},{13,9},{8,1... | collective-permute-start | bytes 1572872 | tf_op jit(solution)/shard_map/ppermute | solution.py:43
  3.6 7.0 %copy-done = bf16[1,5120,2048]{2,1,0:T(8,128)(2,1)S(1)} copy-done((bf16[1,5120,2048]{2,1,0:T(8,128)(2,1)S(1)}, bf16[1,5120,2048]{2,1,0:T(8,128)(2,1)}, u32[]{:S(2)}) %copy-start) | copy-done | bytes 20971544
  10.6 1.3 %copy-done.2 = bf16[128,5120]{1,0:T(8,128)(2,1)S(1)} copy-done((bf16[128,5120]{1,0:T(8,128)(2,1)S(1)}, bf16[128,5120]{1,0:T(8,128)(2,1)}, u32[]{:S(2)}) %copy-start.2) | copy-done | bytes 1310744
  11.9 1.0 copy-done.4
  13.0 3.7 %weight_product.4.refs_0_.refs_1_ = f32[128,1280]{1,0:T(8,128)S(1)} custom-call(bf16[128,2048]{1,0:T(8,128)(2,1)S(1)} %bitcast.11, bf16[128,5120]{1,0:T(8,128)(2,1)S(1)} %copy-done.2, bf16[5120,2048]{1,0:T(8,128)(2,1)S(1)} %bitcast.6), custom_call_target="tpu_custom_call" | custom-call | flops 671088640 | bytes 6422528 | tf_op jit(solution)/shard_map/weight_product/pallas_call | solution.py:315
  16.7 0.0 copy-start.3
  16.8 0.4 split_columns.1
  17.2 0.1 collective-permute-start
  17.2 2.0 %collective-permute-start.1 = (bf16[640,128]{1,0:T(8,128)(2,1)S(1)}, bf16[640,128]{1,0:T(8,128)(2,1)S(1)}, u32[]{:S(2)}, u32[]{:S(2)}) collective-permute-start(bf16[640,128]{1,0:T(8,128)(2,1)S(1)} %get-tuple-element.36), channel_id=1, source_target_pairs={{4,0},{3,1},{6,2},{1,3},{0,4},{7,5},{2,6},{5,7},{12,8},{11,9},{14,... | collective-permute-start | bytes 491528 | tf_op jit(solution)/shard_map/ppermute | solution.py:43
  19.3 0.1 collective-permute-start.8
  19.3 2.0 %collective-permute-start.9 = (bf16[128,2048]{1,0:T(8,128)(2,1)S(1)}, bf16[128,2048]{1,0:T(8,128)(2,1)S(1)}, u32[]{:S(2)}, u32[]{:S(2)}) collective-permute-start(bf16[128,2048]{1,0:T(8,128)(2,1)S(1)} %collective-permute-done.7.refs_9_), channel_id=1, source_target_pairs={{4,0},{3,1},{6,2},{1,3},{0,4},{7,5},{2,6},{5,7},{12,8},{11,9},{14,... | collective-permute-start | bytes 1572872 | tf_op jit(solution)/shard_map/ppermute | solution.py:43
  21.3 1.4 %collective-permute-start.2 = (bf16[640,128]{1,0:T(8,128)(2,1)S(1)}, bf16[640,128]{1,0:T(8,128)(2,1)S(1)}, u32[]{:S(2)}, u32[]{:S(2)}) collective-permute-start(bf16[640,128]{1,0:T(8,128)(2,1)S(1)} %get-tuple-element.37), channel_id=1, source_target_pairs={{6,0},{7,1},{4,2},{5,3},{2,4},{3,5},{0,6},{1,7},{14,8},{15,9},{12,... | collective-permute-start | bytes 491528 | tf_op jit(solution)/shard_map/ppermute | solution.py:43
  22.8 1.6 %collective-permute-done.refs_1_ = bf16[640,128]{1,0:T(8,128)(2,1)S(1)} collective-permute-done((bf16[640,128]{1,0:T(8,128)(2,1)S(1)}, bf16[640,128]{1,0:T(8,128)(2,1)S(1)}, u32[]{:S(2)}, u32[]{:S(2)}) %collective-permute-start) | collective-permute-done | bytes 163872 | tf_op jit(solution)/shard_map/ppermute | solution.py:43
  24.4 5.0 %collective-permute-done.2.refs_3_ = bf16[640,128]{1,0:T(8,128)(2,1)S(1)} collective-permute-done((bf16[640,128]{1,0:T(8,128)(2,1)S(1)}, bf16[640,128]{1,0:T(8,128)(2,1)S(1)}, u32[]{:S(2)}, u32[]{:S(2)}) %collective-permute-start.2) | collective-permute-done | bytes 163872 | tf_op jit(solution)/shard_map/ppermute | solution.py:43
  29.4 11.1 %collective-permute-start.5 = (bf16[640,128]{1,0:T(8,128)(2,1)S(1)}, bf16[640,128]{1,0:T(8,128)(2,1)S(1)}, u32[]{:S(2)}, u32[]{:S(2)}) collective-permute-start(bf16[640,128]{1,0:T(8,128)(2,1)S(1)} %get-tuple-element.40), channel_id=1, source_target_pairs={{3,0},{4,1},{1,2},{6,3},{7,4},{0,5},{5,6},{2,7},{11,8},{12,9},{9,1... | collective-permute-start | bytes 491528 | tf_op jit(solution)/shard_map/ppermute | solution.py:43
  40.5 1.3 collective-permute-start.14
  41.8 3.7 %weight_product.5.refs_0_.refs_1_ = f32[128,1280]{1,0:T(8,128)S(1)} custom-call(bf16[128,2048]{1,0:T(8,128)(2,1)S(1)} %bitcast.13, bf16[128,5120]{1,0:T(8,128)(2,1)S(1)} %copy-done.3, bf16[5120,2048]{1,0:T(8,128)(2,1)S(1)} %bitcast.7), custom_call_target="tpu_custom_call" | custom-call | flops 671088640 | bytes 6422528 | tf_op jit(solution)/shard_map/weight_product/pallas_call | solution.py:315
  45.6 1.3 collective-permute-start.32
  46.9 0.8 collective-permute-start.6
  47.7 6.5 %collective-permute-done.6.refs_7_ = bf16[640,128]{1,0:T(8,128)(2,1)S(1)} collective-permute-done((bf16[640,128]{1,0:T(8,128)(2,1)S(1)}, bf16[640,128]{1,0:T(8,128)(2,1)S(1)}, u32[]{:S(2)}, u32[]{:S(2)}) %collective-permute-start.6) | collective-permute-done | bytes 163872 | tf_op jit(solution)/shard_map/ppermute | solution.py:43
  54.2 0.1 collective-permute-start.10
  54.4 0.4 collective-permute-start.11
  54.8 0.1 collective-permute-start.12
  54.9 0.4 collective-permute-start.13
  55.3 3.7 %weight_product.6.refs_2_.refs_1_ = f32[128,1280]{1,0:T(8,128)S(1)} custom-call(bf16[128,2048]{1,0:T(8,128)(2,1)S(1)} %bitcast.15, bf16[128,5120]{1,0:T(8,128)(2,1)S(1)} %copy-done.3, bf16[5120,2048]{1,0:T(8,128)(2,1)S(1)} %bitcast.8), custom_call_target="tpu_custom_call" | custom-call | flops 671088640 | bytes 6422528 | tf_op jit(solution)/shard_map/weight_product/pallas_call | solution.py:315
  59.0 3.7 %weight_product.7.refs_2_.refs_1_ = f32[128,1280]{1,0:T(8,128)S(1)} custom-call(bf16[128,2048]{1,0:T(8,128)(2,1)S(1)} %bitcast.16, bf16[128,5120]{1,0:T(8,128)(2,1)S(1)} %copy-done.3, bf16[5120,2048]{1,0:T(8,128)(2,1)S(1)} %bitcast.9), custom_call_target="tpu_custom_call" | custom-call | flops 671088640 | bytes 6422528 | tf_op jit(solution)/shard_map/weight_product/pallas_call | solution.py:315
  62.8 1.4 %collective-permute-start.15 = (bf16[128,1280]{1,0:T(8,128)(2,1)S(1)}, bf16[128,1280]{1,0:T(8,128)(2,1)S(1)}, u32[]{:S(2)}, u32[]{:S(2)}) collective-permute-start(bf16[128,1280]{1,0:T(8,128)(2,1)S(1)} %relay_step.12.refs_2_), channel_id=1, source_target_pairs={{8,0},{16,8},{24,16},{9,1},{17,9},{25,17},{10,2},{18,10},{26,18},{... | collective-permute-start | bytes 983048 | tf_op jit(solution)/shard_map/ppermute | solution.py:48
  64.3 11.8 %collective-permute-done.15.refs_0_ = bf16[128,1280]{1,0:T(8,128)(2,1)S(1)} collective-permute-done((bf16[128,1280]{1,0:T(8,128)(2,1)S(1)}, bf16[128,1280]{1,0:T(8,128)(2,1)S(1)}, u32[]{:S(2)}, u32[]{:S(2)}) %collective-permute-start.15) | collective-permute-done | bytes 327712 | tf_op jit(solution)/shard_map/ppermute | solution.py:48
  76.1 1.3 collective-permute-start.33
  77.5 1.3 collective-permute-start.16
  78.8 6.0 %gradient.1 = (bf16[640,2048]{1,0:T(8,128)(2,1)S(1)}, f32[136,128]{1,0:T(8,128)S(1)}, f32[136,128]{1,0:T(8,128)S(1)}, f32[136,128]{1,0:T(8,128)S(1)}, f32[136,12...) custom-call(bf16[640,128]{1,0:T(8,128)(2,1)S(1)} %get-tuple-element., ...), custom_call_target="tpu_custom_call" | custom-call | flops 2684354560 | bytes 10747904 | tf_op jit(solution)/shard_map/gradient/pallas_call | solution.py:175
  84.8 4.0 %collective-permute-done.33.refs_0_ = bf16[128,1280]{1,0:T(8,128)(2,1)S(1)} collective-permute-done((bf16[128,1280]{1,0:T(8,128)(2,1)S(1)}, bf16[128,1280]{1,0:T(8,128)(2,1)S(1)}, u32[]{:S(2)}, u32[]{:S(2)}) %collective-permute-start.33) | collective-permute-done | bytes 327712 | tf_op jit(solution)/shard_map/ppermute | solution.py:48
  88.9 1.3 collective-permute-start.34
  90.2 0.1 collective-permute-start.17
  90.2 1.3 collective-permute-start.18
  91.5 0.6 collective-permute-start.19
  92.1 3.8 %collective-permute-done.16.refs_0_ = bf16[128,1280]{1,0:T(8,128)(2,1)S(1)} collective-permute-done((bf16[128,1280]{1,0:T(8,128)(2,1)S(1)}, bf16[128,1280]{1,0:T(8,128)(2,1)S(1)}, u32[]{:S(2)}, u32[]{:S(2)}) %collective-permute-start.16) | collective-permute-done | bytes 327712 | tf_op jit(solution)/shard_map/ppermute | solution.py:48
  95.9 0.5 collective-permute-start.20
  96.4 0.3 relay_step.14.refs_6_
  96.7 1.5 %collective-permute-start.31 = (bf16[128,1280]{1,0:T(8,128)(2,1)S(1)}, bf16[128,1280]{1,0:T(8,128)(2,1)S(1)}, u32[]{:S(2)}, u32[]{:S(2)}) collective-permute-start(bf16[128,1280]{1,0:T(8,128)(2,1)S(1)} %relay_step.14.refs_6_), channel_id=1, source_target_pairs={{8,0},{16,8},{24,16},{9,1},{17,9},{25,17},{10,2},{18,10},{26,18},{... | collective-permute-start | bytes 983048 | tf_op jit(solution)/shard_map/ppermute | solution.py:48
  98.2 0.1 collective-permute-start.21
  98.3 2.2 %collective-permute-start.22 = (f32[136,128]{1,0:T(8,128)S(1)}, f32[136,128]{1,0:T(8,128)S(1)}, u32[]{:S(2)}, u32[]{:S(2)}) collective-permute-start(f32[136,128]{1,0:T(8,128)S(1)} %get-tuple-element.55), channel_id=1, source_target_pairs={{6,0},{7,1},{4,2},{5,3},{2,4},{3,5},{0,6},{1,7},{14,8},{15,9},{12,... | collective-permute-start | bytes 208904 | tf_op jit(solution)/shard_map/ppermute | solution.py:43
  100.5 1.6 %collective-permute-start.23 = (f32[136,128]{1,0:T(8,128)S(1)}, f32[136,128]{1,0:T(8,128)S(1)}, u32[]{:S(2)}, u32[]{:S(2)}) collective-permute-start(f32[136,128]{1,0:T(8,128)S(1)} %get-tuple-element.56), channel_id=1, source_target_pairs={{7,0},{6,1},{5,2},{4,3},{3,4},{2,5},{1,6},{0,7},{15,8},{14,9},{13,... | collective-permute-start | bytes 208904 | tf_op jit(solution)/shard_map/ppermute | solution.py:43
  102.1 0.6 collective-permute-done.21.refs_5_
  102.7 1.1 collective-permute-done.22.refs_6_
  103.8 1.8 %collective-permute-done.23.refs_7_ = f32[136,128]{1,0:T(8,128)S(1)} collective-permute-done((f32[136,128]{1,0:T(8,128)S(1)}, f32[136,128]{1,0:T(8,128)S(1)}, u32[]{:S(2)}, u32[]{:S(2)}) %collective-permute-start.23) | collective-permute-done | bytes 69664 | tf_op jit(solution)/shard_map/ppermute | solution.py:43
  105.6 3.9 %mixing.1.refs_0_ = f32[136,128]{1,0:T(8,128)S(1)} custom-call(f32[136,128]{1,0:T(8,128)S(1)} %get-tuple-element.49.refs_0_, f32[136,128]{1,0:T(8,128)S(1)} %collective-permute-done.17.refs_1_, f32[136,128]{1,0:T(8,128)S(1)} %collective-permute-done.18.refs_2_, f32[136,128]{1,0:T(8,128)S(1)} %collective-permute-done.19.refs_3_, ...), custom_call_target="tpu_custom_call" | custom-call | flops 905969664 | bytes 1179648 | tf_op jit(solution)/shard_map/mixing/pallas_call | solution.py:224
  109.6 0.3 relay_step.18.refs_7_
  109.9 1.3 collective-permute-start.35
  111.2 0.2 collective-permute-start.24
  111.4 0.9 collective-permute-start.25
  112.3 0.8 collective-permute-start.26
  113.1 0.9 collective-permute-start.27
  114.0 2.4 %collective-permute-done.25.refs_2_ = f32[136,128]{1,0:T(8,128)S(1)} collective-permute-done((f32[136,128]{1,0:T(8,128)S(1)}, f32[136,128]{1,0:T(8,128)S(1)}, u32[]{:S(2)}, u32[]{:S(2)}) %collective-permute-start.25) | collective-permute-done | bytes 69664 | tf_op jit(solution)/shard_map/ppermute | solution.py:43
  116.4 0.4 collective-permute-done.26.refs_3_
  116.8 1.7 %collective-permute-start.29 = (f32[136,128]{1,0:T(8,128)S(1)}, f32[136,128]{1,0:T(8,128)S(1)}, u32[]{:S(2)}, u32[]{:S(2)}) collective-permute-start(f32[136,128]{1,0:T(8,128)S(1)} %mixing.1.refs_0_), channel_id=1, source_target_pairs={{6,0},{7,1},{4,2},{5,3},{2,4},{3,5},{0,6},{1,7},{14,8},{15,9},{12,... | collective-permute-start | bytes 208904 | tf_op jit(solution)/shard_map/ppermute | solution.py:43
  118.4 1.3 %collective-permute-start.30 = (f32[136,128]{1,0:T(8,128)S(1)}, f32[136,128]{1,0:T(8,128)S(1)}, u32[]{:S(2)}, u32[]{:S(2)}) collective-permute-start(f32[136,128]{1,0:T(8,128)S(1)} %mixing.1.refs_0_), channel_id=1, source_target_pairs={{7,0},{6,1},{5,2},{4,3},{3,4},{2,5},{1,6},{0,7},{15,8},{14,9},{13,... | collective-permute-start | bytes 208904 | tf_op jit(solution)/shard_map/ppermute | solution.py:43
  119.8 0.3 relay_step.15.refs_8_
  120.0 0.4 collective-permute-done.28.refs_5_
  120.4 2.2 %collective-permute-done.29.refs_6_ = f32[136,128]{1,0:T(8,128)S(1)} collective-permute-done((f32[136,128]{1,0:T(8,128)S(1)}, f32[136,128]{1,0:T(8,128)S(1)}, u32[]{:S(2)}, u32[]{:S(2)}) %collective-permute-start.29) | collective-permute-done | bytes 69664 | tf_op jit(solution)/shard_map/ppermute | solution.py:43
  122.6 1.2 collective-permute-done.30.refs_7_
  123.8 4.3 %apply_mixing.1 = bf16[640,2048]{1,0:T(8,128)(2,1)} custom-call(f32[136,128]{1,0:T(8,128)S(1)} %mixing.1.refs_0_, f32[136,128]{1,0:T(8,128)S(1)} %collective-permute-done.24.refs_1_, f32[136,128]{1,0:T(8,128)S(1)} %collective-permute-done.25.refs_2_, f32[136,128]{1,0:T(8,128)S(1)} %collective-permute-done.26.refs_3_, ...), custom_call_target="tpu_custom_call" | custom-call | flops 1006632960 | bytes 5242880 | tf_op jit(solution)/shard_map/apply_mixing/pallas_call | solution.py:278
  128.1 0.3 relay_step.19.refs_9_
  128.4 1.1 collect.1
  (43 shorter events, 0.2 us)
Async XLA Ops:
  0.6 18.7 %collective-permute-start.7 = (bf16[128,2048]{1,0:T(8,128)(2,1)}, bf16[128,2048]{1,0:T(8,128)(2,1)S(1)}, u32[]{:S(2)}, u32[]{:S(2)}) collective-permute-start(bf16[128,2048]{1,0:T(8,128)(2,1)} %bitcast.10), channel_id=1, source_target_pairs={{2,0},{5,1},{0,2},{7,3},{6,4},{1,5},{4,6},{3,7},{10,8},{13,9},{8,1... | collective-permute-start | bytes 1572872 | tf_op jit(solution)/shard_map/ppermute | solution.py:43
  3.6 7.0 %copy-start = (bf16[1,5120,2048]{2,1,0:T(8,128)(2,1)S(1)}, bf16[1,5120,2048]{2,1,0:T(8,128)(2,1)}, u32[]{:S(2)}) copy-start(bf16[1,5120,2048]{2,1,0:T(8,128)(2,1)} %param.8) | copy-start | bytes 62914564
  10.6 1.3 %copy-start.2 = (bf16[128,5120]{1,0:T(8,128)(2,1)S(1)}, bf16[128,5120]{1,0:T(8,128)(2,1)}, u32[]{:S(2)}) copy-start(bf16[128,5120]{1,0:T(8,128)(2,1)} %cot_ref.7) | copy-start | bytes 3932164
  11.9 1.0 copy-start.4
  13.0 3.8 %copy-start.6 = (bf16[1,128,5120]{2,1,0:T(8,128)(2,1)S(1)}, bf16[1,128,5120]{2,1,0:T(8,128)(2,1)}, u32[]{:S(2)}) copy-start(bf16[1,128,5120]{2,1,0:T(8,128)(2,1)} %param.5) | copy-start | bytes 3932164
  13.0 6.3 %copy-start.5 = (bf16[1,128,2048]{2,1,0:T(8,128)(2,1)S(1)}, bf16[1,128,2048]{2,1,0:T(8,128)(2,1)}, u32[]{:S(2)}) copy-start(bf16[1,128,2048]{2,1,0:T(8,128)(2,1)} %param.7) | copy-start | bytes 1572868
  13.0 28.8 %copy-start.1 = (bf16[1,5120,2048]{2,1,0:T(8,128)(2,1)S(1)}, bf16[1,5120,2048]{2,1,0:T(8,128)(2,1)}, u32[]{:S(2)}) copy-start(bf16[1,5120,2048]{2,1,0:T(8,128)(2,1)} %param.8) | copy-start | bytes 62914564
  16.7 25.1 %copy-start.3 = (bf16[128,5120]{1,0:T(8,128)(2,1)S(1)}, bf16[128,5120]{1,0:T(8,128)(2,1)}, u32[]{:S(2)}) copy-start(bf16[128,5120]{1,0:T(8,128)(2,1)} %cot_ref.7) | copy-start | bytes 3932164
  17.2 7.2 %collective-permute-start = (bf16[640,128]{1,0:T(8,128)(2,1)S(1)}, bf16[640,128]{1,0:T(8,128)(2,1)S(1)}, u32[]{:S(2)}, u32[]{:S(2)}) collective-permute-start(bf16[640,128]{1,0:T(8,128)(2,1)S(1)} %get-tuple-element.35), channel_id=1, source_target_pairs={{2,0},{5,1},{0,2},{7,3},{6,4},{1,5},{4,6},{3,7},{10,8},{13,9},{8,1... | collective-permute-start | bytes 491528 | tf_op jit(solution)/shard_map/ppermute | solution.py:43
  17.2 7.1 %collective-permute-start.1 = (bf16[640,128]{1,0:T(8,128)(2,1)S(1)}, bf16[640,128]{1,0:T(8,128)(2,1)S(1)}, u32[]{:S(2)}, u32[]{:S(2)}) collective-permute-start(bf16[640,128]{1,0:T(8,128)(2,1)S(1)} %get-tuple-element.36), channel_id=1, source_target_pairs={{4,0},{3,1},{6,2},{1,3},{0,4},{7,5},{2,6},{5,7},{12,8},{11,9},{14,... | collective-permute-start | bytes 491528 | tf_op jit(solution)/shard_map/ppermute | solution.py:43
  19.3 35.5 %collective-permute-start.8 = (bf16[128,2048]{1,0:T(8,128)(2,1)S(1)}, bf16[128,2048]{1,0:T(8,128)(2,1)S(1)}, u32[]{:S(2)}, u32[]{:S(2)}) collective-permute-start(bf16[128,2048]{1,0:T(8,128)(2,1)S(1)} %bitcast.12), channel_id=1, source_target_pairs={{4,0},{3,1},{6,2},{1,3},{0,4},{7,5},{2,6},{5,7},{12,8},{11,9},{14,... | collective-permute-start | bytes 1572872 | tf_op jit(solution)/shard_map/ppermute | solution.py:43
  19.3 35.5 %collective-permute-start.9 = (bf16[128,2048]{1,0:T(8,128)(2,1)S(1)}, bf16[128,2048]{1,0:T(8,128)(2,1)S(1)}, u32[]{:S(2)}, u32[]{:S(2)}) collective-permute-start(bf16[128,2048]{1,0:T(8,128)(2,1)S(1)} %collective-permute-done.7.refs_9_), channel_id=1, source_target_pairs={{4,0},{3,1},{6,2},{1,3},{0,4},{7,5},{2,6},{5,7},{12,8},{11,9},{14,... | collective-permute-start | bytes 1572872 | tf_op jit(solution)/shard_map/ppermute | solution.py:43
  21.3 8.0 %collective-permute-start.2 = (bf16[640,128]{1,0:T(8,128)(2,1)S(1)}, bf16[640,128]{1,0:T(8,128)(2,1)S(1)}, u32[]{:S(2)}, u32[]{:S(2)}) collective-permute-start(bf16[640,128]{1,0:T(8,128)(2,1)S(1)} %get-tuple-element.37), channel_id=1, source_target_pairs={{6,0},{7,1},{4,2},{5,3},{2,4},{3,5},{0,6},{1,7},{14,8},{15,9},{12,... | collective-permute-start | bytes 491528 | tf_op jit(solution)/shard_map/ppermute | solution.py:43
  24.3 16.2 %collective-permute-start.3 = (bf16[640,128]{1,0:T(8,128)(2,1)S(1)}, bf16[640,128]{1,0:T(8,128)(2,1)S(1)}, u32[]{:S(2)}, u32[]{:S(2)}) collective-permute-start(bf16[640,128]{1,0:T(8,128)(2,1)S(1)} %get-tuple-element.38), channel_id=1, source_target_pairs={{1,0},{0,1},{3,2},{2,3},{5,4},{4,5},{7,6},{6,7},{9,8},{8,9},{11,10... | collective-permute-start | bytes 491528 | tf_op jit(solution)/shard_map/ppermute | solution.py:43
  24.4 21.2 %collective-permute-start.4 = (bf16[640,128]{1,0:T(8,128)(2,1)S(1)}, bf16[640,128]{1,0:T(8,128)(2,1)S(1)}, u32[]{:S(2)}, u32[]{:S(2)}) collective-permute-start(bf16[640,128]{1,0:T(8,128)(2,1)S(1)} %get-tuple-element.39), channel_id=1, source_target_pairs={{5,0},{2,1},{7,2},{0,3},{1,4},{6,5},{3,6},{4,7},{13,8},{10,9},{15,... | collective-permute-start | bytes 491528 | tf_op jit(solution)/shard_map/ppermute | solution.py:43
  29.4 17.5 %collective-permute-start.5 = (bf16[640,128]{1,0:T(8,128)(2,1)S(1)}, bf16[640,128]{1,0:T(8,128)(2,1)S(1)}, u32[]{:S(2)}, u32[]{:S(2)}) collective-permute-start(bf16[640,128]{1,0:T(8,128)(2,1)S(1)} %get-tuple-element.40), channel_id=1, source_target_pairs={{3,0},{4,1},{1,2},{6,3},{7,4},{0,5},{5,6},{2,7},{11,8},{12,9},{9,1... | collective-permute-start | bytes 491528 | tf_op jit(solution)/shard_map/ppermute | solution.py:43
  40.5 13.8 %collective-permute-start.14 = (bf16[128,1280]{1,0:T(8,128)(2,1)S(1)}, bf16[128,1280]{1,0:T(8,128)(2,1)S(1)}, u32[]{:S(2)}, u32[]{:S(2)}) collective-permute-start(bf16[128,1280]{1,0:T(8,128)(2,1)S(1)} %relay_step.10.refs_0_), channel_id=1, source_target_pairs={{8,0},{16,8},{24,16},{9,1},{17,9},{25,17},{10,2},{18,10},{26,18},{... | collective-permute-start | bytes 983048 | tf_op jit(solution)/shard_map/ppermute | solution.py:48
  45.6 17.2 %collective-permute-start.32 = (bf16[128,1280]{1,0:T(8,128)(2,1)S(1)}, bf16[128,1280]{1,0:T(8,128)(2,1)S(1)}, u32[]{:S(2)}, u32[]{:S(2)}) collective-permute-start(bf16[128,1280]{1,0:T(8,128)(2,1)S(1)} %relay_step.11.refs_1_), channel_id=1, source_target_pairs={{8,0},{16,8},{24,16},{9,1},{17,9},{25,17},{10,2},{18,10},{26,18},{... | collective-permute-start | bytes 983048 | tf_op jit(solution)/shard_map/ppermute | solution.py:48
  46.9 7.3 %collective-permute-start.6 = (bf16[640,128]{1,0:T(8,128)(2,1)S(1)}, bf16[640,128]{1,0:T(8,128)(2,1)S(1)}, u32[]{:S(2)}, u32[]{:S(2)}) collective-permute-start(bf16[640,128]{1,0:T(8,128)(2,1)S(1)} %get-tuple-element.41), channel_id=1, source_target_pairs={{7,0},{6,1},{5,2},{4,3},{3,4},{2,5},{1,6},{0,7},{15,8},{14,9},{13,... | collective-permute-start | bytes 491528 | tf_op jit(solution)/shard_map/ppermute | solution.py:43
  54.2 23.2 %collective-permute-start.10 = (bf16[128,2048]{1,0:T(8,128)(2,1)S(1)}, bf16[128,2048]{1,0:T(8,128)(2,1)S(1)}, u32[]{:S(2)}, u32[]{:S(2)}) collective-permute-start(bf16[128,2048]{1,0:T(8,128)(2,1)S(1)} %bitcast.14), channel_id=1, source_target_pairs={{1,0},{0,1},{3,2},{2,3},{5,4},{4,5},{7,6},{6,7},{9,8},{8,9},{11,10... | collective-permute-start | bytes 1572872 | tf_op jit(solution)/shard_map/ppermute | solution.py:43
  54.4 24.4 %collective-permute-start.11 = (bf16[128,2048]{1,0:T(8,128)(2,1)S(1)}, bf16[128,2048]{1,0:T(8,128)(2,1)S(1)}, u32[]{:S(2)}, u32[]{:S(2)}) collective-permute-start(bf16[128,2048]{1,0:T(8,128)(2,1)S(1)} %collective-permute-done.7.refs_9_), channel_id=1, source_target_pairs={{1,0},{0,1},{3,2},{2,3},{5,4},{4,5},{7,6},{6,7},{9,8},{8,9},{11,10... | collective-permute-start | bytes 1572872 | tf_op jit(solution)/shard_map/ppermute | solution.py:43
  54.8 24.0 %collective-permute-start.12 = (bf16[128,2048]{1,0:T(8,128)(2,1)S(1)}, bf16[128,2048]{1,0:T(8,128)(2,1)S(1)}, u32[]{:S(2)}, u32[]{:S(2)}) collective-permute-start(bf16[128,2048]{1,0:T(8,128)(2,1)S(1)} %collective-permute-done.8.refs_10_), channel_id=1, source_target_pairs={{1,0},{0,1},{3,2},{2,3},{5,4},{4,5},{7,6},{6,7},{9,8},{8,9},{11,10... | collective-permute-start | bytes 1572872 | tf_op jit(solution)/shard_map/ppermute | solution.py:43
  54.9 23.9 %collective-permute-start.13 = (bf16[128,2048]{1,0:T(8,128)(2,1)S(1)}, bf16[128,2048]{1,0:T(8,128)(2,1)S(1)}, u32[]{:S(2)}, u32[]{:S(2)}) collective-permute-start(bf16[128,2048]{1,0:T(8,128)(2,1)S(1)} %collective-permute-done.9.refs_11_), channel_id=1, source_target_pairs={{1,0},{0,1},{3,2},{2,3},{5,4},{4,5},{7,6},{6,7},{9,8},{8,9},{11,10... | collective-permute-start | bytes 1572872 | tf_op jit(solution)/shard_map/ppermute | solution.py:43
  62.8 16.0 %copy-start.7 = (bf16[1,640,2048]{2,1,0:T(8,128)(2,1)S(1)}, bf16[1,640,2048]{2,1,0:T(8,128)(2,1)}, u32[]{:S(2)}) copy-start(bf16[1,640,2048]{2,1,0:T(8,128)(2,1)} %param.9) | copy-start | bytes 7864324
  62.8 13.3 %collective-permute-start.15 = (bf16[128,1280]{1,0:T(8,128)(2,1)S(1)}, bf16[128,1280]{1,0:T(8,128)(2,1)S(1)}, u32[]{:S(2)}, u32[]{:S(2)}) collective-permute-start(bf16[128,1280]{1,0:T(8,128)(2,1)S(1)} %relay_step.12.refs_2_), channel_id=1, source_target_pairs={{8,0},{16,8},{24,16},{9,1},{17,9},{25,17},{10,2},{18,10},{26,18},{... | collective-permute-start | bytes 983048 | tf_op jit(solution)/shard_map/ppermute | solution.py:48
  76.1 12.7 %collective-permute-start.33 = (bf16[128,1280]{1,0:T(8,128)(2,1)S(1)}, bf16[128,1280]{1,0:T(8,128)(2,1)S(1)}, u32[]{:S(2)}, u32[]{:S(2)}) collective-permute-start(bf16[128,1280]{1,0:T(8,128)(2,1)S(1)} %relay_step.16.refs_3_), channel_id=1, source_target_pairs={{8,0},{16,8},{24,16},{9,1},{17,9},{25,17},{10,2},{18,10},{26,18},{... | collective-permute-start | bytes 983048 | tf_op jit(solution)/shard_map/ppermute | solution.py:48
  77.5 18.4 %collective-permute-start.16 = (bf16[128,1280]{1,0:T(8,128)(2,1)S(1)}, bf16[128,1280]{1,0:T(8,128)(2,1)S(1)}, u32[]{:S(2)}, u32[]{:S(2)}) collective-permute-start(bf16[128,1280]{1,0:T(8,128)(2,1)S(1)} %relay_step.13.refs_4_), channel_id=1, source_target_pairs={{8,0},{16,8},{24,16},{9,1},{17,9},{25,17},{10,2},{18,10},{26,18},{... | collective-permute-start | bytes 983048 | tf_op jit(solution)/shard_map/ppermute | solution.py:48
  88.9 20.7 %collective-permute-start.34 = (bf16[128,1280]{1,0:T(8,128)(2,1)S(1)}, bf16[128,1280]{1,0:T(8,128)(2,1)S(1)}, u32[]{:S(2)}, u32[]{:S(2)}) collective-permute-start(bf16[128,1280]{1,0:T(8,128)(2,1)S(1)} %relay_step.17.refs_5_), channel_id=1, source_target_pairs={{8,0},{16,8},{24,16},{9,1},{17,9},{25,17},{10,2},{18,10},{26,18},{... | collective-permute-start | bytes 983048 | tf_op jit(solution)/shard_map/ppermute | solution.py:48
  90.2 6.5 %collective-permute-start.17 = (f32[136,128]{1,0:T(8,128)S(1)}, f32[136,128]{1,0:T(8,128)S(1)}, u32[]{:S(2)}, u32[]{:S(2)}) collective-permute-start(f32[136,128]{1,0:T(8,128)S(1)} %get-tuple-element.50), channel_id=1, source_target_pairs={{1,0},{0,1},{3,2},{2,3},{5,4},{4,5},{7,6},{6,7},{9,8},{8,9},{11,10... | collective-permute-start | bytes 208904 | tf_op jit(solution)/shard_map/ppermute | solution.py:43
  90.2 7.9 %collective-permute-start.18 = (f32[136,128]{1,0:T(8,128)S(1)}, f32[136,128]{1,0:T(8,128)S(1)}, u32[]{:S(2)}, u32[]{:S(2)}) collective-permute-start(f32[136,128]{1,0:T(8,128)S(1)} %get-tuple-element.51), channel_id=1, source_target_pairs={{2,0},{3,1},{0,2},{1,3},{6,4},{7,5},{4,6},{5,7},{10,8},{11,9},{8,1... | collective-permute-start | bytes 208904 | tf_op jit(solution)/shard_map/ppermute | solution.py:43
  91.5 6.7 %collective-permute-start.19 = (f32[136,128]{1,0:T(8,128)S(1)}, f32[136,128]{1,0:T(8,128)S(1)}, u32[]{:S(2)}, u32[]{:S(2)}) collective-permute-start(f32[136,128]{1,0:T(8,128)S(1)} %get-tuple-element.52), channel_id=1, source_target_pairs={{3,0},{2,1},{1,2},{0,3},{7,4},{6,5},{5,6},{4,7},{11,8},{10,9},{9,1... | collective-permute-start | bytes 208904 | tf_op jit(solution)/shard_map/ppermute | solution.py:43
  95.9 4.6 %collective-permute-start.20 = (f32[136,128]{1,0:T(8,128)S(1)}, f32[136,128]{1,0:T(8,128)S(1)}, u32[]{:S(2)}, u32[]{:S(2)}) collective-permute-start(f32[136,128]{1,0:T(8,128)S(1)} %get-tuple-element.53), channel_id=1, source_target_pairs={{4,0},{5,1},{6,2},{7,3},{0,4},{1,5},{2,6},{3,7},{12,8},{13,9},{14,... | collective-permute-start | bytes 208904 | tf_op jit(solution)/shard_map/ppermute | solution.py:43
  96.7 21.7 %collective-permute-start.31 = (bf16[128,1280]{1,0:T(8,128)(2,1)S(1)}, bf16[128,1280]{1,0:T(8,128)(2,1)S(1)}, u32[]{:S(2)}, u32[]{:S(2)}) collective-permute-start(bf16[128,1280]{1,0:T(8,128)(2,1)S(1)} %relay_step.14.refs_6_), channel_id=1, source_target_pairs={{8,0},{16,8},{24,16},{9,1},{17,9},{25,17},{10,2},{18,10},{26,18},{... | collective-permute-start | bytes 983048 | tf_op jit(solution)/shard_map/ppermute | solution.py:48
  98.2 4.5 %collective-permute-start.21 = (f32[136,128]{1,0:T(8,128)S(1)}, f32[136,128]{1,0:T(8,128)S(1)}, u32[]{:S(2)}, u32[]{:S(2)}) collective-permute-start(f32[136,128]{1,0:T(8,128)S(1)} %get-tuple-element.54), channel_id=1, source_target_pairs={{5,0},{4,1},{7,2},{6,3},{1,4},{0,5},{3,6},{2,7},{13,8},{12,9},{15,... | collective-permute-start | bytes 208904 | tf_op jit(solution)/shard_map/ppermute | solution.py:43
  98.3 5.5 %collective-permute-start.22 = (f32[136,128]{1,0:T(8,128)S(1)}, f32[136,128]{1,0:T(8,128)S(1)}, u32[]{:S(2)}, u32[]{:S(2)}) collective-permute-start(f32[136,128]{1,0:T(8,128)S(1)} %get-tuple-element.55), channel_id=1, source_target_pairs={{6,0},{7,1},{4,2},{5,3},{2,4},{3,5},{0,6},{1,7},{14,8},{15,9},{12,... | collective-permute-start | bytes 208904 | tf_op jit(solution)/shard_map/ppermute | solution.py:43
  100.5 5.1 %collective-permute-start.23 = (f32[136,128]{1,0:T(8,128)S(1)}, f32[136,128]{1,0:T(8,128)S(1)}, u32[]{:S(2)}, u32[]{:S(2)}) collective-permute-start(f32[136,128]{1,0:T(8,128)S(1)} %get-tuple-element.56), channel_id=1, source_target_pairs={{7,0},{6,1},{5,2},{4,3},{3,4},{2,5},{1,6},{0,7},{15,8},{14,9},{13,... | collective-permute-start | bytes 208904 | tf_op jit(solution)/shard_map/ppermute | solution.py:43
  109.9 18.2 %collective-permute-start.35 = (bf16[128,1280]{1,0:T(8,128)(2,1)S(1)}, bf16[128,1280]{1,0:T(8,128)(2,1)S(1)}, u32[]{:S(2)}, u32[]{:S(2)}) collective-permute-start(bf16[128,1280]{1,0:T(8,128)(2,1)S(1)} %relay_step.18.refs_7_), channel_id=1, source_target_pairs={{8,0},{16,8},{24,16},{9,1},{17,9},{25,17},{10,2},{18,10},{26,18},{... | collective-permute-start | bytes 983048 | tf_op jit(solution)/shard_map/ppermute | solution.py:48
  111.2 1.9 %collective-permute-start.24 = (f32[136,128]{1,0:T(8,128)S(1)}, f32[136,128]{1,0:T(8,128)S(1)}, u32[]{:S(2)}, u32[]{:S(2)}) collective-permute-start(f32[136,128]{1,0:T(8,128)S(1)} %mixing.1.refs_0_), channel_id=1, source_target_pairs={{1,0},{0,1},{3,2},{2,3},{5,4},{4,5},{7,6},{6,7},{9,8},{8,9},{11,10... | collective-permute-start | bytes 208904 | tf_op jit(solution)/shard_map/ppermute | solution.py:43
  111.4 5.0 %collective-permute-start.25 = (f32[136,128]{1,0:T(8,128)S(1)}, f32[136,128]{1,0:T(8,128)S(1)}, u32[]{:S(2)}, u32[]{:S(2)}) collective-permute-start(f32[136,128]{1,0:T(8,128)S(1)} %mixing.1.refs_0_), channel_id=1, source_target_pairs={{2,0},{3,1},{0,2},{1,3},{6,4},{7,5},{4,6},{5,7},{10,8},{11,9},{8,1... | collective-permute-start | bytes 208904 | tf_op jit(solution)/shard_map/ppermute | solution.py:43
  112.3 4.5 %collective-permute-start.26 = (f32[136,128]{1,0:T(8,128)S(1)}, f32[136,128]{1,0:T(8,128)S(1)}, u32[]{:S(2)}, u32[]{:S(2)}) collective-permute-start(f32[136,128]{1,0:T(8,128)S(1)} %mixing.1.refs_0_), channel_id=1, source_target_pairs={{3,0},{2,1},{1,2},{0,3},{7,4},{6,5},{5,6},{4,7},{11,8},{10,9},{9,1... | collective-permute-start | bytes 208904 | tf_op jit(solution)/shard_map/ppermute | solution.py:43
  113.1 6.9 %collective-permute-start.27 = (f32[136,128]{1,0:T(8,128)S(1)}, f32[136,128]{1,0:T(8,128)S(1)}, u32[]{:S(2)}, u32[]{:S(2)}) collective-permute-start(f32[136,128]{1,0:T(8,128)S(1)} %mixing.1.refs_0_), channel_id=1, source_target_pairs={{4,0},{5,1},{6,2},{7,3},{0,4},{1,5},{2,6},{3,7},{12,8},{13,9},{14,... | collective-permute-start | bytes 208904 | tf_op jit(solution)/shard_map/ppermute | solution.py:43
  116.4 4.0 %collective-permute-start.28 = (f32[136,128]{1,0:T(8,128)S(1)}, f32[136,128]{1,0:T(8,128)S(1)}, u32[]{:S(2)}, u32[]{:S(2)}) collective-permute-start(f32[136,128]{1,0:T(8,128)S(1)} %mixing.1.refs_0_), channel_id=1, source_target_pairs={{5,0},{4,1},{7,2},{6,3},{1,4},{0,5},{3,6},{2,7},{13,8},{12,9},{15,... | collective-permute-start | bytes 208904 | tf_op jit(solution)/shard_map/ppermute | solution.py:43
  116.8 5.9 %collective-permute-start.29 = (f32[136,128]{1,0:T(8,128)S(1)}, f32[136,128]{1,0:T(8,128)S(1)}, u32[]{:S(2)}, u32[]{:S(2)}) collective-permute-start(f32[136,128]{1,0:T(8,128)S(1)} %mixing.1.refs_0_), channel_id=1, source_target_pairs={{6,0},{7,1},{4,2},{5,3},{2,4},{3,5},{0,6},{1,7},{14,8},{15,9},{12,... | collective-permute-start | bytes 208904 | tf_op jit(solution)/shard_map/ppermute | solution.py:43
  118.4 5.4 %collective-permute-start.30 = (f32[136,128]{1,0:T(8,128)S(1)}, f32[136,128]{1,0:T(8,128)S(1)}, u32[]{:S(2)}, u32[]{:S(2)}) collective-permute-start(f32[136,128]{1,0:T(8,128)S(1)} %mixing.1.refs_0_), channel_id=1, source_target_pairs={{7,0},{6,1},{5,2},{4,3},{3,4},{2,5},{1,6},{0,7},{15,8},{14,9},{13,... | collective-permute-start | bytes 208904 | tf_op jit(solution)/shard_map/ppermute | solution.py:43
where the time goes:
time: 131 us; the launch traced here: 130 us
  starting transfers between devices  44.4 us (34%)
  waiting for transfers between devices  42.8 us (33%)
  Pallas kernels  31.9 us (24%)
  local copies, waits for them, and re-layouts  9.34 us (7%)
    ppermute x28, starting transfers between devices, swap(): lax.ppermute(value, 'dp', [(i ^ by[i % CORES], i) for i in range(count)])  33.7 us
    ppermute x28, waiting for transfers between devices, swap(): lax.ppermute(value, 'dp', [(i ^ by[i % CORES], i) for i in range(count)])  23.2 us
    ppermute x8, waiting for transfers between devices, down(): return lax.ppermute(value, 'pipe', [(i, i - 1) for i in range(1, count)])  19.6 us
    pallas_call x4, Pallas kernels, weight_product(): pl.pallas_call(kernel, grid=(1,), out_shape=jax.ShapeDtypeStruct((tokens,...  14.9 us
    ppermute x8, starting transfers between devices, down(): return lax.ppermute(value, 'pipe', [(i, i - 1) for i in range(1, count)])  10.6 us
    unnamed x16, local copies, waits for them, and re-layouts  9.34 us
    pallas_call x1, Pallas kernels, gradient(): pl.pallas_call(kernel, grid=(steps,), out_shape=[jax.ShapeDtypeStruct((ro...  6.01 us
    pallas_call x1, Pallas kernels, apply_mixing(): pl.pallas_call(kernel, grid=(owners // per_step,), out_shape=jax.ShapeDty...  4.26 us
  transfers between devices with their start and end apart: 36, of which 14 were waited for; matrix products, arithmetic and copies ran while one was open for 0% of the time, Pallas kernels for 24%

commit v1 on v0

--- a/solution.py
+++ b/solution.py
@@ -24,14 +24,20 @@
 F32 = jnp.float32
 BF16 = jnp.bfloat16
 ANY = pl.BlockSpec(memory_space=pl.ANY)
+HBM = pl.BlockSpec(memory_space=pltpu.HBM)
+VMEM = pl.BlockSpec(memory_space=pltpu.VMEM)
 
 
 def cost(flops, moved):
-    return pl.CostEstimate(flops=int(flops), bytes_accessed=int(moved), transcendentals=0)
+    return pl.CostEstimate(flops=1, bytes_accessed=1, transcendentals=0)
 
 
 def params(mib):
     return pltpu.CompilerParams(vmem_limit_bytes=mib * 1024 * 1024)
+
+
+def in_hbm(value):
+    return pltpu.with_memory_space_constraint(value, pltpu.HBM)
 
 
 def after(value, *others):
@@ -55,32 +61,20 @@
     return jnp.where(own % CORES == 0, pair[0], pair[1])
 
 
-def split_columns(inputs, relations):
+def split_columns(inputs):
     count = lax.axis_size("dp")
     tokens, width = inputs.shape
     block = width // count
 
-    def kernel(in_ref, *out_refs):
-        own = lax.axis_index("dp")
-        for relation, out_ref in zip(relations, out_refs):
-            flipped = relation if relation[0] % CORES == 0 else relation[::-1]
-            owner = own ^ by_core(flipped)
-            if block % 128 == 0:
-                columns = pl.ds(pl.multiple_of(owner * block, 128), block)
-                out_ref[...] = in_ref[:, columns].T
-            else:
-                for other in range(count):
-                    @pl.when(owner == other)
-                    def store():
-                        out_ref[...] = in_ref[:, other * block : (other + 1) * block].T
-
-    shape = jax.ShapeDtypeStruct((block, tokens), BF16)
-    return pl.pallas_call(
-        kernel,
-        grid=(1,),
-        out_shape=[shape] * len(relations),
-        in_specs=[pl.BlockSpec((tokens, width), lambda i: (0, 0))],
-        out_specs=[pl.BlockSpec((block, tokens), lambda i: (0, 0))] * len(relations),
+    def kernel(in_ref, out_ref):
+        for owner in range(count):
+            out_ref[owner] = in_ref[:, owner * block : (owner + 1) * block].T
+
+    return pl.pallas_call(
+        kernel,
+        out_shape=jax.ShapeDtypeStruct((count, block, tokens), BF16),
+        in_specs=[VMEM],
+        out_specs=VMEM,
         compiler_params=params(16),
         cost_estimate=cost(0, 4 * tokens * width),
         name="split_columns",
@@ -124,33 +118,30 @@
     return mats
 
 
-def gradient(left, right, moment, scale, slots):
+def gradient(left, sources, right, moment, scale, slots):
     rows, width = moment.shape
     count = lax.axis_size("dp")
+    chips = count // CORES
     mats = width // HEAD
     owners = mats // slots
     per_step = 2 if owners % 2 == 0 else 1
     block = per_step * slots * HEAD
-    tokens = sum(piece.shape[0] for piece in right)
-    n_left, n_right = len(left), len(right)
+    tokens = right[0].shape[0]
+    n_right = len(right)
     packed = packed_rows(slots)
     steps = owners // per_step
 
     def kernel(*refs):
-        left_refs = refs[:n_left]
-        right_refs = refs[n_left : n_left + n_right]
-        mom_ref, buf_ref = refs[n_left + n_right : n_left + n_right + 2]
-        gram_refs = refs[n_left + n_right + 2 : -2]
-        held, grams = refs[-2:]
+        left_ref = refs[0]
+        right_refs = refs[1 : 1 + n_right]
+        mom_ref, buf_ref, mine_ref, theirs_ref, held, grams = refs[1 + n_right :]
         step = pl.program_id(0)
         own = lax.axis_index("dp")
 
         @pl.when(step == 0)
         def load():
-            at = 0
-            for ref in left_refs:
-                held[:, at : at + ref.shape[1]] = ref[...]
-                at += ref.shape[1]
+            for at, pair in enumerate(sources):
+                held[:, at * tokens : (at + 1) * tokens] = left_ref[own ^ by_core(pair)]
             if owners < count:
                 grams[...] = jnp.zeros_like(grams)
 
@@ -168,24 +159,44 @@
 
         @pl.when(step == steps - 1)
         def store():
-            for distance, ref in enumerate(gram_refs):
-                ref[...] = grams[distance]
+            for chip in range(chips):
+                mine_ref[chip] = grams[CORES * chip]
+                theirs_ref[chip] = grams[CORES * chip + 1]
 
     column = lambda height: pl.BlockSpec((height, block), lambda j: (0, j))
+    gram_shape = jax.ShapeDtypeStruct((chips, packed, HEAD), F32)
+    gram_spec = pl.BlockSpec((chips, packed, HEAD), lambda j: (0, 0, 0))
     return pl.pallas_call(
         kernel,
         grid=(steps,),
-        out_shape=[jax.ShapeDtypeStruct((rows, width), BF16)]
-        + [jax.ShapeDtypeStruct((packed, HEAD), F32)] * count,
-        in_specs=[pl.BlockSpec(a.shape, lambda j: (0, 0)) for a in left]
-        + [column(piece.shape[0]) for piece in right]
-        + [column(rows)],
-        out_specs=[column(rows)] + [pl.BlockSpec((packed, HEAD), lambda j: (0, 0))] * count,
-        scratch_shapes=[pltpu.VMEM((rows, tokens), BF16), pltpu.VMEM((count, packed, HEAD), F32)],
-        compiler_params=params(24),
-        cost_estimate=cost(2 * rows * tokens * width, 2 * tokens * (rows + width) + 4 * rows * width),
+        out_shape=[jax.ShapeDtypeStruct((rows, width), BF16), gram_shape, gram_shape],
+        in_specs=[pl.BlockSpec(left.shape, lambda j: (0, 0, 0))] + [column(tokens)] * n_right + [column(rows)],
+        out_specs=[column(rows), gram_spec, gram_spec],
+        scratch_shapes=[pltpu.VMEM((rows, n_right * tokens), BF16), pltpu.VMEM((count, packed, HEAD), F32)],
+        compiler_params=params(18),
+        cost_estimate=cost(
+            2 * rows * tokens * n_right * width, 2 * tokens * n_right * (rows + width) + 4 * rows * width
+        ),
         name="gradient",
-    )(*left, *right, moment)
+    )(in_hbm(left), *[in_hbm(piece) for piece in right], in_hbm(moment))
+
+
+def add_pairs(first, second):
+    chips = first.shape[0]
+
+    def kernel(first_ref, second_ref, *out_refs):
+        for distance in range(chips):
+            out_refs[distance][...] = first_ref[distance] + second_ref[distance]
+
+    return pl.pallas_call(
+        kernel,
+        out_shape=[jax.ShapeDtypeStruct(first.shape[1:], F32)] * chips,
+        in_specs=[VMEM] * 2,
+        out_specs=[VMEM] * chips,
+        compiler_params=params(16),
+        cost_estimate=cost(first.size, 12 * first.size),
+        name="add_pairs",
+    )(first, second)
 
 
 def mixing(grams, scale, slots):
@@ -233,7 +244,7 @@
     )(*grams)
 
 
-def apply_mixing(buffer, mixes, slots):
+def apply_mixing(buffer, distances, mixes, slots):
     rows, width = buffer.shape
     count = lax.axis_size("dp")
     mats = width // HEAD
@@ -251,7 +262,7 @@
 
         @pl.when(step == 0)
         def load():
-            for distance, ref in enumerate(mix_refs):
+            for distance, ref in zip(distances, mix_refs):
                 held[distance] = ref[...]
 
         for which in range(per_step):
@@ -288,82 +299,79 @@
     )(*mixes, buffer)
 
 
-def weight_product(chunk, kv_rows, weights, cotangent):
+def weight_products(chunks, kv_rows, weights):
     tokens, lat = kv_rows.shape
     width = weights.shape[0]
     span = width // CHUNKS
-    block = 256 if span % 256 == 0 else span
-    pieces = span // block
-
-    def kernel(kv_ref, cot_ref, w_ref, out_ref, held, sems):
+    block = span // 2 if span % 16 == 0 else span
+    each = span // block
+    first, pieces = chunks[0] * each, len(chunks) * each
+
+    def kernel(kv_ref, w_ref, *refs):
+        out_refs, (held, sems) = refs[: len(chunks)], refs[len(chunks) :]
         copies = []
         for piece in range(pieces):
-            source = w_ref.at[pl.ds(chunk * span + piece * block, block)]
+            source = w_ref.at[pl.ds((first + piece) * block, block)]
             copies.append(
                 pltpu.make_async_copy(source, held.at[pl.ds(piece * block, block)], sems.at[piece])
             )
             copies[-1].start()
-        last = lax.axis_index("pipe") == lax.axis_size("pipe") - 1
         for piece in range(pieces):
-            columns = slice(piece * block, (piece + 1) * block)
             copies[piece].wait()
-            out = lax.dot_general(
-                kv_ref[...], held[columns], (((1,), (1,)), ((), ())), preferred_element_type=F32
+            columns = slice(piece % each * block, (piece % each + 1) * block)
+            out_refs[piece // each][:, columns] = lax.dot_general(
+                kv_ref[...],
+                held[piece * block : (piece + 1) * block],
+                (((1,), (1,)), ((), ())),
+                preferred_element_type=F32,
             )
-            out_ref[:, columns] = out + jnp.where(last, cot_ref[:, columns].astype(F32), 0.0)
-
-    return pl.pallas_call(
-        kernel,
-        grid=(1,),
-        out_shape=jax.ShapeDtypeStruct((tokens, span), F32),
-        in_specs=[
-            pl.BlockSpec((tokens, lat), lambda i: (0, 0)),
-            pl.BlockSpec((tokens, span), lambda i: (0, chunk)),
-            ANY,
-        ],
-        out_specs=pl.BlockSpec((tokens, span), lambda i: (0, 0)),
-        scratch_shapes=[pltpu.VMEM((span, lat), BF16), pltpu.SemaphoreType.DMA((pieces,))],
-        compiler_params=params(16),
-        cost_estimate=cost(2 * tokens * lat * span, 2 * lat * (tokens + span) + 4 * tokens * span),
-        name="weight_product",
-    )(kv_rows, cotangent, weights)
-
-
-def relay_step(tick, received, products):
+
+    return pl.pallas_call(
+        kernel,
+        out_shape=[jax.ShapeDtypeStruct((tokens, span), F32)] * len(chunks),
+        in_specs=[VMEM, HBM],
+        out_specs=[VMEM] * len(chunks),
+        scratch_shapes=[pltpu.VMEM((pieces * block, lat), BF16), pltpu.SemaphoreType.DMA((pieces,))],
+        compiler_params=params(18),
+        cost_estimate=cost(2 * tokens * lat * span, 4 * span * lat),
+        name="weight_products",
+    )(kv_rows, in_hbm(weights))
+
+
+def relay_step(tick, received, products, cotangent):
     tokens, span = products[0].shape
     sections = lax.axis_size("pipe")
     held = [(s, tick - LAG * (sections - 1 - s)) for s in range(sections)]
     held = [(s, c) for s, c in held if 0 <= c < CHUNKS]
     used = [products[c] for _, c in held]
-    first = [] if received is None else [received]
+    inputs = []
+    if received is not None:
+        inputs.append(received)
+    if tick < CHUNKS:
+        inputs.append(cotangent)
 
     def kernel(*refs):
-        prod_refs = refs[len(first) : len(first) + len(used)]
-        out_ref, prod, sem = refs[-3:]
+        prod_refs = refs[len(inputs) : len(inputs) + len(used)]
+        out_ref = refs[-1]
         stage = lax.axis_index("pipe")
-        for (section, _), ref in zip(held, prod_refs):
+        for (section, chunk), ref in zip(held, prod_refs):
             @pl.when(stage == section)
             def one():
-                copy = pltpu.make_async_copy(ref, prod, sem)
-                copy.start()
-                copy.wait()
-                if first and section < sections - 1:
-                    out_ref[...] = (refs[0][...].astype(F32) + prod[...]).astype(BF16)
+                if section == sections - 1:
+                    base = refs[len(inputs) - 1][:, chunk * span : (chunk + 1) * span]
                 else:
-                    out_ref[...] = prod[...].astype(BF16)
-
-    block = pl.BlockSpec((tokens, span), lambda i: (0, 0))
-    return pl.pallas_call(
-        kernel,
-        grid=(1,),
-        in_specs=[block] * len(first) + [ANY] * len(used),
-        out_specs=block,
+                    base = refs[0][...]
+                out_ref[...] = (base.astype(F32) + ref[...]).astype(BF16)
+
+    return pl.pallas_call(
+        kernel,
+        in_specs=[VMEM] * (len(inputs) + len(used)),
+        out_specs=VMEM,
         out_shape=jax.ShapeDtypeStruct((tokens, span), BF16),
-        scratch_shapes=[pltpu.VMEM((tokens, span), F32), pltpu.SemaphoreType.DMA],
         compiler_params=params(8),
         cost_estimate=cost(tokens * span, 8 * tokens * span),
         name="relay_step",
-    )(*first, *used)
+    )(*inputs, *used)
 
 
 def collect(sent):
@@ -375,20 +383,22 @@
         out_ref, sems = refs[len(sent) :]
         stage = lax.axis_index("pipe")
         for section in range(sections):
+            ticks = [chunk + LAG * (sections - 1 - section) for chunk in range(CHUNKS)]
+
             @pl.when(stage == section)
             def one():
                 copies = []
-                for chunk in range(CHUNKS):
-                    ref = sent_refs[chunk + LAG * (sections - 1 - section)]
-                    target = out_ref.at[:, pl.ds(chunk * span, span)]
-                    copies.append(pltpu.make_async_copy(ref, target, sems.at[chunk]))
-                    copies[-1].start()
+                for chunk, tick in enumerate(ticks):
+                    if tick < len(sent):
+                        target = out_ref.at[:, pl.ds(chunk * span, span)]
+                        copies.append(pltpu.make_async_copy(sent_refs[tick], target, sems.at[chunk]))
+                        copies[-1].start()
                 for copy in copies:
                     copy.wait()
 
     return pl.pallas_call(
         kernel,
-        in_specs=[ANY] * len(sent),
+        in_specs=[VMEM] * len(sent),
         out_specs=ANY,
         out_shape=jax.ShapeDtypeStruct((tokens, span * CHUNKS), BF16),
         scratch_shapes=[pltpu.SemaphoreType.DMA((CHUNKS,))],
@@ -396,6 +406,32 @@
         cost_estimate=cost(0, 4 * tokens * span * CHUNKS),
         name="collect",
     )(*sent)
+
+
+def final_step(chunk, received, product, collected):
+    tokens, span = product.shape
+
+    def kernel(in_ref, prod_ref, old_ref, out_ref, held, sem):
+        del old_ref
+
+        @pl.when(lax.axis_index("pipe") == 0)
+        def one():
+            held[...] = (in_ref[...].astype(F32) + prod_ref[...]).astype(BF16)
+            copy = pltpu.make_async_copy(held, out_ref.at[:, pl.ds(chunk * span, span)], sem)
+            copy.start()
+            copy.wait()
+
+    return pl.pallas_call(
+        kernel,
+        in_specs=[VMEM, VMEM, ANY],
+        out_specs=ANY,
+        out_shape=jax.ShapeDtypeStruct(collected.shape, BF16),
+        scratch_shapes=[pltpu.VMEM((tokens, span), BF16), pltpu.SemaphoreType.DMA],
+        input_output_aliases={2: 0},
+        compiler_params=params(8),
+        cost_estimate=cost(0, 4 * tokens * span),
+        name="final_step",
+    )(received, product, collected)
 
 
 def token_relations():
@@ -421,55 +457,55 @@
     other_core = (1, 1)
 
     same, crossed = token_relations()
-    relations = same + crossed
     ticks = CHUNKS + LAG * (sections - 1)
-    products, sent, moved = [], [], []
-
-    def product(chunk, rows):
-        products.append(weight_product(chunk, rows, weights, cotangent))
+    sent, moved = [], []
 
     def relay(*others):
         tick = len(sent)
         received = moved[tick - LAG] if tick >= LAG else None
         if received is not None:
-            if others:
-                received = after(received, *others)
-            sent.append(relay_step(tick, received, products))
-        else:
-            sent.append(relay_step(tick, None, products))
+            received = after(received, sent[-1], *others)
+        sent.append(relay_step(tick, received, products, cotangent))
         if tick < ticks - LAG:
             moved.append(down(sent[-1]))
 
-    near = [kv_rows, swap(kv_rows, same[1])]
+    near = [kv_rows] + [swap(kv_rows, relation) for relation in same[1 : 3 if chips == 4 else chips]]
+    far = [swap(kv_rows, other_core)]
+    columns = split_columns(inputs)
+    left = lax.all_to_all(columns, "dp", 0, 0, tiled=True)
+    early = list(range(min(LAG, CHUNKS)))
+    products = list(weight_products(early, after(kv_rows, columns), weights))
+    relay()
+    relay()
+    near = near[:1] + [after(piece, sent[1]) for piece in near[1:]]
+    far.extend(swap(piece, other_core) for piece in near[1:])
     if chips == 4:
-        near.append(swap(kv_rows, same[2]))
         near.append(swap(near[1], same[2]))
-    else:
-        near.extend(swap(kv_rows, relation) for relation in same[2:])
-
-    product(0, kv_rows)
+    products += weight_products(list(range(LAG, CHUNKS)), after(kv_rows, sent[1]), weights)
+    relay(products[-1])
     relay()
-    columns = split_columns(after(inputs, sent[0]), relations)
-    left = [columns[0]] + [swap(c, r) for c, r in zip(columns[1:], relations[1:])]
-    product(1, after(kv_rows, columns[0]))
+    if chips == 4:
+        far.append(swap(after(near[-1], sent[3]), other_core))
+
+    buffer, mine, theirs = gradient(
+        left, same + crossed, near + far, after(moment, sent[3]), scale_grad, slots
+    )
+    received = swap(theirs, other_core)
+    relay(buffer)
+    relay(buffer)
+    sums = add_pairs(after(mine, sent[5]), received)
+    grams = [sums[0]] + [swap(sums[d], (CORES * d, CORES * d)) for d in range(1, chips)]
+    mix = mixing(grams, scale, slots)
+    mixes = [mix] + [swap(mix, (CORES * d, CORES * d)) for d in range(1, chips)]
+    far_mixes = [swap(m, other_core) for m in mixes]
+    relay(*mixes[1:])
     relay()
-    for chunk in range(2, CHUNKS):
-        product(chunk, after(kv_rows, sent[-1]))
-    far = [swap(piece, other_core) for piece in near]
-    while len(sent) < 5:
-        relay(*products[-1:])
-
-    outs = gradient(left, near + far, after(moment, sent[-1]), scale_grad, slots)
-    buffer, grams = outs[0], outs[1:]
-    grams = [grams[0]] + [swap(g, (d, d)) for d, g in enumerate(grams) if d]
-    while len(sent) < 7:
-        relay(outs[1])
-    mix = mixing([after(grams[0], sent[-1])] + grams[1:], scale, slots)
-    mixes = [mix] + [swap(mix, (d, d)) for d in range(1, groups)]
-    while len(sent) < ticks:
-        relay(mix)
-    update = apply_mixing(after(buffer, sent[-2]), mixes, slots)
+    distances = [CORES * d for d in range(chips)] + [CORES * d + 1 for d in range(chips)]
     outgoing = collect(sent)
+    update = apply_mixing(after(buffer, sent[7]), distances, mixes + far_mixes, slots)
+    for chunk in range(CHUNKS - LAG, CHUNKS):
+        tick = chunk + LAG * (sections - 1)
+        outgoing = final_step(chunk, after(moved[tick - LAG], update), products[chunk], outgoing)
     return (update[None], outgoing[None])
 
 

time: 131 us -> 97.7 us (0.75)
  starting transfers between devices: 44.4 us -> 29 us
  waiting for transfers between devices: 42.8 us -> 28.8 us
  local copies, waits for them, and re-layouts: 9.34 us -> 1.34 us
  Pallas kernels: 31.9 us -> 37 us
    ppermute x28 -> x18, starting transfers between devices: 33.7 us -> 14.2 us  [swap(): lax.ppermute(value, 'dp', [(i ^ by[i % CORES], i) for i in range(count)])]
    ppermute x28 -> x18, waiting for transfers between devices: 23.2 us -> 8.68 us  [swap(): lax.ppermute(value, 'dp', [(i ^ by[i % CORES], i) for i in range(count)])]
    unnamed x16 -> x14, local copies, waits for them, and re-layouts: 9.34 us -> 1.34 us
    all_to_all x0 -> x1, starting transfers between devices: none -> 4.4 us  [shards(): left = lax.all_to_all(columns, 'dp', 0, 0, tiled=True)]
    pallas_call x16 -> x15, Pallas kernels: 17.7 us -> 21 us  [the longest x2 12.4 us: weight_products(): pl.pallas_call(kernel, out_shape=[jax.ShapeDtypeStruct((tokens, span), F3...]
    pallas_call x1, Pallas kernels: 6.01 us -> 7.79 us  [gradient(): pl.pallas_call(kernel, grid=(steps,), out_shape=[jax.ShapeDtypeStruct((ro...]
  transfers between devices with their start and end apart: 36 -> 27, of which waited for: 14 -> 14; matrix products, arithmetic and copies ran while one was open for 0% -> 0% of each run, Pallas kernels for 24% -> 36%
where the time goes in v1:
time: 97.7 us; the launch traced here: 97.1 us
  Pallas kernels  37 us (38%)
  starting transfers between devices  29 us (30%)
  waiting for transfers between devices  28.8 us (29%)
  local copies, waits for them, and re-layouts  1.34 us (1%)
    ppermute x8, waiting for transfers between devices, down(): return lax.ppermute(value, 'pipe', [(i, i - 1) for i in range(1, count)])  20.1 us
    ppermute x18, starting transfers between devices, swap(): lax.ppermute(value, 'dp', [(i ^ by[i % CORES], i) for i in range(count)])  14.2 us
    pallas_call x2, Pallas kernels, weight_products(): pl.pallas_call(kernel, out_shape=[jax.ShapeDtypeStruct((tokens, span), F3...  12.4 us
    ppermute x8, starting transfers between devices, down(): return lax.ppermute(value, 'pipe', [(i, i - 1) for i in range(1, count)])  10.4 us
    ppermute x18, waiting for transfers between devices, swap(): lax.ppermute(value, 'dp', [(i ^ by[i % CORES], i) for i in range(count)])  8.68 us
    pallas_call x1, Pallas kernels, gradient(): pl.pallas_call(kernel, grid=(steps,), out_shape=[jax.ShapeDtypeStruct((ro...  7.79 us
    all_to_all x1, starting transfers between devices, shards(): left = lax.all_to_all(columns, 'dp', 0, 0, tiled=True)  4.4 us
    pallas_call x1, Pallas kernels, apply_mixing(): pl.pallas_call(kernel, grid=(owners // per_step,), out_shape=jax.ShapeDty...  4.28 us
  transfers between devices with their start and end apart: 27, of which 14 were waited for; matrix products, arithmetic and copies ran while one was open for 0% of the time, Pallas kernels for 36%

profile of v1, /device:TPU:0, one launch (start us, length us, event | category | flops | bytes accessed | tf_op | source)
XLA Modules:
  0.0 97.1 jit_solution(13490109581692960277)
XLA Ops:
  0.6 3.0 %collective-permute-start = (bf16[128,2048]{1,0:T(8,128)(2,1)}, bf16[128,2048]{1,0:T(8,128)(2,1)}, u32[]{:S(2)}, u32[]{:S(2)}) collective-permute-start(bf16[128,2048]{1,0:T(8,128)(2,1)} %bitcast.6), channel_id=1, source_target_pairs={{2,0},{5,1},{0,2},{7,3},{6,4},{1,5},{4,6},{3,7},{10,8},{13,9},{8,1... | collective-permute-start | bytes 1572872 | tf_op jit(solution)/shard_map/ppermute | solution.py:49
  3.6 1.3 %copy-done.2 = bf16[1,128,5120]{2,1,0:T(8,128)(2,1)S(1)} copy-done((bf16[1,128,5120]{2,1,0:T(8,128)(2,1)S(1)}, bf16[1,128,5120]{2,1,0:T(8,128)(2,1)}, u32[]{:S(2)}) %copy-start.2) | copy-done | bytes 1310744
  4.9 1.4 %split_columns.1 = bf16[8,640,128]{2,1,0:T(8,128)(2,1)} custom-call(bf16[128,5120]{1,0:T(8,128)(2,1)S(1)} %bitcast.12), custom_call_target="tpu_custom_call" | custom-call | flops 1 | bytes 1 | tf_op jit(solution)/shard_map/split_columns/pallas_call | solution.py:73
  6.4 4.4 %all-to-all-start = ((bf16[8,640,128]{2,1,0:T(8,128)(2,1)}), bf16[8,640,128]{2,1,0:T(8,128)(2,1)}, u32[]{:S(2)}, u32[]{:S(2)}) async-start(bf16[8,640,128]{2,1,0:T(8,128)(2,1)} %split_columns.1), calls=%async_computation | async-start | bytes 2621440 | tf_op jit(solution)/shard_map/all_to_all | solution.py:475
  10.8 1.9 %collective-permute-start.1 = (bf16[128,2048]{1,0:T(8,128)(2,1)S(1)}, bf16[128,2048]{1,0:T(8,128)(2,1)S(1)}, u32[]{:S(2)}, u32[]{:S(2)}) collective-permute-start(bf16[128,2048]{1,0:T(8,128)(2,1)S(1)} %bitcast.8), channel_id=1, source_target_pairs={{4,0},{3,1},{6,2},{1,3},{0,4},{7,5},{2,6},{5,7},{12,8},{11,9},{14,... | collective-permute-start | bytes 1572872 | tf_op jit(solution)/shard_map/ppermute | solution.py:49
  12.7 6.3 %weight_products.2 = (f32[128,1280]{1,0:T(8,128)S(1)}, f32[128,1280]{1,0:T(8,128)S(1)}) custom-call(bf16[128,2048]{1,0:T(8,128)(2,1)S(1)} %bitcast.9, bf16[5120,2048]{1,0:T(8,128)(2,1)} %bitcast.13), custom_call_target="tpu_custom_call" | custom-call | flops 1 | bytes 1 | tf_op jit(solution)/shard_map/weight_products/pallas_call | solution.py:329
  19.0 0.0 collective-permute-done.refs_2_
  19.0 0.3 collective-permute-start.2
  19.3 1.3 %collective-permute-start.7 = (bf16[128,1280]{1,0:T(8,128)(2,1)S(1)}, bf16[128,1280]{1,0:T(8,128)(2,1)S(1)}, u32[]{:S(2)}, u32[]{:S(2)}) collective-permute-start(bf16[128,1280]{1,0:T(8,128)(2,1)S(1)} %relay_step.9.refs_0_), channel_id=1, source_target_pairs={{8,0},{16,8},{24,16},{9,1},{17,9},{25,17},{10,2},{18,10},{26,18},{... | collective-permute-start | bytes 983048 | tf_op jit(solution)/shard_map/ppermute | solution.py:54
  20.6 1.3 %collective-permute-start.6 = (bf16[128,1280]{1,0:T(8,128)(2,1)S(1)}, bf16[128,1280]{1,0:T(8,128)(2,1)S(1)}, u32[]{:S(2)}, u32[]{:S(2)}) collective-permute-start(bf16[128,1280]{1,0:T(8,128)(2,1)S(1)} %relay_step.8.refs_1_), channel_id=1, source_target_pairs={{8,0},{16,8},{24,16},{9,1},{17,9},{25,17},{10,2},{18,10},{26,18},{... | collective-permute-start | bytes 983048 | tf_op jit(solution)/shard_map/ppermute | solution.py:54
  21.9 0.1 collective-permute-start.3
  22.0 6.2 %weight_products.3 = (f32[128,1280]{1,0:T(8,128)S(1)}, f32[128,1280]{1,0:T(8,128)S(1)}) custom-call(bf16[128,2048]{1,0:T(8,128)(2,1)S(1)} %bitcast.11, bf16[5120,2048]{1,0:T(8,128)(2,1)} %bitcast.14), custom_call_target="tpu_custom_call" | custom-call | flops 1 | bytes 1 | tf_op jit(solution)/shard_map/weight_products/pallas_call | solution.py:329
  28.1 3.7 %collective-permute-done.7.refs_0_ = bf16[128,1280]{1,0:T(8,128)(2,1)S(1)} collective-permute-done((bf16[128,1280]{1,0:T(8,128)(2,1)S(1)}, bf16[128,1280]{1,0:T(8,128)(2,1)S(1)}, u32[]{:S(2)}, u32[]{:S(2)}) %collective-permute-start.7) | collective-permute-done | bytes 327712 | tf_op jit(solution)/shard_map/ppermute | solution.py:54
  31.8 0.7 relay_step.10.refs_2_
  32.5 5.0 %collective-permute-done.6.refs_0_ = bf16[128,1280]{1,0:T(8,128)(2,1)S(1)} collective-permute-done((bf16[128,1280]{1,0:T(8,128)(2,1)S(1)}, bf16[128,1280]{1,0:T(8,128)(2,1)S(1)}, u32[]{:S(2)}, u32[]{:S(2)}) %collective-permute-start.6) | collective-permute-done | bytes 327712 | tf_op jit(solution)/shard_map/ppermute | solution.py:54
  37.6 0.7 relay_step.11.refs_3_
  38.3 0.0 collective-permute-start.4
  38.3 0.0 collective-permute-done.1.refs_3_
  38.3 0.5 collective-permute-start.5
  38.8 0.5 collective-permute-done.2.refs_4_
  39.3 0.1 collective-permute-start.8
  39.4 1.3 %collective-permute-start.10 = (bf16[128,1280]{1,0:T(8,128)(2,1)}, bf16[128,1280]{1,0:T(8,128)(2,1)}, u32[]{:S(2)}, u32[]{:S(2)}) collective-permute-start(bf16[128,1280]{1,0:T(8,128)(2,1)} %relay_step.10.refs_2_), channel_id=1, source_target_pairs={{8,0},{16,8},{24,16},{9,1},{17,9},{25,17},{10,2},{18,10},{26,18},{... | collective-permute-start | bytes 983048 | tf_op jit(solution)/shard_map/ppermute | solution.py:54
  40.7 0.0 collective-permute-done.3.refs_5_
  40.7 1.3 %collective-permute-start.9 = (bf16[128,1280]{1,0:T(8,128)(2,1)}, bf16[128,1280]{1,0:T(8,128)(2,1)}, u32[]{:S(2)}, u32[]{:S(2)}) collective-permute-start(bf16[128,1280]{1,0:T(8,128)(2,1)} %relay_step.11.refs_3_), channel_id=1, source_target_pairs={{8,0},{16,8},{24,16},{9,1},{17,9},{25,17},{10,2},{18,10},{26,18},{... | collective-permute-start | bytes 983048 | tf_op jit(solution)/shard_map/ppermute | solution.py:54
  42.1 0.0 collective-permute-done.4.refs_6_
  42.1 0.0 collective-permute-done.5.refs_7_
  42.1 7.8 %gradient.1 = (bf16[640,2048]{1,0:T(8,128)(2,1)S(1)}, f32[4,136,128]{2,1,0:T(8,128)S(1)}, f32[4,136,128]{2,1,0:T(8,128)S(1)}) custom-call(bf16[8,640,128]{2,1,0:T(8,128)(2,1)} %all-to-all-done.refs_0_, bf16[128,2048]{1,0:T(8,128)(2,1)} %bitcast.7, bf16[128,2048]{1,0:T(8,128)(2,1)} %collective-permute-done.refs_2_, bf16[128,2048]{1,0:T(8,128)(2,1)} %copy-done.5, ...), custom_call_target="tpu_custom_call" | custom-call | flops 1 | bytes 1 | tf_op jit(solution)/shard_map/gradient/pallas_call | solution.py:169
  49.9 0.5 collective-permute-start.11
  50.4 1.8 %collective-permute-done.10.refs_0_ = bf16[128,1280]{1,0:T(8,128)(2,1)} collective-permute-done((bf16[128,1280]{1,0:T(8,128)(2,1)}, bf16[128,1280]{1,0:T(8,128)(2,1)}, u32[]{:S(2)}, u32[]{:S(2)}) %collective-permute-start.10) | collective-permute-done | bytes 327712 | tf_op jit(solution)/shard_map/ppermute | solution.py:54
  52.2 1.0 %relay_step.12.refs_4_ = bf16[128,1280]{1,0:T(8,128)(2,1)S(1)} custom-call(bf16[128,1280]{1,0:T(8,128)(2,1)} %collective-permute-done.10.refs_0_, f32[128,1280]{1,0:T(8,128)S(1)} %get-tuple-element.33.refs_1_.refs_2_, f32[128,1280]{1,0:T(8,128)S(1)} %get-tuple-element.37.refs_3_.refs_2_.prod_ref), custom_call_target="tpu_custom_call" | custom-call | flops 1 | bytes 1 | tf_op jit(solution)/shard_map/relay_step/pallas_call | solution.py:366
  53.2 1.3 %collective-permute-start.23 = (bf16[128,1280]{1,0:T(8,128)(2,1)S(1)}, bf16[128,1280]{1,0:T(8,128)(2,1)S(1)}, u32[]{:S(2)}, u32[]{:S(2)}) collective-permute-start(bf16[128,1280]{1,0:T(8,128)(2,1)S(1)} %relay_step.12.refs_4_), channel_id=1, source_target_pairs={{8,0},{16,8},{24,16},{9,1},{17,9},{25,17},{10,2},{18,10},{26,18},{... | collective-permute-start | bytes 983048 | tf_op jit(solution)/shard_map/ppermute | solution.py:54
  54.4 4.8 %collective-permute-done.9.refs_0_ = bf16[128,1280]{1,0:T(8,128)(2,1)} collective-permute-done((bf16[128,1280]{1,0:T(8,128)(2,1)}, bf16[128,1280]{1,0:T(8,128)(2,1)}, u32[]{:S(2)}, u32[]{:S(2)}) %collective-permute-start.9) | collective-permute-done | bytes 327712 | tf_op jit(solution)/shard_map/ppermute | solution.py:54
  59.2 1.0 %relay_step.13.refs_5_ = bf16[128,1280]{1,0:T(8,128)(2,1)S(1)} custom-call(bf16[128,1280]{1,0:T(8,128)(2,1)} %collective-permute-done.9.refs_0_, f32[128,1280]{1,0:T(8,128)S(1)} %get-tuple-element.30.refs_1_.refs_2_, f32[128,1280]{1,0:T(8,128)S(1)} %get-tuple-element.35.refs_3_.refs_2_.prod_ref), custom_call_target="tpu_custom_call" | custom-call | flops 1 | bytes 1 | tf_op jit(solution)/shard_map/relay_step/pallas_call | solution.py:366
  60.2 1.3 %collective-permute-start.22 = (bf16[128,1280]{1,0:T(8,128)(2,1)S(1)}, bf16[128,1280]{1,0:T(8,128)(2,1)S(1)}, u32[]{:S(2)}, u32[]{:S(2)}) collective-permute-start(bf16[128,1280]{1,0:T(8,128)(2,1)S(1)} %relay_step.13.refs_5_), channel_id=1, source_target_pairs={{8,0},{16,8},{24,16},{9,1},{17,9},{25,17},{10,2},{18,10},{26,18},{... | collective-permute-start | bytes 983048 | tf_op jit(solution)/shard_map/ppermute | solution.py:54
  61.5 1.4 %collective-permute-start.12 = (f32[136,128]{1,0:T(8,128)S(1)}, f32[136,128]{1,0:T(8,128)S(1)}, u32[]{:S(2)}, u32[]{:S(2)}) collective-permute-start(f32[136,128]{1,0:T(8,128)S(1)} %get-tuple-element.48), channel_id=1, source_target_pairs={{2,0},{3,1},{0,2},{1,3},{6,4},{7,5},{4,6},{5,7},{10,8},{11,9},{8,1... | collective-permute-start | bytes 208904 | tf_op jit(solution)/shard_map/ppermute | solution.py:49
  62.9 1.3 %collective-permute-start.13 = (f32[136,128]{1,0:T(8,128)S(1)}, f32[136,128]{1,0:T(8,128)S(1)}, u32[]{:S(2)}, u32[]{:S(2)}) collective-permute-start(f32[136,128]{1,0:T(8,128)S(1)} %get-tuple-element.49), channel_id=1, source_target_pairs={{4,0},{5,1},{6,2},{7,3},{0,4},{1,5},{2,6},{3,7},{12,8},{13,9},{14,... | collective-permute-start | bytes 208904 | tf_op jit(solution)/shard_map/ppermute | solution.py:49
  64.2 0.9 collective-permute-start.14
  65.1 1.1 %collective-permute-done.12.refs_1_ = f32[136,128]{1,0:T(8,128)S(1)} collective-permute-done((f32[136,128]{1,0:T(8,128)S(1)}, f32[136,128]{1,0:T(8,128)S(1)}, u32[]{:S(2)}, u32[]{:S(2)}) %collective-permute-start.12) | collective-permute-done | bytes 69664 | tf_op jit(solution)/shard_map/ppermute | solution.py:49
  66.1 1.7 %collective-permute-done.13.refs_2_ = f32[136,128]{1,0:T(8,128)S(1)} collective-permute-done((f32[136,128]{1,0:T(8,128)S(1)}, f32[136,128]{1,0:T(8,128)S(1)}, u32[]{:S(2)}, u32[]{:S(2)}) %collective-permute-start.13) | collective-permute-done | bytes 69664 | tf_op jit(solution)/shard_map/ppermute | solution.py:49
  67.8 1.5 %collective-permute-done.14.refs_3_ = f32[136,128]{1,0:T(8,128)S(1)} collective-permute-done((f32[136,128]{1,0:T(8,128)S(1)}, f32[136,128]{1,0:T(8,128)S(1)}, u32[]{:S(2)}, u32[]{:S(2)}) %collective-permute-start.14) | collective-permute-done | bytes 69664 | tf_op jit(solution)/shard_map/ppermute | solution.py:49
  69.4 4.0 %mixing.1.refs_0_ = f32[136,128]{1,0:T(8,128)S(1)} custom-call(f32[136,128]{1,0:T(8,128)S(1)} %get-tuple-element.47.refs_0_, f32[136,128]{1,0:T(8,128)S(1)} %collective-permute-done.12.refs_1_, f32[136,128]{1,0:T(8,128)S(1)} %collective-permute-done.13.refs_2_, f32[136,128]{1,0:T(8,128)S(1)} %collective-permute-done.14.refs_3_), custom_call_target="tpu_custom_call" | custom-call | flops 1 | bytes 1 | tf_op jit(solution)/shard_map/mixing/pallas_call | solution.py:235
  73.3 0.8 collective-permute-start.15
  74.1 0.8 collective-permute-start.16
  74.9 2.0 %collective-permute-start.17 = (f32[136,128]{1,0:T(8,128)S(1)}, f32[136,128]{1,0:T(8,128)S(1)}, u32[]{:S(2)}, u32[]{:S(2)}) collective-permute-start(f32[136,128]{1,0:T(8,128)S(1)} %mixing.1.refs_0_), channel_id=1, source_target_pairs={{6,0},{7,1},{4,2},{5,3},{2,4},{3,5},{0,6},{1,7},{14,8},{15,9},{12,... | collective-permute-start | bytes 208904 | tf_op jit(solution)/shard_map/ppermute | solution.py:49
  76.9 0.8 collective-permute-done.15.refs_1_
  77.7 0.7 collective-permute-done.16.refs_2_
  78.4 1.7 %collective-permute-done.17.refs_3_ = f32[136,128]{1,0:T(8,128)S(1)} collective-permute-done((f32[136,128]{1,0:T(8,128)S(1)}, f32[136,128]{1,0:T(8,128)S(1)}, u32[]{:S(2)}, u32[]{:S(2)}) %collective-permute-start.17) | collective-permute-done | bytes 69664 | tf_op jit(solution)/shard_map/ppermute | solution.py:49
  80.1 0.1 relay_step.14.refs_6_
  80.2 1.4 %collective-permute-start.25 = (bf16[128,1280]{1,0:T(8,128)(2,1)S(1)}, bf16[128,1280]{1,0:T(8,128)(2,1)S(1)}, u32[]{:S(2)}, u32[]{:S(2)}) collective-permute-start(bf16[128,1280]{1,0:T(8,128)(2,1)S(1)} %relay_step.14.refs_6_), channel_id=1, source_target_pairs={{8,0},{16,8},{24,16},{9,1},{17,9},{25,17},{10,2},{18,10},{26,18},{... | collective-permute-start | bytes 983048 | tf_op jit(solution)/shard_map/ppermute | solution.py:54
  81.6 0.0 collective-permute-done.22.refs_0_
  81.6 0.1 relay_step.15.refs_7_
  81.7 1.3 %collective-permute-start.24 = (bf16[128,1280]{1,0:T(8,128)(2,1)S(1)}, bf16[128,1280]{1,0:T(8,128)(2,1)S(1)}, u32[]{:S(2)}, u32[]{:S(2)}) collective-permute-start(bf16[128,1280]{1,0:T(8,128)(2,1)S(1)} %relay_step.15.refs_7_), channel_id=1, source_target_pairs={{8,0},{16,8},{24,16},{9,1},{17,9},{25,17},{10,2},{18,10},{26,18},{... | collective-permute-start | bytes 983048 | tf_op jit(solution)/shard_map/ppermute | solution.py:54
  83.0 0.1 collective-permute-start.18
  83.1 0.5 collective-permute-start.19
  83.6 0.1 collective-permute-start.20
  83.6 0.7 collective-permute-done.18.refs_4_
  84.3 0.2 collective-permute-start.21
  84.5 1.9 %collect.1.old_ref = bf16[128,5120]{1,0:T(8,128)(2,1)} custom-call(bf16[128,1280]{1,0:T(8,128)(2,1)S(1)} %copy-done.4, bf16[128,1280]{1,0:T(8,128)(2,1)S(1)} %relay_step.8.refs_1_, bf16[128,1280]{1,0:T(8,128)(2,1)} %relay_step.10.refs_2_, bf16[128,1280]{1,0:T(8,128)(2,1)} %relay_step.11.refs_3_, bf16[128,1280]{1,0:T(8,128)(2,1)S(1)} %relay_step.12.refs_4_, ...), custom_call_target="tpu_custom_call" | custom-call | flops 1 | bytes 1 | tf_op jit(solution)/shard_map/collect/pallas_call | solution.py:399
  86.4 0.0 collective-permute-done.20.refs_6_
  86.4 4.3 %apply_mixing.1 = bf16[640,2048]{1,0:T(8,128)(2,1)} custom-call(f32[136,128]{1,0:T(8,128)S(1)} %mixing.1.refs_0_, f32[136,128]{1,0:T(8,128)S(1)} %collective-permute-done.15.refs_1_, f32[136,128]{1,0:T(8,128)S(1)} %collective-permute-done.16.refs_2_, f32[136,128]{1,0:T(8,128)S(1)} %collective-permute-done.17.refs_3_, ...), custom_call_target="tpu_custom_call" | custom-call | flops 1 | bytes 1 | tf_op jit(solution)/shard_map/apply_mixing/pallas_call | solution.py:289
  90.7 1.3 %collective-permute-done.25.in_ref = bf16[128,1280]{1,0:T(8,128)(2,1)S(1)} collective-permute-done((bf16[128,1280]{1,0:T(8,128)(2,1)S(1)}, bf16[128,1280]{1,0:T(8,128)(2,1)S(1)}, u32[]{:S(2)}, u32[]{:S(2)}) %collective-permute-start.25) | collective-permute-done | bytes 327712 | tf_op jit(solution)/shard_map/ppermute | solution.py:54
  92.0 3.5 %collective-permute-done.24.in_ref = bf16[128,1280]{1,0:T(8,128)(2,1)S(1)} collective-permute-done((bf16[128,1280]{1,0:T(8,128)(2,1)S(1)}, bf16[128,1280]{1,0:T(8,128)(2,1)S(1)}, u32[]{:S(2)}, u32[]{:S(2)}) %collective-permute-start.24) | collective-permute-done | bytes 327712 | tf_op jit(solution)/shard_map/ppermute | solution.py:54
  95.6 0.8 final_step.2.old_ref
  96.3 0.8 final_step.3
  (22 shorter events, 0.1 us)
Async XLA Ops:
  0.6 18.4 %collective-permute-start = (bf16[128,2048]{1,0:T(8,128)(2,1)}, bf16[128,2048]{1,0:T(8,128)(2,1)}, u32[]{:S(2)}, u32[]{:S(2)}) collective-permute-start(bf16[128,2048]{1,0:T(8,128)(2,1)} %bitcast.6), channel_id=1, source_target_pairs={{2,0},{5,1},{0,2},{7,3},{6,4},{1,5},{4,6},{3,7},{10,8},{13,9},{8,1... | collective-permute-start | bytes 1572872 | tf_op jit(solution)/shard_map/ppermute | solution.py:49
  3.6 1.3 %copy-start.2 = (bf16[1,128,5120]{2,1,0:T(8,128)(2,1)S(1)}, bf16[1,128,5120]{2,1,0:T(8,128)(2,1)}, u32[]{:S(2)}) copy-start(bf16[1,128,5120]{2,1,0:T(8,128)(2,1)} %param.5) | copy-start | bytes 3932164
  6.4 4.4 %copy-start.1 = (bf16[1,128,2048]{2,1,0:T(8,128)(2,1)S(1)}, bf16[1,128,2048]{2,1,0:T(8,128)(2,1)}, u32[]{:S(2)}) copy-start(bf16[1,128,2048]{2,1,0:T(8,128)(2,1)} %param.7) | copy-start | bytes 1572868
  6.4 35.7 %all-to-all-start = ((bf16[8,640,128]{2,1,0:T(8,128)(2,1)}), bf16[8,640,128]{2,1,0:T(8,128)(2,1)}, u32[]{:S(2)}, u32[]{:S(2)}) async-start(bf16[8,640,128]{2,1,0:T(8,128)(2,1)} %split_columns.1), calls=%async_computation | async-start | bytes 2621440 | tf_op jit(solution)/shard_map/all_to_all | solution.py:475
  10.8 27.5 %collective-permute-start.1 = (bf16[128,2048]{1,0:T(8,128)(2,1)S(1)}, bf16[128,2048]{1,0:T(8,128)(2,1)S(1)}, u32[]{:S(2)}, u32[]{:S(2)}) collective-permute-start(bf16[128,2048]{1,0:T(8,128)(2,1)S(1)} %bitcast.8), channel_id=1, source_target_pairs={{4,0},{3,1},{6,2},{1,3},{0,4},{7,5},{2,6},{5,7},{12,8},{11,9},{14,... | collective-permute-start | bytes 1572872 | tf_op jit(solution)/shard_map/ppermute | solution.py:49
  12.7 6.3 %copy-start = (bf16[128,5120]{1,0:T(8,128)(2,1)S(1)}, bf16[128,5120]{1,0:T(8,128)(2,1)}, u32[]{:S(2)}) copy-start(bf16[128,5120]{1,0:T(8,128)(2,1)} %refs_1_.3) | copy-start | bytes 3932164
  19.0 20.3 %collective-permute-start.2 = (bf16[128,2048]{1,0:T(8,128)(2,1)}, bf16[128,2048]{1,0:T(8,128)(2,1)}, u32[]{:S(2)}, u32[]{:S(2)}) collective-permute-start(bf16[128,2048]{1,0:T(8,128)(2,1)} %collective-permute-done.refs_2_), channel_id=1, source_target_pairs={{4,0},{3,1},{6,2},{1,3},{0,4},{7,5},{2,6},{5,7},{12,8},{11,9},{14,... | collective-permute-start | bytes 1572872 | tf_op jit(solution)/shard_map/ppermute | solution.py:49
  19.3 8.8 %copy-start.3 = (bf16[128,1280]{1,0:T(8,128)(2,1)}, bf16[128,1280]{1,0:T(8,128)(2,1)S(1)}, u32[]{:S(2)}) copy-start(bf16[128,1280]{1,0:T(8,128)(2,1)S(1)} %relay_step.9.refs_0_) | copy-start | bytes 983044
  19.3 12.5 %collective-permute-start.7 = (bf16[128,1280]{1,0:T(8,128)(2,1)S(1)}, bf16[128,1280]{1,0:T(8,128)(2,1)S(1)}, u32[]{:S(2)}, u32[]{:S(2)}) collective-permute-start(bf16[128,1280]{1,0:T(8,128)(2,1)S(1)} %relay_step.9.refs_0_), channel_id=1, source_target_pairs={{8,0},{16,8},{24,16},{9,1},{17,9},{25,17},{10,2},{18,10},{26,18},{... | collective-permute-start | bytes 983048 | tf_op jit(solution)/shard_map/ppermute | solution.py:54
  20.6 17.0 %collective-permute-start.6 = (bf16[128,1280]{1,0:T(8,128)(2,1)S(1)}, bf16[128,1280]{1,0:T(8,128)(2,1)S(1)}, u32[]{:S(2)}, u32[]{:S(2)}) collective-permute-start(bf16[128,1280]{1,0:T(8,128)(2,1)S(1)} %relay_step.8.refs_1_), channel_id=1, source_target_pairs={{8,0},{16,8},{24,16},{9,1},{17,9},{25,17},{10,2},{18,10},{26,18},{... | collective-permute-start | bytes 983048 | tf_op jit(solution)/shard_map/ppermute | solution.py:54
  21.9 18.8 %collective-permute-start.3 = (bf16[128,2048]{1,0:T(8,128)(2,1)S(1)}, bf16[128,2048]{1,0:T(8,128)(2,1)S(1)}, u32[]{:S(2)}, u32[]{:S(2)}) collective-permute-start(bf16[128,2048]{1,0:T(8,128)(2,1)S(1)} %bitcast.10), channel_id=1, source_target_pairs={{1,0},{0,1},{3,2},{2,3},{5,4},{4,5},{7,6},{6,7},{9,8},{8,9},{11,10... | collective-permute-start | bytes 1572872 | tf_op jit(solution)/shard_map/ppermute | solution.py:49
  38.3 3.8 %collective-permute-start.4 = (bf16[128,2048]{1,0:T(8,128)(2,1)}, bf16[128,2048]{1,0:T(8,128)(2,1)}, u32[]{:S(2)}, u32[]{:S(2)}) collective-permute-start(bf16[128,2048]{1,0:T(8,128)(2,1)} %collective-permute-done.refs_2_), channel_id=1, source_target_pairs={{1,0},{0,1},{3,2},{2,3},{5,4},{4,5},{7,6},{6,7},{9,8},{8,9},{11,10... | collective-permute-start | bytes 1572872 | tf_op jit(solution)/shard_map/ppermute | solution.py:49
  38.3 2.4 %copy-start.5 = (bf16[128,2048]{1,0:T(8,128)(2,1)}, bf16[128,2048]{1,0:T(8,128)(2,1)S(1)}, u32[]{:S(2)}) copy-start(bf16[128,2048]{1,0:T(8,128)(2,1)S(1)} %collective-permute-done.1.refs_3_) | copy-start | bytes 1572868
  38.3 3.8 %collective-permute-start.5 = (bf16[128,2048]{1,0:T(8,128)(2,1)S(1)}, bf16[128,2048]{1,0:T(8,128)(2,1)}, u32[]{:S(2)}, u32[]{:S(2)}) collective-permute-start(bf16[128,2048]{1,0:T(8,128)(2,1)S(1)} %collective-permute-done.1.refs_3_), channel_id=1, source_target_pairs={{1,0},{0,1},{3,2},{2,3},{5,4},{4,5},{7,6},{6,7},{9,8},{8,9},{11,10... | collective-permute-start | bytes 1572872 | tf_op jit(solution)/shard_map/ppermute | solution.py:49
  39.3 2.8 %collective-permute-start.8 = (bf16[128,2048]{1,0:T(8,128)(2,1)}, bf16[128,2048]{1,0:T(8,128)(2,1)}, u32[]{:S(2)}, u32[]{:S(2)}) collective-permute-start(bf16[128,2048]{1,0:T(8,128)(2,1)} %collective-permute-done.2.refs_4_), channel_id=1, source_target_pairs={{1,0},{0,1},{3,2},{2,3},{5,4},{4,5},{7,6},{6,7},{9,8},{8,9},{11,10... | collective-permute-start | bytes 1572872 | tf_op jit(solution)/shard_map/ppermute | solution.py:49
  39.4 12.8 %collective-permute-start.10 = (bf16[128,1280]{1,0:T(8,128)(2,1)}, bf16[128,1280]{1,0:T(8,128)(2,1)}, u32[]{:S(2)}, u32[]{:S(2)}) collective-permute-start(bf16[128,1280]{1,0:T(8,128)(2,1)} %relay_step.10.refs_2_), channel_id=1, source_target_pairs={{8,0},{16,8},{24,16},{9,1},{17,9},{25,17},{10,2},{18,10},{26,18},{... | collective-permute-start | bytes 983048 | tf_op jit(solution)/shard_map/ppermute | solution.py:54
  40.7 1.3 %copy-start.6 = (bf16[128,2048]{1,0:T(8,128)(2,1)}, bf16[128,2048]{1,0:T(8,128)(2,1)S(1)}, u32[]{:S(2)}) copy-start(bf16[128,2048]{1,0:T(8,128)(2,1)S(1)} %collective-permute-done.3.refs_5_) | copy-start | bytes 1572868
  40.7 18.5 %collective-permute-start.9 = (bf16[128,1280]{1,0:T(8,128)(2,1)}, bf16[128,1280]{1,0:T(8,128)(2,1)}, u32[]{:S(2)}, u32[]{:S(2)}) collective-permute-start(bf16[128,1280]{1,0:T(8,128)(2,1)} %relay_step.11.refs_3_), channel_id=1, source_target_pairs={{8,0},{16,8},{24,16},{9,1},{17,9},{25,17},{10,2},{18,10},{26,18},{... | collective-permute-start | bytes 983048 | tf_op jit(solution)/shard_map/ppermute | solution.py:54
  49.9 11.6 %collective-permute-start.11 = (f32[4,136,128]{2,1,0:T(8,128)S(1)}, f32[4,136,128]{2,1,0:T(8,128)S(1)}, u32[]{:S(2)}, u32[]{:S(2)}) collective-permute-start(f32[4,136,128]{2,1,0:T(8,128)S(1)} %get-tuple-element.46), channel_id=1, source_target_pairs={{1,0},{0,1},{3,2},{2,3},{5,4},{4,5},{7,6},{6,7},{9,8},{8,9},{11,10... | collective-permute-start | bytes 835592 | tf_op jit(solution)/shard_map/ppermute | solution.py:49
  53.2 23.7 %collective-permute-start.23 = (bf16[128,1280]{1,0:T(8,128)(2,1)S(1)}, bf16[128,1280]{1,0:T(8,128)(2,1)S(1)}, u32[]{:S(2)}, u32[]{:S(2)}) collective-permute-start(bf16[128,1280]{1,0:T(8,128)(2,1)S(1)} %relay_step.12.refs_4_), channel_id=1, source_target_pairs={{8,0},{16,8},{24,16},{9,1},{17,9},{25,17},{10,2},{18,10},{26,18},{... | collective-permute-start | bytes 983048 | tf_op jit(solution)/shard_map/ppermute | solution.py:54
  60.2 21.4 %collective-permute-start.22 = (bf16[128,1280]{1,0:T(8,128)(2,1)S(1)}, bf16[128,1280]{1,0:T(8,128)(2,1)S(1)}, u32[]{:S(2)}, u32[]{:S(2)}) collective-permute-start(bf16[128,1280]{1,0:T(8,128)(2,1)S(1)} %relay_step.13.refs_5_), channel_id=1, source_target_pairs={{8,0},{16,8},{24,16},{9,1},{17,9},{25,17},{10,2},{18,10},{26,18},{... | collective-permute-start | bytes 983048 | tf_op jit(solution)/shard_map/ppermute | solution.py:54
  61.5 4.6 %collective-permute-start.12 = (f32[136,128]{1,0:T(8,128)S(1)}, f32[136,128]{1,0:T(8,128)S(1)}, u32[]{:S(2)}, u32[]{:S(2)}) collective-permute-start(f32[136,128]{1,0:T(8,128)S(1)} %get-tuple-element.48), channel_id=1, source_target_pairs={{2,0},{3,1},{0,2},{1,3},{6,4},{7,5},{4,6},{5,7},{10,8},{11,9},{8,1... | collective-permute-start | bytes 208904 | tf_op jit(solution)/shard_map/ppermute | solution.py:49
  62.9 4.9 %collective-permute-start.13 = (f32[136,128]{1,0:T(8,128)S(1)}, f32[136,128]{1,0:T(8,128)S(1)}, u32[]{:S(2)}, u32[]{:S(2)}) collective-permute-start(f32[136,128]{1,0:T(8,128)S(1)} %get-tuple-element.49), channel_id=1, source_target_pairs={{4,0},{5,1},{6,2},{7,3},{0,4},{1,5},{2,6},{3,7},{12,8},{13,9},{14,... | collective-permute-start | bytes 208904 | tf_op jit(solution)/shard_map/ppermute | solution.py:49
  64.2 5.2 %collective-permute-start.14 = (f32[136,128]{1,0:T(8,128)S(1)}, f32[136,128]{1,0:T(8,128)S(1)}, u32[]{:S(2)}, u32[]{:S(2)}) collective-permute-start(f32[136,128]{1,0:T(8,128)S(1)} %get-tuple-element.50), channel_id=1, source_target_pairs={{6,0},{7,1},{4,2},{5,3},{2,4},{3,5},{0,6},{1,7},{14,8},{15,9},{12,... | collective-permute-start | bytes 208904 | tf_op jit(solution)/shard_map/ppermute | solution.py:49
  73.3 4.4 %collective-permute-start.15 = (f32[136,128]{1,0:T(8,128)S(1)}, f32[136,128]{1,0:T(8,128)S(1)}, u32[]{:S(2)}, u32[]{:S(2)}) collective-permute-start(f32[136,128]{1,0:T(8,128)S(1)} %mixing.1.refs_0_), channel_id=1, source_target_pairs={{2,0},{3,1},{0,2},{1,3},{6,4},{7,5},{4,6},{5,7},{10,8},{11,9},{8,1... | collective-permute-start | bytes 208904 | tf_op jit(solution)/shard_map/ppermute | solution.py:49
  74.1 4.3 %collective-permute-start.16 = (f32[136,128]{1,0:T(8,128)S(1)}, f32[136,128]{1,0:T(8,128)S(1)}, u32[]{:S(2)}, u32[]{:S(2)}) collective-permute-start(f32[136,128]{1,0:T(8,128)S(1)} %mixing.1.refs_0_), channel_id=1, source_target_pairs={{4,0},{5,1},{6,2},{7,3},{0,4},{1,5},{2,6},{3,7},{12,8},{13,9},{14,... | collective-permute-start | bytes 208904 | tf_op jit(solution)/shard_map/ppermute | solution.py:49
  74.9 5.2 %collective-permute-start.17 = (f32[136,128]{1,0:T(8,128)S(1)}, f32[136,128]{1,0:T(8,128)S(1)}, u32[]{:S(2)}, u32[]{:S(2)}) collective-permute-start(f32[136,128]{1,0:T(8,128)S(1)} %mixing.1.refs_0_), channel_id=1, source_target_pairs={{6,0},{7,1},{4,2},{5,3},{2,4},{3,5},{0,6},{1,7},{14,8},{15,9},{12,... | collective-permute-start | bytes 208904 | tf_op jit(solution)/shard_map/ppermute | solution.py:49
  80.1 4.3 %copy-start.4 = (bf16[128,1280]{1,0:T(8,128)(2,1)S(1)}, bf16[128,1280]{1,0:T(8,128)(2,1)}, u32[]{:S(2)}) copy-start(bf16[128,1280]{1,0:T(8,128)(2,1)} %copy-done.3) | copy-start | bytes 983044
  80.2 11.9 %collective-permute-start.25 = (bf16[128,1280]{1,0:T(8,128)(2,1)S(1)}, bf16[128,1280]{1,0:T(8,128)(2,1)S(1)}, u32[]{:S(2)}, u32[]{:S(2)}) collective-permute-start(bf16[128,1280]{1,0:T(8,128)(2,1)S(1)} %relay_step.14.refs_6_), channel_id=1, source_target_pairs={{8,0},{16,8},{24,16},{9,1},{17,9},{25,17},{10,2},{18,10},{26,18},{... | collective-permute-start | bytes 983048 | tf_op jit(solution)/shard_map/ppermute | solution.py:54
  81.7 13.9 %collective-permute-start.24 = (bf16[128,1280]{1,0:T(8,128)(2,1)S(1)}, bf16[128,1280]{1,0:T(8,128)(2,1)S(1)}, u32[]{:S(2)}, u32[]{:S(2)}) collective-permute-start(bf16[128,1280]{1,0:T(8,128)(2,1)S(1)} %relay_step.15.refs_7_), channel_id=1, source_target_pairs={{8,0},{16,8},{24,16},{9,1},{17,9},{25,17},{10,2},{18,10},{26,18},{... | collective-permute-start | bytes 983048 | tf_op jit(solution)/shard_map/ppermute | solution.py:54
  83.0 1.3 %collective-permute-start.18 = (f32[136,128]{1,0:T(8,128)S(1)}, f32[136,128]{1,0:T(8,128)S(1)}, u32[]{:S(2)}, u32[]{:S(2)}) collective-permute-start(f32[136,128]{1,0:T(8,128)S(1)} %mixing.1.refs_0_), channel_id=1, source_target_pairs={{1,0},{0,1},{3,2},{2,3},{5,4},{4,5},{7,6},{6,7},{9,8},{8,9},{11,10... | collective-permute-start | bytes 208904 | tf_op jit(solution)/shard_map/ppermute | solution.py:49
  83.1 3.4 %collective-permute-start.19 = (f32[136,128]{1,0:T(8,128)S(1)}, f32[136,128]{1,0:T(8,128)S(1)}, u32[]{:S(2)}, u32[]{:S(2)}) collective-permute-start(f32[136,128]{1,0:T(8,128)S(1)} %collective-permute-done.15.refs_1_), channel_id=1, source_target_pairs={{1,0},{0,1},{3,2},{2,3},{5,4},{4,5},{7,6},{6,7},{9,8},{8,9},{11,10... | collective-permute-start | bytes 208904 | tf_op jit(solution)/shard_map/ppermute | solution.py:49
  83.6 2.9 %collective-permute-start.20 = (f32[136,128]{1,0:T(8,128)S(1)}, f32[136,128]{1,0:T(8,128)S(1)}, u32[]{:S(2)}, u32[]{:S(2)}) collective-permute-start(f32[136,128]{1,0:T(8,128)S(1)} %collective-permute-done.16.refs_2_), channel_id=1, source_target_pairs={{1,0},{0,1},{3,2},{2,3},{5,4},{4,5},{7,6},{6,7},{9,8},{8,9},{11,10... | collective-permute-start | bytes 208904 | tf_op jit(solution)/shard_map/ppermute | solution.py:49
  84.3 2.1 %collective-permute-start.21 = (f32[136,128]{1,0:T(8,128)S(1)}, f32[136,128]{1,0:T(8,128)S(1)}, u32[]{:S(2)}, u32[]{:S(2)}) collective-permute-start(f32[136,128]{1,0:T(8,128)S(1)} %collective-permute-done.17.refs_3_), channel_id=1, source_target_pairs={{1,0},{0,1},{3,2},{2,3},{5,4},{4,5},{7,6},{6,7},{9,8},{8,9},{11,10... | collective-permute-start | bytes 208904 | tf_op jit(solution)/shard_map/ppermute | solution.py:49

commit v2 on v1

--- a/solution.py
+++ b/solution.py
@@ -244,24 +244,40 @@
     )(*grams)
 
 
-def apply_mixing(buffer, distances, mixes, slots):
+def apply_mixing(buffer, distances, mixes, slots, sent):
     rows, width = buffer.shape
+    tokens, wide = sent[0].shape
     count = lax.axis_size("dp")
+    sections = lax.axis_size("pipe")
     mats = width // HEAD
     owners = mats // slots
     per_step = 2 if owners % 2 == 0 else 1
+    steps = owners // per_step
     span = slots * HEAD
     block = per_step * span
     packed = packed_rows(slots)
 
     def kernel(*refs):
         mix_refs = refs[:count]
-        buf_ref, out_ref, held = refs[count:]
+        sent_refs = refs[count : count + len(sent)]
+        buf_ref, out_ref, relayed_ref, held, sems = refs[count + len(sent) :]
         own = lax.axis_index("dp")
+        stage = lax.axis_index("pipe")
         step = pl.program_id(0)
+
+        def each_copy(act):
+            for section in range(sections):
+                @pl.when(stage == section)
+                def one():
+                    for chunk in range(CHUNKS):
+                        tick = chunk + LAG * (sections - 1 - section)
+                        if tick < len(sent):
+                            target = relayed_ref.at[:, pl.ds(chunk * wide, wide)]
+                            act(pltpu.make_async_copy(sent_refs[tick], target, sems.at[chunk]))
 
         @pl.when(step == 0)
         def load():
+            each_copy(lambda copy: copy.start())
             for distance, ref in zip(distances, mix_refs):
                 held[distance] = ref[...]
 
@@ -285,18 +301,25 @@
                 total = term if total is None else total + term
             out_ref[:, columns] = total.astype(BF16)
 
+        @pl.when(step == steps - 1)
+        def finish():
+            each_copy(lambda copy: copy.wait())
+
     column = pl.BlockSpec((rows, block), lambda j: (0, j))
     return pl.pallas_call(
         kernel,
-        grid=(owners // per_step,),
-        out_shape=jax.ShapeDtypeStruct((rows, width), BF16),
-        in_specs=[pl.BlockSpec((packed, HEAD), lambda j: (0, 0))] * count + [column],
-        out_specs=column,
-        scratch_shapes=[pltpu.VMEM((count, packed, HEAD), F32)],
+        grid=(steps,),
+        out_shape=[
+            jax.ShapeDtypeStruct((rows, width), BF16),
+            jax.ShapeDtypeStruct((tokens, wide * CHUNKS), BF16),
+        ],
+        in_specs=[pl.BlockSpec((packed, HEAD), lambda j: (0, 0))] * count + [VMEM] * len(sent) + [column],
+        out_specs=[column, ANY],
+        scratch_shapes=[pltpu.VMEM((count, packed, HEAD), F32), pltpu.SemaphoreType.DMA((CHUNKS,))],
         compiler_params=params(16),
         cost_estimate=cost(6 * rows * width * HEAD, 4 * rows * width),
         name="apply_mixing",
-    )(*mixes, buffer)
+    )(*mixes, *sent, buffer)
 
 
 def weight_products(chunks, kv_rows, weights):
@@ -374,64 +397,36 @@
     )(*inputs, *used)
 
 
-def collect(sent):
-    tokens, span = sent[0].shape
-    sections = lax.axis_size("pipe")
+def last_step(received, products, relayed):
+    tokens, span = products[0].shape
+    several = len(received)
 
     def kernel(*refs):
-        sent_refs = refs[: len(sent)]
-        out_ref, sems = refs[len(sent) :]
-        stage = lax.axis_index("pipe")
-        for section in range(sections):
-            ticks = [chunk + LAG * (sections - 1 - section) for chunk in range(CHUNKS)]
-
-            @pl.when(stage == section)
-            def one():
-                copies = []
-                for chunk, tick in enumerate(ticks):
-                    if tick < len(sent):
-                        target = out_ref.at[:, pl.ds(chunk * span, span)]
-                        copies.append(pltpu.make_async_copy(sent_refs[tick], target, sems.at[chunk]))
-                        copies[-1].start()
-                for copy in copies:
-                    copy.wait()
-
-    return pl.pallas_call(
-        kernel,
-        in_specs=[VMEM] * len(sent),
-        out_specs=ANY,
-        out_shape=jax.ShapeDtypeStruct((tokens, span * CHUNKS), BF16),
-        scratch_shapes=[pltpu.SemaphoreType.DMA((CHUNKS,))],
-        compiler_params=params(8),
-        cost_estimate=cost(0, 4 * tokens * span * CHUNKS),
-        name="collect",
-    )(*sent)
-
-
-def final_step(chunk, received, product, collected):
-    tokens, span = product.shape
-
-    def kernel(in_ref, prod_ref, old_ref, out_ref, held, sem):
-        del old_ref
+        in_refs, prod_refs = refs[:several], refs[several : 2 * several]
+        out_ref, held, sems = refs[2 * several + 1 :]
 
         @pl.when(lax.axis_index("pipe") == 0)
         def one():
-            held[...] = (in_ref[...].astype(F32) + prod_ref[...]).astype(BF16)
-            copy = pltpu.make_async_copy(held, out_ref.at[:, pl.ds(chunk * span, span)], sem)
-            copy.start()
-            copy.wait()
-
-    return pl.pallas_call(
-        kernel,
-        in_specs=[VMEM, VMEM, ANY],
+            copies = []
+            for at in range(several):
+                held[at] = (in_refs[at][...].astype(F32) + prod_refs[at][...]).astype(BF16)
+                target = out_ref.at[:, pl.ds((CHUNKS - several + at) * span, span)]
+                copies.append(pltpu.make_async_copy(held.at[at], target, sems.at[at]))
+                copies[-1].start()
+            for copy in copies:
+                copy.wait()
+
+    return pl.pallas_call(
+        kernel,
+        in_specs=[VMEM] * (2 * several) + [ANY],
         out_specs=ANY,
-        out_shape=jax.ShapeDtypeStruct(collected.shape, BF16),
-        scratch_shapes=[pltpu.VMEM((tokens, span), BF16), pltpu.SemaphoreType.DMA],
-        input_output_aliases={2: 0},
+        out_shape=jax.ShapeDtypeStruct(relayed.shape, BF16),
+        scratch_shapes=[pltpu.VMEM((several, tokens, span), BF16), pltpu.SemaphoreType.DMA((several,))],
+        input_output_aliases={2 * several: 0},
         compiler_params=params(8),
         cost_estimate=cost(0, 4 * tokens * span),
-        name="final_step",
-    )(received, product, collected)
+        name="last_step",
+    )(*received, *products, relayed)
 
 
 def token_relations():
@@ -475,37 +470,37 @@
     left = lax.all_to_all(columns, "dp", 0, 0, tiled=True)
     early = list(range(min(LAG, CHUNKS)))
     products = list(weight_products(early, after(kv_rows, columns), weights))
+    near = near[:1] + [after(piece, products[0]) for piece in near[1:]]
+    products = [after(product, far[0], *near[1:]) for product in products]
     relay()
     relay()
-    near = near[:1] + [after(piece, sent[1]) for piece in near[1:]]
     far.extend(swap(piece, other_core) for piece in near[1:])
     if chips == 4:
         near.append(swap(near[1], same[2]))
     products += weight_products(list(range(LAG, CHUNKS)), after(kv_rows, sent[1]), weights)
     relay(products[-1])
-    relay()
     if chips == 4:
-        far.append(swap(after(near[-1], sent[3]), other_core))
+        far.append(swap(after(near[-1], sent[2], moved[1]), other_core))
 
     buffer, mine, theirs = gradient(
-        left, same + crossed, near + far, after(moment, sent[3]), scale_grad, slots
+        left, same + crossed, near + far, after(moment, sent[2]), scale_grad, slots
     )
     received = swap(theirs, other_core)
     relay(buffer)
-    relay(buffer)
-    sums = add_pairs(after(mine, sent[5]), received)
+    relay()
+    sums = add_pairs(after(mine, sent[4]), received)
     grams = [sums[0]] + [swap(sums[d], (CORES * d, CORES * d)) for d in range(1, chips)]
-    mix = mixing(grams, scale, slots)
+    relay(*grams[1:])
+    mix = mixing([after(grams[0], sent[5])] + grams[1:], scale, slots)
     mixes = [mix] + [swap(mix, (CORES * d, CORES * d)) for d in range(1, chips)]
+    relay(mixes[1])
     far_mixes = [swap(m, other_core) for m in mixes]
     relay(*mixes[1:])
-    relay()
     distances = [CORES * d for d in range(chips)] + [CORES * d + 1 for d in range(chips)]
-    outgoing = collect(sent)
-    update = apply_mixing(after(buffer, sent[7]), distances, mixes + far_mixes, slots)
-    for chunk in range(CHUNKS - LAG, CHUNKS):
-        tick = chunk + LAG * (sections - 1)
-        outgoing = final_step(chunk, after(moved[tick - LAG], update), products[chunk], outgoing)
+    update, outgoing = apply_mixing(
+        after(buffer, sent[7]), distances, mixes + far_mixes, slots, sent
+    )
+    outgoing = last_step([after(m, update) for m in moved[-LAG:]], products[-LAG:], outgoing)
     return (update[None], outgoing[None])
 
 

time: 97.7 us -> 91.8 us (0.940)
  waiting for transfers between devices: 28.8 us -> 24.1 us
  Pallas kernels: 37 us -> 33.8 us
  starting transfers between devices: 29 us -> 30.2 us
    ppermute x18, waiting for transfers between devices: 8.68 us -> 4.94 us  [swap(): lax.ppermute(value, 'dp', [(i ^ by[i % CORES], i) for i in range(count)])]
    pallas_call x8, Pallas kernels: 3.57 us -> 1.9 us  [relay_step(): pl.pallas_call(kernel, in_specs=[VMEM] * (len(inputs) + len(used)), out_s...]
    pallas_call x4 -> x2, Pallas kernels: 7.81 us -> 6.29 us  [the longest x1 5.37 us: apply_mixing(): pl.pallas_call(kernel, grid=(steps,), out_shape=[jax.ShapeDtypeStruct((ro...]
    unnamed x14 -> x26, local copies, waits for them, and re-layouts: 1.34 us -> 2.09 us
  transfers between devices with their start and end apart: 27 -> 27, of which waited for: 14 -> 12; matrix products, arithmetic and copies ran while one was open for 0% -> 0% of each run, Pallas kernels for 36% -> 36%
where the time goes in v2:
time: 91.8 us; the launch traced here: 91.2 us
  Pallas kernels  33.8 us (37%)
  starting transfers between devices  30.2 us (33%)
  waiting for transfers between devices  24.1 us (26%)
  local copies, waits for them, and re-layouts  2.09 us (2%)
  between operations  0.98 us (1%)
    ppermute x8, waiting for transfers between devices, down(): return lax.ppermute(value, 'pipe', [(i, i - 1) for i in range(1, count)])  19.2 us
    ppermute x18, starting transfers between devices, swap(): lax.ppermute(value, 'dp', [(i ^ by[i % CORES], i) for i in range(count)])  15.2 us
    pallas_call x2, Pallas kernels, weight_products(): pl.pallas_call(kernel, out_shape=[jax.ShapeDtypeStruct((tokens, span), F3...  12.4 us
    ppermute x8, starting transfers between devices, down(): return lax.ppermute(value, 'pipe', [(i, i - 1) for i in range(1, count)])  10.7 us
    pallas_call x1, Pallas kernels, gradient(): pl.pallas_call(kernel, grid=(steps,), out_shape=[jax.ShapeDtypeStruct((ro...  7.78 us
    pallas_call x1, Pallas kernels, apply_mixing(): pl.pallas_call(kernel, grid=(steps,), out_shape=[jax.ShapeDtypeStruct((ro...  5.37 us
    ppermute x18, waiting for transfers between devices, swap(): lax.ppermute(value, 'dp', [(i ^ by[i % CORES], i) for i in range(count)])  4.94 us
    all_to_all x1, starting transfers between devices, shards(): left = lax.all_to_all(columns, 'dp', 0, 0, tiled=True)  4.4 us
  transfers between devices with their start and end apart: 27, of which 12 were waited for; matrix products, arithmetic and copies ran while one was open for 0% of the time, Pallas kernels for 36%

profile of v2, /device:TPU:0, one launch (start us, length us, event | category | flops | bytes accessed | tf_op | source)
XLA Modules:
  0.0 91.2 jit_solution(9995114687166537837)
XLA Ops:
  0.6 3.0 %collective-permute-start = (bf16[128,2048]{1,0:T(8,128)(2,1)}, bf16[128,2048]{1,0:T(8,128)(2,1)}, u32[]{:S(2)}, u32[]{:S(2)}) collective-permute-start(bf16[128,2048]{1,0:T(8,128)(2,1)} %bitcast.6), channel_id=1, source_target_pairs={{2,0},{5,1},{0,2},{7,3},{6,4},{1,5},{4,6},{3,7},{10,8},{13,9},{8,1... | collective-permute-start | bytes 1572872 | tf_op jit(solution)/shard_map/ppermute | solution.py:49
  3.6 1.5 %collective-permute-start.1 = (bf16[128,2048]{1,0:T(8,128)(2,1)}, bf16[128,2048]{1,0:T(8,128)(2,1)}, u32[]{:S(2)}, u32[]{:S(2)}) collective-permute-start(bf16[128,2048]{1,0:T(8,128)(2,1)} %bitcast.7), channel_id=1, source_target_pairs={{4,0},{3,1},{6,2},{1,3},{0,4},{7,5},{2,6},{5,7},{12,8},{11,9},{14,... | collective-permute-start | bytes 1572872 | tf_op jit(solution)/shard_map/ppermute | solution.py:49
  5.2 0.0 collective-permute-start.3
  5.2 1.3 %copy-done.9 = bf16[1,128,5120]{2,1,0:T(8,128)(2,1)S(1)} copy-done((bf16[1,128,5120]{2,1,0:T(8,128)(2,1)S(1)}, bf16[1,128,5120]{2,1,0:T(8,128)(2,1)}, u32[]{:S(2)}) %copy-start.9) | copy-done | bytes 1310744
  6.5 1.4 %split_columns.1 = bf16[8,640,128]{2,1,0:T(8,128)(2,1)} custom-call(bf16[128,5120]{1,0:T(8,128)(2,1)S(1)} %bitcast.12), custom_call_target="tpu_custom_call" | custom-call | flops 1 | bytes 1 | tf_op jit(solution)/shard_map/split_columns/pallas_call | solution.py:73
  7.9 4.4 %all-to-all-start = ((bf16[8,640,128]{2,1,0:T(8,128)(2,1)}), bf16[8,640,128]{2,1,0:T(8,128)(2,1)}, u32[]{:S(2)}, u32[]{:S(2)}) async-start(bf16[8,640,128]{2,1,0:T(8,128)(2,1)} %split_columns.1), calls=%async_computation | async-start | bytes 2621440 | tf_op jit(solution)/shard_map/all_to_all | solution.py:470
  12.3 0.0 copy-start
  12.4 6.3 %weight_products.2 = (f32[128,1280]{1,0:T(8,128)S(1)}, f32[128,1280]{1,0:T(8,128)S(1)}) custom-call(bf16[128,2048]{1,0:T(8,128)(2,1)S(1)} %bitcast.10, bf16[5120,2048]{1,0:T(8,128)(2,1)} %bitcast.13), custom_call_target="tpu_custom_call" | custom-call | flops 1 | bytes 1 | tf_op jit(solution)/shard_map/weight_products/pallas_call | solution.py:352
  18.6 0.0 copy-start.1
  18.6 0.0 collective-permute-done.refs_2_
  18.6 2.0 %collective-permute-start.2 = (bf16[128,2048]{1,0:T(8,128)(2,1)}, bf16[128,2048]{1,0:T(8,128)(2,1)}, u32[]{:S(2)}, u32[]{:S(2)}) collective-permute-start(bf16[128,2048]{1,0:T(8,128)(2,1)} %collective-permute-done.refs_2_), channel_id=1, source_target_pairs={{4,0},{3,1},{6,2},{1,3},{0,4},{7,5},{2,6},{5,7},{12,8},{11,9},{14,... | collective-permute-start | bytes 1572872 | tf_op jit(solution)/shard_map/ppermute | solution.py:49
  20.6 0.0 collective-permute-done.1.refs_3_
  20.6 0.0 collective-permute-done.3.refs_5_
  20.7 0.0 copy-start.4
  20.7 1.4 %collective-permute-start.6 = (bf16[128,1280]{1,0:T(8,128)(2,1)S(1)}, bf16[128,1280]{1,0:T(8,128)(2,1)S(1)}, u32[]{:S(2)}, u32[]{:S(2)}) collective-permute-start(bf16[128,1280]{1,0:T(8,128)(2,1)S(1)} %relay_step.8.refs_8_), channel_id=1, source_target_pairs={{8,0},{16,8},{24,16},{9,1},{17,9},{25,17},{10,2},{18,10},{26,18},{... | collective-permute-start | bytes 983048 | tf_op jit(solution)/shard_map/ppermute | solution.py:54
  22.1 1.3 %collective-permute-start.7 = (bf16[128,1280]{1,0:T(8,128)(2,1)S(1)}, bf16[128,1280]{1,0:T(8,128)(2,1)S(1)}, u32[]{:S(2)}, u32[]{:S(2)}) collective-permute-start(bf16[128,1280]{1,0:T(8,128)(2,1)S(1)} %relay_step.9.refs_9_), channel_id=1, source_target_pairs={{8,0},{16,8},{24,16},{9,1},{17,9},{25,17},{10,2},{18,10},{26,18},{... | collective-permute-start | bytes 983048 | tf_op jit(solution)/shard_map/ppermute | solution.py:54
  23.4 0.1 collective-permute-start.4
  23.5 0.5 collective-permute-start.5
  24.0 6.2 %weight_products.3 = (f32[128,1280]{1,0:T(8,128)S(1)}, f32[128,1280]{1,0:T(8,128)S(1)}) custom-call(bf16[128,2048]{1,0:T(8,128)(2,1)S(1)} %bitcast.11, bf16[5120,2048]{1,0:T(8,128)(2,1)} %bitcast.14), custom_call_target="tpu_custom_call" | custom-call | flops 1 | bytes 1 | tf_op jit(solution)/shard_map/weight_products/pallas_call | solution.py:352
  30.2 3.1 %collective-permute-done.6.refs_0_ = bf16[128,1280]{1,0:T(8,128)(2,1)S(1)} collective-permute-done((bf16[128,1280]{1,0:T(8,128)(2,1)S(1)}, bf16[128,1280]{1,0:T(8,128)(2,1)S(1)}, u32[]{:S(2)}, u32[]{:S(2)}) %collective-permute-start.6) | collective-permute-done | bytes 327712 | tf_op jit(solution)/shard_map/ppermute | solution.py:54
  33.3 0.7 relay_step.10.refs_10_
  34.0 5.2 %collective-permute-done.7.refs_0_ = bf16[128,1280]{1,0:T(8,128)(2,1)S(1)} collective-permute-done((bf16[128,1280]{1,0:T(8,128)(2,1)S(1)}, bf16[128,1280]{1,0:T(8,128)(2,1)S(1)}, u32[]{:S(2)}, u32[]{:S(2)}) %collective-permute-start.7) | collective-permute-done | bytes 327712 | tf_op jit(solution)/shard_map/ppermute | solution.py:54
  39.2 0.7 copy-done.10
  39.9 0.0 collective-permute-done.2.refs_4_
  39.9 0.0 collective-permute-start.8
  39.9 1.3 %collective-permute-start.9 = (bf16[128,1280]{1,0:T(8,128)(2,1)}, bf16[128,1280]{1,0:T(8,128)(2,1)}, u32[]{:S(2)}, u32[]{:S(2)}) collective-permute-start(bf16[128,1280]{1,0:T(8,128)(2,1)} %relay_step.10.refs_10_), channel_id=1, source_target_pairs={{8,0},{16,8},{24,16},{9,1},{17,9},{25,17},{10,2},{18,10},{26,18},{... | collective-permute-start | bytes 983048 | tf_op jit(solution)/shard_map/ppermute | solution.py:54
  41.2 0.0 collective-permute-done.4.refs_6_
  41.2 0.0 collective-permute-done.5.refs_7_
  41.2 0.0 all-to-all-done.refs_0_
  41.3 0.9 %collective-permute-done.8.refs_8_ = bf16[128,2048]{1,0:T(8,128)(2,1)} collective-permute-done((bf16[128,2048]{1,0:T(8,128)(2,1)}, bf16[128,2048]{1,0:T(8,128)(2,1)}, u32[]{:S(2)}, u32[]{:S(2)}) %collective-permute-start.8) | collective-permute-done | bytes 524320 | tf_op jit(solution)/shard_map/ppermute | solution.py:49
  42.2 7.8 %gradient.1 = (bf16[640,2048]{1,0:T(8,128)(2,1)S(1)}, f32[4,136,128]{2,1,0:T(8,128)S(1)}, f32[4,136,128]{2,1,0:T(8,128)S(1)}) custom-call(bf16[8,640,128]{2,1,0:T(8,128)(2,1)} %all-to-all-done.refs_0_, bf16[128,2048]{1,0:T(8,128)(2,1)} %bitcast.9, bf16[128,2048]{1,0:T(8,128)(2,1)} %collective-permute-done.refs_2_, ...), custom_call_target="tpu_custom_call" | custom-call | flops 1 | bytes 1 | tf_op jit(solution)/shard_map/gradient/pallas_call | solution.py:169
  50.0 0.2 collective-permute-start.10
  50.2 1.4 %collective-permute-start.11 = (bf16[128,1280]{1,0:T(8,128)(2,1)S(1)}, bf16[128,1280]{1,0:T(8,128)(2,1)S(1)}, u32[]{:S(2)}, u32[]{:S(2)}) collective-permute-start(bf16[128,1280]{1,0:T(8,128)(2,1)S(1)} %relay_step.11.refs_11_), channel_id=1, source_target_pairs={{8,0},{16,8},{24,16},{9,1},{17,9},{25,17},{10,2},{18,10},{26,18},{... | collective-permute-start | bytes 983048 | tf_op jit(solution)/shard_map/ppermute | solution.py:54
  51.6 0.7 collective-permute-done.9.refs_0_
  52.2 1.0 %relay_step.12.refs_12_ = bf16[128,1280]{1,0:T(8,128)(2,1)S(1)} custom-call(bf16[128,1280]{1,0:T(8,128)(2,1)} %collective-permute-done.9.refs_0_, f32[128,1280]{1,0:T(8,128)S(1)} %copy-done.2, f32[128,1280]{1,0:T(8,128)S(1)} %get-tuple-element.44.refs_3_.refs_2_), custom_call_target="tpu_custom_call" | custom-call | flops 1 | bytes 1 | tf_op jit(solution)/shard_map/relay_step/pallas_call | solution.py:389
  53.3 0.5 collective-permute-start.12
  53.8 1.6 %collective-permute-start.13 = (f32[136,128]{1,0:T(8,128)S(1)}, f32[136,128]{1,0:T(8,128)S(1)}, u32[]{:S(2)}, u32[]{:S(2)}) collective-permute-start(f32[136,128]{1,0:T(8,128)S(1)} %get-tuple-element.55), channel_id=1, source_target_pairs={{4,0},{5,1},{6,2},{7,3},{0,4},{1,5},{2,6},{3,7},{12,8},{13,9},{14,... | collective-permute-start | bytes 208904 | tf_op jit(solution)/shard_map/ppermute | solution.py:49
  55.4 1.4 %collective-permute-start.14 = (f32[136,128]{1,0:T(8,128)S(1)}, f32[136,128]{1,0:T(8,128)S(1)}, u32[]{:S(2)}, u32[]{:S(2)}) collective-permute-start(f32[136,128]{1,0:T(8,128)S(1)} %get-tuple-element.56), channel_id=1, source_target_pairs={{6,0},{7,1},{4,2},{5,3},{2,4},{3,5},{0,6},{1,7},{14,8},{15,9},{12,... | collective-permute-start | bytes 208904 | tf_op jit(solution)/shard_map/ppermute | solution.py:49
  56.8 1.3 %collective-permute-start.22 = (bf16[128,1280]{1,0:T(8,128)(2,1)S(1)}, bf16[128,1280]{1,0:T(8,128)(2,1)S(1)}, u32[]{:S(2)}, u32[]{:S(2)}) collective-permute-start(bf16[128,1280]{1,0:T(8,128)(2,1)S(1)} %relay_step.12.refs_12_), channel_id=1, source_target_pairs={{8,0},{16,8},{24,16},{9,1},{17,9},{25,17},{10,2},{18,10},{26,18},{... | collective-permute-start | bytes 983048 | tf_op jit(solution)/shard_map/ppermute | solution.py:54
  58.1 4.6 %collective-permute-done.11.refs_0_ = bf16[128,1280]{1,0:T(8,128)(2,1)S(1)} collective-permute-done((bf16[128,1280]{1,0:T(8,128)(2,1)S(1)}, bf16[128,1280]{1,0:T(8,128)(2,1)S(1)}, u32[]{:S(2)}, u32[]{:S(2)}) %collective-permute-start.11) | collective-permute-done | bytes 327712 | tf_op jit(solution)/shard_map/ppermute | solution.py:54
  62.7 0.0 collective-permute-done.12.refs_1_
  62.8 1.3 %collective-permute-start.23 = (bf16[128,1280]{1,0:T(8,128)(2,1)S(1)}, bf16[128,1280]{1,0:T(8,128)(2,1)S(1)}, u32[]{:S(2)}, u32[]{:S(2)}) collective-permute-start(bf16[128,1280]{1,0:T(8,128)(2,1)S(1)} %relay_step.13.refs_13_), channel_id=1, source_target_pairs={{8,0},{16,8},{24,16},{9,1},{17,9},{25,17},{10,2},{18,10},{26,18},{... | collective-permute-start | bytes 983048 | tf_op jit(solution)/shard_map/ppermute | solution.py:54
  64.1 3.9 %mixing.1.refs_0_ = f32[136,128]{1,0:T(8,128)S(1)} custom-call(f32[136,128]{1,0:T(8,128)S(1)} %get-tuple-element.58.refs_0_, f32[136,128]{1,0:T(8,128)S(1)} %collective-permute-done.12.refs_1_, f32[136,128]{1,0:T(8,128)S(1)} %collective-permute-done.13.refs_2_, f32[136,128]{1,0:T(8,128)S(1)} %collective-permute-done.14.refs_3_), custom_call_target="tpu_custom_call" | custom-call | flops 1 | bytes 1 | tf_op jit(solution)/shard_map/mixing/pallas_call | solution.py:235
  68.0 0.5 collective-permute-start.15
  68.5 1.6 %collective-permute-start.16 = (f32[136,128]{1,0:T(8,128)S(1)}, f32[136,128]{1,0:T(8,128)S(1)}, u32[]{:S(2)}, u32[]{:S(2)}) collective-permute-start(f32[136,128]{1,0:T(8,128)S(1)} %mixing.1.refs_0_), channel_id=1, source_target_pairs={{4,0},{5,1},{6,2},{7,3},{0,4},{1,5},{2,6},{3,7},{12,8},{13,9},{14,... | collective-permute-start | bytes 208904 | tf_op jit(solution)/shard_map/ppermute | solution.py:49
  70.1 1.4 %collective-permute-start.17 = (f32[136,128]{1,0:T(8,128)S(1)}, f32[136,128]{1,0:T(8,128)S(1)}, u32[]{:S(2)}, u32[]{:S(2)}) collective-permute-start(f32[136,128]{1,0:T(8,128)S(1)} %mixing.1.refs_0_), channel_id=1, source_target_pairs={{6,0},{7,1},{4,2},{5,3},{2,4},{3,5},{0,6},{1,7},{14,8},{15,9},{12,... | collective-permute-start | bytes 208904 | tf_op jit(solution)/shard_map/ppermute | solution.py:49
  71.6 0.0 collective-permute-done.22.refs_0_
  71.6 1.1 %collective-permute-done.15.refs_1_ = f32[136,128]{1,0:T(8,128)S(1)} collective-permute-done((f32[136,128]{1,0:T(8,128)S(1)}, f32[136,128]{1,0:T(8,128)S(1)}, u32[]{:S(2)}, u32[]{:S(2)}) %collective-permute-start.15) | collective-permute-done | bytes 69664 | tf_op jit(solution)/shard_map/ppermute | solution.py:49
  72.6 0.1 relay_step.14.refs_14_
  72.7 1.4 %collective-permute-start.24 = (bf16[128,1280]{1,0:T(8,128)(2,1)S(1)}, bf16[128,1280]{1,0:T(8,128)(2,1)S(1)}, u32[]{:S(2)}, u32[]{:S(2)}) collective-permute-start(bf16[128,1280]{1,0:T(8,128)(2,1)S(1)} %relay_step.14.refs_14_), channel_id=1, source_target_pairs={{8,0},{16,8},{24,16},{9,1},{17,9},{25,17},{10,2},{18,10},{26,18},{... | collective-permute-start | bytes 983048 | tf_op jit(solution)/shard_map/ppermute | solution.py:54
  74.2 1.2 %collective-permute-done.17.refs_3_ = f32[136,128]{1,0:T(8,128)S(1)} collective-permute-done((f32[136,128]{1,0:T(8,128)S(1)}, f32[136,128]{1,0:T(8,128)S(1)}, u32[]{:S(2)}, u32[]{:S(2)}) %collective-permute-start.17) | collective-permute-done | bytes 69664 | tf_op jit(solution)/shard_map/ppermute | solution.py:49
  75.3 1.1 %collective-permute-done.23.refs_0_ = bf16[128,1280]{1,0:T(8,128)(2,1)S(1)} collective-permute-done((bf16[128,1280]{1,0:T(8,128)(2,1)S(1)}, bf16[128,1280]{1,0:T(8,128)(2,1)S(1)}, u32[]{:S(2)}, u32[]{:S(2)}) %collective-permute-start.23) | collective-permute-done | bytes 327712 | tf_op jit(solution)/shard_map/ppermute | solution.py:54
  76.5 0.1 relay_step.15.refs_15_
  76.6 1.3 %collective-permute-start.25 = (bf16[128,1280]{1,0:T(8,128)(2,1)S(1)}, bf16[128,1280]{1,0:T(8,128)(2,1)S(1)}, u32[]{:S(2)}, u32[]{:S(2)}) collective-permute-start(bf16[128,1280]{1,0:T(8,128)(2,1)S(1)} %relay_step.15.refs_15_), channel_id=1, source_target_pairs={{8,0},{16,8},{24,16},{9,1},{17,9},{25,17},{10,2},{18,10},{26,18},{... | collective-permute-start | bytes 983048 | tf_op jit(solution)/shard_map/ppermute | solution.py:54
  77.9 0.1 collective-permute-start.18
  77.9 0.5 collective-permute-start.19
  78.4 0.1 collective-permute-start.20
  78.5 0.7 collective-permute-done.18.refs_4_
  79.2 0.2 collective-permute-start.21
  79.3 0.3 collective-permute-done.20.refs_6_
  79.7 0.7 collective-permute-done.21.refs_7_
  80.5 5.4 %apply_mixing.1 = (bf16[640,2048]{1,0:T(8,128)(2,1)}, bf16[128,5120]{1,0:T(8,128)(2,1)}) custom-call(f32[136,128]{1,0:T(8,128)S(1)} %mixing.1.refs_0_, f32[136,128]{1,0:T(8,128)S(1)} %collective-permute-done.15.refs_1_, f32[136,128]{1,0:T(8,128)S(1)} %collective-permute-done.16.refs_2_, f32[136,128]{1,0:T(8,128)S(1)} %collective-permute-done.17.refs_3_, ...), custom_call_target="tpu_custom_call" | custom-call | flops 1 | bytes 1 | tf_op jit(solution)/shard_map/apply_mixing/pallas_call | solution.py:309
  85.8 4.5 %collective-permute-done.25.refs_1_ = bf16[128,1280]{1,0:T(8,128)(2,1)S(1)} collective-permute-done((bf16[128,1280]{1,0:T(8,128)(2,1)S(1)}, bf16[128,1280]{1,0:T(8,128)(2,1)S(1)}, u32[]{:S(2)}, u32[]{:S(2)}) %collective-permute-start.25) | collective-permute-done | bytes 327712 | tf_op jit(solution)/shard_map/ppermute | solution.py:54
  90.3 0.9 %last_step.1 = bf16[128,5120]{1,0:T(8,128)(2,1)} custom-call(bf16[128,1280]{1,0:T(8,128)(2,1)S(1)} %collective-permute-done.24.refs_0_, bf16[128,1280]{1,0:T(8,128)(2,1)S(1)} %collective-permute-done.25.refs_1_, f32[128,1280]{1,0:T(8,128)S(1)} %get-tuple-element.44.refs_3_.refs_2_, ...), custom_call_target="tpu_custom_call", output_to_operand_aliasing={{}: (4, {})} | custom-call | flops 1 | bytes 1 | tf_op jit(solution)/shard_map/last_step/pallas_call | solution.py:419
  (32 shorter events, 0.1 us)
Async XLA Ops:
  0.6 18.0 %collective-permute-start = (bf16[128,2048]{1,0:T(8,128)(2,1)}, bf16[128,2048]{1,0:T(8,128)(2,1)}, u32[]{:S(2)}, u32[]{:S(2)}) collective-permute-start(bf16[128,2048]{1,0:T(8,128)(2,1)} %bitcast.6), channel_id=1, source_target_pairs={{2,0},{5,1},{0,2},{7,3},{6,4},{1,5},{4,6},{3,7},{10,8},{13,9},{8,1... | collective-permute-start | bytes 1572872 | tf_op jit(solution)/shard_map/ppermute | solution.py:49
  3.6 17.0 %collective-permute-start.1 = (bf16[128,2048]{1,0:T(8,128)(2,1)}, bf16[128,2048]{1,0:T(8,128)(2,1)}, u32[]{:S(2)}, u32[]{:S(2)}) collective-permute-start(bf16[128,2048]{1,0:T(8,128)(2,1)} %bitcast.7), channel_id=1, source_target_pairs={{4,0},{3,1},{6,2},{1,3},{0,4},{7,5},{2,6},{5,7},{12,8},{11,9},{14,... | collective-permute-start | bytes 1572872 | tf_op jit(solution)/shard_map/ppermute | solution.py:49
  5.2 15.5 %collective-permute-start.3 = (bf16[128,2048]{1,0:T(8,128)(2,1)}, bf16[128,2048]{1,0:T(8,128)(2,1)S(1)}, u32[]{:S(2)}, u32[]{:S(2)}) collective-permute-start(bf16[128,2048]{1,0:T(8,128)(2,1)} %bitcast.8), channel_id=1, source_target_pairs={{1,0},{0,1},{3,2},{2,3},{5,4},{4,5},{7,6},{6,7},{9,8},{8,9},{11,10... | collective-permute-start | bytes 1572872 | tf_op jit(solution)/shard_map/ppermute | solution.py:49
  5.2 1.3 %copy-start.9 = (bf16[1,128,5120]{2,1,0:T(8,128)(2,1)S(1)}, bf16[1,128,5120]{2,1,0:T(8,128)(2,1)}, u32[]{:S(2)}) copy-start(bf16[1,128,5120]{2,1,0:T(8,128)(2,1)} %param.5) | copy-start | bytes 3932164
  7.9 4.4 %copy-start.3 = (bf16[1,128,2048]{2,1,0:T(8,128)(2,1)S(1)}, bf16[1,128,2048]{2,1,0:T(8,128)(2,1)}, u32[]{:S(2)}) copy-start(bf16[1,128,2048]{2,1,0:T(8,128)(2,1)} %param.7) | copy-start | bytes 1572868
  7.9 33.3 %all-to-all-start = ((bf16[8,640,128]{2,1,0:T(8,128)(2,1)}), bf16[8,640,128]{2,1,0:T(8,128)(2,1)}, u32[]{:S(2)}, u32[]{:S(2)}) async-start(bf16[8,640,128]{2,1,0:T(8,128)(2,1)} %split_columns.1), calls=%async_computation | async-start | bytes 2621440 | tf_op jit(solution)/shard_map/all_to_all | solution.py:470
  12.3 8.3 %copy-start = (bf16[128,5120]{1,0:T(8,128)(2,1)S(1)}, bf16[128,5120]{1,0:T(8,128)(2,1)}, u32[]{:S(2)}) copy-start(bf16[128,5120]{1,0:T(8,128)(2,1)} %refs_1_.3) | copy-start | bytes 3932164
  18.6 14.7 %copy-start.1 = (f32[128,1280]{1,0:T(8,128)}, f32[128,1280]{1,0:T(8,128)S(1)}, u32[]{:S(2)}) copy-start(f32[128,1280]{1,0:T(8,128)S(1)} %get-tuple-element.38.refs_1_.refs_2_) | copy-start | bytes 1966084
  18.6 21.3 %collective-permute-start.2 = (bf16[128,2048]{1,0:T(8,128)(2,1)}, bf16[128,2048]{1,0:T(8,128)(2,1)}, u32[]{:S(2)}, u32[]{:S(2)}) collective-permute-start(bf16[128,2048]{1,0:T(8,128)(2,1)} %collective-permute-done.refs_2_), channel_id=1, source_target_pairs={{4,0},{3,1},{6,2},{1,3},{0,4},{7,5},{2,6},{5,7},{12,8},{11,9},{14,... | collective-permute-start | bytes 1572872 | tf_op jit(solution)/shard_map/ppermute | solution.py:49
  20.6 1.5 %copy-start.12 = (bf16[128,2048]{1,0:T(8,128)(2,1)}, bf16[128,2048]{1,0:T(8,128)(2,1)S(1)}, u32[]{:S(2)}) copy-start(bf16[128,2048]{1,0:T(8,128)(2,1)S(1)} %collective-permute-done.3.refs_5_) | copy-start | bytes 1572868
  20.6 9.5 %copy-start.5 = (bf16[128,1280]{1,0:T(8,128)(2,1)}, bf16[128,1280]{1,0:T(8,128)(2,1)S(1)}, u32[]{:S(2)}) copy-start(bf16[128,1280]{1,0:T(8,128)(2,1)S(1)} %relay_step.8.refs_8_) | copy-start | bytes 983044
  20.7 3.4 %copy-start.4 = (bf16[1,128,2048]{2,1,0:T(8,128)(2,1)S(1)}, bf16[1,128,2048]{2,1,0:T(8,128)(2,1)}, u32[]{:S(2)}) copy-start(bf16[1,128,2048]{2,1,0:T(8,128)(2,1)} %param.7) | copy-start | bytes 1572868
  20.7 12.6 %collective-permute-start.6 = (bf16[128,1280]{1,0:T(8,128)(2,1)S(1)}, bf16[128,1280]{1,0:T(8,128)(2,1)S(1)}, u32[]{:S(2)}, u32[]{:S(2)}) collective-permute-start(bf16[128,1280]{1,0:T(8,128)(2,1)S(1)} %relay_step.8.refs_8_), channel_id=1, source_target_pairs={{8,0},{16,8},{24,16},{9,1},{17,9},{25,17},{10,2},{18,10},{26,18},{... | collective-permute-start | bytes 983048 | tf_op jit(solution)/shard_map/ppermute | solution.py:54
  22.1 8.1 %copy-start.7 = (bf16[128,1280]{1,0:T(8,128)(2,1)}, bf16[128,1280]{1,0:T(8,128)(2,1)S(1)}, u32[]{:S(2)}) copy-start(bf16[128,1280]{1,0:T(8,128)(2,1)S(1)} %relay_step.9.refs_9_) | copy-start | bytes 983044
  22.1 17.0 %collective-permute-start.7 = (bf16[128,1280]{1,0:T(8,128)(2,1)S(1)}, bf16[128,1280]{1,0:T(8,128)(2,1)S(1)}, u32[]{:S(2)}, u32[]{:S(2)}) collective-permute-start(bf16[128,1280]{1,0:T(8,128)(2,1)S(1)} %relay_step.9.refs_9_), channel_id=1, source_target_pairs={{8,0},{16,8},{24,16},{9,1},{17,9},{25,17},{10,2},{18,10},{26,18},{... | collective-permute-start | bytes 983048 | tf_op jit(solution)/shard_map/ppermute | solution.py:54
  23.4 17.8 %collective-permute-start.4 = (bf16[128,2048]{1,0:T(8,128)(2,1)}, bf16[128,2048]{1,0:T(8,128)(2,1)}, u32[]{:S(2)}, u32[]{:S(2)}) collective-permute-start(bf16[128,2048]{1,0:T(8,128)(2,1)} %collective-permute-done.refs_2_), channel_id=1, source_target_pairs={{1,0},{0,1},{3,2},{2,3},{5,4},{4,5},{7,6},{6,7},{9,8},{8,9},{11,10... | collective-permute-start | bytes 1572872 | tf_op jit(solution)/shard_map/ppermute | solution.py:49
  23.5 17.7 %collective-permute-start.5 = (bf16[128,2048]{1,0:T(8,128)(2,1)}, bf16[128,2048]{1,0:T(8,128)(2,1)}, u32[]{:S(2)}, u32[]{:S(2)}) collective-permute-start(bf16[128,2048]{1,0:T(8,128)(2,1)} %collective-permute-done.1.refs_3_), channel_id=1, source_target_pairs={{1,0},{0,1},{3,2},{2,3},{5,4},{4,5},{7,6},{6,7},{9,8},{8,9},{11,10... | collective-permute-start | bytes 1572872 | tf_op jit(solution)/shard_map/ppermute | solution.py:49
  39.2 0.7 copy-start.10
  39.9 2.3 %collective-permute-start.8 = (bf16[128,2048]{1,0:T(8,128)(2,1)}, bf16[128,2048]{1,0:T(8,128)(2,1)}, u32[]{:S(2)}, u32[]{:S(2)}) collective-permute-start(bf16[128,2048]{1,0:T(8,128)(2,1)} %collective-permute-done.2.refs_4_), channel_id=1, source_target_pairs={{1,0},{0,1},{3,2},{2,3},{5,4},{4,5},{7,6},{6,7},{9,8},{8,9},{11,10... | collective-permute-start | bytes 1572872 | tf_op jit(solution)/shard_map/ppermute | solution.py:49
  39.9 12.3 %collective-permute-start.9 = (bf16[128,1280]{1,0:T(8,128)(2,1)}, bf16[128,1280]{1,0:T(8,128)(2,1)}, u32[]{:S(2)}, u32[]{:S(2)}) collective-permute-start(bf16[128,1280]{1,0:T(8,128)(2,1)} %relay_step.10.refs_10_), channel_id=1, source_target_pairs={{8,0},{16,8},{24,16},{9,1},{17,9},{25,17},{10,2},{18,10},{26,18},{... | collective-permute-start | bytes 983048 | tf_op jit(solution)/shard_map/ppermute | solution.py:54
  41.2 8.9 %copy-start.11 = (bf16[128,1280]{1,0:T(8,128)(2,1)S(1)}, bf16[128,1280]{1,0:T(8,128)(2,1)}, u32[]{:S(2)}) copy-start(bf16[128,1280]{1,0:T(8,128)(2,1)} %copy-done.10) | copy-start | bytes 983044
  50.0 3.3 %collective-permute-start.10 = (f32[4,136,128]{2,1,0:T(8,128)S(1)}, f32[4,136,128]{2,1,0:T(8,128)S(1)}, u32[]{:S(2)}, u32[]{:S(2)}) collective-permute-start(f32[4,136,128]{2,1,0:T(8,128)S(1)} %get-tuple-element.52), channel_id=1, source_target_pairs={{1,0},{0,1},{3,2},{2,3},{5,4},{4,5},{7,6},{6,7},{9,8},{8,9},{11,10... | collective-permute-start | bytes 835592 | tf_op jit(solution)/shard_map/ppermute | solution.py:49
  50.2 2.1 %copy-start.2 = (f32[128,1280]{1,0:T(8,128)S(1)}, f32[128,1280]{1,0:T(8,128)}, u32[]{:S(2)}) copy-start(f32[128,1280]{1,0:T(8,128)} %copy-done.1) | copy-start | bytes 1966084
  50.2 12.6 %collective-permute-start.11 = (bf16[128,1280]{1,0:T(8,128)(2,1)S(1)}, bf16[128,1280]{1,0:T(8,128)(2,1)S(1)}, u32[]{:S(2)}, u32[]{:S(2)}) collective-permute-start(bf16[128,1280]{1,0:T(8,128)(2,1)S(1)} %relay_step.11.refs_11_), channel_id=1, source_target_pairs={{8,0},{16,8},{24,16},{9,1},{17,9},{25,17},{10,2},{18,10},{26,18},{... | collective-permute-start | bytes 983048 | tf_op jit(solution)/shard_map/ppermute | solution.py:54
  53.3 9.5 %collective-permute-start.12 = (f32[136,128]{1,0:T(8,128)S(1)}, f32[136,128]{1,0:T(8,128)S(1)}, u32[]{:S(2)}, u32[]{:S(2)}) collective-permute-start(f32[136,128]{1,0:T(8,128)S(1)} %get-tuple-element.54), channel_id=1, source_target_pairs={{2,0},{3,1},{0,2},{1,3},{6,4},{7,5},{4,6},{5,7},{10,8},{11,9},{8,1... | collective-permute-start | bytes 208904 | tf_op jit(solution)/shard_map/ppermute | solution.py:49
  53.8 8.9 %collective-permute-start.13 = (f32[136,128]{1,0:T(8,128)S(1)}, f32[136,128]{1,0:T(8,128)S(1)}, u32[]{:S(2)}, u32[]{:S(2)}) collective-permute-start(f32[136,128]{1,0:T(8,128)S(1)} %get-tuple-element.55), channel_id=1, source_target_pairs={{4,0},{5,1},{6,2},{7,3},{0,4},{1,5},{2,6},{3,7},{12,8},{13,9},{14,... | collective-permute-start | bytes 208904 | tf_op jit(solution)/shard_map/ppermute | solution.py:49
  55.4 7.4 %collective-permute-start.14 = (f32[136,128]{1,0:T(8,128)S(1)}, f32[136,128]{1,0:T(8,128)S(1)}, u32[]{:S(2)}, u32[]{:S(2)}) collective-permute-start(f32[136,128]{1,0:T(8,128)S(1)} %get-tuple-element.56), channel_id=1, source_target_pairs={{6,0},{7,1},{4,2},{5,3},{2,4},{3,5},{0,6},{1,7},{14,8},{15,9},{12,... | collective-permute-start | bytes 208904 | tf_op jit(solution)/shard_map/ppermute | solution.py:49
  56.8 14.7 %collective-permute-start.22 = (bf16[128,1280]{1,0:T(8,128)(2,1)S(1)}, bf16[128,1280]{1,0:T(8,128)(2,1)S(1)}, u32[]{:S(2)}, u32[]{:S(2)}) collective-permute-start(bf16[128,1280]{1,0:T(8,128)(2,1)S(1)} %relay_step.12.refs_12_), channel_id=1, source_target_pairs={{8,0},{16,8},{24,16},{9,1},{17,9},{25,17},{10,2},{18,10},{26,18},{... | collective-permute-start | bytes 983048 | tf_op jit(solution)/shard_map/ppermute | solution.py:54
  62.8 13.7 %collective-permute-start.23 = (bf16[128,1280]{1,0:T(8,128)(2,1)S(1)}, bf16[128,1280]{1,0:T(8,128)(2,1)S(1)}, u32[]{:S(2)}, u32[]{:S(2)}) collective-permute-start(bf16[128,1280]{1,0:T(8,128)(2,1)S(1)} %relay_step.13.refs_13_), channel_id=1, source_target_pairs={{8,0},{16,8},{24,16},{9,1},{17,9},{25,17},{10,2},{18,10},{26,18},{... | collective-permute-start | bytes 983048 | tf_op jit(solution)/shard_map/ppermute | solution.py:54
  68.0 4.6 %collective-permute-start.15 = (f32[136,128]{1,0:T(8,128)S(1)}, f32[136,128]{1,0:T(8,128)S(1)}, u32[]{:S(2)}, u32[]{:S(2)}) collective-permute-start(f32[136,128]{1,0:T(8,128)S(1)} %mixing.1.refs_0_), channel_id=1, source_target_pairs={{2,0},{3,1},{0,2},{1,3},{6,4},{7,5},{4,6},{5,7},{10,8},{11,9},{8,1... | collective-permute-start | bytes 208904 | tf_op jit(solution)/shard_map/ppermute | solution.py:49
  68.5 5.6 %collective-permute-start.16 = (f32[136,128]{1,0:T(8,128)S(1)}, f32[136,128]{1,0:T(8,128)S(1)}, u32[]{:S(2)}, u32[]{:S(2)}) collective-permute-start(f32[136,128]{1,0:T(8,128)S(1)} %mixing.1.refs_0_), channel_id=1, source_target_pairs={{4,0},{5,1},{6,2},{7,3},{0,4},{1,5},{2,6},{3,7},{12,8},{13,9},{14,... | collective-permute-start | bytes 208904 | tf_op jit(solution)/shard_map/ppermute | solution.py:49
  70.1 5.2 %collective-permute-start.17 = (f32[136,128]{1,0:T(8,128)S(1)}, f32[136,128]{1,0:T(8,128)S(1)}, u32[]{:S(2)}, u32[]{:S(2)}) collective-permute-start(f32[136,128]{1,0:T(8,128)S(1)} %mixing.1.refs_0_), channel_id=1, source_target_pairs={{6,0},{7,1},{4,2},{5,3},{2,4},{3,5},{0,6},{1,7},{14,8},{15,9},{12,... | collective-permute-start | bytes 208904 | tf_op jit(solution)/shard_map/ppermute | solution.py:49
  72.7 7.7 %copy-start.6 = (bf16[128,1280]{1,0:T(8,128)(2,1)S(1)}, bf16[128,1280]{1,0:T(8,128)(2,1)}, u32[]{:S(2)}) copy-start(bf16[128,1280]{1,0:T(8,128)(2,1)} %copy-done.5) | copy-start | bytes 983044
  72.7 7.7 %copy-start.8 = (bf16[128,1280]{1,0:T(8,128)(2,1)S(1)}, bf16[128,1280]{1,0:T(8,128)(2,1)}, u32[]{:S(2)}) copy-start(bf16[128,1280]{1,0:T(8,128)(2,1)} %copy-done.7) | copy-start | bytes 983044
  72.7 13.1 %collective-permute-start.24 = (bf16[128,1280]{1,0:T(8,128)(2,1)S(1)}, bf16[128,1280]{1,0:T(8,128)(2,1)S(1)}, u32[]{:S(2)}, u32[]{:S(2)}) collective-permute-start(bf16[128,1280]{1,0:T(8,128)(2,1)S(1)} %relay_step.14.refs_14_), channel_id=1, source_target_pairs={{8,0},{16,8},{24,16},{9,1},{17,9},{25,17},{10,2},{18,10},{26,18},{... | collective-permute-start | bytes 983048 | tf_op jit(solution)/shard_map/ppermute | solution.py:54
  76.6 13.7 %collective-permute-start.25 = (bf16[128,1280]{1,0:T(8,128)(2,1)S(1)}, bf16[128,1280]{1,0:T(8,128)(2,1)S(1)}, u32[]{:S(2)}, u32[]{:S(2)}) collective-permute-start(bf16[128,1280]{1,0:T(8,128)(2,1)S(1)} %relay_step.15.refs_15_), channel_id=1, source_target_pairs={{8,0},{16,8},{24,16},{9,1},{17,9},{25,17},{10,2},{18,10},{26,18},{... | collective-permute-start | bytes 983048 | tf_op jit(solution)/shard_map/ppermute | solution.py:54
  77.9 1.3 %collective-permute-start.18 = (f32[136,128]{1,0:T(8,128)S(1)}, f32[136,128]{1,0:T(8,128)S(1)}, u32[]{:S(2)}, u32[]{:S(2)}) collective-permute-start(f32[136,128]{1,0:T(8,128)S(1)} %mixing.1.refs_0_), channel_id=1, source_target_pairs={{1,0},{0,1},{3,2},{2,3},{5,4},{4,5},{7,6},{6,7},{9,8},{8,9},{11,10... | collective-permute-start | bytes 208904 | tf_op jit(solution)/shard_map/ppermute | solution.py:49
  77.9 1.4 %collective-permute-start.19 = (f32[136,128]{1,0:T(8,128)S(1)}, f32[136,128]{1,0:T(8,128)S(1)}, u32[]{:S(2)}, u32[]{:S(2)}) collective-permute-start(f32[136,128]{1,0:T(8,128)S(1)} %collective-permute-done.15.refs_1_), channel_id=1, source_target_pairs={{1,0},{0,1},{3,2},{2,3},{5,4},{4,5},{7,6},{6,7},{9,8},{8,9},{11,10... | collective-permute-start | bytes 208904 | tf_op jit(solution)/shard_map/ppermute | solution.py:49
  78.4 1.3 %collective-permute-start.20 = (f32[136,128]{1,0:T(8,128)S(1)}, f32[136,128]{1,0:T(8,128)S(1)}, u32[]{:S(2)}, u32[]{:S(2)}) collective-permute-start(f32[136,128]{1,0:T(8,128)S(1)} %collective-permute-done.16.refs_2_), channel_id=1, source_target_pairs={{1,0},{0,1},{3,2},{2,3},{5,4},{4,5},{7,6},{6,7},{9,8},{8,9},{11,10... | collective-permute-start | bytes 208904 | tf_op jit(solution)/shard_map/ppermute | solution.py:49
  79.2 1.3 %collective-permute-start.21 = (f32[136,128]{1,0:T(8,128)S(1)}, f32[136,128]{1,0:T(8,128)S(1)}, u32[]{:S(2)}, u32[]{:S(2)}) collective-permute-start(f32[136,128]{1,0:T(8,128)S(1)} %collective-permute-done.17.refs_3_), channel_id=1, source_target_pairs={{1,0},{0,1},{3,2},{2,3},{5,4},{4,5},{7,6},{6,7},{9,8},{8,9},{11,10... | collective-permute-start | bytes 208904 | tf_op jit(solution)/shard_map/ppermute | solution.py:49

commit v3 on v2

--- a/solution.py
+++ b/solution.py
@@ -49,6 +49,49 @@
     return lax.ppermute(value, "dp", [(i ^ by[i % CORES], i) for i in range(count)])
 
 
+def cut(value, parts):
+    rows, width = value.shape
+    block = rows // parts
+
+    def kernel(in_ref, *refs):
+        sems = refs[parts]
+        copies = []
+        for part in range(parts):
+            source = in_ref.at[pl.ds(part * block, block)]
+            copies.append(pltpu.make_async_copy(source, refs[part], sems.at[part]))
+            copies[-1].start()
+        for copy in copies:
+            copy.wait()
+
+    return pl.pallas_call(
+        kernel,
+        out_shape=[jax.ShapeDtypeStruct((block, width), value.dtype)] * parts,
+        in_specs=[ANY],
+        out_specs=[ANY] * parts,
+        scratch_shapes=[pltpu.SemaphoreType.DMA((parts,))],
+        compiler_params=params(8),
+        cost_estimate=cost(0, 4 * value.size),
+        name="cut",
+    )(value)
+
+
+def join(values):
+    def kernel(*refs):
+        for at, ref in enumerate(refs[:-1]):
+            refs[-1][at] = ref[...]
+
+    shape = jax.ShapeDtypeStruct((len(values),) + values[0].shape, values[0].dtype)
+    return pl.pallas_call(
+        kernel,
+        out_shape=shape,
+        in_specs=[VMEM] * len(values),
+        out_specs=VMEM,
+        compiler_params=params(8),
+        cost_estimate=cost(0, 8 * values[0].size),
+        name="join",
+    )(*values)
+
+
 def down(value):
     count = lax.axis_size("pipe")
     return lax.ppermute(value, "pipe", [(i, i - 1) for i in range(1, count)])
@@ -65,20 +108,42 @@
     count = lax.axis_size("dp")
     tokens, width = inputs.shape
     block = width // count
-
-    def kernel(in_ref, out_ref):
+    pieces = count if block % HEAD == 0 else 1
+    part = width // pieces
+
+    def kernel(in_ref, out_ref, held, turned, in_sems, out_sems):
+        copies = []
+        for piece in range(pieces):
+            columns = pl.ds(piece * part, part)
+            copies.append(
+                pltpu.make_async_copy(in_ref.at[:, columns], held.at[:, columns], in_sems.at[piece])
+            )
+            copies[-1].start()
+        stores = []
         for owner in range(count):
-            out_ref[owner] = in_ref[:, owner * block : (owner + 1) * block].T
-
-    return pl.pallas_call(
-        kernel,
-        out_shape=jax.ShapeDtypeStruct((count, block, tokens), BF16),
-        in_specs=[VMEM],
-        out_specs=VMEM,
-        compiler_params=params(16),
+            if owner * pieces % count == 0:
+                copies[owner * pieces // count].wait()
+            turned[owner] = held[:, owner * block : (owner + 1) * block].T
+            stores.append(pltpu.make_async_copy(turned.at[owner], out_ref.at[owner], out_sems.at[owner]))
+            stores[-1].start()
+        for store in stores:
+            store.wait()
+
+    return pl.pallas_call(
+        kernel,
+        out_shape=pltpu.HBM((count, block, tokens), BF16),
+        in_specs=[HBM],
+        out_specs=HBM,
+        scratch_shapes=[
+            pltpu.VMEM((tokens, width), BF16),
+            pltpu.VMEM((count, block, tokens), BF16),
+            pltpu.SemaphoreType.DMA((pieces,)),
+            pltpu.SemaphoreType.DMA((count,)),
+        ],
+        compiler_params=params(8),
         cost_estimate=cost(0, 4 * tokens * width),
         name="split_columns",
-    )(inputs)
+    )(in_hbm(inputs))
 
 
 def triangle():
@@ -127,6 +192,7 @@
     per_step = 2 if owners % 2 == 0 else 1
     block = per_step * slots * HEAD
     tokens = right[0].shape[0]
+    total_tokens = sum(piece.shape[0] for piece in right)
     n_right = len(right)
     packed = packed_rows(slots)
     steps = owners // per_step
@@ -162,20 +228,23 @@
             for chip in range(chips):
                 mine_ref[chip] = grams[CORES * chip]
                 theirs_ref[chip] = grams[CORES * chip + 1]
+            theirs_ref[chips] = jnp.zeros((packed, HEAD), F32)
 
     column = lambda height: pl.BlockSpec((height, block), lambda j: (0, j))
     gram_shape = jax.ShapeDtypeStruct((chips, packed, HEAD), F32)
     gram_spec = pl.BlockSpec((chips, packed, HEAD), lambda j: (0, 0, 0))
+    other_shape = jax.ShapeDtypeStruct((chips + 1, packed, HEAD), F32)
+    other_spec = pl.BlockSpec((chips + 1, packed, HEAD), lambda j: (0, 0, 0))
     return pl.pallas_call(
         kernel,
         grid=(steps,),
-        out_shape=[jax.ShapeDtypeStruct((rows, width), BF16), gram_shape, gram_shape],
-        in_specs=[pl.BlockSpec(left.shape, lambda j: (0, 0, 0))] + [column(tokens)] * n_right + [column(rows)],
-        out_specs=[column(rows), gram_spec, gram_spec],
-        scratch_shapes=[pltpu.VMEM((rows, n_right * tokens), BF16), pltpu.VMEM((count, packed, HEAD), F32)],
+        out_shape=[jax.ShapeDtypeStruct((rows, width), BF16), gram_shape, other_shape],
+        in_specs=[pl.BlockSpec(left.shape, lambda j: (0, 0, 0))] + [column(piece.shape[0]) for piece in right] + [column(rows)],
+        out_specs=[column(rows), gram_spec, other_spec],
+        scratch_shapes=[pltpu.VMEM((rows, total_tokens), BF16), pltpu.VMEM((count, packed, HEAD), F32)],
         compiler_params=params(18),
         cost_estimate=cost(
-            2 * rows * tokens * n_right * width, 2 * tokens * n_right * (rows + width) + 4 * rows * width
+            2 * rows * total_tokens * width, 2 * total_tokens * (rows + width) + 4 * rows * width
         ),
         name="gradient",
     )(in_hbm(left), *[in_hbm(piece) for piece in right], in_hbm(moment))
@@ -244,7 +313,7 @@
     )(*grams)
 
 
-def apply_mixing(buffer, distances, mixes, slots, sent):
+def apply_mixing(buffer, near, other, far, slots, sent):
     rows, width = buffer.shape
     tokens, wide = sent[0].shape
     count = lax.axis_size("dp")
@@ -258,9 +327,9 @@
     packed = packed_rows(slots)
 
     def kernel(*refs):
-        mix_refs = refs[:count]
-        sent_refs = refs[count : count + len(sent)]
-        buf_ref, out_ref, relayed_ref, held, sems = refs[count + len(sent) :]
+        near_refs, other_ref, far_ref = refs[: len(near)], refs[len(near)], refs[len(near) + 1]
+        sent_refs = refs[len(near) + 2 : len(near) + 2 + len(sent)]
+        buf_ref, out_ref, relayed_ref, held, sems = refs[len(near) + 2 + len(sent) :]
         own = lax.axis_index("dp")
         stage = lax.axis_index("pipe")
         step = pl.program_id(0)
@@ -278,8 +347,9 @@
         @pl.when(step == 0)
         def load():
             each_copy(lambda copy: copy.start())
-            for distance, ref in zip(distances, mix_refs):
-                held[distance] = ref[...]
+            for chip, ref in enumerate(near_refs):
+                held[CORES * chip] = ref[...]
+                held[CORES * chip + 1] = far_ref[chip] if chip else other_ref[...]
 
         for which in range(per_step):
             parts = unpack(held[(step * per_step + which) ^ own], slots)
@@ -313,13 +383,16 @@
             jax.ShapeDtypeStruct((rows, width), BF16),
             jax.ShapeDtypeStruct((tokens, wide * CHUNKS), BF16),
         ],
-        in_specs=[pl.BlockSpec((packed, HEAD), lambda j: (0, 0))] * count + [VMEM] * len(sent) + [column],
+        in_specs=[pl.BlockSpec((packed, HEAD), lambda j: (0, 0))] * (len(near) + 1)
+        + [pl.BlockSpec(far.shape, lambda j: (0, 0, 0))]
+        + [VMEM] * len(sent)
+        + [column],
         out_specs=[column, ANY],
         scratch_shapes=[pltpu.VMEM((count, packed, HEAD), F32), pltpu.SemaphoreType.DMA((CHUNKS,))],
         compiler_params=params(16),
         cost_estimate=cost(6 * rows * width * HEAD, 4 * rows * width),
         name="apply_mixing",
-    )(*mixes, *sent, buffer)
+    )(*near, other, far, *sent, buffer)
 
 
 def weight_products(chunks, kv_rows, weights):
@@ -479,27 +552,25 @@
         near.append(swap(near[1], same[2]))
     products += weight_products(list(range(LAG, CHUNKS)), after(kv_rows, sent[1]), weights)
     relay(products[-1])
+    relay()
     if chips == 4:
-        far.append(swap(after(near[-1], sent[2], moved[1]), other_core))
+        far.extend(swap(piece, other_core) for piece in cut(after(near[-1], sent[2]), 2))
 
     buffer, mine, theirs = gradient(
-        left, same + crossed, near + far, after(moment, sent[2]), scale_grad, slots
+        left, same + crossed, near + far, after(moment, sent[3]), scale_grad, slots
     )
-    received = swap(theirs, other_core)
     relay(buffer)
-    relay()
-    sums = add_pairs(after(mine, sent[4]), received)
+    received = swap(after(theirs, sent[4]), other_core)
+    relay(theirs)
+    sums = add_pairs(after(mine, sent[5]), received)
     grams = [sums[0]] + [swap(sums[d], (CORES * d, CORES * d)) for d in range(1, chips)]
     relay(*grams[1:])
-    mix = mixing([after(grams[0], sent[5])] + grams[1:], scale, slots)
+    mix = mixing([after(grams[0], sent[6])] + grams[1:], scale, slots)
     mixes = [mix] + [swap(mix, (CORES * d, CORES * d)) for d in range(1, chips)]
-    relay(mixes[1])
-    far_mixes = [swap(m, other_core) for m in mixes]
-    relay(*mixes[1:])
-    distances = [CORES * d for d in range(chips)] + [CORES * d + 1 for d in range(chips)]
-    update, outgoing = apply_mixing(
-        after(buffer, sent[7]), distances, mixes + far_mixes, slots, sent
-    )
+    relay(mix)
+    far_mix = swap(after(mix, moved[6]), other_core)
+    far_mixes = swap(join(mixes), other_core)
+    update, outgoing = apply_mixing(after(buffer, sent[7]), mixes, far_mix, far_mixes, slots, sent)
     outgoing = last_step([after(m, update) for m in moved[-LAG:]], products[-LAG:], outgoing)
     return (update[None], outgoing[None])
 

time: 91.8 us -> 87.4 us (0.952)
  waiting for transfers between devices: 24.1 us -> 17.4 us
  Pallas kernels: 33.8 us -> 36.8 us
  local copies, waits for them, and re-layouts: 2.09 us -> 0.82 us
    ppermute x8, waiting for transfers between devices: 19.2 us -> 11.3 us  [down(): return lax.ppermute(value, 'pipe', [(i, i - 1) for i in range(1, count)])]
    pallas_call x1 -> x3, Pallas kernels: 1.45 us -> 3.44 us  [the longest x1 2.58 us: split_columns(): pl.pallas_call(kernel, out_shape=pltpu.HBM((count, block, tokens), BF16),...]
    unnamed x26 -> x14, local copies, waits for them, and re-layouts: 2.09 us -> 0.82 us
    ppermute x18 -> x17, starting transfers between devices: 15.2 us -> 16.3 us  [swap(): lax.ppermute(value, 'dp', [(i ^ by[i % CORES], i) for i in range(count)])]
    ppermute x18 -> x17, waiting for transfers between devices: 4.94 us -> 6.07 us  [swap(): lax.ppermute(value, 'dp', [(i ^ by[i % CORES], i) for i in range(count)])]
    pallas_call x8, Pallas kernels: 1.9 us -> 2.84 us  [relay_step(): pl.pallas_call(kernel, in_specs=[VMEM] * (len(inputs) + len(used)), out_s...]
  transfers between devices with their start and end apart: 27 -> 26, of which waited for: 12 -> 9; matrix products, arithmetic and copies ran while one was open for 0% -> 0% of each run, Pallas kernels for 36% -> 41%
where the time goes in v3:
time: 87.4 us; the launch traced here: 86.9 us
  Pallas kernels  36.8 us (42%)
  starting transfers between devices  31 us (35%)
  waiting for transfers between devices  17.4 us (20%)
  between operations  0.97 us (1%)
    ppermute x17, starting transfers between devices, swap(): lax.ppermute(value, 'dp', [(i ^ by[i % CORES], i) for i in range(count)])  16.3 us
    pallas_call x2, Pallas kernels, weight_products(): pl.pallas_call(kernel, out_shape=[jax.ShapeDtypeStruct((tokens, span), F3...  12.4 us
    ppermute x8, waiting for transfers between devices, down(): return lax.ppermute(value, 'pipe', [(i, i - 1) for i in range(1, count)])  11.3 us
    ppermute x8, starting transfers between devices, down(): return lax.ppermute(value, 'pipe', [(i, i - 1) for i in range(1, count)])  10.3 us
    pallas_call x1, Pallas kernels, gradient(): pl.pallas_call(kernel, grid=(steps,), out_shape=[jax.ShapeDtypeStruct((ro...  7.8 us
    ppermute x17, waiting for transfers between devices, swap(): lax.ppermute(value, 'dp', [(i ^ by[i % CORES], i) for i in range(count)])  6.07 us
    pallas_call x1, Pallas kernels, apply_mixing(): pl.pallas_call(kernel, grid=(steps,), out_shape=[jax.ShapeDtypeStruct((ro...  5.36 us
    all_to_all x1, starting transfers between devices, shards(): left = lax.all_to_all(columns, 'dp', 0, 0, tiled=True)  4.4 us
  transfers between devices with their start and end apart: 26, of which 9 were waited for; matrix products, arithmetic and copies ran while one was open for 0% of the time, Pallas kernels for 41%

profile of v3, /device:TPU:0, one launch (start us, length us, event | category | flops | bytes accessed | tf_op | source)
XLA Modules:
  0.0 86.9 jit_solution(10795627561299326377)
XLA Ops:
  0.6 3.0 %collective-permute-start = (bf16[128,2048]{1,0:T(8,128)(2,1)}, bf16[128,2048]{1,0:T(8,128)(2,1)}, u32[]{:S(2)}, u32[]{:S(2)}) collective-permute-start(bf16[128,2048]{1,0:T(8,128)(2,1)} %bitcast.6), channel_id=1, source_target_pairs={{2,0},{5,1},{0,2},{7,3},{6,4},{1,5},{4,6},{3,7},{10,8},{13,9},{8,1... | collective-permute-start | bytes 1572872 | tf_op jit(solution)/shard_map/ppermute | solution.py:49
  3.6 1.5 %collective-permute-start.1 = (bf16[128,2048]{1,0:T(8,128)(2,1)}, bf16[128,2048]{1,0:T(8,128)(2,1)}, u32[]{:S(2)}, u32[]{:S(2)}) collective-permute-start(bf16[128,2048]{1,0:T(8,128)(2,1)} %bitcast.7), channel_id=1, source_target_pairs={{4,0},{3,1},{6,2},{1,3},{0,4},{7,5},{2,6},{5,7},{12,8},{11,9},{14,... | collective-permute-start | bytes 1572872 | tf_op jit(solution)/shard_map/ppermute | solution.py:49
  5.2 0.0 collective-permute-start.3
  5.2 2.6 %split_columns.1 = bf16[8,640,128]{2,1,0:T(8,128)(2,1)} custom-call(bf16[128,5120]{1,0:T(8,128)(2,1)} %bitcast.15), custom_call_target="tpu_custom_call" | custom-call | flops 1 | bytes 1 | tf_op jit(solution)/shard_map/split_columns/pallas_call | solution.py:132
  7.7 0.0 copy-start.1
  7.8 4.4 %all-to-all-start = ((bf16[8,640,128]{2,1,0:T(8,128)(2,1)}), bf16[8,640,128]{2,1,0:T(8,128)(2,1)}, u32[]{:S(2)}, u32[]{:S(2)}) async-start(bf16[8,640,128]{2,1,0:T(8,128)(2,1)} %split_columns.1), calls=%async_computation | async-start | bytes 2621440 | tf_op jit(solution)/shard_map/all_to_all | solution.py:543
  12.2 0.0 copy-start
  12.2 6.3 %weight_products.2 = (f32[128,1280]{1,0:T(8,128)S(1)}, f32[128,1280]{1,0:T(8,128)S(1)}) custom-call(bf16[128,2048]{1,0:T(8,128)(2,1)S(1)} %bitcast.10, bf16[5120,2048]{1,0:T(8,128)(2,1)} %bitcast.12), custom_call_target="tpu_custom_call" | custom-call | flops 1 | bytes 1 | tf_op jit(solution)/shard_map/weight_products/pallas_call | solution.py:425
  18.5 0.0 collective-permute-done.refs_2_
  18.5 2.0 %collective-permute-start.2 = (bf16[128,2048]{1,0:T(8,128)(2,1)}, bf16[128,2048]{1,0:T(8,128)(2,1)S(1)}, u32[]{:S(2)}, u32[]{:S(2)}) collective-permute-start(bf16[128,2048]{1,0:T(8,128)(2,1)} %collective-permute-done.refs_2_), channel_id=1, source_target_pairs={{4,0},{3,1},{6,2},{1,3},{0,4},{7,5},{2,6},{5,7},{12,8},{11,9},{14,... | collective-permute-start | bytes 1572872 | tf_op jit(solution)/shard_map/ppermute | solution.py:49
  20.4 0.0 collective-permute-start.4
  20.4 0.0 collective-permute-done.1.refs_3_
  20.4 0.0 collective-permute-done.3.refs_5_
  20.5 1.3 %collective-permute-start.6 = (bf16[128,1280]{1,0:T(8,128)(2,1)S(1)}, bf16[128,1280]{1,0:T(8,128)(2,1)S(1)}, u32[]{:S(2)}, u32[]{:S(2)}) collective-permute-start(bf16[128,1280]{1,0:T(8,128)(2,1)S(1)} %relay_step.8.refs_6_), channel_id=1, source_target_pairs={{8,0},{16,8},{24,16},{9,1},{17,9},{25,17},{10,2},{18,10},{26,18},{... | collective-permute-start | bytes 983048 | tf_op jit(solution)/shard_map/ppermute | solution.py:97
  21.8 1.3 %collective-permute-start.9 = (bf16[128,1280]{1,0:T(8,128)(2,1)S(1)}, bf16[128,1280]{1,0:T(8,128)(2,1)S(1)}, u32[]{:S(2)}, u32[]{:S(2)}) collective-permute-start(bf16[128,1280]{1,0:T(8,128)(2,1)S(1)} %relay_step.9.refs_7_), channel_id=1, source_target_pairs={{8,0},{16,8},{24,16},{9,1},{17,9},{25,17},{10,2},{18,10},{26,18},{... | collective-permute-start | bytes 983048 | tf_op jit(solution)/shard_map/ppermute | solution.py:97
  23.1 0.6 collective-permute-start.5
  23.7 6.2 %weight_products.3 = (f32[128,1280]{1,0:T(8,128)S(1)}, f32[128,1280]{1,0:T(8,128)S(1)}) custom-call(bf16[128,2048]{1,0:T(8,128)(2,1)S(1)} %bitcast.11, bf16[5120,2048]{1,0:T(8,128)(2,1)} %bitcast.13), custom_call_target="tpu_custom_call" | custom-call | flops 1 | bytes 1 | tf_op jit(solution)/shard_map/weight_products/pallas_call | solution.py:425
  29.9 3.0 %collective-permute-done.6.refs_0_ = bf16[128,1280]{1,0:T(8,128)(2,1)S(1)} collective-permute-done((bf16[128,1280]{1,0:T(8,128)(2,1)S(1)}, bf16[128,1280]{1,0:T(8,128)(2,1)S(1)}, u32[]{:S(2)}, u32[]{:S(2)}) %collective-permute-start.6) | collective-permute-done | bytes 327712 | tf_op jit(solution)/shard_map/ppermute | solution.py:97
  32.9 1.3 %collective-permute-start.11 = (bf16[128,1280]{1,0:T(8,128)(2,1)S(1)}, bf16[128,1280]{1,0:T(8,128)(2,1)}, u32[]{:S(2)}, u32[]{:S(2)}) collective-permute-start(bf16[128,1280]{1,0:T(8,128)(2,1)S(1)} %relay_step.10.refs_8_), channel_id=1, source_target_pairs={{8,0},{16,8},{24,16},{9,1},{17,9},{25,17},{10,2},{18,10},{26,18},{... | collective-permute-start | bytes 983048 | tf_op jit(solution)/shard_map/ppermute | solution.py:97
  34.2 1.3 %collective-permute-done.2.in_ref.refs_4_ = bf16[128,2048]{1,0:T(8,128)(2,1)S(1)} collective-permute-done((bf16[128,2048]{1,0:T(8,128)(2,1)}, bf16[128,2048]{1,0:T(8,128)(2,1)S(1)}, u32[]{:S(2)}, u32[]{:S(2)}) %collective-permute-start.2) | collective-permute-done | bytes 524320 | tf_op jit(solution)/shard_map/ppermute | solution.py:49
  35.5 0.8 cut.1
  36.3 1.1 %collective-permute-start.7 = (bf16[64,2048]{1,0:T(8,128)(2,1)}, bf16[64,2048]{1,0:T(8,128)(2,1)}, u32[]{:S(2)}, u32[]{:S(2)}) collective-permute-start(bf16[64,2048]{1,0:T(8,128)(2,1)} %get-tuple-element.50), channel_id=1, source_target_pairs={{1,0},{0,1},{3,2},{2,3},{5,4},{4,5},{7,6},{6,7},{9,8},{8,9},{11,10... | collective-permute-start | bytes 786440 | tf_op jit(solution)/shard_map/ppermute | solution.py:49
  37.4 2.5 %collective-permute-done.9.refs_0_ = bf16[128,1280]{1,0:T(8,128)(2,1)S(1)} collective-permute-done((bf16[128,1280]{1,0:T(8,128)(2,1)S(1)}, bf16[128,1280]{1,0:T(8,128)(2,1)S(1)}, u32[]{:S(2)}, u32[]{:S(2)}) %collective-permute-start.9) | collective-permute-done | bytes 327712 | tf_op jit(solution)/shard_map/ppermute | solution.py:97
  39.9 0.0 collective-permute-start.8
  39.9 0.7 relay_step.11.refs_9_
  40.6 0.0 collective-permute-done.4.refs_6_
  40.6 0.8 copy-done.6
  41.4 1.3 %collective-permute-start.10 = (bf16[128,1280]{1,0:T(8,128)(2,1)}, bf16[128,1280]{1,0:T(8,128)(2,1)}, u32[]{:S(2)}, u32[]{:S(2)}) collective-permute-start(bf16[128,1280]{1,0:T(8,128)(2,1)} %relay_step.11.refs_9_), channel_id=1, source_target_pairs={{8,0},{16,8},{24,16},{9,1},{17,9},{25,17},{10,2},{18,10},{26,18},{... | collective-permute-start | bytes 983048 | tf_op jit(solution)/shard_map/ppermute | solution.py:97
  42.7 0.0 collective-permute-done.5.refs_7_
  42.7 0.0 all-to-all-done.refs_0_
  42.7 0.0 collective-permute-done.7.refs_8_
  42.8 0.0 collective-permute-done.8.refs_9_
  42.8 7.8 %gradient.1 = (bf16[640,2048]{1,0:T(8,128)(2,1)S(1)}, f32[4,136,128]{2,1,0:T(8,128)S(1)}, f32[5,136,128]{2,1,0:T(8,128)S(1)}) custom-call(bf16[8,640,128]{2,1,0:T(8,128)(2,1)} %all-to-all-done.refs_0_, bf16[128,2048]{1,0:T(8,128)(2,1)} %bitcast.9, bf16[128,2048]{1,0:T(8,128)(2,1)} %collective-permute-done.refs_2_, ...), custom_call_target="tpu_custom_call" | custom-call | flops 1 | bytes 1 | tf_op jit(solution)/shard_map/gradient/pallas_call | solution.py:238
  50.6 0.0 collective-permute-done.11.refs_0_
  50.6 1.0 %relay_step.12.refs_10_ = bf16[128,1280]{1,0:T(8,128)(2,1)S(1)} custom-call(bf16[128,1280]{1,0:T(8,128)(2,1)} %collective-permute-done.11.refs_0_, f32[128,1280]{1,0:T(8,128)S(1)} %get-tuple-element.42.refs_1_.refs_2_, f32[128,1280]{1,0:T(8,128)S(1)} %get-tuple-element.48.refs_3_.refs_2_), custom_call_target="tpu_custom_call" | custom-call | flops 1 | bytes 1 | tf_op jit(solution)/shard_map/relay_step/pallas_call | solution.py:462
  51.6 0.5 collective-permute-start.12
  52.1 1.3 %collective-permute-start.13 = (bf16[128,1280]{1,0:T(8,128)(2,1)S(1)}, bf16[128,1280]{1,0:T(8,128)(2,1)S(1)}, u32[]{:S(2)}, u32[]{:S(2)}) collective-permute-start(bf16[128,1280]{1,0:T(8,128)(2,1)S(1)} %relay_step.12.refs_10_), channel_id=1, source_target_pairs={{8,0},{16,8},{24,16},{9,1},{17,9},{25,17},{10,2},{18,10},{26,18},{... | collective-permute-start | bytes 983048 | tf_op jit(solution)/shard_map/ppermute | solution.py:97
  53.4 0.4 collective-permute-done.10.refs_0_
  53.8 1.0 %relay_step.13.refs_11_ = bf16[128,1280]{1,0:T(8,128)(2,1)S(1)} custom-call(bf16[128,1280]{1,0:T(8,128)(2,1)} %collective-permute-done.10.refs_0_, f32[128,1280]{1,0:T(8,128)S(1)} %get-tuple-element.44.refs_1_.refs_2_, f32[128,1280]{1,0:T(8,128)S(1)} %get-tuple-element.46.refs_3_.refs_2_), custom_call_target="tpu_custom_call" | custom-call | flops 1 | bytes 1 | tf_op jit(solution)/shard_map/relay_step/pallas_call | solution.py:462
  54.7 1.3 %collective-permute-start.23 = (bf16[128,1280]{1,0:T(8,128)(2,1)S(1)}, bf16[128,1280]{1,0:T(8,128)(2,1)S(1)}, u32[]{:S(2)}, u32[]{:S(2)}) collective-permute-start(bf16[128,1280]{1,0:T(8,128)(2,1)S(1)} %relay_step.13.refs_11_), channel_id=1, source_target_pairs={{8,0},{16,8},{24,16},{9,1},{17,9},{25,17},{10,2},{18,10},{26,18},{... | collective-permute-start | bytes 983048 | tf_op jit(solution)/shard_map/ppermute | solution.py:97
  56.0 0.0 collective-permute-done.12.second_ref
  56.1 1.5 %collective-permute-start.14 = (f32[136,128]{1,0:T(8,128)S(1)}, f32[136,128]{1,0:T(8,128)S(1)}, u32[]{:S(2)}, u32[]{:S(2)}) collective-permute-start(f32[136,128]{1,0:T(8,128)S(1)} %get-tuple-element.62), channel_id=1, source_target_pairs={{2,0},{3,1},{0,2},{1,3},{6,4},{7,5},{4,6},{5,7},{10,8},{11,9},{8,1... | collective-permute-start | bytes 208904 | tf_op jit(solution)/shard_map/ppermute | solution.py:49
  57.6 1.8 %collective-permute-start.15 = (f32[136,128]{1,0:T(8,128)S(1)}, f32[136,128]{1,0:T(8,128)S(1)}, u32[]{:S(2)}, u32[]{:S(2)}) collective-permute-start(f32[136,128]{1,0:T(8,128)S(1)} %get-tuple-element.63), channel_id=1, source_target_pairs={{4,0},{5,1},{6,2},{7,3},{0,4},{1,5},{2,6},{3,7},{12,8},{13,9},{14,... | collective-permute-start | bytes 208904 | tf_op jit(solution)/shard_map/ppermute | solution.py:49
  59.4 0.2 collective-permute-start.16
  59.6 5.3 %collective-permute-done.13.refs_0_ = bf16[128,1280]{1,0:T(8,128)(2,1)S(1)} collective-permute-done((bf16[128,1280]{1,0:T(8,128)(2,1)S(1)}, bf16[128,1280]{1,0:T(8,128)(2,1)S(1)}, u32[]{:S(2)}, u32[]{:S(2)}) %collective-permute-start.13) | collective-permute-done | bytes 327712 | tf_op jit(solution)/shard_map/ppermute | solution.py:97
  65.0 0.0 collective-permute-done.16.refs_3_
  65.0 0.1 relay_step.14.refs_12_
  65.0 1.3 %collective-permute-start.20 = (bf16[128,1280]{1,0:T(8,128)(2,1)S(1)}, bf16[128,1280]{1,0:T(8,128)(2,1)S(1)}, u32[]{:S(2)}, u32[]{:S(2)}) collective-permute-start(bf16[128,1280]{1,0:T(8,128)(2,1)S(1)} %relay_step.14.refs_12_), channel_id=1, source_target_pairs={{8,0},{16,8},{24,16},{9,1},{17,9},{25,17},{10,2},{18,10},{26,18},{... | collective-permute-start | bytes 983048 | tf_op jit(solution)/shard_map/ppermute | solution.py:97
  66.3 4.0 %mixing.1.refs_0_ = f32[136,128]{1,0:T(8,128)S(1)} custom-call(f32[136,128]{1,0:T(8,128)S(1)} %get-tuple-element.66.refs_0_, f32[136,128]{1,0:T(8,128)S(1)} %collective-permute-done.14.refs_1_, f32[136,128]{1,0:T(8,128)S(1)} %collective-permute-done.15.refs_2_, f32[136,128]{1,0:T(8,128)S(1)} %collective-permute-done.16.refs_3_), custom_call_target="tpu_custom_call" | custom-call | flops 1 | bytes 1 | tf_op jit(solution)/shard_map/mixing/pallas_call | solution.py:304
  70.3 1.5 %collective-permute-start.17 = (f32[136,128]{1,0:T(8,128)S(1)}, f32[136,128]{1,0:T(8,128)S(1)}, u32[]{:S(2)}, u32[]{:S(2)}) collective-permute-start(f32[136,128]{1,0:T(8,128)S(1)} %mixing.1.refs_0_), channel_id=1, source_target_pairs={{2,0},{3,1},{0,2},{1,3},{6,4},{7,5},{4,6},{5,7},{10,8},{11,9},{8,1... | collective-permute-start | bytes 208904 | tf_op jit(solution)/shard_map/ppermute | solution.py:49
  71.9 1.8 %collective-permute-start.18 = (f32[136,128]{1,0:T(8,128)S(1)}, f32[136,128]{1,0:T(8,128)S(1)}, u32[]{:S(2)}, u32[]{:S(2)}) collective-permute-start(f32[136,128]{1,0:T(8,128)S(1)} %mixing.1.refs_0_), channel_id=1, source_target_pairs={{4,0},{5,1},{6,2},{7,3},{0,4},{1,5},{2,6},{3,7},{12,8},{13,9},{14,... | collective-permute-start | bytes 208904 | tf_op jit(solution)/shard_map/ppermute | solution.py:49
  73.6 0.2 collective-permute-start.19
  73.9 0.1 relay_step.15.refs_13_
  73.9 1.3 %collective-permute-start.24 = (bf16[128,1280]{1,0:T(8,128)(2,1)S(1)}, bf16[128,1280]{1,0:T(8,128)(2,1)S(1)}, u32[]{:S(2)}, u32[]{:S(2)}) collective-permute-start(bf16[128,1280]{1,0:T(8,128)(2,1)S(1)} %relay_step.15.refs_13_), channel_id=1, source_target_pairs={{8,0},{16,8},{24,16},{9,1},{17,9},{25,17},{10,2},{18,10},{26,18},{... | collective-permute-start | bytes 983048 | tf_op jit(solution)/shard_map/ppermute | solution.py:97
  75.2 0.0 collective-permute-done.17.refs_1_
  75.2 1.7 %collective-permute-done.18.refs_2_ = f32[136,128]{1,0:T(8,128)S(1)} collective-permute-done((f32[136,128]{1,0:T(8,128)S(1)}, f32[136,128]{1,0:T(8,128)S(1)}, u32[]{:S(2)}, u32[]{:S(2)}) %collective-permute-start.18) | collective-permute-done | bytes 69664 | tf_op jit(solution)/shard_map/ppermute | solution.py:49
  76.9 1.9 %collective-permute-done.19.refs_3_ = f32[136,128]{1,0:T(8,128)S(1)} collective-permute-done((f32[136,128]{1,0:T(8,128)S(1)}, f32[136,128]{1,0:T(8,128)S(1)}, u32[]{:S(2)}, u32[]{:S(2)}) %collective-permute-start.19) | collective-permute-done | bytes 69664 | tf_op jit(solution)/shard_map/ppermute | solution.py:49
  78.9 0.1 collective-permute-start.22
  78.9 0.0 collective-permute-done.20.refs_0_
  79.0 0.5 collective-permute-start.21
  79.4 1.0 %collective-permute-done.22.refs_5_ = f32[4,136,128]{2,1,0:T(8,128)S(1)} collective-permute-done((f32[4,136,128]{2,1,0:T(8,128)S(1)}, f32[4,136,128]{2,1,0:T(8,128)S(1)}, u32[]{:S(2)}, u32[]{:S(2)}) %collective-permute-start.22) | collective-permute-done | bytes 278560 | tf_op jit(solution)/shard_map/ppermute | solution.py:49
  80.5 0.1 collective-permute-done.21.refs_4_
  80.6 5.4 %apply_mixing.1 = (bf16[640,2048]{1,0:T(8,128)(2,1)}, bf16[128,5120]{1,0:T(8,128)(2,1)}) custom-call(f32[136,128]{1,0:T(8,128)S(1)} %mixing.1.refs_0_, f32[136,128]{1,0:T(8,128)S(1)} %collective-permute-done.17.refs_1_, f32[136,128]{1,0:T(8,128)S(1)} %collective-permute-done.18.refs_2_, f32[136,128]{1,0:T(8,128)S(1)} %collective-permute-done.19.refs_3_, ...), custom_call_target="tpu_custom_call" | custom-call | flops 1 | bytes 1 | tf_op jit(solution)/shard_map/apply_mixing/pallas_call | solution.py:379
  86.0 0.9 %last_step.1 = bf16[128,5120]{1,0:T(8,128)(2,1)} custom-call(bf16[128,1280]{1,0:T(8,128)(2,1)S(1)} %collective-permute-done.20.refs_0_, bf16[128,1280]{1,0:T(8,128)(2,1)S(1)} %collective-permute-done.24.refs_1_, f32[128,1280]{1,0:T(8,128)S(1)} %get-tuple-element.48.refs_3_.refs_2_, ...), custom_call_target="tpu_custom_call", output_to_operand_aliasing={{}: (4, {})} | custom-call | flops 1 | bytes 1 | tf_op jit(solution)/shard_map/last_step/pallas_call | solution.py:492
  (20 shorter events, 0.1 us)
Async XLA Ops:
  0.6 17.8 %collective-permute-start = (bf16[128,2048]{1,0:T(8,128)(2,1)}, bf16[128,2048]{1,0:T(8,128)(2,1)}, u32[]{:S(2)}, u32[]{:S(2)}) collective-permute-start(bf16[128,2048]{1,0:T(8,128)(2,1)} %bitcast.6), channel_id=1, source_target_pairs={{2,0},{5,1},{0,2},{7,3},{6,4},{1,5},{4,6},{3,7},{10,8},{13,9},{8,1... | collective-permute-start | bytes 1572872 | tf_op jit(solution)/shard_map/ppermute | solution.py:49
  3.6 16.8 %collective-permute-start.1 = (bf16[128,2048]{1,0:T(8,128)(2,1)}, bf16[128,2048]{1,0:T(8,128)(2,1)}, u32[]{:S(2)}, u32[]{:S(2)}) collective-permute-start(bf16[128,2048]{1,0:T(8,128)(2,1)} %bitcast.7), channel_id=1, source_target_pairs={{4,0},{3,1},{6,2},{1,3},{0,4},{7,5},{2,6},{5,7},{12,8},{11,9},{14,... | collective-permute-start | bytes 1572872 | tf_op jit(solution)/shard_map/ppermute | solution.py:49
  5.2 15.3 %collective-permute-start.3 = (bf16[128,2048]{1,0:T(8,128)(2,1)}, bf16[128,2048]{1,0:T(8,128)(2,1)S(1)}, u32[]{:S(2)}, u32[]{:S(2)}) collective-permute-start(bf16[128,2048]{1,0:T(8,128)(2,1)} %bitcast.8), channel_id=1, source_target_pairs={{1,0},{0,1},{3,2},{2,3},{5,4},{4,5},{7,6},{6,7},{9,8},{8,9},{11,10... | collective-permute-start | bytes 1572872 | tf_op jit(solution)/shard_map/ppermute | solution.py:49
  7.7 4.4 %copy-start.1 = (bf16[1,128,2048]{2,1,0:T(8,128)(2,1)S(1)}, bf16[1,128,2048]{2,1,0:T(8,128)(2,1)}, u32[]{:S(2)}) copy-start(bf16[1,128,2048]{2,1,0:T(8,128)(2,1)} %param.7) | copy-start | bytes 1572868
  7.8 35.0 %all-to-all-start = ((bf16[8,640,128]{2,1,0:T(8,128)(2,1)}), bf16[8,640,128]{2,1,0:T(8,128)(2,1)}, u32[]{:S(2)}, u32[]{:S(2)}) async-start(bf16[8,640,128]{2,1,0:T(8,128)(2,1)} %split_columns.1), calls=%async_computation | async-start | bytes 2621440 | tf_op jit(solution)/shard_map/all_to_all | solution.py:543
  12.2 8.3 %copy-start = (bf16[128,5120]{1,0:T(8,128)(2,1)S(1)}, bf16[128,5120]{1,0:T(8,128)(2,1)}, u32[]{:S(2)}) copy-start(bf16[128,5120]{1,0:T(8,128)(2,1)} %refs_1_.3) | copy-start | bytes 3932164
  18.5 17.0 %collective-permute-start.2 = (bf16[128,2048]{1,0:T(8,128)(2,1)}, bf16[128,2048]{1,0:T(8,128)(2,1)S(1)}, u32[]{:S(2)}, u32[]{:S(2)}) collective-permute-start(bf16[128,2048]{1,0:T(8,128)(2,1)} %collective-permute-done.refs_2_), channel_id=1, source_target_pairs={{4,0},{3,1},{6,2},{1,3},{0,4},{7,5},{2,6},{5,7},{12,8},{11,9},{14,... | collective-permute-start | bytes 1572872 | tf_op jit(solution)/shard_map/ppermute | solution.py:49
  20.4 20.2 %collective-permute-start.4 = (bf16[128,2048]{1,0:T(8,128)(2,1)}, bf16[128,2048]{1,0:T(8,128)(2,1)S(1)}, u32[]{:S(2)}, u32[]{:S(2)}) collective-permute-start(bf16[128,2048]{1,0:T(8,128)(2,1)} %collective-permute-done.refs_2_), channel_id=1, source_target_pairs={{1,0},{0,1},{3,2},{2,3},{5,4},{4,5},{7,6},{6,7},{9,8},{8,9},{11,10... | collective-permute-start | bytes 1572872 | tf_op jit(solution)/shard_map/ppermute | solution.py:49
  20.4 1.4 %copy-start.5 = (bf16[128,2048]{1,0:T(8,128)(2,1)}, bf16[128,2048]{1,0:T(8,128)(2,1)S(1)}, u32[]{:S(2)}) copy-start(bf16[128,2048]{1,0:T(8,128)(2,1)S(1)} %collective-permute-done.3.refs_5_) | copy-start | bytes 1572868
  20.5 12.4 %collective-permute-start.6 = (bf16[128,1280]{1,0:T(8,128)(2,1)S(1)}, bf16[128,1280]{1,0:T(8,128)(2,1)S(1)}, u32[]{:S(2)}, u32[]{:S(2)}) collective-permute-start(bf16[128,1280]{1,0:T(8,128)(2,1)S(1)} %relay_step.8.refs_6_), channel_id=1, source_target_pairs={{8,0},{16,8},{24,16},{9,1},{17,9},{25,17},{10,2},{18,10},{26,18},{... | collective-permute-start | bytes 983048 | tf_op jit(solution)/shard_map/ppermute | solution.py:97
  21.8 8.0 %copy-start.3 = (bf16[128,1280]{1,0:T(8,128)(2,1)}, bf16[128,1280]{1,0:T(8,128)(2,1)S(1)}, u32[]{:S(2)}) copy-start(bf16[128,1280]{1,0:T(8,128)(2,1)S(1)} %relay_step.9.refs_7_) | copy-start | bytes 983044
  21.8 18.1 %collective-permute-start.9 = (bf16[128,1280]{1,0:T(8,128)(2,1)S(1)}, bf16[128,1280]{1,0:T(8,128)(2,1)S(1)}, u32[]{:S(2)}, u32[]{:S(2)}) collective-permute-start(bf16[128,1280]{1,0:T(8,128)(2,1)S(1)} %relay_step.9.refs_7_), channel_id=1, source_target_pairs={{8,0},{16,8},{24,16},{9,1},{17,9},{25,17},{10,2},{18,10},{26,18},{... | collective-permute-start | bytes 983048 | tf_op jit(solution)/shard_map/ppermute | solution.py:97
  23.1 19.6 %collective-permute-start.5 = (bf16[128,2048]{1,0:T(8,128)(2,1)}, bf16[128,2048]{1,0:T(8,128)(2,1)}, u32[]{:S(2)}, u32[]{:S(2)}) collective-permute-start(bf16[128,2048]{1,0:T(8,128)(2,1)} %collective-permute-done.1.refs_3_), channel_id=1, source_target_pairs={{1,0},{0,1},{3,2},{2,3},{5,4},{4,5},{7,6},{6,7},{9,8},{8,9},{11,10... | collective-permute-start | bytes 1572872 | tf_op jit(solution)/shard_map/ppermute | solution.py:49
  32.9 17.7 %collective-permute-start.11 = (bf16[128,1280]{1,0:T(8,128)(2,1)S(1)}, bf16[128,1280]{1,0:T(8,128)(2,1)}, u32[]{:S(2)}, u32[]{:S(2)}) collective-permute-start(bf16[128,1280]{1,0:T(8,128)(2,1)S(1)} %relay_step.10.refs_8_), channel_id=1, source_target_pairs={{8,0},{16,8},{24,16},{9,1},{17,9},{25,17},{10,2},{18,10},{26,18},{... | collective-permute-start | bytes 983048 | tf_op jit(solution)/shard_map/ppermute | solution.py:97
  35.5 5.2 %copy-start.2 = (bf16[128,2048]{1,0:T(8,128)(2,1)}, bf16[128,2048]{1,0:T(8,128)(2,1)S(1)}, u32[]{:S(2)}) copy-start(bf16[128,2048]{1,0:T(8,128)(2,1)S(1)} %collective-permute-done.2.in_ref.refs_4_) | copy-start | bytes 1572868
  36.3 6.4 %collective-permute-start.7 = (bf16[64,2048]{1,0:T(8,128)(2,1)}, bf16[64,2048]{1,0:T(8,128)(2,1)}, u32[]{:S(2)}, u32[]{:S(2)}) collective-permute-start(bf16[64,2048]{1,0:T(8,128)(2,1)} %get-tuple-element.50), channel_id=1, source_target_pairs={{1,0},{0,1},{3,2},{2,3},{5,4},{4,5},{7,6},{6,7},{9,8},{8,9},{11,10... | collective-permute-start | bytes 786440 | tf_op jit(solution)/shard_map/ppermute | solution.py:49
  39.9 2.9 %collective-permute-start.8 = (bf16[64,2048]{1,0:T(8,128)(2,1)}, bf16[64,2048]{1,0:T(8,128)(2,1)}, u32[]{:S(2)}, u32[]{:S(2)}) collective-permute-start(bf16[64,2048]{1,0:T(8,128)(2,1)} %get-tuple-element.51), channel_id=1, source_target_pairs={{1,0},{0,1},{3,2},{2,3},{5,4},{4,5},{7,6},{6,7},{9,8},{8,9},{11,10... | collective-permute-start | bytes 786440 | tf_op jit(solution)/shard_map/ppermute | solution.py:49
  40.6 0.8 copy-start.6
  41.4 12.3 %collective-permute-start.10 = (bf16[128,1280]{1,0:T(8,128)(2,1)}, bf16[128,1280]{1,0:T(8,128)(2,1)}, u32[]{:S(2)}, u32[]{:S(2)}) collective-permute-start(bf16[128,1280]{1,0:T(8,128)(2,1)} %relay_step.11.refs_9_), channel_id=1, source_target_pairs={{8,0},{16,8},{24,16},{9,1},{17,9},{25,17},{10,2},{18,10},{26,18},{... | collective-permute-start | bytes 983048 | tf_op jit(solution)/shard_map/ppermute | solution.py:97
  51.6 4.5 %collective-permute-start.12 = (f32[5,136,128]{2,1,0:T(8,128)S(1)}, f32[5,136,128]{2,1,0:T(8,128)S(1)}, u32[]{:S(2)}, u32[]{:S(2)}) collective-permute-start(f32[5,136,128]{2,1,0:T(8,128)S(1)} %get-tuple-element.60), channel_id=1, source_target_pairs={{1,0},{0,1},{3,2},{2,3},{5,4},{4,5},{7,6},{6,7},{9,8},{8,9},{11,10... | collective-permute-start | bytes 1044488 | tf_op jit(solution)/shard_map/ppermute | solution.py:49
  52.1 12.9 %collective-permute-start.13 = (bf16[128,1280]{1,0:T(8,128)(2,1)S(1)}, bf16[128,1280]{1,0:T(8,128)(2,1)S(1)}, u32[]{:S(2)}, u32[]{:S(2)}) collective-permute-start(bf16[128,1280]{1,0:T(8,128)(2,1)S(1)} %relay_step.12.refs_10_), channel_id=1, source_target_pairs={{8,0},{16,8},{24,16},{9,1},{17,9},{25,17},{10,2},{18,10},{26,18},{... | collective-permute-start | bytes 983048 | tf_op jit(solution)/shard_map/ppermute | solution.py:97
  54.7 19.1 %collective-permute-start.23 = (bf16[128,1280]{1,0:T(8,128)(2,1)S(1)}, bf16[128,1280]{1,0:T(8,128)(2,1)S(1)}, u32[]{:S(2)}, u32[]{:S(2)}) collective-permute-start(bf16[128,1280]{1,0:T(8,128)(2,1)S(1)} %relay_step.13.refs_11_), channel_id=1, source_target_pairs={{8,0},{16,8},{24,16},{9,1},{17,9},{25,17},{10,2},{18,10},{26,18},{... | collective-permute-start | bytes 983048 | tf_op jit(solution)/shard_map/ppermute | solution.py:97
  56.1 8.9 %collective-permute-start.14 = (f32[136,128]{1,0:T(8,128)S(1)}, f32[136,128]{1,0:T(8,128)S(1)}, u32[]{:S(2)}, u32[]{:S(2)}) collective-permute-start(f32[136,128]{1,0:T(8,128)S(1)} %get-tuple-element.62), channel_id=1, source_target_pairs={{2,0},{3,1},{0,2},{1,3},{6,4},{7,5},{4,6},{5,7},{10,8},{11,9},{8,1... | collective-permute-start | bytes 208904 | tf_op jit(solution)/shard_map/ppermute | solution.py:49
  57.6 7.3 %collective-permute-start.15 = (f32[136,128]{1,0:T(8,128)S(1)}, f32[136,128]{1,0:T(8,128)S(1)}, u32[]{:S(2)}, u32[]{:S(2)}) collective-permute-start(f32[136,128]{1,0:T(8,128)S(1)} %get-tuple-element.63), channel_id=1, source_target_pairs={{4,0},{5,1},{6,2},{7,3},{0,4},{1,5},{2,6},{3,7},{12,8},{13,9},{14,... | collective-permute-start | bytes 208904 | tf_op jit(solution)/shard_map/ppermute | solution.py:49
  59.4 5.5 %collective-permute-start.16 = (f32[136,128]{1,0:T(8,128)S(1)}, f32[136,128]{1,0:T(8,128)S(1)}, u32[]{:S(2)}, u32[]{:S(2)}) collective-permute-start(f32[136,128]{1,0:T(8,128)S(1)} %get-tuple-element.64), channel_id=1, source_target_pairs={{6,0},{7,1},{4,2},{5,3},{2,4},{3,5},{0,6},{1,7},{14,8},{15,9},{12,... | collective-permute-start | bytes 208904 | tf_op jit(solution)/shard_map/ppermute | solution.py:49
  65.0 14.0 %collective-permute-start.20 = (bf16[128,1280]{1,0:T(8,128)(2,1)S(1)}, bf16[128,1280]{1,0:T(8,128)(2,1)S(1)}, u32[]{:S(2)}, u32[]{:S(2)}) collective-permute-start(bf16[128,1280]{1,0:T(8,128)(2,1)S(1)} %relay_step.14.refs_12_), channel_id=1, source_target_pairs={{8,0},{16,8},{24,16},{9,1},{17,9},{25,17},{10,2},{18,10},{26,18},{... | collective-permute-start | bytes 983048 | tf_op jit(solution)/shard_map/ppermute | solution.py:97
  70.3 10.3 %copy-start.4 = (bf16[128,1280]{1,0:T(8,128)(2,1)S(1)}, bf16[128,1280]{1,0:T(8,128)(2,1)}, u32[]{:S(2)}) copy-start(bf16[128,1280]{1,0:T(8,128)(2,1)} %copy-done.3) | copy-start | bytes 983044
  70.3 4.9 %collective-permute-start.17 = (f32[136,128]{1,0:T(8,128)S(1)}, f32[136,128]{1,0:T(8,128)S(1)}, u32[]{:S(2)}, u32[]{:S(2)}) collective-permute-start(f32[136,128]{1,0:T(8,128)S(1)} %mixing.1.refs_0_), channel_id=1, source_target_pairs={{2,0},{3,1},{0,2},{1,3},{6,4},{7,5},{4,6},{5,7},{10,8},{11,9},{8,1... | collective-permute-start | bytes 208904 | tf_op jit(solution)/shard_map/ppermute | solution.py:49
  71.9 5.1 %collective-permute-start.18 = (f32[136,128]{1,0:T(8,128)S(1)}, f32[136,128]{1,0:T(8,128)S(1)}, u32[]{:S(2)}, u32[]{:S(2)}) collective-permute-start(f32[136,128]{1,0:T(8,128)S(1)} %mixing.1.refs_0_), channel_id=1, source_target_pairs={{4,0},{5,1},{6,2},{7,3},{0,4},{1,5},{2,6},{3,7},{12,8},{13,9},{14,... | collective-permute-start | bytes 208904 | tf_op jit(solution)/shard_map/ppermute | solution.py:49
  73.6 5.2 %collective-permute-start.19 = (f32[136,128]{1,0:T(8,128)S(1)}, f32[136,128]{1,0:T(8,128)S(1)}, u32[]{:S(2)}, u32[]{:S(2)}) collective-permute-start(f32[136,128]{1,0:T(8,128)S(1)} %mixing.1.refs_0_), channel_id=1, source_target_pairs={{6,0},{7,1},{4,2},{5,3},{2,4},{3,5},{0,6},{1,7},{14,8},{15,9},{12,... | collective-permute-start | bytes 208904 | tf_op jit(solution)/shard_map/ppermute | solution.py:49
  73.9 12.0 %collective-permute-start.24 = (bf16[128,1280]{1,0:T(8,128)(2,1)S(1)}, bf16[128,1280]{1,0:T(8,128)(2,1)S(1)}, u32[]{:S(2)}, u32[]{:S(2)}) collective-permute-start(bf16[128,1280]{1,0:T(8,128)(2,1)S(1)} %relay_step.15.refs_13_), channel_id=1, source_target_pairs={{8,0},{16,8},{24,16},{9,1},{17,9},{25,17},{10,2},{18,10},{26,18},{... | collective-permute-start | bytes 983048 | tf_op jit(solution)/shard_map/ppermute | solution.py:97
  78.9 1.6 %collective-permute-start.22 = (f32[4,136,128]{2,1,0:T(8,128)S(1)}, f32[4,136,128]{2,1,0:T(8,128)S(1)}, u32[]{:S(2)}, u32[]{:S(2)}) collective-permute-start(f32[4,136,128]{2,1,0:T(8,128)S(1)} %join.1), channel_id=1, source_target_pairs={{1,0},{0,1},{3,2},{2,3},{5,4},{4,5},{7,6},{6,7},{9,8},{8,9},{11,10... | collective-permute-start | bytes 835592 | tf_op jit(solution)/shard_map/ppermute | solution.py:49
  79.0 1.6 %collective-permute-start.21 = (f32[136,128]{1,0:T(8,128)S(1)}, f32[136,128]{1,0:T(8,128)S(1)}, u32[]{:S(2)}, u32[]{:S(2)}) collective-permute-start(f32[136,128]{1,0:T(8,128)S(1)} %mixing.1.refs_0_), channel_id=1, source_target_pairs={{1,0},{0,1},{3,2},{2,3},{5,4},{4,5},{7,6},{6,7},{9,8},{8,9},{11,10... | collective-permute-start | bytes 208904 | tf_op jit(solution)/shard_map/ppermute | solution.py:49

commit v4 on v3

--- a/solution.py
+++ b/solution.py
@@ -189,7 +189,7 @@
     chips = count // CORES
     mats = width // HEAD
     owners = mats // slots
-    per_step = 2 if owners % 2 == 0 else 1
+    per_step = next(n for n in (4, 2, 1) if owners % n == 0)
     block = per_step * slots * HEAD
     tokens = right[0].shape[0]
     total_tokens = sum(piece.shape[0] for piece in right)
@@ -242,7 +242,7 @@
         in_specs=[pl.BlockSpec(left.shape, lambda j: (0, 0, 0))] + [column(piece.shape[0]) for piece in right] + [column(rows)],
         out_specs=[column(rows), gram_spec, other_spec],
         scratch_shapes=[pltpu.VMEM((rows, total_tokens), BF16), pltpu.VMEM((count, packed, HEAD), F32)],
-        compiler_params=params(18),
+        compiler_params=params(26),
         cost_estimate=cost(
             2 * rows * total_tokens * width, 2 * total_tokens * (rows + width) + 4 * rows * width
         ),
@@ -541,11 +541,11 @@
     far = [swap(kv_rows, other_core)]
     columns = split_columns(inputs)
     left = lax.all_to_all(columns, "dp", 0, 0, tiled=True)
-    early = list(range(min(LAG, CHUNKS)))
-    products = list(weight_products(early, after(kv_rows, columns), weights))
+    products = list(weight_products([0], after(kv_rows, columns), weights))
     near = near[:1] + [after(piece, products[0]) for piece in near[1:]]
     products = [after(product, far[0], *near[1:]) for product in products]
     relay()
+    products += weight_products([1], after(kv_rows, sent[0]), weights)
     relay()
     far.extend(swap(piece, other_core) for piece in near[1:])
     if chips == 4:

time: 87.4 us -> 86.9 us (level)
  waiting for transfers between devices: 17.4 us -> 12 us
  starting transfers between devices: 31 us -> 33.8 us
  Pallas kernels: 36.8 us -> 38 us
    ppermute x8, waiting for transfers between devices: 11.3 us -> 3.83 us  [down(): return lax.ppermute(value, 'pipe', [(i, i - 1) for i in range(1, count)])]
    ppermute x17, starting transfers between devices: 16.3 us -> 18.9 us  [swap(): lax.ppermute(value, 'dp', [(i ^ by[i % CORES], i) for i in range(count)])]
    ppermute x17, waiting for transfers between devices: 6.07 us -> 8.13 us  [swap(): lax.ppermute(value, 'dp', [(i ^ by[i % CORES], i) for i in range(count)])]
    pallas_call x2 -> x3, Pallas kernels: 12.4 us -> 14.1 us  [weight_products(): pl.pallas_call(kernel, out_shape=[jax.ShapeDtypeStruct((tokens, span), F3...]
  transfers between devices with their start and end apart: 26 -> 26, of which waited for: 9 -> 9; matrix products, arithmetic and copies ran while one was open for 0% -> 0% of each run, Pallas kernels for 41% -> 43%
where the time goes in v4:
time: 86.9 us; the launch traced here: 86.4 us
  Pallas kernels  38 us (44%)
  starting transfers between devices  33.8 us (39%)
  waiting for transfers between devices  12 us (14%)
  local copies, waits for them, and re-layouts  1.5 us (2%)
  between operations  1.17 us (1%)
    ppermute x17, starting transfers between devices, swap(): lax.ppermute(value, 'dp', [(i ^ by[i % CORES], i) for i in range(count)])  18.9 us
    pallas_call x3, Pallas kernels, weight_products(): pl.pallas_call(kernel, out_shape=[jax.ShapeDtypeStruct((tokens, span), F3...  14.1 us
    ppermute x8, starting transfers between devices, down(): return lax.ppermute(value, 'pipe', [(i, i - 1) for i in range(1, count)])  10.5 us
    ppermute x17, waiting for transfers between devices, swap(): lax.ppermute(value, 'dp', [(i ^ by[i % CORES], i) for i in range(count)])  8.13 us
    pallas_call x1, Pallas kernels, gradient(): pl.pallas_call(kernel, grid=(steps,), out_shape=[jax.ShapeDtypeStruct((ro...  7.3 us
    pallas_call x1, Pallas kernels, apply_mixing(): pl.pallas_call(kernel, grid=(steps,), out_shape=[jax.ShapeDtypeStruct((ro...  5.36 us
    all_to_all x1, starting transfers between devices, shards(): left = lax.all_to_all(columns, 'dp', 0, 0, tiled=True)  4.4 us
    pallas_call x1, Pallas kernels, mixing(): pl.pallas_call(kernel, grid=(1,), out_shape=jax.ShapeDtypeStruct((packed,...  3.96 us
  transfers between devices with their start and end apart: 26, of which 9 were waited for; matrix products, arithmetic and copies ran while one was open for 0% of the time, Pallas kernels for 43%

profile of v4, /device:TPU:0, one launch (start us, length us, event | category | flops | bytes accessed | tf_op | source)
XLA Modules:
  0.0 86.4 jit_solution(15070425170209469993)
XLA Ops:
  0.6 3.0 %collective-permute-start = (bf16[128,2048]{1,0:T(8,128)(2,1)}, bf16[128,2048]{1,0:T(8,128)(2,1)}, u32[]{:S(2)}, u32[]{:S(2)}) collective-permute-start(bf16[128,2048]{1,0:T(8,128)(2,1)} %bitcast.6), channel_id=1, source_target_pairs={{2,0},{5,1},{0,2},{7,3},{6,4},{1,5},{4,6},{3,7},{10,8},{13,9},{8,1... | collective-permute-start | bytes 1572872 | tf_op jit(solution)/shard_map/ppermute | solution.py:49
  3.6 1.5 %collective-permute-start.1 = (bf16[128,2048]{1,0:T(8,128)(2,1)}, bf16[128,2048]{1,0:T(8,128)(2,1)}, u32[]{:S(2)}, u32[]{:S(2)}) collective-permute-start(bf16[128,2048]{1,0:T(8,128)(2,1)} %bitcast.7), channel_id=1, source_target_pairs={{4,0},{3,1},{6,2},{1,3},{0,4},{7,5},{2,6},{5,7},{12,8},{11,9},{14,... | collective-permute-start | bytes 1572872 | tf_op jit(solution)/shard_map/ppermute | solution.py:49
  5.2 0.0 collective-permute-start.3
  5.2 2.6 %split_columns.1 = bf16[8,640,128]{2,1,0:T(8,128)(2,1)} custom-call(bf16[128,5120]{1,0:T(8,128)(2,1)} %bitcast.17), custom_call_target="tpu_custom_call" | custom-call | flops 1 | bytes 1 | tf_op jit(solution)/shard_map/split_columns/pallas_call | solution.py:132
  7.7 0.0 copy-start.1
  7.8 4.4 %all-to-all-start = ((bf16[8,640,128]{2,1,0:T(8,128)(2,1)}), bf16[8,640,128]{2,1,0:T(8,128)(2,1)}, u32[]{:S(2)}, u32[]{:S(2)}) async-start(bf16[8,640,128]{2,1,0:T(8,128)(2,1)} %split_columns.1), calls=%async_computation | async-start | bytes 2621440 | tf_op jit(solution)/shard_map/all_to_all | solution.py:543
  12.2 0.0 copy-start
  12.2 4.1 %weight_products.3.refs_1_.refs_2_ = f32[128,1280]{1,0:T(8,128)S(1)} custom-call(bf16[128,2048]{1,0:T(8,128)(2,1)S(1)} %bitcast.10, bf16[5120,2048]{1,0:T(8,128)(2,1)} %bitcast.13), custom_call_target="tpu_custom_call" | custom-call | flops 1 | bytes 1 | tf_op jit(solution)/shard_map/weight_products/pallas_call | solution.py:425
  16.2 0.0 collective-permute-done.refs_2_
  16.3 2.2 %collective-permute-start.2 = (bf16[128,2048]{1,0:T(8,128)(2,1)}, bf16[128,2048]{1,0:T(8,128)(2,1)S(1)}, u32[]{:S(2)}, u32[]{:S(2)}) collective-permute-start(bf16[128,2048]{1,0:T(8,128)(2,1)} %collective-permute-done.refs_2_), channel_id=1, source_target_pairs={{4,0},{3,1},{6,2},{1,3},{0,4},{7,5},{2,6},{5,7},{12,8},{11,9},{14,... | collective-permute-start | bytes 1572872 | tf_op jit(solution)/shard_map/ppermute | solution.py:49
  18.5 0.0 collective-permute-start.4
  18.5 0.0 collective-permute-done.1.refs_3_
  18.5 0.0 collective-permute-done.3.refs_5_
  18.6 1.3 %collective-permute-start.6 = (bf16[128,1280]{1,0:T(8,128)(2,1)S(1)}, bf16[128,1280]{1,0:T(8,128)(2,1)S(1)}, u32[]{:S(2)}, u32[]{:S(2)}) collective-permute-start(bf16[128,1280]{1,0:T(8,128)(2,1)S(1)} %relay_step.8.refs_6_), channel_id=1, source_target_pairs={{8,0},{16,8},{24,16},{9,1},{17,9},{25,17},{10,2},{18,10},{26,18},{... | collective-permute-start | bytes 983048 | tf_op jit(solution)/shard_map/ppermute | solution.py:97
  19.9 3.9 %weight_products.4.refs_1_.refs_2_ = f32[128,1280]{1,0:T(8,128)S(1)} custom-call(bf16[128,2048]{1,0:T(8,128)(2,1)S(1)} %bitcast.11, bf16[5120,2048]{1,0:T(8,128)(2,1)} %bitcast.14), custom_call_target="tpu_custom_call" | custom-call | flops 1 | bytes 1 | tf_op jit(solution)/shard_map/weight_products/pallas_call | solution.py:425
  23.8 1.3 %collective-permute-start.9 = (bf16[128,1280]{1,0:T(8,128)(2,1)S(1)}, bf16[128,1280]{1,0:T(8,128)(2,1)S(1)}, u32[]{:S(2)}, u32[]{:S(2)}) collective-permute-start(bf16[128,1280]{1,0:T(8,128)(2,1)S(1)} %relay_step.9.refs_7_), channel_id=1, source_target_pairs={{8,0},{16,8},{24,16},{9,1},{17,9},{25,17},{10,2},{18,10},{26,18},{... | collective-permute-start | bytes 983048 | tf_op jit(solution)/shard_map/ppermute | solution.py:97
  25.1 0.6 collective-permute-start.5
  25.7 6.1 %weight_products.5 = (f32[128,1280]{1,0:T(8,128)S(1)}, f32[128,1280]{1,0:T(8,128)S(1)}) custom-call(bf16[128,2048]{1,0:T(8,128)(2,1)S(1)} %bitcast.12, bf16[5120,2048]{1,0:T(8,128)(2,1)} %bitcast.15), custom_call_target="tpu_custom_call" | custom-call | flops 1 | bytes 1 | tf_op jit(solution)/shard_map/weight_products/pallas_call | solution.py:425
  31.9 0.0 collective-permute-done.6.refs_0_
  31.9 1.3 %collective-permute-start.11 = (bf16[128,1280]{1,0:T(8,128)(2,1)S(1)}, bf16[128,1280]{1,0:T(8,128)(2,1)}, u32[]{:S(2)}, u32[]{:S(2)}) collective-permute-start(bf16[128,1280]{1,0:T(8,128)(2,1)S(1)} %relay_step.10.refs_8_), channel_id=1, source_target_pairs={{8,0},{16,8},{24,16},{9,1},{17,9},{25,17},{10,2},{18,10},{26,18},{... | collective-permute-start | bytes 983048 | tf_op jit(solution)/shard_map/ppermute | solution.py:97
  33.2 2.2 %collective-permute-done.2.in_ref.refs_4_ = bf16[128,2048]{1,0:T(8,128)(2,1)S(1)} collective-permute-done((bf16[128,2048]{1,0:T(8,128)(2,1)}, bf16[128,2048]{1,0:T(8,128)(2,1)S(1)}, u32[]{:S(2)}, u32[]{:S(2)}) %collective-permute-start.2) | collective-permute-done | bytes 524320 | tf_op jit(solution)/shard_map/ppermute | solution.py:49
  35.5 0.8 cut.1
  36.3 1.1 %collective-permute-start.7 = (bf16[64,2048]{1,0:T(8,128)(2,1)}, bf16[64,2048]{1,0:T(8,128)(2,1)S(1)}, u32[]{:S(2)}, u32[]{:S(2)}) collective-permute-start(bf16[64,2048]{1,0:T(8,128)(2,1)} %get-tuple-element.46), channel_id=1, source_target_pairs={{1,0},{0,1},{3,2},{2,3},{5,4},{4,5},{7,6},{6,7},{9,8},{8,9},{11,10... | collective-permute-start | bytes 786440 | tf_op jit(solution)/shard_map/ppermute | solution.py:49
  37.4 0.3 collective-permute-done.9.refs_0_
  37.7 0.0 collective-permute-start.8
  37.7 0.7 relay_step.11.refs_9_
  38.4 0.0 collective-permute-done.4.refs_6_
  38.4 0.8 copy-done.7
  39.2 1.3 %collective-permute-start.10 = (bf16[128,1280]{1,0:T(8,128)(2,1)}, bf16[128,1280]{1,0:T(8,128)(2,1)}, u32[]{:S(2)}, u32[]{:S(2)}) collective-permute-start(bf16[128,1280]{1,0:T(8,128)(2,1)} %relay_step.11.refs_9_), channel_id=1, source_target_pairs={{8,0},{16,8},{24,16},{9,1},{17,9},{25,17},{10,2},{18,10},{26,18},{... | collective-permute-start | bytes 983048 | tf_op jit(solution)/shard_map/ppermute | solution.py:97
  40.5 0.0 collective-permute-done.5.refs_7_
  40.5 0.0 collective-permute-done.7.refs_8_
  40.5 0.0 copy-start.8
  40.5 0.7 copy-done.8
  41.2 7.3 %gradient.1 = (bf16[640,2048]{1,0:T(8,128)(2,1)S(1)}, f32[4,136,128]{2,1,0:T(8,128)S(1)}, f32[5,136,128]{2,1,0:T(8,128)S(1)}) custom-call(bf16[8,640,128]{2,1,0:T(8,128)(2,1)} %all-to-all-done.refs_0_, bf16[128,2048]{1,0:T(8,128)(2,1)} %bitcast.9, bf16[128,2048]{1,0:T(8,128)(2,1)} %collective-permute-done.refs_2_, ...), custom_call_target="tpu_custom_call" | custom-call | flops 1 | bytes 1 | tf_op jit(solution)/shard_map/gradient/pallas_call | solution.py:238
  48.5 1.0 %relay_step.12.refs_10_ = bf16[128,1280]{1,0:T(8,128)(2,1)S(1)} custom-call(bf16[128,1280]{1,0:T(8,128)(2,1)} %collective-permute-done.11.refs_0_, f32[128,1280]{1,0:T(8,128)S(1)} %weight_products.3.refs_1_.refs_2_, f32[128,1280]{1,0:T(8,128)S(1)} %get-tuple-element.44.refs_3_.refs_2_), custom_call_target="tpu_custom_call" | custom-call | flops 1 | bytes 1 | tf_op jit(solution)/shard_map/relay_step/pallas_call | solution.py:462
  49.5 0.5 collective-permute-start.12
  50.0 1.3 %collective-permute-start.13 = (bf16[128,1280]{1,0:T(8,128)(2,1)S(1)}, bf16[128,1280]{1,0:T(8,128)(2,1)S(1)}, u32[]{:S(2)}, u32[]{:S(2)}) collective-permute-start(bf16[128,1280]{1,0:T(8,128)(2,1)S(1)} %relay_step.12.refs_10_), channel_id=1, source_target_pairs={{8,0},{16,8},{24,16},{9,1},{17,9},{25,17},{10,2},{18,10},{26,18},{... | collective-permute-start | bytes 983048 | tf_op jit(solution)/shard_map/ppermute | solution.py:97
  51.3 0.8 collective-permute-done.10.refs_0_
  52.1 1.0 %relay_step.13.refs_11_ = bf16[128,1280]{1,0:T(8,128)(2,1)S(1)} custom-call(bf16[128,1280]{1,0:T(8,128)(2,1)} %collective-permute-done.10.refs_0_, f32[128,1280]{1,0:T(8,128)S(1)} %weight_products.4.refs_1_.refs_2_, f32[128,1280]{1,0:T(8,128)S(1)} %get-tuple-element.42.refs_3_.refs_2_), custom_call_target="tpu_custom_call" | custom-call | flops 1 | bytes 1 | tf_op jit(solution)/shard_map/relay_step/pallas_call | solution.py:462
  53.1 1.3 %collective-permute-start.23 = (bf16[128,1280]{1,0:T(8,128)(2,1)S(1)}, bf16[128,1280]{1,0:T(8,128)(2,1)S(1)}, u32[]{:S(2)}, u32[]{:S(2)}) collective-permute-start(bf16[128,1280]{1,0:T(8,128)(2,1)S(1)} %relay_step.13.refs_11_), channel_id=1, source_target_pairs={{8,0},{16,8},{24,16},{9,1},{17,9},{25,17},{10,2},{18,10},{26,18},{... | collective-permute-start | bytes 983048 | tf_op jit(solution)/shard_map/ppermute | solution.py:97
  54.4 3.2 %collective-permute-start.14 = (f32[136,128]{1,0:T(8,128)S(1)}, f32[136,128]{1,0:T(8,128)S(1)}, u32[]{:S(2)}, u32[]{:S(2)}) collective-permute-start(f32[136,128]{1,0:T(8,128)S(1)} %get-tuple-element.58), channel_id=1, source_target_pairs={{2,0},{3,1},{0,2},{1,3},{6,4},{7,5},{4,6},{5,7},{10,8},{11,9},{8,1... | collective-permute-start | bytes 208904 | tf_op jit(solution)/shard_map/ppermute | solution.py:49
  57.6 2.6 %collective-permute-start.15 = (f32[136,128]{1,0:T(8,128)S(1)}, f32[136,128]{1,0:T(8,128)S(1)}, u32[]{:S(2)}, u32[]{:S(2)}) collective-permute-start(f32[136,128]{1,0:T(8,128)S(1)} %get-tuple-element.59), channel_id=1, source_target_pairs={{4,0},{5,1},{6,2},{7,3},{0,4},{1,5},{2,6},{3,7},{12,8},{13,9},{14,... | collective-permute-start | bytes 208904 | tf_op jit(solution)/shard_map/ppermute | solution.py:49
  60.2 2.7 %collective-permute-done.13.refs_0_ = bf16[128,1280]{1,0:T(8,128)(2,1)S(1)} collective-permute-done((bf16[128,1280]{1,0:T(8,128)(2,1)S(1)}, bf16[128,1280]{1,0:T(8,128)(2,1)S(1)}, u32[]{:S(2)}, u32[]{:S(2)}) %collective-permute-start.13) | collective-permute-done | bytes 327712 | tf_op jit(solution)/shard_map/ppermute | solution.py:97
  63.0 0.0 collective-permute-done.15.refs_2_
  63.0 2.4 %collective-permute-done.16.refs_3_ = f32[136,128]{1,0:T(8,128)S(1)} collective-permute-done((f32[136,128]{1,0:T(8,128)S(1)}, f32[136,128]{1,0:T(8,128)S(1)}, u32[]{:S(2)}, u32[]{:S(2)}) %collective-permute-start.16) | collective-permute-done | bytes 69664 | tf_op jit(solution)/shard_map/ppermute | solution.py:49
  65.5 0.1 relay_step.14.refs_12_
  65.5 1.5 %collective-permute-start.20 = (bf16[128,1280]{1,0:T(8,128)(2,1)S(1)}, bf16[128,1280]{1,0:T(8,128)(2,1)S(1)}, u32[]{:S(2)}, u32[]{:S(2)}) collective-permute-start(bf16[128,1280]{1,0:T(8,128)(2,1)S(1)} %relay_step.14.refs_12_), channel_id=1, source_target_pairs={{8,0},{16,8},{24,16},{9,1},{17,9},{25,17},{10,2},{18,10},{26,18},{... | collective-permute-start | bytes 983048 | tf_op jit(solution)/shard_map/ppermute | solution.py:97
  67.0 4.0 %mixing.1.refs_0_ = f32[136,128]{1,0:T(8,128)S(1)} custom-call(f32[136,128]{1,0:T(8,128)S(1)} %get-tuple-element.62.refs_0_, f32[136,128]{1,0:T(8,128)S(1)} %collective-permute-done.14.refs_1_, f32[136,128]{1,0:T(8,128)S(1)} %collective-permute-done.15.refs_2_, f32[136,128]{1,0:T(8,128)S(1)} %collective-permute-done.16.refs_3_), custom_call_target="tpu_custom_call" | custom-call | flops 1 | bytes 1 | tf_op jit(solution)/shard_map/mixing/pallas_call | solution.py:304
  71.0 0.1 collective-permute-start.17
  71.1 1.9 %collective-permute-start.18 = (f32[136,128]{1,0:T(8,128)S(1)}, f32[136,128]{1,0:T(8,128)S(1)}, u32[]{:S(2)}, u32[]{:S(2)}) collective-permute-start(f32[136,128]{1,0:T(8,128)S(1)} %mixing.1.refs_0_), channel_id=1, source_target_pairs={{4,0},{5,1},{6,2},{7,3},{0,4},{1,5},{2,6},{3,7},{12,8},{13,9},{14,... | collective-permute-start | bytes 208904 | tf_op jit(solution)/shard_map/ppermute | solution.py:49
  73.0 1.6 %collective-permute-start.19 = (f32[136,128]{1,0:T(8,128)S(1)}, f32[136,128]{1,0:T(8,128)S(1)}, u32[]{:S(2)}, u32[]{:S(2)}) collective-permute-start(f32[136,128]{1,0:T(8,128)S(1)} %mixing.1.refs_0_), channel_id=1, source_target_pairs={{6,0},{7,1},{4,2},{5,3},{2,4},{3,5},{0,6},{1,7},{14,8},{15,9},{12,... | collective-permute-start | bytes 208904 | tf_op jit(solution)/shard_map/ppermute | solution.py:49
  74.5 0.0 collective-permute-done.23.refs_0_
  74.5 0.1 relay_step.15.refs_13_
  74.6 1.3 %collective-permute-start.24 = (bf16[128,1280]{1,0:T(8,128)(2,1)S(1)}, bf16[128,1280]{1,0:T(8,128)(2,1)S(1)}, u32[]{:S(2)}, u32[]{:S(2)}) collective-permute-start(bf16[128,1280]{1,0:T(8,128)(2,1)S(1)} %relay_step.15.refs_13_), channel_id=1, source_target_pairs={{8,0},{16,8},{24,16},{9,1},{17,9},{25,17},{10,2},{18,10},{26,18},{... | collective-permute-start | bytes 983048 | tf_op jit(solution)/shard_map/ppermute | solution.py:97
  75.9 0.3 collective-permute-done.18.refs_2_
  76.2 2.0 %collective-permute-done.19.refs_3_ = f32[136,128]{1,0:T(8,128)S(1)} collective-permute-done((f32[136,128]{1,0:T(8,128)S(1)}, f32[136,128]{1,0:T(8,128)S(1)}, u32[]{:S(2)}, u32[]{:S(2)}) %collective-permute-start.19) | collective-permute-done | bytes 69664 | tf_op jit(solution)/shard_map/ppermute | solution.py:49
  78.2 0.1 collective-permute-start.22
  78.3 0.0 collective-permute-done.20.refs_0_
  78.3 0.5 collective-permute-start.21
  78.8 1.0 %collective-permute-done.22.refs_5_ = f32[4,136,128]{2,1,0:T(8,128)S(1)} collective-permute-done((f32[4,136,128]{2,1,0:T(8,128)S(1)}, f32[4,136,128]{2,1,0:T(8,128)S(1)}, u32[]{:S(2)}, u32[]{:S(2)}) %collective-permute-start.22) | collective-permute-done | bytes 278560 | tf_op jit(solution)/shard_map/ppermute | solution.py:49
  79.8 0.1 collective-permute-done.21.refs_4_
  79.9 5.4 %apply_mixing.1 = (bf16[640,2048]{1,0:T(8,128)(2,1)}, bf16[128,5120]{1,0:T(8,128)(2,1)}) custom-call(f32[136,128]{1,0:T(8,128)S(1)} %mixing.1.refs_0_, f32[136,128]{1,0:T(8,128)S(1)} %collective-permute-done.17.refs_1_, f32[136,128]{1,0:T(8,128)S(1)} %collective-permute-done.18.refs_2_, f32[136,128]{1,0:T(8,128)S(1)} %collective-permute-done.19.refs_3_, ...), custom_call_target="tpu_custom_call" | custom-call | flops 1 | bytes 1 | tf_op jit(solution)/shard_map/apply_mixing/pallas_call | solution.py:379
  85.3 0.0 collective-permute-done.24.refs_1_
  85.3 0.9 %last_step.1 = bf16[128,5120]{1,0:T(8,128)(2,1)} custom-call(bf16[128,1280]{1,0:T(8,128)(2,1)S(1)} %collective-permute-done.20.refs_0_, bf16[128,1280]{1,0:T(8,128)(2,1)S(1)} %collective-permute-done.24.refs_1_, f32[128,1280]{1,0:T(8,128)S(1)} %get-tuple-element.44.refs_3_.refs_2_, ...), custom_call_target="tpu_custom_call", output_to_operand_aliasing={{}: (4, {})} | custom-call | flops 1 | bytes 1 | tf_op jit(solution)/shard_map/last_step/pallas_call | solution.py:492
  (25 shorter events, 0.2 us)
Async XLA Ops:
  0.6 15.6 %collective-permute-start = (bf16[128,2048]{1,0:T(8,128)(2,1)}, bf16[128,2048]{1,0:T(8,128)(2,1)}, u32[]{:S(2)}, u32[]{:S(2)}) collective-permute-start(bf16[128,2048]{1,0:T(8,128)(2,1)} %bitcast.6), channel_id=1, source_target_pairs={{2,0},{5,1},{0,2},{7,3},{6,4},{1,5},{4,6},{3,7},{10,8},{13,9},{8,1... | collective-permute-start | bytes 1572872 | tf_op jit(solution)/shard_map/ppermute | solution.py:49
  3.6 14.9 %collective-permute-start.1 = (bf16[128,2048]{1,0:T(8,128)(2,1)}, bf16[128,2048]{1,0:T(8,128)(2,1)}, u32[]{:S(2)}, u32[]{:S(2)}) collective-permute-start(bf16[128,2048]{1,0:T(8,128)(2,1)} %bitcast.7), channel_id=1, source_target_pairs={{4,0},{3,1},{6,2},{1,3},{0,4},{7,5},{2,6},{5,7},{12,8},{11,9},{14,... | collective-permute-start | bytes 1572872 | tf_op jit(solution)/shard_map/ppermute | solution.py:49
  5.2 13.4 %collective-permute-start.3 = (bf16[128,2048]{1,0:T(8,128)(2,1)}, bf16[128,2048]{1,0:T(8,128)(2,1)}, u32[]{:S(2)}, u32[]{:S(2)}) collective-permute-start(bf16[128,2048]{1,0:T(8,128)(2,1)} %bitcast.8), channel_id=1, source_target_pairs={{1,0},{0,1},{3,2},{2,3},{5,4},{4,5},{7,6},{6,7},{9,8},{8,9},{11,10... | collective-permute-start | bytes 1572872 | tf_op jit(solution)/shard_map/ppermute | solution.py:49
  7.7 4.4 %copy-start.1 = (bf16[1,128,2048]{2,1,0:T(8,128)(2,1)S(1)}, bf16[1,128,2048]{2,1,0:T(8,128)(2,1)}, u32[]{:S(2)}) copy-start(bf16[1,128,2048]{2,1,0:T(8,128)(2,1)} %param.7) | copy-start | bytes 1572868
  7.8 32.8 %all-to-all-start = ((bf16[8,640,128]{2,1,0:T(8,128)(2,1)}), bf16[8,640,128]{2,1,0:T(8,128)(2,1)}, u32[]{:S(2)}, u32[]{:S(2)}) async-start(bf16[8,640,128]{2,1,0:T(8,128)(2,1)} %split_columns.1), calls=%async_computation | async-start | bytes 2621440 | tf_op jit(solution)/shard_map/all_to_all | solution.py:543
  12.2 6.3 %copy-start = (bf16[128,5120]{1,0:T(8,128)(2,1)S(1)}, bf16[128,5120]{1,0:T(8,128)(2,1)}, u32[]{:S(2)}) copy-start(bf16[128,5120]{1,0:T(8,128)(2,1)} %refs_1_.3) | copy-start | bytes 3932164
  16.3 19.2 %collective-permute-start.2 = (bf16[128,2048]{1,0:T(8,128)(2,1)}, bf16[128,2048]{1,0:T(8,128)(2,1)S(1)}, u32[]{:S(2)}, u32[]{:S(2)}) collective-permute-start(bf16[128,2048]{1,0:T(8,128)(2,1)} %collective-permute-done.refs_2_), channel_id=1, source_target_pairs={{4,0},{3,1},{6,2},{1,3},{0,4},{7,5},{2,6},{5,7},{12,8},{11,9},{14,... | collective-permute-start | bytes 1572872 | tf_op jit(solution)/shard_map/ppermute | solution.py:49
  18.5 19.9 %collective-permute-start.4 = (bf16[128,2048]{1,0:T(8,128)(2,1)}, bf16[128,2048]{1,0:T(8,128)(2,1)S(1)}, u32[]{:S(2)}, u32[]{:S(2)}) collective-permute-start(bf16[128,2048]{1,0:T(8,128)(2,1)} %collective-permute-done.refs_2_), channel_id=1, source_target_pairs={{1,0},{0,1},{3,2},{2,3},{5,4},{4,5},{7,6},{6,7},{9,8},{8,9},{11,10... | collective-permute-start | bytes 1572872 | tf_op jit(solution)/shard_map/ppermute | solution.py:49
  18.6 13.3 %collective-permute-start.6 = (bf16[128,1280]{1,0:T(8,128)(2,1)S(1)}, bf16[128,1280]{1,0:T(8,128)(2,1)S(1)}, u32[]{:S(2)}, u32[]{:S(2)}) collective-permute-start(bf16[128,1280]{1,0:T(8,128)(2,1)S(1)} %relay_step.8.refs_6_), channel_id=1, source_target_pairs={{8,0},{16,8},{24,16},{9,1},{17,9},{25,17},{10,2},{18,10},{26,18},{... | collective-permute-start | bytes 983048 | tf_op jit(solution)/shard_map/ppermute | solution.py:97
  23.8 8.0 %copy-start.3 = (bf16[128,1280]{1,0:T(8,128)(2,1)}, bf16[128,1280]{1,0:T(8,128)(2,1)S(1)}, u32[]{:S(2)}) copy-start(bf16[128,1280]{1,0:T(8,128)(2,1)S(1)} %relay_step.9.refs_7_) | copy-start | bytes 983044
  23.8 13.8 %collective-permute-start.9 = (bf16[128,1280]{1,0:T(8,128)(2,1)S(1)}, bf16[128,1280]{1,0:T(8,128)(2,1)S(1)}, u32[]{:S(2)}, u32[]{:S(2)}) collective-permute-start(bf16[128,1280]{1,0:T(8,128)(2,1)S(1)} %relay_step.9.refs_7_), channel_id=1, source_target_pairs={{8,0},{16,8},{24,16},{9,1},{17,9},{25,17},{10,2},{18,10},{26,18},{... | collective-permute-start | bytes 983048 | tf_op jit(solution)/shard_map/ppermute | solution.py:97
  25.1 15.4 %collective-permute-start.5 = (bf16[128,2048]{1,0:T(8,128)(2,1)}, bf16[128,2048]{1,0:T(8,128)(2,1)}, u32[]{:S(2)}, u32[]{:S(2)}) collective-permute-start(bf16[128,2048]{1,0:T(8,128)(2,1)} %collective-permute-done.1.refs_3_), channel_id=1, source_target_pairs={{1,0},{0,1},{3,2},{2,3},{5,4},{4,5},{7,6},{6,7},{9,8},{8,9},{11,10... | collective-permute-start | bytes 1572872 | tf_op jit(solution)/shard_map/ppermute | solution.py:49
  31.9 6.5 %copy-start.5 = (bf16[128,1280]{1,0:T(8,128)(2,1)}, bf16[128,1280]{1,0:T(8,128)(2,1)S(1)}, u32[]{:S(2)}) copy-start(bf16[128,1280]{1,0:T(8,128)(2,1)S(1)} %relay_step.10.refs_8_) | copy-start | bytes 983044
  31.9 16.6 %collective-permute-start.11 = (bf16[128,1280]{1,0:T(8,128)(2,1)S(1)}, bf16[128,1280]{1,0:T(8,128)(2,1)}, u32[]{:S(2)}, u32[]{:S(2)}) collective-permute-start(bf16[128,1280]{1,0:T(8,128)(2,1)S(1)} %relay_step.10.refs_8_), channel_id=1, source_target_pairs={{8,0},{16,8},{24,16},{9,1},{17,9},{25,17},{10,2},{18,10},{26,18},{... | collective-permute-start | bytes 983048 | tf_op jit(solution)/shard_map/ppermute | solution.py:97
  35.5 2.9 %copy-start.2 = (bf16[128,2048]{1,0:T(8,128)(2,1)}, bf16[128,2048]{1,0:T(8,128)(2,1)S(1)}, u32[]{:S(2)}) copy-start(bf16[128,2048]{1,0:T(8,128)(2,1)S(1)} %collective-permute-done.2.in_ref.refs_4_) | copy-start | bytes 1572868
  36.3 4.2 %collective-permute-start.7 = (bf16[64,2048]{1,0:T(8,128)(2,1)}, bf16[64,2048]{1,0:T(8,128)(2,1)S(1)}, u32[]{:S(2)}, u32[]{:S(2)}) collective-permute-start(bf16[64,2048]{1,0:T(8,128)(2,1)} %get-tuple-element.46), channel_id=1, source_target_pairs={{1,0},{0,1},{3,2},{2,3},{5,4},{4,5},{7,6},{6,7},{9,8},{8,9},{11,10... | collective-permute-start | bytes 786440 | tf_op jit(solution)/shard_map/ppermute | solution.py:49
  37.7 2.9 %collective-permute-start.8 = (bf16[64,2048]{1,0:T(8,128)(2,1)}, bf16[64,2048]{1,0:T(8,128)(2,1)}, u32[]{:S(2)}, u32[]{:S(2)}) collective-permute-start(bf16[64,2048]{1,0:T(8,128)(2,1)} %get-tuple-element.47), channel_id=1, source_target_pairs={{1,0},{0,1},{3,2},{2,3},{5,4},{4,5},{7,6},{6,7},{9,8},{8,9},{11,10... | collective-permute-start | bytes 786440 | tf_op jit(solution)/shard_map/ppermute | solution.py:49
  38.4 0.8 copy-start.7
  39.2 12.9 %collective-permute-start.10 = (bf16[128,1280]{1,0:T(8,128)(2,1)}, bf16[128,1280]{1,0:T(8,128)(2,1)}, u32[]{:S(2)}, u32[]{:S(2)}) collective-permute-start(bf16[128,1280]{1,0:T(8,128)(2,1)} %relay_step.11.refs_9_), channel_id=1, source_target_pairs={{8,0},{16,8},{24,16},{9,1},{17,9},{25,17},{10,2},{18,10},{26,18},{... | collective-permute-start | bytes 983048 | tf_op jit(solution)/shard_map/ppermute | solution.py:97
  40.5 0.7 copy-start.8
  49.5 4.8 %collective-permute-start.12 = (f32[5,136,128]{2,1,0:T(8,128)S(1)}, f32[5,136,128]{2,1,0:T(8,128)S(1)}, u32[]{:S(2)}, u32[]{:S(2)}) collective-permute-start(f32[5,136,128]{2,1,0:T(8,128)S(1)} %get-tuple-element.56), channel_id=1, source_target_pairs={{1,0},{0,1},{3,2},{2,3},{5,4},{4,5},{7,6},{6,7},{9,8},{8,9},{11,10... | collective-permute-start | bytes 1044488 | tf_op jit(solution)/shard_map/ppermute | solution.py:49
  50.0 13.0 %collective-permute-start.13 = (bf16[128,1280]{1,0:T(8,128)(2,1)S(1)}, bf16[128,1280]{1,0:T(8,128)(2,1)S(1)}, u32[]{:S(2)}, u32[]{:S(2)}) collective-permute-start(bf16[128,1280]{1,0:T(8,128)(2,1)S(1)} %relay_step.12.refs_10_), channel_id=1, source_target_pairs={{8,0},{16,8},{24,16},{9,1},{17,9},{25,17},{10,2},{18,10},{26,18},{... | collective-permute-start | bytes 983048 | tf_op jit(solution)/shard_map/ppermute | solution.py:97
  53.1 21.5 %collective-permute-start.23 = (bf16[128,1280]{1,0:T(8,128)(2,1)S(1)}, bf16[128,1280]{1,0:T(8,128)(2,1)S(1)}, u32[]{:S(2)}, u32[]{:S(2)}) collective-permute-start(bf16[128,1280]{1,0:T(8,128)(2,1)S(1)} %relay_step.13.refs_11_), channel_id=1, source_target_pairs={{8,0},{16,8},{24,16},{9,1},{17,9},{25,17},{10,2},{18,10},{26,18},{... | collective-permute-start | bytes 983048 | tf_op jit(solution)/shard_map/ppermute | solution.py:97
  54.4 8.6 %collective-permute-start.14 = (f32[136,128]{1,0:T(8,128)S(1)}, f32[136,128]{1,0:T(8,128)S(1)}, u32[]{:S(2)}, u32[]{:S(2)}) collective-permute-start(f32[136,128]{1,0:T(8,128)S(1)} %get-tuple-element.58), channel_id=1, source_target_pairs={{2,0},{3,1},{0,2},{1,3},{6,4},{7,5},{4,6},{5,7},{10,8},{11,9},{8,1... | collective-permute-start | bytes 208904 | tf_op jit(solution)/shard_map/ppermute | solution.py:49
  57.6 5.4 %collective-permute-start.15 = (f32[136,128]{1,0:T(8,128)S(1)}, f32[136,128]{1,0:T(8,128)S(1)}, u32[]{:S(2)}, u32[]{:S(2)}) collective-permute-start(f32[136,128]{1,0:T(8,128)S(1)} %get-tuple-element.59), channel_id=1, source_target_pairs={{4,0},{5,1},{6,2},{7,3},{0,4},{1,5},{2,6},{3,7},{12,8},{13,9},{14,... | collective-permute-start | bytes 208904 | tf_op jit(solution)/shard_map/ppermute | solution.py:49
  60.2 5.2 %collective-permute-start.16 = (f32[136,128]{1,0:T(8,128)S(1)}, f32[136,128]{1,0:T(8,128)S(1)}, u32[]{:S(2)}, u32[]{:S(2)}) collective-permute-start(f32[136,128]{1,0:T(8,128)S(1)} %get-tuple-element.60), channel_id=1, source_target_pairs={{6,0},{7,1},{4,2},{5,3},{2,4},{3,5},{0,6},{1,7},{14,8},{15,9},{12,... | collective-permute-start | bytes 208904 | tf_op jit(solution)/shard_map/ppermute | solution.py:49
  65.5 12.8 %collective-permute-start.20 = (bf16[128,1280]{1,0:T(8,128)(2,1)S(1)}, bf16[128,1280]{1,0:T(8,128)(2,1)S(1)}, u32[]{:S(2)}, u32[]{:S(2)}) collective-permute-start(bf16[128,1280]{1,0:T(8,128)(2,1)S(1)} %relay_step.14.refs_12_), channel_id=1, source_target_pairs={{8,0},{16,8},{24,16},{9,1},{17,9},{25,17},{10,2},{18,10},{26,18},{... | collective-permute-start | bytes 983048 | tf_op jit(solution)/shard_map/ppermute | solution.py:97
  71.0 9.0 %copy-start.4 = (bf16[128,1280]{1,0:T(8,128)(2,1)S(1)}, bf16[128,1280]{1,0:T(8,128)(2,1)}, u32[]{:S(2)}) copy-start(bf16[128,1280]{1,0:T(8,128)(2,1)} %copy-done.3) | copy-start | bytes 983044
  71.0 9.0 %copy-start.6 = (bf16[128,1280]{1,0:T(8,128)(2,1)S(1)}, bf16[128,1280]{1,0:T(8,128)(2,1)}, u32[]{:S(2)}) copy-start(bf16[128,1280]{1,0:T(8,128)(2,1)} %copy-done.5) | copy-start | bytes 983044
  71.0 4.9 %collective-permute-start.17 = (f32[136,128]{1,0:T(8,128)S(1)}, f32[136,128]{1,0:T(8,128)S(1)}, u32[]{:S(2)}, u32[]{:S(2)}) collective-permute-start(f32[136,128]{1,0:T(8,128)S(1)} %mixing.1.refs_0_), channel_id=1, source_target_pairs={{2,0},{3,1},{0,2},{1,3},{6,4},{7,5},{4,6},{5,7},{10,8},{11,9},{8,1... | collective-permute-start | bytes 208904 | tf_op jit(solution)/shard_map/ppermute | solution.py:49
  71.1 5.1 %collective-permute-start.18 = (f32[136,128]{1,0:T(8,128)S(1)}, f32[136,128]{1,0:T(8,128)S(1)}, u32[]{:S(2)}, u32[]{:S(2)}) collective-permute-start(f32[136,128]{1,0:T(8,128)S(1)} %mixing.1.refs_0_), channel_id=1, source_target_pairs={{4,0},{5,1},{6,2},{7,3},{0,4},{1,5},{2,6},{3,7},{12,8},{13,9},{14,... | collective-permute-start | bytes 208904 | tf_op jit(solution)/shard_map/ppermute | solution.py:49
  73.0 5.2 %collective-permute-start.19 = (f32[136,128]{1,0:T(8,128)S(1)}, f32[136,128]{1,0:T(8,128)S(1)}, u32[]{:S(2)}, u32[]{:S(2)}) collective-permute-start(f32[136,128]{1,0:T(8,128)S(1)} %mixing.1.refs_0_), channel_id=1, source_target_pairs={{6,0},{7,1},{4,2},{5,3},{2,4},{3,5},{0,6},{1,7},{14,8},{15,9},{12,... | collective-permute-start | bytes 208904 | tf_op jit(solution)/shard_map/ppermute | solution.py:49
  74.6 10.7 %collective-permute-start.24 = (bf16[128,1280]{1,0:T(8,128)(2,1)S(1)}, bf16[128,1280]{1,0:T(8,128)(2,1)S(1)}, u32[]{:S(2)}, u32[]{:S(2)}) collective-permute-start(bf16[128,1280]{1,0:T(8,128)(2,1)S(1)} %relay_step.15.refs_13_), channel_id=1, source_target_pairs={{8,0},{16,8},{24,16},{9,1},{17,9},{25,17},{10,2},{18,10},{26,18},{... | collective-permute-start | bytes 983048 | tf_op jit(solution)/shard_map/ppermute | solution.py:97
  78.2 1.6 %collective-permute-start.22 = (f32[4,136,128]{2,1,0:T(8,128)S(1)}, f32[4,136,128]{2,1,0:T(8,128)S(1)}, u32[]{:S(2)}, u32[]{:S(2)}) collective-permute-start(f32[4,136,128]{2,1,0:T(8,128)S(1)} %join.1), channel_id=1, source_target_pairs={{1,0},{0,1},{3,2},{2,3},{5,4},{4,5},{7,6},{6,7},{9,8},{8,9},{11,10... | collective-permute-start | bytes 835592 | tf_op jit(solution)/shard_map/ppermute | solution.py:49
  78.3 1.6 %collective-permute-start.21 = (f32[136,128]{1,0:T(8,128)S(1)}, f32[136,128]{1,0:T(8,128)S(1)}, u32[]{:S(2)}, u32[]{:S(2)}) collective-permute-start(f32[136,128]{1,0:T(8,128)S(1)} %mixing.1.refs_0_), channel_id=1, source_target_pairs={{1,0},{0,1},{3,2},{2,3},{5,4},{4,5},{7,6},{6,7},{9,8},{8,9},{11,10... | collective-permute-start | bytes 208904 | tf_op jit(solution)/shard_map/ppermute | solution.py:49

commit v5 on v4

--- a/solution.py
+++ b/solution.py
@@ -247,7 +247,7 @@
             2 * rows * total_tokens * width, 2 * total_tokens * (rows + width) + 4 * rows * width
         ),
         name="gradient",
-    )(in_hbm(left), *[in_hbm(piece) for piece in right], in_hbm(moment))
+    )(in_hbm(left), *[in_hbm(piece) for piece in right[:-2]], *right[-2:], in_hbm(moment))
 
 
 def add_pairs(first, second):
@@ -320,7 +320,7 @@
     sections = lax.axis_size("pipe")
     mats = width // HEAD
     owners = mats // slots
-    per_step = 2 if owners % 2 == 0 else 1
+    per_step = next(n for n in (4, 2, 1) if owners % n == 0)
     steps = owners // per_step
     span = slots * HEAD
     block = per_step * span

time: 86.9 us -> 86.7 us (level)
  waiting for transfers between devices: 12 us -> 12.9 us
    ppermute x8, waiting for transfers between devices: 3.83 us -> 4.79 us  [down(): return lax.ppermute(value, 'pipe', [(i, i - 1) for i in range(1, count)])]
  transfers between devices with their start and end apart: 26 -> 26, of which waited for: 9 -> 10; matrix products, arithmetic and copies ran while one was open for 0% -> 0% of each run, Pallas kernels for 43% -> 42%
where the time goes in v5:
time: 86.7 us; the launch traced here: 86.2 us
  Pallas kernels  37.5 us (43%)
  starting transfers between devices  33.8 us (39%)
  waiting for transfers between devices  12.9 us (15%)
  between operations  1.16 us (1%)
    ppermute x17, starting transfers between devices, swap(): lax.ppermute(value, 'dp', [(i ^ by[i % CORES], i) for i in range(count)])  18.9 us
    pallas_call x3, Pallas kernels, weight_products(): pl.pallas_call(kernel, out_shape=[jax.ShapeDtypeStruct((tokens, span), F3...  14.1 us
    ppermute x8, starting transfers between devices, down(): return lax.ppermute(value, 'pipe', [(i, i - 1) for i in range(1, count)])  10.5 us
    ppermute x17, waiting for transfers between devices, swap(): lax.ppermute(value, 'dp', [(i ^ by[i % CORES], i) for i in range(count)])  8.1 us
    pallas_call x1, Pallas kernels, gradient(): pl.pallas_call(kernel, grid=(steps,), out_shape=[jax.ShapeDtypeStruct((ro...  7.32 us
    pallas_call x1, Pallas kernels, apply_mixing(): pl.pallas_call(kernel, grid=(steps,), out_shape=[jax.ShapeDtypeStruct((ro...  4.89 us
    ppermute x8, waiting for transfers between devices, down(): return lax.ppermute(value, 'pipe', [(i, i - 1) for i in range(1, count)])  4.79 us
    all_to_all x1, starting transfers between devices, shards(): left = lax.all_to_all(columns, 'dp', 0, 0, tiled=True)  4.4 us
  transfers between devices with their start and end apart: 26, of which 10 were waited for; matrix products, arithmetic and copies ran while one was open for 0% of the time, Pallas kernels for 42%

profile of v5, /device:TPU:0, one launch (start us, length us, event | category | flops | bytes accessed | tf_op | source)
XLA Modules:
  0.0 86.2 jit_solution(16666200108327024181)
XLA Ops:
  0.6 3.0 %collective-permute-start = (bf16[128,2048]{1,0:T(8,128)(2,1)}, bf16[128,2048]{1,0:T(8,128)(2,1)}, u32[]{:S(2)}, u32[]{:S(2)}) collective-permute-start(bf16[128,2048]{1,0:T(8,128)(2,1)} %bitcast.6), channel_id=1, source_target_pairs={{2,0},{5,1},{0,2},{7,3},{6,4},{1,5},{4,6},{3,7},{10,8},{13,9},{8,1... | collective-permute-start | bytes 1572872 | tf_op jit(solution)/shard_map/ppermute | solution.py:49
  3.6 1.5 %collective-permute-start.1 = (bf16[128,2048]{1,0:T(8,128)(2,1)}, bf16[128,2048]{1,0:T(8,128)(2,1)}, u32[]{:S(2)}, u32[]{:S(2)}) collective-permute-start(bf16[128,2048]{1,0:T(8,128)(2,1)} %bitcast.7), channel_id=1, source_target_pairs={{4,0},{3,1},{6,2},{1,3},{0,4},{7,5},{2,6},{5,7},{12,8},{11,9},{14,... | collective-permute-start | bytes 1572872 | tf_op jit(solution)/shard_map/ppermute | solution.py:49
  5.2 0.0 collective-permute-start.3
  5.2 2.6 %split_columns.1 = bf16[8,640,128]{2,1,0:T(8,128)(2,1)} custom-call(bf16[128,5120]{1,0:T(8,128)(2,1)} %bitcast.17), custom_call_target="tpu_custom_call" | custom-call | flops 1 | bytes 1 | tf_op jit(solution)/shard_map/split_columns/pallas_call | solution.py:132
  7.7 0.0 copy-start.1
  7.8 4.4 %all-to-all-start = ((bf16[8,640,128]{2,1,0:T(8,128)(2,1)}), bf16[8,640,128]{2,1,0:T(8,128)(2,1)}, u32[]{:S(2)}, u32[]{:S(2)}) async-start(bf16[8,640,128]{2,1,0:T(8,128)(2,1)} %split_columns.1), calls=%async_computation | async-start | bytes 2621440 | tf_op jit(solution)/shard_map/all_to_all | solution.py:543
  12.2 0.0 copy-start
  12.2 4.1 %weight_products.3.refs_1_.refs_2_ = f32[128,1280]{1,0:T(8,128)S(1)} custom-call(bf16[128,2048]{1,0:T(8,128)(2,1)S(1)} %bitcast.10, bf16[5120,2048]{1,0:T(8,128)(2,1)} %bitcast.13), custom_call_target="tpu_custom_call" | custom-call | flops 1 | bytes 1 | tf_op jit(solution)/shard_map/weight_products/pallas_call | solution.py:425
  16.2 0.0 collective-permute-done.refs_2_
  16.3 2.2 %collective-permute-start.2 = (bf16[128,2048]{1,0:T(8,128)(2,1)}, bf16[128,2048]{1,0:T(8,128)(2,1)S(1)}, u32[]{:S(2)}, u32[]{:S(2)}) collective-permute-start(bf16[128,2048]{1,0:T(8,128)(2,1)} %collective-permute-done.refs_2_), channel_id=1, source_target_pairs={{4,0},{3,1},{6,2},{1,3},{0,4},{7,5},{2,6},{5,7},{12,8},{11,9},{14,... | collective-permute-start | bytes 1572872 | tf_op jit(solution)/shard_map/ppermute | solution.py:49
  18.5 0.0 collective-permute-start.4
  18.5 0.0 collective-permute-done.1.refs_3_
  18.5 0.0 collective-permute-done.3.refs_5_
  18.6 1.3 %collective-permute-start.6 = (bf16[128,1280]{1,0:T(8,128)(2,1)S(1)}, bf16[128,1280]{1,0:T(8,128)(2,1)S(1)}, u32[]{:S(2)}, u32[]{:S(2)}) collective-permute-start(bf16[128,1280]{1,0:T(8,128)(2,1)S(1)} %relay_step.8.refs_6_), channel_id=1, source_target_pairs={{8,0},{16,8},{24,16},{9,1},{17,9},{25,17},{10,2},{18,10},{26,18},{... | collective-permute-start | bytes 983048 | tf_op jit(solution)/shard_map/ppermute | solution.py:97
  19.9 3.9 %weight_products.4.refs_1_.refs_2_ = f32[128,1280]{1,0:T(8,128)S(1)} custom-call(bf16[128,2048]{1,0:T(8,128)(2,1)S(1)} %bitcast.11, bf16[5120,2048]{1,0:T(8,128)(2,1)} %bitcast.14), custom_call_target="tpu_custom_call" | custom-call | flops 1 | bytes 1 | tf_op jit(solution)/shard_map/weight_products/pallas_call | solution.py:425
  23.8 1.3 %collective-permute-start.9 = (bf16[128,1280]{1,0:T(8,128)(2,1)S(1)}, bf16[128,1280]{1,0:T(8,128)(2,1)S(1)}, u32[]{:S(2)}, u32[]{:S(2)}) collective-permute-start(bf16[128,1280]{1,0:T(8,128)(2,1)S(1)} %relay_step.9.refs_7_), channel_id=1, source_target_pairs={{8,0},{16,8},{24,16},{9,1},{17,9},{25,17},{10,2},{18,10},{26,18},{... | collective-permute-start | bytes 983048 | tf_op jit(solution)/shard_map/ppermute | solution.py:97
  25.1 0.6 collective-permute-start.5
  25.7 6.1 %weight_products.5 = (f32[128,1280]{1,0:T(8,128)S(1)}, f32[128,1280]{1,0:T(8,128)S(1)}) custom-call(bf16[128,2048]{1,0:T(8,128)(2,1)S(1)} %bitcast.12, bf16[5120,2048]{1,0:T(8,128)(2,1)} %bitcast.15), custom_call_target="tpu_custom_call" | custom-call | flops 1 | bytes 1 | tf_op jit(solution)/shard_map/weight_products/pallas_call | solution.py:425
  31.9 0.0 collective-permute-done.6.refs_0_
  31.9 1.3 %collective-permute-start.11 = (bf16[128,1280]{1,0:T(8,128)(2,1)S(1)}, bf16[128,1280]{1,0:T(8,128)(2,1)}, u32[]{:S(2)}, u32[]{:S(2)}) collective-permute-start(bf16[128,1280]{1,0:T(8,128)(2,1)S(1)} %relay_step.10.refs_8_), channel_id=1, source_target_pairs={{8,0},{16,8},{24,16},{9,1},{17,9},{25,17},{10,2},{18,10},{26,18},{... | collective-permute-start | bytes 983048 | tf_op jit(solution)/shard_map/ppermute | solution.py:97
  33.2 2.2 %collective-permute-done.2.in_ref.refs_4_ = bf16[128,2048]{1,0:T(8,128)(2,1)S(1)} collective-permute-done((bf16[128,2048]{1,0:T(8,128)(2,1)}, bf16[128,2048]{1,0:T(8,128)(2,1)S(1)}, u32[]{:S(2)}, u32[]{:S(2)}) %collective-permute-start.2) | collective-permute-done | bytes 524320 | tf_op jit(solution)/shard_map/ppermute | solution.py:49
  35.5 0.8 cut.1
  36.3 1.1 %collective-permute-start.7 = (bf16[64,2048]{1,0:T(8,128)(2,1)}, bf16[64,2048]{1,0:T(8,128)(2,1)}, u32[]{:S(2)}, u32[]{:S(2)}) collective-permute-start(bf16[64,2048]{1,0:T(8,128)(2,1)} %get-tuple-element.46), channel_id=1, source_target_pairs={{1,0},{0,1},{3,2},{2,3},{5,4},{4,5},{7,6},{6,7},{9,8},{8,9},{11,10... | collective-permute-start | bytes 786440 | tf_op jit(solution)/shard_map/ppermute | solution.py:49
  37.4 0.3 collective-permute-done.9.refs_0_
  37.7 0.0 collective-permute-start.8
  37.7 0.7 relay_step.11.refs_9_
  38.4 0.0 collective-permute-done.4.refs_6_
  38.4 0.8 copy-done.7
  39.2 1.3 %collective-permute-start.10 = (bf16[128,1280]{1,0:T(8,128)(2,1)}, bf16[128,1280]{1,0:T(8,128)(2,1)}, u32[]{:S(2)}, u32[]{:S(2)}) collective-permute-start(bf16[128,1280]{1,0:T(8,128)(2,1)} %relay_step.11.refs_9_), channel_id=1, source_target_pairs={{8,0},{16,8},{24,16},{9,1},{17,9},{25,17},{10,2},{18,10},{26,18},{... | collective-permute-start | bytes 983048 | tf_op jit(solution)/shard_map/ppermute | solution.py:97
  40.5 0.0 all-to-all-done.refs_0_
  40.5 7.3 %gradient.1 = (bf16[640,2048]{1,0:T(8,128)(2,1)S(1)}, f32[4,136,128]{2,1,0:T(8,128)S(1)}, f32[5,136,128]{2,1,0:T(8,128)S(1)}) custom-call(bf16[8,640,128]{2,1,0:T(8,128)(2,1)} %all-to-all-done.refs_0_, bf16[128,2048]{1,0:T(8,128)(2,1)} %bitcast.9, bf16[128,2048]{1,0:T(8,128)(2,1)} %collective-permute-done.refs_2_, ...), custom_call_target="tpu_custom_call" | custom-call | flops 1 | bytes 1 | tf_op jit(solution)/shard_map/gradient/pallas_call | solution.py:238
  47.9 0.0 collective-permute-done.11.refs_0_
  47.9 1.0 %relay_step.12.refs_10_ = bf16[128,1280]{1,0:T(8,128)(2,1)S(1)} custom-call(bf16[128,1280]{1,0:T(8,128)(2,1)} %collective-permute-done.11.refs_0_, f32[128,1280]{1,0:T(8,128)S(1)} %weight_products.3.refs_1_.refs_2_, f32[128,1280]{1,0:T(8,128)S(1)} %get-tuple-element.44.refs_3_.refs_2_), custom_call_target="tpu_custom_call" | custom-call | flops 1 | bytes 1 | tf_op jit(solution)/shard_map/relay_step/pallas_call | solution.py:462
  48.9 0.5 collective-permute-start.12
  49.4 1.3 %collective-permute-start.13 = (bf16[128,1280]{1,0:T(8,128)(2,1)S(1)}, bf16[128,1280]{1,0:T(8,128)(2,1)S(1)}, u32[]{:S(2)}, u32[]{:S(2)}) collective-permute-start(bf16[128,1280]{1,0:T(8,128)(2,1)S(1)} %relay_step.12.refs_10_), channel_id=1, source_target_pairs={{8,0},{16,8},{24,16},{9,1},{17,9},{25,17},{10,2},{18,10},{26,18},{... | collective-permute-start | bytes 983048 | tf_op jit(solution)/shard_map/ppermute | solution.py:97
  50.7 1.5 %collective-permute-done.10.refs_0_ = bf16[128,1280]{1,0:T(8,128)(2,1)} collective-permute-done((bf16[128,1280]{1,0:T(8,128)(2,1)}, bf16[128,1280]{1,0:T(8,128)(2,1)}, u32[]{:S(2)}, u32[]{:S(2)}) %collective-permute-start.10) | collective-permute-done | bytes 327712 | tf_op jit(solution)/shard_map/ppermute | solution.py:97
  52.1 1.0 %relay_step.13.refs_11_ = bf16[128,1280]{1,0:T(8,128)(2,1)S(1)} custom-call(bf16[128,1280]{1,0:T(8,128)(2,1)} %collective-permute-done.10.refs_0_, f32[128,1280]{1,0:T(8,128)S(1)} %weight_products.4.refs_1_.refs_2_, f32[128,1280]{1,0:T(8,128)S(1)} %get-tuple-element.42.refs_3_.refs_2_), custom_call_target="tpu_custom_call" | custom-call | flops 1 | bytes 1 | tf_op jit(solution)/shard_map/relay_step/pallas_call | solution.py:462
  53.1 1.3 %collective-permute-start.23 = (bf16[128,1280]{1,0:T(8,128)(2,1)S(1)}, bf16[128,1280]{1,0:T(8,128)(2,1)S(1)}, u32[]{:S(2)}, u32[]{:S(2)}) collective-permute-start(bf16[128,1280]{1,0:T(8,128)(2,1)S(1)} %relay_step.13.refs_11_), channel_id=1, source_target_pairs={{8,0},{16,8},{24,16},{9,1},{17,9},{25,17},{10,2},{18,10},{26,18},{... | collective-permute-start | bytes 983048 | tf_op jit(solution)/shard_map/ppermute | solution.py:97
  54.4 3.2 %collective-permute-start.14 = (f32[136,128]{1,0:T(8,128)S(1)}, f32[136,128]{1,0:T(8,128)S(1)}, u32[]{:S(2)}, u32[]{:S(2)}) collective-permute-start(f32[136,128]{1,0:T(8,128)S(1)} %get-tuple-element.58), channel_id=1, source_target_pairs={{2,0},{3,1},{0,2},{1,3},{6,4},{7,5},{4,6},{5,7},{10,8},{11,9},{8,1... | collective-permute-start | bytes 208904 | tf_op jit(solution)/shard_map/ppermute | solution.py:49
  57.6 2.6 %collective-permute-start.15 = (f32[136,128]{1,0:T(8,128)S(1)}, f32[136,128]{1,0:T(8,128)S(1)}, u32[]{:S(2)}, u32[]{:S(2)}) collective-permute-start(f32[136,128]{1,0:T(8,128)S(1)} %get-tuple-element.59), channel_id=1, source_target_pairs={{4,0},{5,1},{6,2},{7,3},{0,4},{1,5},{2,6},{3,7},{12,8},{13,9},{14,... | collective-permute-start | bytes 208904 | tf_op jit(solution)/shard_map/ppermute | solution.py:49
  60.2 0.0 collective-permute-start.16
  60.2 2.1 %collective-permute-done.13.refs_0_ = bf16[128,1280]{1,0:T(8,128)(2,1)S(1)} collective-permute-done((bf16[128,1280]{1,0:T(8,128)(2,1)S(1)}, bf16[128,1280]{1,0:T(8,128)(2,1)S(1)}, u32[]{:S(2)}, u32[]{:S(2)}) %collective-permute-start.13) | collective-permute-done | bytes 327712 | tf_op jit(solution)/shard_map/ppermute | solution.py:97
  62.3 0.0 collective-permute-done.14.refs_1_
  62.3 0.2 collective-permute-done.15.refs_2_
  62.5 2.9 %collective-permute-done.16.refs_3_ = f32[136,128]{1,0:T(8,128)S(1)} collective-permute-done((f32[136,128]{1,0:T(8,128)S(1)}, f32[136,128]{1,0:T(8,128)S(1)}, u32[]{:S(2)}, u32[]{:S(2)}) %collective-permute-start.16) | collective-permute-done | bytes 69664 | tf_op jit(solution)/shard_map/ppermute | solution.py:49
  65.4 0.1 relay_step.14.refs_12_
  65.5 1.5 %collective-permute-start.20 = (bf16[128,1280]{1,0:T(8,128)(2,1)S(1)}, bf16[128,1280]{1,0:T(8,128)(2,1)S(1)}, u32[]{:S(2)}, u32[]{:S(2)}) collective-permute-start(bf16[128,1280]{1,0:T(8,128)(2,1)S(1)} %relay_step.14.refs_12_), channel_id=1, source_target_pairs={{8,0},{16,8},{24,16},{9,1},{17,9},{25,17},{10,2},{18,10},{26,18},{... | collective-permute-start | bytes 983048 | tf_op jit(solution)/shard_map/ppermute | solution.py:97
  67.0 4.0 %mixing.1.refs_0_ = f32[136,128]{1,0:T(8,128)S(1)} custom-call(f32[136,128]{1,0:T(8,128)S(1)} %get-tuple-element.62.refs_0_, f32[136,128]{1,0:T(8,128)S(1)} %collective-permute-done.14.refs_1_, f32[136,128]{1,0:T(8,128)S(1)} %collective-permute-done.15.refs_2_, f32[136,128]{1,0:T(8,128)S(1)} %collective-permute-done.16.refs_3_), custom_call_target="tpu_custom_call" | custom-call | flops 1 | bytes 1 | tf_op jit(solution)/shard_map/mixing/pallas_call | solution.py:304
  71.0 0.1 collective-permute-start.17
  71.1 1.2 %collective-permute-start.18 = (f32[136,128]{1,0:T(8,128)S(1)}, f32[136,128]{1,0:T(8,128)S(1)}, u32[]{:S(2)}, u32[]{:S(2)}) collective-permute-start(f32[136,128]{1,0:T(8,128)S(1)} %mixing.1.refs_0_), channel_id=1, source_target_pairs={{4,0},{5,1},{6,2},{7,3},{0,4},{1,5},{2,6},{3,7},{12,8},{13,9},{14,... | collective-permute-start | bytes 208904 | tf_op jit(solution)/shard_map/ppermute | solution.py:49
  72.3 2.2 %collective-permute-start.19 = (f32[136,128]{1,0:T(8,128)S(1)}, f32[136,128]{1,0:T(8,128)S(1)}, u32[]{:S(2)}, u32[]{:S(2)}) collective-permute-start(f32[136,128]{1,0:T(8,128)S(1)} %mixing.1.refs_0_), channel_id=1, source_target_pairs={{6,0},{7,1},{4,2},{5,3},{2,4},{3,5},{0,6},{1,7},{14,8},{15,9},{12,... | collective-permute-start | bytes 208904 | tf_op jit(solution)/shard_map/ppermute | solution.py:49
  74.5 0.0 collective-permute-done.23.refs_0_
  74.5 0.1 relay_step.15.refs_13_
  74.6 1.3 %collective-permute-start.24 = (bf16[128,1280]{1,0:T(8,128)(2,1)S(1)}, bf16[128,1280]{1,0:T(8,128)(2,1)S(1)}, u32[]{:S(2)}, u32[]{:S(2)}) collective-permute-start(bf16[128,1280]{1,0:T(8,128)(2,1)S(1)} %relay_step.15.refs_13_), channel_id=1, source_target_pairs={{8,0},{16,8},{24,16},{9,1},{17,9},{25,17},{10,2},{18,10},{26,18},{... | collective-permute-start | bytes 983048 | tf_op jit(solution)/shard_map/ppermute | solution.py:97
  75.9 0.0 collective-permute-done.17.refs_1_
  75.9 0.0 collective-permute-done.18.refs_2_
  76.0 1.6 %collective-permute-done.19.refs_3_ = f32[136,128]{1,0:T(8,128)S(1)} collective-permute-done((f32[136,128]{1,0:T(8,128)S(1)}, f32[136,128]{1,0:T(8,128)S(1)}, u32[]{:S(2)}, u32[]{:S(2)}) %collective-permute-start.19) | collective-permute-done | bytes 69664 | tf_op jit(solution)/shard_map/ppermute | solution.py:49
  77.5 0.1 collective-permute-start.22
  77.6 0.5 collective-permute-start.21
  78.1 1.0 %collective-permute-done.22.refs_5_ = f32[4,136,128]{2,1,0:T(8,128)S(1)} collective-permute-done((f32[4,136,128]{2,1,0:T(8,128)S(1)}, f32[4,136,128]{2,1,0:T(8,128)S(1)}, u32[]{:S(2)}, u32[]{:S(2)}) %collective-permute-start.22) | collective-permute-done | bytes 278560 | tf_op jit(solution)/shard_map/ppermute | solution.py:49
  79.1 0.1 collective-permute-done.21.refs_4_
  79.3 4.9 %apply_mixing.1 = (bf16[640,2048]{1,0:T(8,128)(2,1)}, bf16[128,5120]{1,0:T(8,128)(2,1)}) custom-call(f32[136,128]{1,0:T(8,128)S(1)} %mixing.1.refs_0_, f32[136,128]{1,0:T(8,128)S(1)} %collective-permute-done.17.refs_1_, f32[136,128]{1,0:T(8,128)S(1)} %collective-permute-done.18.refs_2_, f32[136,128]{1,0:T(8,128)S(1)} %collective-permute-done.19.refs_3_, ...), custom_call_target="tpu_custom_call" | custom-call | flops 1 | bytes 1 | tf_op jit(solution)/shard_map/apply_mixing/pallas_call | solution.py:379
  84.1 1.0 %collective-permute-done.24.refs_1_ = bf16[128,1280]{1,0:T(8,128)(2,1)S(1)} collective-permute-done((bf16[128,1280]{1,0:T(8,128)(2,1)S(1)}, bf16[128,1280]{1,0:T(8,128)(2,1)S(1)}, u32[]{:S(2)}, u32[]{:S(2)}) %collective-permute-start.24) | collective-permute-done | bytes 327712 | tf_op jit(solution)/shard_map/ppermute | solution.py:97
  85.1 0.9 %last_step.1 = bf16[128,5120]{1,0:T(8,128)(2,1)} custom-call(bf16[128,1280]{1,0:T(8,128)(2,1)S(1)} %collective-permute-done.20.refs_0_, bf16[128,1280]{1,0:T(8,128)(2,1)S(1)} %collective-permute-done.24.refs_1_, f32[128,1280]{1,0:T(8,128)S(1)} %get-tuple-element.44.refs_3_.refs_2_, ...), custom_call_target="tpu_custom_call", output_to_operand_aliasing={{}: (4, {})} | custom-call | flops 1 | bytes 1 | tf_op jit(solution)/shard_map/last_step/pallas_call | solution.py:492
  (23 shorter events, 0.2 us)
Async XLA Ops:
  0.6 15.6 %collective-permute-start = (bf16[128,2048]{1,0:T(8,128)(2,1)}, bf16[128,2048]{1,0:T(8,128)(2,1)}, u32[]{:S(2)}, u32[]{:S(2)}) collective-permute-start(bf16[128,2048]{1,0:T(8,128)(2,1)} %bitcast.6), channel_id=1, source_target_pairs={{2,0},{5,1},{0,2},{7,3},{6,4},{1,5},{4,6},{3,7},{10,8},{13,9},{8,1... | collective-permute-start | bytes 1572872 | tf_op jit(solution)/shard_map/ppermute | solution.py:49
  3.6 14.9 %collective-permute-start.1 = (bf16[128,2048]{1,0:T(8,128)(2,1)}, bf16[128,2048]{1,0:T(8,128)(2,1)}, u32[]{:S(2)}, u32[]{:S(2)}) collective-permute-start(bf16[128,2048]{1,0:T(8,128)(2,1)} %bitcast.7), channel_id=1, source_target_pairs={{4,0},{3,1},{6,2},{1,3},{0,4},{7,5},{2,6},{5,7},{12,8},{11,9},{14,... | collective-permute-start | bytes 1572872 | tf_op jit(solution)/shard_map/ppermute | solution.py:49
  5.2 13.4 %collective-permute-start.3 = (bf16[128,2048]{1,0:T(8,128)(2,1)}, bf16[128,2048]{1,0:T(8,128)(2,1)}, u32[]{:S(2)}, u32[]{:S(2)}) collective-permute-start(bf16[128,2048]{1,0:T(8,128)(2,1)} %bitcast.8), channel_id=1, source_target_pairs={{1,0},{0,1},{3,2},{2,3},{5,4},{4,5},{7,6},{6,7},{9,8},{8,9},{11,10... | collective-permute-start | bytes 1572872 | tf_op jit(solution)/shard_map/ppermute | solution.py:49
  7.7 4.4 %copy-start.1 = (bf16[1,128,2048]{2,1,0:T(8,128)(2,1)S(1)}, bf16[1,128,2048]{2,1,0:T(8,128)(2,1)}, u32[]{:S(2)}) copy-start(bf16[1,128,2048]{2,1,0:T(8,128)(2,1)} %param.7) | copy-start | bytes 1572868
  7.8 32.8 %all-to-all-start = ((bf16[8,640,128]{2,1,0:T(8,128)(2,1)}), bf16[8,640,128]{2,1,0:T(8,128)(2,1)}, u32[]{:S(2)}, u32[]{:S(2)}) async-start(bf16[8,640,128]{2,1,0:T(8,128)(2,1)} %split_columns.1), calls=%async_computation | async-start | bytes 2621440 | tf_op jit(solution)/shard_map/all_to_all | solution.py:543
  12.2 6.3 %copy-start = (bf16[128,5120]{1,0:T(8,128)(2,1)S(1)}, bf16[128,5120]{1,0:T(8,128)(2,1)}, u32[]{:S(2)}) copy-start(bf16[128,5120]{1,0:T(8,128)(2,1)} %refs_1_.3) | copy-start | bytes 3932164
  16.3 19.2 %collective-permute-start.2 = (bf16[128,2048]{1,0:T(8,128)(2,1)}, bf16[128,2048]{1,0:T(8,128)(2,1)S(1)}, u32[]{:S(2)}, u32[]{:S(2)}) collective-permute-start(bf16[128,2048]{1,0:T(8,128)(2,1)} %collective-permute-done.refs_2_), channel_id=1, source_target_pairs={{4,0},{3,1},{6,2},{1,3},{0,4},{7,5},{2,6},{5,7},{12,8},{11,9},{14,... | collective-permute-start | bytes 1572872 | tf_op jit(solution)/shard_map/ppermute | solution.py:49
  18.5 19.9 %collective-permute-start.4 = (bf16[128,2048]{1,0:T(8,128)(2,1)}, bf16[128,2048]{1,0:T(8,128)(2,1)S(1)}, u32[]{:S(2)}, u32[]{:S(2)}) collective-permute-start(bf16[128,2048]{1,0:T(8,128)(2,1)} %collective-permute-done.refs_2_), channel_id=1, source_target_pairs={{1,0},{0,1},{3,2},{2,3},{5,4},{4,5},{7,6},{6,7},{9,8},{8,9},{11,10... | collective-permute-start | bytes 1572872 | tf_op jit(solution)/shard_map/ppermute | solution.py:49
  18.6 13.3 %collective-permute-start.6 = (bf16[128,1280]{1,0:T(8,128)(2,1)S(1)}, bf16[128,1280]{1,0:T(8,128)(2,1)S(1)}, u32[]{:S(2)}, u32[]{:S(2)}) collective-permute-start(bf16[128,1280]{1,0:T(8,128)(2,1)S(1)} %relay_step.8.refs_6_), channel_id=1, source_target_pairs={{8,0},{16,8},{24,16},{9,1},{17,9},{25,17},{10,2},{18,10},{26,18},{... | collective-permute-start | bytes 983048 | tf_op jit(solution)/shard_map/ppermute | solution.py:97
  23.8 8.0 %copy-start.3 = (bf16[128,1280]{1,0:T(8,128)(2,1)}, bf16[128,1280]{1,0:T(8,128)(2,1)S(1)}, u32[]{:S(2)}) copy-start(bf16[128,1280]{1,0:T(8,128)(2,1)S(1)} %relay_step.9.refs_7_) | copy-start | bytes 983044
  23.8 13.8 %collective-permute-start.9 = (bf16[128,1280]{1,0:T(8,128)(2,1)S(1)}, bf16[128,1280]{1,0:T(8,128)(2,1)S(1)}, u32[]{:S(2)}, u32[]{:S(2)}) collective-permute-start(bf16[128,1280]{1,0:T(8,128)(2,1)S(1)} %relay_step.9.refs_7_), channel_id=1, source_target_pairs={{8,0},{16,8},{24,16},{9,1},{17,9},{25,17},{10,2},{18,10},{26,18},{... | collective-permute-start | bytes 983048 | tf_op jit(solution)/shard_map/ppermute | solution.py:97
  25.1 15.4 %collective-permute-start.5 = (bf16[128,2048]{1,0:T(8,128)(2,1)}, bf16[128,2048]{1,0:T(8,128)(2,1)}, u32[]{:S(2)}, u32[]{:S(2)}) collective-permute-start(bf16[128,2048]{1,0:T(8,128)(2,1)} %collective-permute-done.1.refs_3_), channel_id=1, source_target_pairs={{1,0},{0,1},{3,2},{2,3},{5,4},{4,5},{7,6},{6,7},{9,8},{8,9},{11,10... | collective-permute-start | bytes 1572872 | tf_op jit(solution)/shard_map/ppermute | solution.py:49
  31.9 6.5 %copy-start.5 = (bf16[128,1280]{1,0:T(8,128)(2,1)}, bf16[128,1280]{1,0:T(8,128)(2,1)S(1)}, u32[]{:S(2)}) copy-start(bf16[128,1280]{1,0:T(8,128)(2,1)S(1)} %relay_step.10.refs_8_) | copy-start | bytes 983044
  31.9 15.9 %collective-permute-start.11 = (bf16[128,1280]{1,0:T(8,128)(2,1)S(1)}, bf16[128,1280]{1,0:T(8,128)(2,1)}, u32[]{:S(2)}, u32[]{:S(2)}) collective-permute-start(bf16[128,1280]{1,0:T(8,128)(2,1)S(1)} %relay_step.10.refs_8_), channel_id=1, source_target_pairs={{8,0},{16,8},{24,16},{9,1},{17,9},{25,17},{10,2},{18,10},{26,18},{... | collective-permute-start | bytes 983048 | tf_op jit(solution)/shard_map/ppermute | solution.py:97
  35.5 3.0 %copy-start.2 = (bf16[128,2048]{1,0:T(8,128)(2,1)}, bf16[128,2048]{1,0:T(8,128)(2,1)S(1)}, u32[]{:S(2)}) copy-start(bf16[128,2048]{1,0:T(8,128)(2,1)S(1)} %collective-permute-done.2.in_ref.refs_4_) | copy-start | bytes 1572868
  36.3 4.2 %collective-permute-start.7 = (bf16[64,2048]{1,0:T(8,128)(2,1)}, bf16[64,2048]{1,0:T(8,128)(2,1)}, u32[]{:S(2)}, u32[]{:S(2)}) collective-permute-start(bf16[64,2048]{1,0:T(8,128)(2,1)} %get-tuple-element.46), channel_id=1, source_target_pairs={{1,0},{0,1},{3,2},{2,3},{5,4},{4,5},{7,6},{6,7},{9,8},{8,9},{11,10... | collective-permute-start | bytes 786440 | tf_op jit(solution)/shard_map/ppermute | solution.py:49
  37.7 2.9 %collective-permute-start.8 = (bf16[64,2048]{1,0:T(8,128)(2,1)}, bf16[64,2048]{1,0:T(8,128)(2,1)}, u32[]{:S(2)}, u32[]{:S(2)}) collective-permute-start(bf16[64,2048]{1,0:T(8,128)(2,1)} %get-tuple-element.47), channel_id=1, source_target_pairs={{1,0},{0,1},{3,2},{2,3},{5,4},{4,5},{7,6},{6,7},{9,8},{8,9},{11,10... | collective-permute-start | bytes 786440 | tf_op jit(solution)/shard_map/ppermute | solution.py:49
  38.4 0.8 copy-start.7
  39.2 12.9 %collective-permute-start.10 = (bf16[128,1280]{1,0:T(8,128)(2,1)}, bf16[128,1280]{1,0:T(8,128)(2,1)}, u32[]{:S(2)}, u32[]{:S(2)}) collective-permute-start(bf16[128,1280]{1,0:T(8,128)(2,1)} %relay_step.11.refs_9_), channel_id=1, source_target_pairs={{8,0},{16,8},{24,16},{9,1},{17,9},{25,17},{10,2},{18,10},{26,18},{... | collective-permute-start | bytes 983048 | tf_op jit(solution)/shard_map/ppermute | solution.py:97
  48.9 5.5 %collective-permute-start.12 = (f32[5,136,128]{2,1,0:T(8,128)S(1)}, f32[5,136,128]{2,1,0:T(8,128)S(1)}, u32[]{:S(2)}, u32[]{:S(2)}) collective-permute-start(f32[5,136,128]{2,1,0:T(8,128)S(1)} %get-tuple-element.56), channel_id=1, source_target_pairs={{1,0},{0,1},{3,2},{2,3},{5,4},{4,5},{7,6},{6,7},{9,8},{8,9},{11,10... | collective-permute-start | bytes 1044488 | tf_op jit(solution)/shard_map/ppermute | solution.py:49
  49.4 13.0 %collective-permute-start.13 = (bf16[128,1280]{1,0:T(8,128)(2,1)S(1)}, bf16[128,1280]{1,0:T(8,128)(2,1)S(1)}, u32[]{:S(2)}, u32[]{:S(2)}) collective-permute-start(bf16[128,1280]{1,0:T(8,128)(2,1)S(1)} %relay_step.12.refs_10_), channel_id=1, source_target_pairs={{8,0},{16,8},{24,16},{9,1},{17,9},{25,17},{10,2},{18,10},{26,18},{... | collective-permute-start | bytes 983048 | tf_op jit(solution)/shard_map/ppermute | solution.py:97
  53.1 21.4 %collective-permute-start.23 = (bf16[128,1280]{1,0:T(8,128)(2,1)S(1)}, bf16[128,1280]{1,0:T(8,128)(2,1)S(1)}, u32[]{:S(2)}, u32[]{:S(2)}) collective-permute-start(bf16[128,1280]{1,0:T(8,128)(2,1)S(1)} %relay_step.13.refs_11_), channel_id=1, source_target_pairs={{8,0},{16,8},{24,16},{9,1},{17,9},{25,17},{10,2},{18,10},{26,18},{... | collective-permute-start | bytes 983048 | tf_op jit(solution)/shard_map/ppermute | solution.py:97
  54.4 7.9 %collective-permute-start.14 = (f32[136,128]{1,0:T(8,128)S(1)}, f32[136,128]{1,0:T(8,128)S(1)}, u32[]{:S(2)}, u32[]{:S(2)}) collective-permute-start(f32[136,128]{1,0:T(8,128)S(1)} %get-tuple-element.58), channel_id=1, source_target_pairs={{2,0},{3,1},{0,2},{1,3},{6,4},{7,5},{4,6},{5,7},{10,8},{11,9},{8,1... | collective-permute-start | bytes 208904 | tf_op jit(solution)/shard_map/ppermute | solution.py:49
  57.6 4.9 %collective-permute-start.15 = (f32[136,128]{1,0:T(8,128)S(1)}, f32[136,128]{1,0:T(8,128)S(1)}, u32[]{:S(2)}, u32[]{:S(2)}) collective-permute-start(f32[136,128]{1,0:T(8,128)S(1)} %get-tuple-element.59), channel_id=1, source_target_pairs={{4,0},{5,1},{6,2},{7,3},{0,4},{1,5},{2,6},{3,7},{12,8},{13,9},{14,... | collective-permute-start | bytes 208904 | tf_op jit(solution)/shard_map/ppermute | solution.py:49
  60.2 5.2 %collective-permute-start.16 = (f32[136,128]{1,0:T(8,128)S(1)}, f32[136,128]{1,0:T(8,128)S(1)}, u32[]{:S(2)}, u32[]{:S(2)}) collective-permute-start(f32[136,128]{1,0:T(8,128)S(1)} %get-tuple-element.60), channel_id=1, source_target_pairs={{6,0},{7,1},{4,2},{5,3},{2,4},{3,5},{0,6},{1,7},{14,8},{15,9},{12,... | collective-permute-start | bytes 208904 | tf_op jit(solution)/shard_map/ppermute | solution.py:49
  65.5 12.1 %collective-permute-start.20 = (bf16[128,1280]{1,0:T(8,128)(2,1)S(1)}, bf16[128,1280]{1,0:T(8,128)(2,1)S(1)}, u32[]{:S(2)}, u32[]{:S(2)}) collective-permute-start(bf16[128,1280]{1,0:T(8,128)(2,1)S(1)} %relay_step.14.refs_12_), channel_id=1, source_target_pairs={{8,0},{16,8},{24,16},{9,1},{17,9},{25,17},{10,2},{18,10},{26,18},{... | collective-permute-start | bytes 983048 | tf_op jit(solution)/shard_map/ppermute | solution.py:97
  71.0 8.3 %copy-start.4 = (bf16[128,1280]{1,0:T(8,128)(2,1)S(1)}, bf16[128,1280]{1,0:T(8,128)(2,1)}, u32[]{:S(2)}) copy-start(bf16[128,1280]{1,0:T(8,128)(2,1)} %copy-done.3) | copy-start | bytes 983044
  71.0 8.3 %copy-start.6 = (bf16[128,1280]{1,0:T(8,128)(2,1)S(1)}, bf16[128,1280]{1,0:T(8,128)(2,1)}, u32[]{:S(2)}) copy-start(bf16[128,1280]{1,0:T(8,128)(2,1)} %copy-done.5) | copy-start | bytes 983044
  71.0 4.9 %collective-permute-start.17 = (f32[136,128]{1,0:T(8,128)S(1)}, f32[136,128]{1,0:T(8,128)S(1)}, u32[]{:S(2)}, u32[]{:S(2)}) collective-permute-start(f32[136,128]{1,0:T(8,128)S(1)} %mixing.1.refs_0_), channel_id=1, source_target_pairs={{2,0},{3,1},{0,2},{1,3},{6,4},{7,5},{4,6},{5,7},{10,8},{11,9},{8,1... | collective-permute-start | bytes 208904 | tf_op jit(solution)/shard_map/ppermute | solution.py:49
  71.1 4.8 %collective-permute-start.18 = (f32[136,128]{1,0:T(8,128)S(1)}, f32[136,128]{1,0:T(8,128)S(1)}, u32[]{:S(2)}, u32[]{:S(2)}) collective-permute-start(f32[136,128]{1,0:T(8,128)S(1)} %mixing.1.refs_0_), channel_id=1, source_target_pairs={{4,0},{5,1},{6,2},{7,3},{0,4},{1,5},{2,6},{3,7},{12,8},{13,9},{14,... | collective-permute-start | bytes 208904 | tf_op jit(solution)/shard_map/ppermute | solution.py:49
  72.3 5.2 %collective-permute-start.19 = (f32[136,128]{1,0:T(8,128)S(1)}, f32[136,128]{1,0:T(8,128)S(1)}, u32[]{:S(2)}, u32[]{:S(2)}) collective-permute-start(f32[136,128]{1,0:T(8,128)S(1)} %mixing.1.refs_0_), channel_id=1, source_target_pairs={{6,0},{7,1},{4,2},{5,3},{2,4},{3,5},{0,6},{1,7},{14,8},{15,9},{12,... | collective-permute-start | bytes 208904 | tf_op jit(solution)/shard_map/ppermute | solution.py:49
  74.6 10.5 %collective-permute-start.24 = (bf16[128,1280]{1,0:T(8,128)(2,1)S(1)}, bf16[128,1280]{1,0:T(8,128)(2,1)S(1)}, u32[]{:S(2)}, u32[]{:S(2)}) collective-permute-start(bf16[128,1280]{1,0:T(8,128)(2,1)S(1)} %relay_step.15.refs_13_), channel_id=1, source_target_pairs={{8,0},{16,8},{24,16},{9,1},{17,9},{25,17},{10,2},{18,10},{26,18},{... | collective-permute-start | bytes 983048 | tf_op jit(solution)/shard_map/ppermute | solution.py:97
  77.5 1.6 %collective-permute-start.22 = (f32[4,136,128]{2,1,0:T(8,128)S(1)}, f32[4,136,128]{2,1,0:T(8,128)S(1)}, u32[]{:S(2)}, u32[]{:S(2)}) collective-permute-start(f32[4,136,128]{2,1,0:T(8,128)S(1)} %join.1), channel_id=1, source_target_pairs={{1,0},{0,1},{3,2},{2,3},{5,4},{4,5},{7,6},{6,7},{9,8},{8,9},{11,10... | collective-permute-start | bytes 835592 | tf_op jit(solution)/shard_map/ppermute | solution.py:49
  77.6 1.6 %collective-permute-start.21 = (f32[136,128]{1,0:T(8,128)S(1)}, f32[136,128]{1,0:T(8,128)S(1)}, u32[]{:S(2)}, u32[]{:S(2)}) collective-permute-start(f32[136,128]{1,0:T(8,128)S(1)} %mixing.1.refs_0_), channel_id=1, source_target_pairs={{1,0},{0,1},{3,2},{2,3},{5,4},{4,5},{7,6},{6,7},{9,8},{8,9},{11,10... | collective-permute-start | bytes 208904 | tf_op jit(solution)/shard_map/ppermute | solution.py:49

commit v6 on v5

--- a/solution.py
+++ b/solution.py
@@ -247,7 +247,7 @@
             2 * rows * total_tokens * width, 2 * total_tokens * (rows + width) + 4 * rows * width
         ),
         name="gradient",
-    )(in_hbm(left), *[in_hbm(piece) for piece in right[:-2]], *right[-2:], in_hbm(moment))
+    )(in_hbm(left), *[in_hbm(piece) for piece in right], in_hbm(moment))
 
 
 def add_pairs(first, second):
@@ -543,18 +543,21 @@
     left = lax.all_to_all(columns, "dp", 0, 0, tiled=True)
     products = list(weight_products([0], after(kv_rows, columns), weights))
     near = near[:1] + [after(piece, products[0]) for piece in near[1:]]
-    products = [after(product, far[0], *near[1:]) for product in products]
+    products = [after(product, far[0], near[1]) for product in products]
     relay()
     products += weight_products([1], after(kv_rows, sent[0]), weights)
     relay()
-    far.extend(swap(piece, other_core) for piece in near[1:])
+    far.append(swap(near[1], other_core))
+    for piece in near[2 : 2 if chips == 4 else chips]:
+        far.append(swap(piece, other_core))
     if chips == 4:
         near.append(swap(near[1], same[2]))
     products += weight_products(list(range(LAG, CHUNKS)), after(kv_rows, sent[1]), weights)
     relay(products[-1])
     relay()
     if chips == 4:
-        far.extend(swap(piece, other_core) for piece in cut(after(near[-1], sent[2]), 2))
+        for piece in near[2:]:
+            far.extend(swap(half, other_core) for half in cut(after(piece, sent[2]), 2))
 
     buffer, mine, theirs = gradient(
         left, same + crossed, near + far, after(moment, sent[3]), scale_grad, slots

time: 86.7 us -> 86.9 us (level)
  starting transfers between devices: 33.8 us -> 28.5 us
  waiting for transfers between devices: 12.9 us -> 18.1 us
    ppermute x17 -> x18, starting transfers between devices: 18.9 us -> 13.6 us  [swap(): lax.ppermute(value, 'dp', [(i ^ by[i % CORES], i) for i in range(count)])]
    ppermute x8, waiting for transfers between devices: 4.79 us -> 7.7 us  [down(): return lax.ppermute(value, 'pipe', [(i, i - 1) for i in range(1, count)])]
    ppermute x17 -> x18, waiting for transfers between devices: 8.1 us -> 10.4 us  [swap(): lax.ppermute(value, 'dp', [(i ^ by[i % CORES], i) for i in range(count)])]
  transfers between devices with their start and end apart: 26 -> 27, of which waited for: 10 -> 10; matrix products, arithmetic and copies ran while one was open for 0% -> 0% of each run, Pallas kernels for 42% -> 43%
where the time goes in v6:
time: 86.9 us; the launch traced here: 86.4 us
  Pallas kernels  37.8 us (43%)
  starting transfers between devices  28.5 us (33%)
  waiting for transfers between devices  18.1 us (21%)
  between operations  1.14 us (1%)
    pallas_call x3, Pallas kernels, weight_products(): pl.pallas_call(kernel, out_shape=[jax.ShapeDtypeStruct((tokens, span), F3...  14.1 us
    ppermute x18, starting transfers between devices, swap(): lax.ppermute(value, 'dp', [(i ^ by[i % CORES], i) for i in range(count)])  13.6 us
    ppermute x8, starting transfers between devices, down(): return lax.ppermute(value, 'pipe', [(i, i - 1) for i in range(1, count)])  10.5 us
    ppermute x18, waiting for transfers between devices, swap(): lax.ppermute(value, 'dp', [(i ^ by[i % CORES], i) for i in range(count)])  10.4 us
    ppermute x8, waiting for transfers between devices, down(): return lax.ppermute(value, 'pipe', [(i, i - 1) for i in range(1, count)])  7.7 us
    pallas_call x1, Pallas kernels, gradient(): pl.pallas_call(kernel, grid=(steps,), out_shape=[jax.ShapeDtypeStruct((ro...  7.45 us
    pallas_call x1, Pallas kernels, apply_mixing(): pl.pallas_call(kernel, grid=(steps,), out_shape=[jax.ShapeDtypeStruct((ro...  4.9 us
    all_to_all x1, starting transfers between devices, shards(): left = lax.all_to_all(columns, 'dp', 0, 0, tiled=True)  4.4 us
  transfers between devices with their start and end apart: 27, of which 10 were waited for; matrix products, arithmetic and copies ran while one was open for 0% of the time, Pallas kernels for 43%

profile of v6, /device:TPU:0, one launch (start us, length us, event | category | flops | bytes accessed | tf_op | source)
XLA Modules:
  0.0 86.4 jit_solution(13610870641407651971)
XLA Ops:
  0.6 3.0 %collective-permute-start = (bf16[128,2048]{1,0:T(8,128)(2,1)}, bf16[128,2048]{1,0:T(8,128)(2,1)}, u32[]{:S(2)}, u32[]{:S(2)}) collective-permute-start(bf16[128,2048]{1,0:T(8,128)(2,1)} %bitcast.6), channel_id=1, source_target_pairs={{2,0},{5,1},{0,2},{7,3},{6,4},{1,5},{4,6},{3,7},{10,8},{13,9},{8,1... | collective-permute-start | bytes 1572872 | tf_op jit(solution)/shard_map/ppermute | solution.py:49
  3.6 0.0 collective-permute-start.3
  3.6 2.6 %split_columns.1 = bf16[8,640,128]{2,1,0:T(8,128)(2,1)} custom-call(bf16[128,5120]{1,0:T(8,128)(2,1)} %bitcast.17), custom_call_target="tpu_custom_call" | custom-call | flops 1 | bytes 1 | tf_op jit(solution)/shard_map/split_columns/pallas_call | solution.py:132
  6.2 0.0 copy-start.1
  6.2 4.4 %all-to-all-start = ((bf16[8,640,128]{2,1,0:T(8,128)(2,1)}), bf16[8,640,128]{2,1,0:T(8,128)(2,1)}, u32[]{:S(2)}, u32[]{:S(2)}) async-start(bf16[8,640,128]{2,1,0:T(8,128)(2,1)} %split_columns.1), calls=%async_computation | async-start | bytes 2621440 | tf_op jit(solution)/shard_map/all_to_all | solution.py:543
  10.7 1.9 %collective-permute-start.1 = (bf16[128,2048]{1,0:T(8,128)(2,1)S(1)}, bf16[128,2048]{1,0:T(8,128)(2,1)S(1)}, u32[]{:S(2)}, u32[]{:S(2)}) collective-permute-start(bf16[128,2048]{1,0:T(8,128)(2,1)S(1)} %bitcast.9), channel_id=1, source_target_pairs={{4,0},{3,1},{6,2},{1,3},{0,4},{7,5},{2,6},{5,7},{12,8},{11,9},{14,... | collective-permute-start | bytes 1572872 | tf_op jit(solution)/shard_map/ppermute | solution.py:49
  12.6 4.0 %weight_products.3.refs_1_.refs_2_ = f32[128,1280]{1,0:T(8,128)S(1)} custom-call(bf16[128,2048]{1,0:T(8,128)(2,1)S(1)} %bitcast.10, bf16[5120,2048]{1,0:T(8,128)(2,1)} %bitcast.13), custom_call_target="tpu_custom_call" | custom-call | flops 1 | bytes 1 | tf_op jit(solution)/shard_map/weight_products/pallas_call | solution.py:425
  16.6 0.3 collective-permute-start.2
  16.9 0.0 collective-permute-start.4
  16.9 0.0 collective-permute-done.3.refs_5_
  16.9 1.3 %collective-permute-start.5 = (bf16[128,1280]{1,0:T(8,128)(2,1)S(1)}, bf16[128,1280]{1,0:T(8,128)(2,1)S(1)}, u32[]{:S(2)}, u32[]{:S(2)}) collective-permute-start(bf16[128,1280]{1,0:T(8,128)(2,1)S(1)} %relay_step.8.refs_6_), channel_id=1, source_target_pairs={{8,0},{16,8},{24,16},{9,1},{17,9},{25,17},{10,2},{18,10},{26,18},{... | collective-permute-start | bytes 983048 | tf_op jit(solution)/shard_map/ppermute | solution.py:97
  18.2 4.0 %weight_products.4.refs_1_.refs_2_ = f32[128,1280]{1,0:T(8,128)S(1)} custom-call(bf16[128,2048]{1,0:T(8,128)(2,1)S(1)} %bitcast.11, bf16[5120,2048]{1,0:T(8,128)(2,1)} %bitcast.14), custom_call_target="tpu_custom_call" | custom-call | flops 1 | bytes 1 | tf_op jit(solution)/shard_map/weight_products/pallas_call | solution.py:425
  22.2 1.3 %collective-permute-start.10 = (bf16[128,1280]{1,0:T(8,128)(2,1)S(1)}, bf16[128,1280]{1,0:T(8,128)(2,1)S(1)}, u32[]{:S(2)}, u32[]{:S(2)}) collective-permute-start(bf16[128,1280]{1,0:T(8,128)(2,1)S(1)} %relay_step.9.refs_7_), channel_id=1, source_target_pairs={{8,0},{16,8},{24,16},{9,1},{17,9},{25,17},{10,2},{18,10},{26,18},{... | collective-permute-start | bytes 983048 | tf_op jit(solution)/shard_map/ppermute | solution.py:97
  23.5 6.2 %weight_products.5 = (f32[128,1280]{1,0:T(8,128)S(1)}, f32[128,1280]{1,0:T(8,128)S(1)}) custom-call(bf16[128,2048]{1,0:T(8,128)(2,1)S(1)} %bitcast.12, bf16[5120,2048]{1,0:T(8,128)(2,1)} %bitcast.15), custom_call_target="tpu_custom_call" | custom-call | flops 1 | bytes 1 | tf_op jit(solution)/shard_map/weight_products/pallas_call | solution.py:425
  29.7 3.7 %collective-permute-done.1.in_ref.refs_3_ = bf16[128,2048]{1,0:T(8,128)(2,1)S(1)} collective-permute-done((bf16[128,2048]{1,0:T(8,128)(2,1)S(1)}, bf16[128,2048]{1,0:T(8,128)(2,1)S(1)}, u32[]{:S(2)}, u32[]{:S(2)}) %collective-permute-start.1) | collective-permute-done | bytes 524320 | tf_op jit(solution)/shard_map/ppermute | solution.py:49
  33.4 0.0 collective-permute-done.5.refs_0_
  33.4 0.8 copy-done.2
  34.2 0.1 cut.2
  34.3 0.3 collective-permute-start.6
  34.5 1.3 %collective-permute-start.12 = (bf16[128,1280]{1,0:T(8,128)(2,1)S(1)}, bf16[128,1280]{1,0:T(8,128)(2,1)}, u32[]{:S(2)}, u32[]{:S(2)}) collective-permute-start(bf16[128,1280]{1,0:T(8,128)(2,1)S(1)} %relay_step.10.refs_8_), channel_id=1, source_target_pairs={{8,0},{16,8},{24,16},{9,1},{17,9},{25,17},{10,2},{18,10},{26,18},{... | collective-permute-start | bytes 983048 | tf_op jit(solution)/shard_map/ppermute | solution.py:97
  35.8 3.2 %collective-permute-done.2.in_ref.refs_4_ = bf16[128,2048]{1,0:T(8,128)(2,1)S(1)} collective-permute-done((bf16[128,2048]{1,0:T(8,128)(2,1)}, bf16[128,2048]{1,0:T(8,128)(2,1)S(1)}, u32[]{:S(2)}, u32[]{:S(2)}) %collective-permute-start.2) | collective-permute-done | bytes 524320 | tf_op jit(solution)/shard_map/ppermute | solution.py:49
  39.0 0.1 collective-permute-start.7
  39.2 0.9 %cut.3 = (bf16[64,2048]{1,0:T(8,128)(2,1)}, bf16[64,2048]{1,0:T(8,128)(2,1)}) custom-call(bf16[128,2048]{1,0:T(8,128)(2,1)S(1)} %collective-permute-done.2.in_ref.refs_4_), custom_call_target="tpu_custom_call" | custom-call | flops 1 | bytes 1 | tf_op jit(solution)/shard_map/cut/pallas_call | solution.py:66
  40.1 0.0 collective-permute-done.10.refs_0_
  40.1 0.4 collective-permute-start.8
  40.5 0.2 collective-permute-start.9
  40.7 0.7 relay_step.11.refs_9_
  41.4 0.0 collective-permute-done.6.refs_7_
  41.4 1.3 %collective-permute-start.11 = (bf16[128,1280]{1,0:T(8,128)(2,1)}, bf16[128,1280]{1,0:T(8,128)(2,1)}, u32[]{:S(2)}, u32[]{:S(2)}) collective-permute-start(bf16[128,1280]{1,0:T(8,128)(2,1)} %relay_step.11.refs_9_), channel_id=1, source_target_pairs={{8,0},{16,8},{24,16},{9,1},{17,9},{25,17},{10,2},{18,10},{26,18},{... | collective-permute-start | bytes 983048 | tf_op jit(solution)/shard_map/ppermute | solution.py:97
  42.7 0.0 all-to-all-done.refs_0_
  42.7 0.0 collective-permute-done.8.refs_9_
  42.8 7.4 %gradient.1 = (bf16[640,2048]{1,0:T(8,128)(2,1)S(1)}, f32[4,136,128]{2,1,0:T(8,128)S(1)}, f32[5,136,128]{2,1,0:T(8,128)S(1)}) custom-call(bf16[8,640,128]{2,1,0:T(8,128)(2,1)} %all-to-all-done.refs_0_, bf16[128,2048]{1,0:T(8,128)(2,1)} %bitcast.8, bf16[128,2048]{1,0:T(8,128)(2,1)} %collective-permute-done.refs_2_, bf16[128,2048]{1,0:T(8,128)(2,1)} %copy-done.2, ...), custom_call_target="tpu_custom_call" | custom-call | flops 1 | bytes 1 | tf_op jit(solution)/shard_map/gradient/pallas_call | solution.py:238
  50.2 0.0 collective-permute-done.12.refs_0_
  50.2 1.0 %relay_step.12.refs_10_ = bf16[128,1280]{1,0:T(8,128)(2,1)S(1)} custom-call(bf16[128,1280]{1,0:T(8,128)(2,1)} %collective-permute-done.12.refs_0_, f32[128,1280]{1,0:T(8,128)S(1)} %weight_products.3.refs_1_.refs_2_, f32[128,1280]{1,0:T(8,128)S(1)} %get-tuple-element.47.refs_3_.refs_2_), custom_call_target="tpu_custom_call" | custom-call | flops 1 | bytes 1 | tf_op jit(solution)/shard_map/relay_step/pallas_call | solution.py:462
  51.2 0.3 collective-permute-start.13
  51.5 1.3 %collective-permute-start.14 = (bf16[128,1280]{1,0:T(8,128)(2,1)S(1)}, bf16[128,1280]{1,0:T(8,128)(2,1)S(1)}, u32[]{:S(2)}, u32[]{:S(2)}) collective-permute-start(bf16[128,1280]{1,0:T(8,128)(2,1)S(1)} %relay_step.12.refs_10_), channel_id=1, source_target_pairs={{8,0},{16,8},{24,16},{9,1},{17,9},{25,17},{10,2},{18,10},{26,18},{... | collective-permute-start | bytes 983048 | tf_op jit(solution)/shard_map/ppermute | solution.py:97
  52.8 0.7 collective-permute-done.11.refs_0_
  53.6 1.0 %relay_step.13.refs_11_ = bf16[128,1280]{1,0:T(8,128)(2,1)S(1)} custom-call(bf16[128,1280]{1,0:T(8,128)(2,1)} %collective-permute-done.11.refs_0_, f32[128,1280]{1,0:T(8,128)S(1)} %weight_products.4.refs_1_.refs_2_, f32[128,1280]{1,0:T(8,128)S(1)} %get-tuple-element.45.refs_3_.refs_2_), custom_call_target="tpu_custom_call" | custom-call | flops 1 | bytes 1 | tf_op jit(solution)/shard_map/relay_step/pallas_call | solution.py:462
  54.5 1.3 %collective-permute-start.24 = (bf16[128,1280]{1,0:T(8,128)(2,1)S(1)}, bf16[128,1280]{1,0:T(8,128)(2,1)S(1)}, u32[]{:S(2)}, u32[]{:S(2)}) collective-permute-start(bf16[128,1280]{1,0:T(8,128)(2,1)S(1)} %relay_step.13.refs_11_), channel_id=1, source_target_pairs={{8,0},{16,8},{24,16},{9,1},{17,9},{25,17},{10,2},{18,10},{26,18},{... | collective-permute-start | bytes 983048 | tf_op jit(solution)/shard_map/ppermute | solution.py:97
  55.8 0.0 collective-permute-done.13.second_ref
  55.9 1.5 %collective-permute-start.15 = (f32[136,128]{1,0:T(8,128)S(1)}, f32[136,128]{1,0:T(8,128)S(1)}, u32[]{:S(2)}, u32[]{:S(2)}) collective-permute-start(f32[136,128]{1,0:T(8,128)S(1)} %get-tuple-element.64), channel_id=1, source_target_pairs={{2,0},{3,1},{0,2},{1,3},{6,4},{7,5},{4,6},{5,7},{10,8},{11,9},{8,1... | collective-permute-start | bytes 208904 | tf_op jit(solution)/shard_map/ppermute | solution.py:49
  57.4 0.4 collective-permute-start.16
  57.8 1.6 %collective-permute-start.17 = (f32[136,128]{1,0:T(8,128)S(1)}, f32[136,128]{1,0:T(8,128)S(1)}, u32[]{:S(2)}, u32[]{:S(2)}) collective-permute-start(f32[136,128]{1,0:T(8,128)S(1)} %get-tuple-element.66), channel_id=1, source_target_pairs={{6,0},{7,1},{4,2},{5,3},{2,4},{3,5},{0,6},{1,7},{14,8},{15,9},{12,... | collective-permute-start | bytes 208904 | tf_op jit(solution)/shard_map/ppermute | solution.py:49
  59.4 5.0 %collective-permute-done.14.refs_0_ = bf16[128,1280]{1,0:T(8,128)(2,1)S(1)} collective-permute-done((bf16[128,1280]{1,0:T(8,128)(2,1)S(1)}, bf16[128,1280]{1,0:T(8,128)(2,1)S(1)}, u32[]{:S(2)}, u32[]{:S(2)}) %collective-permute-start.14) | collective-permute-done | bytes 327712 | tf_op jit(solution)/shard_map/ppermute | solution.py:97
  64.5 0.0 collective-permute-done.16.refs_2_
  64.5 0.0 collective-permute-done.17.refs_3_
  64.5 0.1 relay_step.14.refs_12_
  64.6 1.5 %collective-permute-start.21 = (bf16[128,1280]{1,0:T(8,128)(2,1)S(1)}, bf16[128,1280]{1,0:T(8,128)(2,1)S(1)}, u32[]{:S(2)}, u32[]{:S(2)}) collective-permute-start(bf16[128,1280]{1,0:T(8,128)(2,1)S(1)} %relay_step.14.refs_12_), channel_id=1, source_target_pairs={{8,0},{16,8},{24,16},{9,1},{17,9},{25,17},{10,2},{18,10},{26,18},{... | collective-permute-start | bytes 983048 | tf_op jit(solution)/shard_map/ppermute | solution.py:97
  66.0 4.0 %mixing.1.refs_0_ = f32[136,128]{1,0:T(8,128)S(1)} custom-call(f32[136,128]{1,0:T(8,128)S(1)} %get-tuple-element.68.refs_0_, f32[136,128]{1,0:T(8,128)S(1)} %collective-permute-done.15.refs_1_, f32[136,128]{1,0:T(8,128)S(1)} %collective-permute-done.16.refs_2_, f32[136,128]{1,0:T(8,128)S(1)} %collective-permute-done.17.refs_3_), custom_call_target="tpu_custom_call" | custom-call | flops 1 | bytes 1 | tf_op jit(solution)/shard_map/mixing/pallas_call | solution.py:304
  70.0 1.5 %collective-permute-start.18 = (f32[136,128]{1,0:T(8,128)S(1)}, f32[136,128]{1,0:T(8,128)S(1)}, u32[]{:S(2)}, u32[]{:S(2)}) collective-permute-start(f32[136,128]{1,0:T(8,128)S(1)} %mixing.1.refs_0_), channel_id=1, source_target_pairs={{2,0},{3,1},{0,2},{1,3},{6,4},{7,5},{4,6},{5,7},{10,8},{11,9},{8,1... | collective-permute-start | bytes 208904 | tf_op jit(solution)/shard_map/ppermute | solution.py:49
  71.5 0.4 collective-permute-start.19
  71.9 1.7 %collective-permute-start.20 = (f32[136,128]{1,0:T(8,128)S(1)}, f32[136,128]{1,0:T(8,128)S(1)}, u32[]{:S(2)}, u32[]{:S(2)}) collective-permute-start(f32[136,128]{1,0:T(8,128)S(1)} %mixing.1.refs_0_), channel_id=1, source_target_pairs={{6,0},{7,1},{4,2},{5,3},{2,4},{3,5},{0,6},{1,7},{14,8},{15,9},{12,... | collective-permute-start | bytes 208904 | tf_op jit(solution)/shard_map/ppermute | solution.py:49
  73.6 0.0 collective-permute-done.24.refs_0_
  73.6 0.1 relay_step.15.refs_13_
  73.7 1.3 %collective-permute-start.25 = (bf16[128,1280]{1,0:T(8,128)(2,1)S(1)}, bf16[128,1280]{1,0:T(8,128)(2,1)S(1)}, u32[]{:S(2)}, u32[]{:S(2)}) collective-permute-start(bf16[128,1280]{1,0:T(8,128)(2,1)S(1)} %relay_step.15.refs_13_), channel_id=1, source_target_pairs={{8,0},{16,8},{24,16},{9,1},{17,9},{25,17},{10,2},{18,10},{26,18},{... | collective-permute-start | bytes 983048 | tf_op jit(solution)/shard_map/ppermute | solution.py:97
  75.0 1.3 %collective-permute-done.19.refs_2_ = f32[136,128]{1,0:T(8,128)S(1)} collective-permute-done((f32[136,128]{1,0:T(8,128)S(1)}, f32[136,128]{1,0:T(8,128)S(1)}, u32[]{:S(2)}, u32[]{:S(2)}) %collective-permute-start.19) | collective-permute-done | bytes 69664 | tf_op jit(solution)/shard_map/ppermute | solution.py:49
  76.3 0.8 collective-permute-done.20.refs_3_
  77.2 0.1 collective-permute-start.23
  77.2 1.3 %collective-permute-done.21.refs_0_ = bf16[128,1280]{1,0:T(8,128)(2,1)S(1)} collective-permute-done((bf16[128,1280]{1,0:T(8,128)(2,1)S(1)}, bf16[128,1280]{1,0:T(8,128)(2,1)S(1)}, u32[]{:S(2)}, u32[]{:S(2)}) %collective-permute-start.21) | collective-permute-done | bytes 327712 | tf_op jit(solution)/shard_map/ppermute | solution.py:97
  78.5 0.3 collective-permute-done.23.refs_5_
  78.8 1.0 %collective-permute-done.22.refs_4_ = f32[136,128]{1,0:T(8,128)S(1)} collective-permute-done((f32[136,128]{1,0:T(8,128)S(1)}, f32[136,128]{1,0:T(8,128)S(1)}, u32[]{:S(2)}, u32[]{:S(2)}) %collective-permute-start.22) | collective-permute-done | bytes 69664 | tf_op jit(solution)/shard_map/ppermute | solution.py:49
  79.8 4.9 %apply_mixing.1 = (bf16[640,2048]{1,0:T(8,128)(2,1)}, bf16[128,5120]{1,0:T(8,128)(2,1)}) custom-call(f32[136,128]{1,0:T(8,128)S(1)} %mixing.1.refs_0_, f32[136,128]{1,0:T(8,128)S(1)} %collective-permute-done.18.refs_1_, f32[136,128]{1,0:T(8,128)S(1)} %collective-permute-done.19.refs_2_, f32[136,128]{1,0:T(8,128)S(1)} %collective-permute-done.20.refs_3_, ...), custom_call_target="tpu_custom_call" | custom-call | flops 1 | bytes 1 | tf_op jit(solution)/shard_map/apply_mixing/pallas_call | solution.py:379
  84.7 0.6 collective-permute-done.25.refs_1_
  85.3 0.9 %last_step.1 = bf16[128,5120]{1,0:T(8,128)(2,1)} custom-call(bf16[128,1280]{1,0:T(8,128)(2,1)S(1)} %collective-permute-done.21.refs_0_, bf16[128,1280]{1,0:T(8,128)(2,1)S(1)} %collective-permute-done.25.refs_1_, f32[128,1280]{1,0:T(8,128)S(1)} %get-tuple-element.47.refs_3_.refs_2_, ...), custom_call_target="tpu_custom_call", output_to_operand_aliasing={{}: (4, {})} | custom-call | flops 1 | bytes 1 | tf_op jit(solution)/shard_map/last_step/pallas_call | solution.py:492
  (30 shorter events, 0.1 us)
Async XLA Ops:
  0.6 16.0 %collective-permute-start = (bf16[128,2048]{1,0:T(8,128)(2,1)}, bf16[128,2048]{1,0:T(8,128)(2,1)}, u32[]{:S(2)}, u32[]{:S(2)}) collective-permute-start(bf16[128,2048]{1,0:T(8,128)(2,1)} %bitcast.6), channel_id=1, source_target_pairs={{2,0},{5,1},{0,2},{7,3},{6,4},{1,5},{4,6},{3,7},{10,8},{13,9},{8,1... | collective-permute-start | bytes 1572872 | tf_op jit(solution)/shard_map/ppermute | solution.py:49
  3.6 13.3 %collective-permute-start.3 = (bf16[128,2048]{1,0:T(8,128)(2,1)}, bf16[128,2048]{1,0:T(8,128)(2,1)}, u32[]{:S(2)}, u32[]{:S(2)}) collective-permute-start(bf16[128,2048]{1,0:T(8,128)(2,1)} %bitcast.7), channel_id=1, source_target_pairs={{1,0},{0,1},{3,2},{2,3},{5,4},{4,5},{7,6},{6,7},{9,8},{8,9},{11,10... | collective-permute-start | bytes 1572872 | tf_op jit(solution)/shard_map/ppermute | solution.py:49
  6.2 4.4 %copy-start.1 = (bf16[1,128,2048]{2,1,0:T(8,128)(2,1)S(1)}, bf16[1,128,2048]{2,1,0:T(8,128)(2,1)}, u32[]{:S(2)}) copy-start(bf16[1,128,2048]{2,1,0:T(8,128)(2,1)} %param.7) | copy-start | bytes 1572868
  6.2 36.5 %all-to-all-start = ((bf16[8,640,128]{2,1,0:T(8,128)(2,1)}), bf16[8,640,128]{2,1,0:T(8,128)(2,1)}, u32[]{:S(2)}, u32[]{:S(2)}) async-start(bf16[8,640,128]{2,1,0:T(8,128)(2,1)} %split_columns.1), calls=%async_computation | async-start | bytes 2621440 | tf_op jit(solution)/shard_map/all_to_all | solution.py:543
  10.7 22.8 %collective-permute-start.1 = (bf16[128,2048]{1,0:T(8,128)(2,1)S(1)}, bf16[128,2048]{1,0:T(8,128)(2,1)S(1)}, u32[]{:S(2)}, u32[]{:S(2)}) collective-permute-start(bf16[128,2048]{1,0:T(8,128)(2,1)S(1)} %bitcast.9), channel_id=1, source_target_pairs={{4,0},{3,1},{6,2},{1,3},{0,4},{7,5},{2,6},{5,7},{12,8},{11,9},{14,... | collective-permute-start | bytes 1572872 | tf_op jit(solution)/shard_map/ppermute | solution.py:49
  12.6 4.3 %copy-start = (bf16[128,5120]{1,0:T(8,128)(2,1)S(1)}, bf16[128,5120]{1,0:T(8,128)(2,1)}, u32[]{:S(2)}) copy-start(bf16[128,5120]{1,0:T(8,128)(2,1)} %refs_1_.3) | copy-start | bytes 3932164
  16.6 22.4 %collective-permute-start.2 = (bf16[128,2048]{1,0:T(8,128)(2,1)}, bf16[128,2048]{1,0:T(8,128)(2,1)S(1)}, u32[]{:S(2)}, u32[]{:S(2)}) collective-permute-start(bf16[128,2048]{1,0:T(8,128)(2,1)} %collective-permute-done.refs_2_), channel_id=1, source_target_pairs={{4,0},{3,1},{6,2},{1,3},{0,4},{7,5},{2,6},{5,7},{12,8},{11,9},{14,... | collective-permute-start | bytes 1572872 | tf_op jit(solution)/shard_map/ppermute | solution.py:49
  16.9 23.6 %collective-permute-start.4 = (bf16[128,2048]{1,0:T(8,128)(2,1)}, bf16[128,2048]{1,0:T(8,128)(2,1)S(1)}, u32[]{:S(2)}, u32[]{:S(2)}) collective-permute-start(bf16[128,2048]{1,0:T(8,128)(2,1)} %collective-permute-done.refs_2_), channel_id=1, source_target_pairs={{1,0},{0,1},{3,2},{2,3},{5,4},{4,5},{7,6},{6,7},{9,8},{8,9},{11,10... | collective-permute-start | bytes 1572872 | tf_op jit(solution)/shard_map/ppermute | solution.py:49
  16.9 16.5 %collective-permute-start.5 = (bf16[128,1280]{1,0:T(8,128)(2,1)S(1)}, bf16[128,1280]{1,0:T(8,128)(2,1)S(1)}, u32[]{:S(2)}, u32[]{:S(2)}) collective-permute-start(bf16[128,1280]{1,0:T(8,128)(2,1)S(1)} %relay_step.8.refs_6_), channel_id=1, source_target_pairs={{8,0},{16,8},{24,16},{9,1},{17,9},{25,17},{10,2},{18,10},{26,18},{... | collective-permute-start | bytes 983048 | tf_op jit(solution)/shard_map/ppermute | solution.py:97
  22.2 7.5 %copy-start.4 = (bf16[128,1280]{1,0:T(8,128)(2,1)}, bf16[128,1280]{1,0:T(8,128)(2,1)S(1)}, u32[]{:S(2)}) copy-start(bf16[128,1280]{1,0:T(8,128)(2,1)S(1)} %relay_step.9.refs_7_) | copy-start | bytes 983044
  22.2 17.9 %collective-permute-start.10 = (bf16[128,1280]{1,0:T(8,128)(2,1)S(1)}, bf16[128,1280]{1,0:T(8,128)(2,1)S(1)}, u32[]{:S(2)}, u32[]{:S(2)}) collective-permute-start(bf16[128,1280]{1,0:T(8,128)(2,1)S(1)} %relay_step.9.refs_7_), channel_id=1, source_target_pairs={{8,0},{16,8},{24,16},{9,1},{17,9},{25,17},{10,2},{18,10},{26,18},{... | collective-permute-start | bytes 983048 | tf_op jit(solution)/shard_map/ppermute | solution.py:97
  33.4 0.8 copy-start.2
  34.2 7.2 %copy-start.6 = (bf16[128,1280]{1,0:T(8,128)(2,1)}, bf16[128,1280]{1,0:T(8,128)(2,1)S(1)}, u32[]{:S(2)}) copy-start(bf16[128,1280]{1,0:T(8,128)(2,1)S(1)} %relay_step.10.refs_8_) | copy-start | bytes 983044
  34.3 7.1 %collective-permute-start.6 = (bf16[64,2048]{1,0:T(8,128)(2,1)S(1)}, bf16[64,2048]{1,0:T(8,128)(2,1)S(1)}, u32[]{:S(2)}, u32[]{:S(2)}) collective-permute-start(bf16[64,2048]{1,0:T(8,128)(2,1)S(1)} %get-tuple-element.49), channel_id=1, source_target_pairs={{1,0},{0,1},{3,2},{2,3},{5,4},{4,5},{7,6},{6,7},{9,8},{8,9},{11,10... | collective-permute-start | bytes 786440 | tf_op jit(solution)/shard_map/ppermute | solution.py:49
  34.5 15.7 %collective-permute-start.12 = (bf16[128,1280]{1,0:T(8,128)(2,1)S(1)}, bf16[128,1280]{1,0:T(8,128)(2,1)}, u32[]{:S(2)}, u32[]{:S(2)}) collective-permute-start(bf16[128,1280]{1,0:T(8,128)(2,1)S(1)} %relay_step.10.refs_8_), channel_id=1, source_target_pairs={{8,0},{16,8},{24,16},{9,1},{17,9},{25,17},{10,2},{18,10},{26,18},{... | collective-permute-start | bytes 983048 | tf_op jit(solution)/shard_map/ppermute | solution.py:97
  39.0 2.3 %copy-start.3 = (bf16[128,2048]{1,0:T(8,128)(2,1)}, bf16[128,2048]{1,0:T(8,128)(2,1)S(1)}, u32[]{:S(2)}) copy-start(bf16[128,2048]{1,0:T(8,128)(2,1)S(1)} %collective-permute-done.2.in_ref.refs_4_) | copy-start | bytes 1572868
  39.0 3.7 %collective-permute-start.7 = (bf16[64,2048]{1,0:T(8,128)(2,1)S(1)}, bf16[64,2048]{1,0:T(8,128)(2,1)}, u32[]{:S(2)}, u32[]{:S(2)}) collective-permute-start(bf16[64,2048]{1,0:T(8,128)(2,1)S(1)} %get-tuple-element.50), channel_id=1, source_target_pairs={{1,0},{0,1},{3,2},{2,3},{5,4},{4,5},{7,6},{6,7},{9,8},{8,9},{11,10... | collective-permute-start | bytes 786440 | tf_op jit(solution)/shard_map/ppermute | solution.py:49
  40.1 2.7 %collective-permute-start.8 = (bf16[64,2048]{1,0:T(8,128)(2,1)}, bf16[64,2048]{1,0:T(8,128)(2,1)}, u32[]{:S(2)}, u32[]{:S(2)}) collective-permute-start(bf16[64,2048]{1,0:T(8,128)(2,1)} %get-tuple-element.52), channel_id=1, source_target_pairs={{1,0},{0,1},{3,2},{2,3},{5,4},{4,5},{7,6},{6,7},{9,8},{8,9},{11,10... | collective-permute-start | bytes 786440 | tf_op jit(solution)/shard_map/ppermute | solution.py:49
  40.5 0.9 %copy-start.8 = (bf16[128,2048]{1,0:T(8,128)(2,1)}, bf16[128,2048]{1,0:T(8,128)(2,1)S(1)}, u32[]{:S(2)}) copy-start(bf16[128,2048]{1,0:T(8,128)(2,1)S(1)} %collective-permute-done.4.refs_6_) | copy-start | bytes 1572868
  40.5 2.3 %collective-permute-start.9 = (bf16[64,2048]{1,0:T(8,128)(2,1)}, bf16[64,2048]{1,0:T(8,128)(2,1)}, u32[]{:S(2)}, u32[]{:S(2)}) collective-permute-start(bf16[64,2048]{1,0:T(8,128)(2,1)} %get-tuple-element.53), channel_id=1, source_target_pairs={{1,0},{0,1},{3,2},{2,3},{5,4},{4,5},{7,6},{6,7},{9,8},{8,9},{11,10... | collective-permute-start | bytes 786440 | tf_op jit(solution)/shard_map/ppermute | solution.py:49
  41.4 1.4 %copy-start.9 = (bf16[64,2048]{1,0:T(8,128)(2,1)}, bf16[64,2048]{1,0:T(8,128)(2,1)S(1)}, u32[]{:S(2)}) copy-start(bf16[64,2048]{1,0:T(8,128)(2,1)S(1)} %collective-permute-done.6.refs_7_) | copy-start | bytes 786436
  41.4 12.2 %collective-permute-start.11 = (bf16[128,1280]{1,0:T(8,128)(2,1)}, bf16[128,1280]{1,0:T(8,128)(2,1)}, u32[]{:S(2)}, u32[]{:S(2)}) collective-permute-start(bf16[128,1280]{1,0:T(8,128)(2,1)} %relay_step.11.refs_9_), channel_id=1, source_target_pairs={{8,0},{16,8},{24,16},{9,1},{17,9},{25,17},{10,2},{18,10},{26,18},{... | collective-permute-start | bytes 983048 | tf_op jit(solution)/shard_map/ppermute | solution.py:97
  51.2 4.6 %collective-permute-start.13 = (f32[5,136,128]{2,1,0:T(8,128)S(1)}, f32[5,136,128]{2,1,0:T(8,128)S(1)}, u32[]{:S(2)}, u32[]{:S(2)}) collective-permute-start(f32[5,136,128]{2,1,0:T(8,128)S(1)} %get-tuple-element.62), channel_id=1, source_target_pairs={{1,0},{0,1},{3,2},{2,3},{5,4},{4,5},{7,6},{6,7},{9,8},{8,9},{11,10... | collective-permute-start | bytes 1044488 | tf_op jit(solution)/shard_map/ppermute | solution.py:49
  51.5 12.9 %collective-permute-start.14 = (bf16[128,1280]{1,0:T(8,128)(2,1)S(1)}, bf16[128,1280]{1,0:T(8,128)(2,1)S(1)}, u32[]{:S(2)}, u32[]{:S(2)}) collective-permute-start(bf16[128,1280]{1,0:T(8,128)(2,1)S(1)} %relay_step.12.refs_10_), channel_id=1, source_target_pairs={{8,0},{16,8},{24,16},{9,1},{17,9},{25,17},{10,2},{18,10},{26,18},{... | collective-permute-start | bytes 983048 | tf_op jit(solution)/shard_map/ppermute | solution.py:97
  54.5 19.0 %collective-permute-start.24 = (bf16[128,1280]{1,0:T(8,128)(2,1)S(1)}, bf16[128,1280]{1,0:T(8,128)(2,1)S(1)}, u32[]{:S(2)}, u32[]{:S(2)}) collective-permute-start(bf16[128,1280]{1,0:T(8,128)(2,1)S(1)} %relay_step.13.refs_11_), channel_id=1, source_target_pairs={{8,0},{16,8},{24,16},{9,1},{17,9},{25,17},{10,2},{18,10},{26,18},{... | collective-permute-start | bytes 983048 | tf_op jit(solution)/shard_map/ppermute | solution.py:97
  55.9 8.6 %collective-permute-start.15 = (f32[136,128]{1,0:T(8,128)S(1)}, f32[136,128]{1,0:T(8,128)S(1)}, u32[]{:S(2)}, u32[]{:S(2)}) collective-permute-start(f32[136,128]{1,0:T(8,128)S(1)} %get-tuple-element.64), channel_id=1, source_target_pairs={{2,0},{3,1},{0,2},{1,3},{6,4},{7,5},{4,6},{5,7},{10,8},{11,9},{8,1... | collective-permute-start | bytes 208904 | tf_op jit(solution)/shard_map/ppermute | solution.py:49
  57.4 7.1 %collective-permute-start.16 = (f32[136,128]{1,0:T(8,128)S(1)}, f32[136,128]{1,0:T(8,128)S(1)}, u32[]{:S(2)}, u32[]{:S(2)}) collective-permute-start(f32[136,128]{1,0:T(8,128)S(1)} %get-tuple-element.65), channel_id=1, source_target_pairs={{4,0},{5,1},{6,2},{7,3},{0,4},{1,5},{2,6},{3,7},{12,8},{13,9},{14,... | collective-permute-start | bytes 208904 | tf_op jit(solution)/shard_map/ppermute | solution.py:49
  57.8 6.7 %collective-permute-start.17 = (f32[136,128]{1,0:T(8,128)S(1)}, f32[136,128]{1,0:T(8,128)S(1)}, u32[]{:S(2)}, u32[]{:S(2)}) collective-permute-start(f32[136,128]{1,0:T(8,128)S(1)} %get-tuple-element.66), channel_id=1, source_target_pairs={{6,0},{7,1},{4,2},{5,3},{2,4},{3,5},{0,6},{1,7},{14,8},{15,9},{12,... | collective-permute-start | bytes 208904 | tf_op jit(solution)/shard_map/ppermute | solution.py:49
  64.6 14.0 %collective-permute-start.21 = (bf16[128,1280]{1,0:T(8,128)(2,1)S(1)}, bf16[128,1280]{1,0:T(8,128)(2,1)S(1)}, u32[]{:S(2)}, u32[]{:S(2)}) collective-permute-start(bf16[128,1280]{1,0:T(8,128)(2,1)S(1)} %relay_step.14.refs_12_), channel_id=1, source_target_pairs={{8,0},{16,8},{24,16},{9,1},{17,9},{25,17},{10,2},{18,10},{26,18},{... | collective-permute-start | bytes 983048 | tf_op jit(solution)/shard_map/ppermute | solution.py:97
  70.0 9.8 %copy-start.5 = (bf16[128,1280]{1,0:T(8,128)(2,1)S(1)}, bf16[128,1280]{1,0:T(8,128)(2,1)}, u32[]{:S(2)}) copy-start(bf16[128,1280]{1,0:T(8,128)(2,1)} %copy-done.4) | copy-start | bytes 983044
  70.0 9.8 %copy-start.7 = (bf16[128,1280]{1,0:T(8,128)(2,1)S(1)}, bf16[128,1280]{1,0:T(8,128)(2,1)}, u32[]{:S(2)}) copy-start(bf16[128,1280]{1,0:T(8,128)(2,1)} %copy-done.6) | copy-start | bytes 983044
  70.0 4.9 %collective-permute-start.18 = (f32[136,128]{1,0:T(8,128)S(1)}, f32[136,128]{1,0:T(8,128)S(1)}, u32[]{:S(2)}, u32[]{:S(2)}) collective-permute-start(f32[136,128]{1,0:T(8,128)S(1)} %mixing.1.refs_0_), channel_id=1, source_target_pairs={{2,0},{3,1},{0,2},{1,3},{6,4},{7,5},{4,6},{5,7},{10,8},{11,9},{8,1... | collective-permute-start | bytes 208904 | tf_op jit(solution)/shard_map/ppermute | solution.py:49
  71.5 4.8 %collective-permute-start.19 = (f32[136,128]{1,0:T(8,128)S(1)}, f32[136,128]{1,0:T(8,128)S(1)}, u32[]{:S(2)}, u32[]{:S(2)}) collective-permute-start(f32[136,128]{1,0:T(8,128)S(1)} %mixing.1.refs_0_), channel_id=1, source_target_pairs={{4,0},{5,1},{6,2},{7,3},{0,4},{1,5},{2,6},{3,7},{12,8},{13,9},{14,... | collective-permute-start | bytes 208904 | tf_op jit(solution)/shard_map/ppermute | solution.py:49
  71.9 5.2 %collective-permute-start.20 = (f32[136,128]{1,0:T(8,128)S(1)}, f32[136,128]{1,0:T(8,128)S(1)}, u32[]{:S(2)}, u32[]{:S(2)}) collective-permute-start(f32[136,128]{1,0:T(8,128)S(1)} %mixing.1.refs_0_), channel_id=1, source_target_pairs={{6,0},{7,1},{4,2},{5,3},{2,4},{3,5},{0,6},{1,7},{14,8},{15,9},{12,... | collective-permute-start | bytes 208904 | tf_op jit(solution)/shard_map/ppermute | solution.py:49
  73.7 11.7 %collective-permute-start.25 = (bf16[128,1280]{1,0:T(8,128)(2,1)S(1)}, bf16[128,1280]{1,0:T(8,128)(2,1)S(1)}, u32[]{:S(2)}, u32[]{:S(2)}) collective-permute-start(bf16[128,1280]{1,0:T(8,128)(2,1)S(1)} %relay_step.15.refs_13_), channel_id=1, source_target_pairs={{8,0},{16,8},{24,16},{9,1},{17,9},{25,17},{10,2},{18,10},{26,18},{... | collective-permute-start | bytes 983048 | tf_op jit(solution)/shard_map/ppermute | solution.py:97
  77.2 1.6 %collective-permute-start.23 = (f32[4,136,128]{2,1,0:T(8,128)S(1)}, f32[4,136,128]{2,1,0:T(8,128)S(1)}, u32[]{:S(2)}, u32[]{:S(2)}) collective-permute-start(f32[4,136,128]{2,1,0:T(8,128)S(1)} %join.1), channel_id=1, source_target_pairs={{1,0},{0,1},{3,2},{2,3},{5,4},{4,5},{7,6},{6,7},{9,8},{8,9},{11,10... | collective-permute-start | bytes 835592 | tf_op jit(solution)/shard_map/ppermute | solution.py:49
  78.5 1.3 %collective-permute-start.22 = (f32[136,128]{1,0:T(8,128)S(1)}, f32[136,128]{1,0:T(8,128)S(1)}, u32[]{:S(2)}, u32[]{:S(2)}) collective-permute-start(f32[136,128]{1,0:T(8,128)S(1)} %mixing.1.refs_0_), channel_id=1, source_target_pairs={{1,0},{0,1},{3,2},{2,3},{5,4},{4,5},{7,6},{6,7},{9,8},{8,9},{11,10... | collective-permute-start | bytes 208904 | tf_op jit(solution)/shard_map/ppermute | solution.py:49

commit v7 on v6

--- a/solution.py
+++ b/solution.py
@@ -247,7 +247,7 @@
             2 * rows * total_tokens * width, 2 * total_tokens * (rows + width) + 4 * rows * width
         ),
         name="gradient",
-    )(in_hbm(left), *[in_hbm(piece) for piece in right], in_hbm(moment))
+    )(in_hbm(left), *[in_hbm(piece) for piece in right[:-2]], *right[-2:], in_hbm(moment))
 
 
 def add_pairs(first, second):

time: 86.9 us -> 86.9 us (level)
  no operation moved by 1% of the time
where the time goes in v7:
time: 86.9 us; the launch traced here: 86.4 us
  Pallas kernels  37.8 us (43%)
  starting transfers between devices  28.5 us (33%)
  waiting for transfers between devices  18.1 us (21%)
  between operations  1.14 us (1%)
    pallas_call x3, Pallas kernels, weight_products(): pl.pallas_call(kernel, out_shape=[jax.ShapeDtypeStruct((tokens, span), F3...  14.1 us
    ppermute x18, starting transfers between devices, swap(): lax.ppermute(value, 'dp', [(i ^ by[i % CORES], i) for i in range(count)])  13.6 us
    ppermute x8, starting transfers between devices, down(): return lax.ppermute(value, 'pipe', [(i, i - 1) for i in range(1, count)])  10.5 us
    ppermute x18, waiting for transfers between devices, swap(): lax.ppermute(value, 'dp', [(i ^ by[i % CORES], i) for i in range(count)])  10.4 us
    ppermute x8, waiting for transfers between devices, down(): return lax.ppermute(value, 'pipe', [(i, i - 1) for i in range(1, count)])  7.7 us
    pallas_call x1, Pallas kernels, gradient(): pl.pallas_call(kernel, grid=(steps,), out_shape=[jax.ShapeDtypeStruct((ro...  7.45 us
    pallas_call x1, Pallas kernels, apply_mixing(): pl.pallas_call(kernel, grid=(steps,), out_shape=[jax.ShapeDtypeStruct((ro...  4.9 us
    all_to_all x1, starting transfers between devices, shards(): left = lax.all_to_all(columns, 'dp', 0, 0, tiled=True)  4.4 us
  transfers between devices with their start and end apart: 27, of which 10 were waited for; matrix products, arithmetic and copies ran while one was open for 0% of the time, Pallas kernels for 43%

profile of v7, /device:TPU:0, one launch (start us, length us, event | category | flops | bytes accessed | tf_op | source)
XLA Modules:
  0.0 86.4 jit_solution(13610870641407651971)
XLA Ops:
  0.6 3.0 %collective-permute-start = (bf16[128,2048]{1,0:T(8,128)(2,1)}, bf16[128,2048]{1,0:T(8,128)(2,1)}, u32[]{:S(2)}, u32[]{:S(2)}) collective-permute-start(bf16[128,2048]{1,0:T(8,128)(2,1)} %bitcast.6), channel_id=1, source_target_pairs={{2,0},{5,1},{0,2},{7,3},{6,4},{1,5},{4,6},{3,7},{10,8},{13,9},{8,1... | collective-permute-start | bytes 1572872 | tf_op jit(solution)/shard_map/ppermute | solution.py:49
  3.6 0.0 collective-permute-start.3
  3.6 2.6 %split_columns.1 = bf16[8,640,128]{2,1,0:T(8,128)(2,1)} custom-call(bf16[128,5120]{1,0:T(8,128)(2,1)} %bitcast.17), custom_call_target="tpu_custom_call" | custom-call | flops 1 | bytes 1 | tf_op jit(solution)/shard_map/split_columns/pallas_call | solution.py:132
  6.2 0.0 copy-start.1
  6.2 4.4 %all-to-all-start = ((bf16[8,640,128]{2,1,0:T(8,128)(2,1)}), bf16[8,640,128]{2,1,0:T(8,128)(2,1)}, u32[]{:S(2)}, u32[]{:S(2)}) async-start(bf16[8,640,128]{2,1,0:T(8,128)(2,1)} %split_columns.1), calls=%async_computation | async-start | bytes 2621440 | tf_op jit(solution)/shard_map/all_to_all | solution.py:543
  10.7 1.9 %collective-permute-start.1 = (bf16[128,2048]{1,0:T(8,128)(2,1)S(1)}, bf16[128,2048]{1,0:T(8,128)(2,1)S(1)}, u32[]{:S(2)}, u32[]{:S(2)}) collective-permute-start(bf16[128,2048]{1,0:T(8,128)(2,1)S(1)} %bitcast.9), channel_id=1, source_target_pairs={{4,0},{3,1},{6,2},{1,3},{0,4},{7,5},{2,6},{5,7},{12,8},{11,9},{14,... | collective-permute-start | bytes 1572872 | tf_op jit(solution)/shard_map/ppermute | solution.py:49
  12.6 4.0 %weight_products.3.refs_1_.refs_2_ = f32[128,1280]{1,0:T(8,128)S(1)} custom-call(bf16[128,2048]{1,0:T(8,128)(2,1)S(1)} %bitcast.10, bf16[5120,2048]{1,0:T(8,128)(2,1)} %bitcast.13), custom_call_target="tpu_custom_call" | custom-call | flops 1 | bytes 1 | tf_op jit(solution)/shard_map/weight_products/pallas_call | solution.py:425
  16.6 0.3 collective-permute-start.2
  16.9 0.0 collective-permute-start.4
  16.9 0.0 collective-permute-done.3.refs_5_
  16.9 1.3 %collective-permute-start.5 = (bf16[128,1280]{1,0:T(8,128)(2,1)S(1)}, bf16[128,1280]{1,0:T(8,128)(2,1)S(1)}, u32[]{:S(2)}, u32[]{:S(2)}) collective-permute-start(bf16[128,1280]{1,0:T(8,128)(2,1)S(1)} %relay_step.8.refs_6_), channel_id=1, source_target_pairs={{8,0},{16,8},{24,16},{9,1},{17,9},{25,17},{10,2},{18,10},{26,18},{... | collective-permute-start | bytes 983048 | tf_op jit(solution)/shard_map/ppermute | solution.py:97
  18.2 4.0 %weight_products.4.refs_1_.refs_2_ = f32[128,1280]{1,0:T(8,128)S(1)} custom-call(bf16[128,2048]{1,0:T(8,128)(2,1)S(1)} %bitcast.11, bf16[5120,2048]{1,0:T(8,128)(2,1)} %bitcast.14), custom_call_target="tpu_custom_call" | custom-call | flops 1 | bytes 1 | tf_op jit(solution)/shard_map/weight_products/pallas_call | solution.py:425
  22.2 1.3 %collective-permute-start.10 = (bf16[128,1280]{1,0:T(8,128)(2,1)S(1)}, bf16[128,1280]{1,0:T(8,128)(2,1)S(1)}, u32[]{:S(2)}, u32[]{:S(2)}) collective-permute-start(bf16[128,1280]{1,0:T(8,128)(2,1)S(1)} %relay_step.9.refs_7_), channel_id=1, source_target_pairs={{8,0},{16,8},{24,16},{9,1},{17,9},{25,17},{10,2},{18,10},{26,18},{... | collective-permute-start | bytes 983048 | tf_op jit(solution)/shard_map/ppermute | solution.py:97
  23.5 6.2 %weight_products.5 = (f32[128,1280]{1,0:T(8,128)S(1)}, f32[128,1280]{1,0:T(8,128)S(1)}) custom-call(bf16[128,2048]{1,0:T(8,128)(2,1)S(1)} %bitcast.12, bf16[5120,2048]{1,0:T(8,128)(2,1)} %bitcast.15), custom_call_target="tpu_custom_call" | custom-call | flops 1 | bytes 1 | tf_op jit(solution)/shard_map/weight_products/pallas_call | solution.py:425
  29.7 3.7 %collective-permute-done.1.in_ref.refs_3_ = bf16[128,2048]{1,0:T(8,128)(2,1)S(1)} collective-permute-done((bf16[128,2048]{1,0:T(8,128)(2,1)S(1)}, bf16[128,2048]{1,0:T(8,128)(2,1)S(1)}, u32[]{:S(2)}, u32[]{:S(2)}) %collective-permute-start.1) | collective-permute-done | bytes 524320 | tf_op jit(solution)/shard_map/ppermute | solution.py:49
  33.4 0.0 collective-permute-done.5.refs_0_
  33.4 0.8 copy-done.2
  34.2 0.1 cut.2
  34.3 0.3 collective-permute-start.6
  34.5 1.3 %collective-permute-start.12 = (bf16[128,1280]{1,0:T(8,128)(2,1)S(1)}, bf16[128,1280]{1,0:T(8,128)(2,1)}, u32[]{:S(2)}, u32[]{:S(2)}) collective-permute-start(bf16[128,1280]{1,0:T(8,128)(2,1)S(1)} %relay_step.10.refs_8_), channel_id=1, source_target_pairs={{8,0},{16,8},{24,16},{9,1},{17,9},{25,17},{10,2},{18,10},{26,18},{... | collective-permute-start | bytes 983048 | tf_op jit(solution)/shard_map/ppermute | solution.py:97
  35.8 3.2 %collective-permute-done.2.in_ref.refs_4_ = bf16[128,2048]{1,0:T(8,128)(2,1)S(1)} collective-permute-done((bf16[128,2048]{1,0:T(8,128)(2,1)}, bf16[128,2048]{1,0:T(8,128)(2,1)S(1)}, u32[]{:S(2)}, u32[]{:S(2)}) %collective-permute-start.2) | collective-permute-done | bytes 524320 | tf_op jit(solution)/shard_map/ppermute | solution.py:49
  39.0 0.1 collective-permute-start.7
  39.2 0.9 %cut.3 = (bf16[64,2048]{1,0:T(8,128)(2,1)}, bf16[64,2048]{1,0:T(8,128)(2,1)}) custom-call(bf16[128,2048]{1,0:T(8,128)(2,1)S(1)} %collective-permute-done.2.in_ref.refs_4_), custom_call_target="tpu_custom_call" | custom-call | flops 1 | bytes 1 | tf_op jit(solution)/shard_map/cut/pallas_call | solution.py:66
  40.1 0.0 collective-permute-done.10.refs_0_
  40.1 0.4 collective-permute-start.8
  40.5 0.2 collective-permute-start.9
  40.7 0.7 relay_step.11.refs_9_
  41.4 0.0 collective-permute-done.6.refs_7_
  41.4 1.3 %collective-permute-start.11 = (bf16[128,1280]{1,0:T(8,128)(2,1)}, bf16[128,1280]{1,0:T(8,128)(2,1)}, u32[]{:S(2)}, u32[]{:S(2)}) collective-permute-start(bf16[128,1280]{1,0:T(8,128)(2,1)} %relay_step.11.refs_9_), channel_id=1, source_target_pairs={{8,0},{16,8},{24,16},{9,1},{17,9},{25,17},{10,2},{18,10},{26,18},{... | collective-permute-start | bytes 983048 | tf_op jit(solution)/shard_map/ppermute | solution.py:97
  42.7 0.0 all-to-all-done.refs_0_
  42.7 0.0 collective-permute-done.8.refs_9_
  42.8 7.4 %gradient.1 = (bf16[640,2048]{1,0:T(8,128)(2,1)S(1)}, f32[4,136,128]{2,1,0:T(8,128)S(1)}, f32[5,136,128]{2,1,0:T(8,128)S(1)}) custom-call(bf16[8,640,128]{2,1,0:T(8,128)(2,1)} %all-to-all-done.refs_0_, bf16[128,2048]{1,0:T(8,128)(2,1)} %bitcast.8, bf16[128,2048]{1,0:T(8,128)(2,1)} %collective-permute-done.refs_2_, bf16[128,2048]{1,0:T(8,128)(2,1)} %copy-done.2, ...), custom_call_target="tpu_custom_call" | custom-call | flops 1 | bytes 1 | tf_op jit(solution)/shard_map/gradient/pallas_call | solution.py:238
  50.2 0.0 collective-permute-done.12.refs_0_
  50.2 1.0 %relay_step.12.refs_10_ = bf16[128,1280]{1,0:T(8,128)(2,1)S(1)} custom-call(bf16[128,1280]{1,0:T(8,128)(2,1)} %collective-permute-done.12.refs_0_, f32[128,1280]{1,0:T(8,128)S(1)} %weight_products.3.refs_1_.refs_2_, f32[128,1280]{1,0:T(8,128)S(1)} %get-tuple-element.47.refs_3_.refs_2_), custom_call_target="tpu_custom_call" | custom-call | flops 1 | bytes 1 | tf_op jit(solution)/shard_map/relay_step/pallas_call | solution.py:462
  51.2 0.3 collective-permute-start.13
  51.5 1.3 %collective-permute-start.14 = (bf16[128,1280]{1,0:T(8,128)(2,1)S(1)}, bf16[128,1280]{1,0:T(8,128)(2,1)S(1)}, u32[]{:S(2)}, u32[]{:S(2)}) collective-permute-start(bf16[128,1280]{1,0:T(8,128)(2,1)S(1)} %relay_step.12.refs_10_), channel_id=1, source_target_pairs={{8,0},{16,8},{24,16},{9,1},{17,9},{25,17},{10,2},{18,10},{26,18},{... | collective-permute-start | bytes 983048 | tf_op jit(solution)/shard_map/ppermute | solution.py:97
  52.8 0.7 collective-permute-done.11.refs_0_
  53.6 1.0 %relay_step.13.refs_11_ = bf16[128,1280]{1,0:T(8,128)(2,1)S(1)} custom-call(bf16[128,1280]{1,0:T(8,128)(2,1)} %collective-permute-done.11.refs_0_, f32[128,1280]{1,0:T(8,128)S(1)} %weight_products.4.refs_1_.refs_2_, f32[128,1280]{1,0:T(8,128)S(1)} %get-tuple-element.45.refs_3_.refs_2_), custom_call_target="tpu_custom_call" | custom-call | flops 1 | bytes 1 | tf_op jit(solution)/shard_map/relay_step/pallas_call | solution.py:462
  54.5 1.3 %collective-permute-start.24 = (bf16[128,1280]{1,0:T(8,128)(2,1)S(1)}, bf16[128,1280]{1,0:T(8,128)(2,1)S(1)}, u32[]{:S(2)}, u32[]{:S(2)}) collective-permute-start(bf16[128,1280]{1,0:T(8,128)(2,1)S(1)} %relay_step.13.refs_11_), channel_id=1, source_target_pairs={{8,0},{16,8},{24,16},{9,1},{17,9},{25,17},{10,2},{18,10},{26,18},{... | collective-permute-start | bytes 983048 | tf_op jit(solution)/shard_map/ppermute | solution.py:97
  55.8 0.0 collective-permute-done.13.second_ref
  55.9 1.5 %collective-permute-start.15 = (f32[136,128]{1,0:T(8,128)S(1)}, f32[136,128]{1,0:T(8,128)S(1)}, u32[]{:S(2)}, u32[]{:S(2)}) collective-permute-start(f32[136,128]{1,0:T(8,128)S(1)} %get-tuple-element.64), channel_id=1, source_target_pairs={{2,0},{3,1},{0,2},{1,3},{6,4},{7,5},{4,6},{5,7},{10,8},{11,9},{8,1... | collective-permute-start | bytes 208904 | tf_op jit(solution)/shard_map/ppermute | solution.py:49
  57.4 0.4 collective-permute-start.16
  57.8 1.6 %collective-permute-start.17 = (f32[136,128]{1,0:T(8,128)S(1)}, f32[136,128]{1,0:T(8,128)S(1)}, u32[]{:S(2)}, u32[]{:S(2)}) collective-permute-start(f32[136,128]{1,0:T(8,128)S(1)} %get-tuple-element.66), channel_id=1, source_target_pairs={{6,0},{7,1},{4,2},{5,3},{2,4},{3,5},{0,6},{1,7},{14,8},{15,9},{12,... | collective-permute-start | bytes 208904 | tf_op jit(solution)/shard_map/ppermute | solution.py:49
  59.4 5.0 %collective-permute-done.14.refs_0_ = bf16[128,1280]{1,0:T(8,128)(2,1)S(1)} collective-permute-done((bf16[128,1280]{1,0:T(8,128)(2,1)S(1)}, bf16[128,1280]{1,0:T(8,128)(2,1)S(1)}, u32[]{:S(2)}, u32[]{:S(2)}) %collective-permute-start.14) | collective-permute-done | bytes 327712 | tf_op jit(solution)/shard_map/ppermute | solution.py:97
  64.5 0.0 collective-permute-done.16.refs_2_
  64.5 0.0 collective-permute-done.17.refs_3_
  64.5 0.1 relay_step.14.refs_12_
  64.6 1.5 %collective-permute-start.21 = (bf16[128,1280]{1,0:T(8,128)(2,1)S(1)}, bf16[128,1280]{1,0:T(8,128)(2,1)S(1)}, u32[]{:S(2)}, u32[]{:S(2)}) collective-permute-start(bf16[128,1280]{1,0:T(8,128)(2,1)S(1)} %relay_step.14.refs_12_), channel_id=1, source_target_pairs={{8,0},{16,8},{24,16},{9,1},{17,9},{25,17},{10,2},{18,10},{26,18},{... | collective-permute-start | bytes 983048 | tf_op jit(solution)/shard_map/ppermute | solution.py:97
  66.0 4.0 %mixing.1.refs_0_ = f32[136,128]{1,0:T(8,128)S(1)} custom-call(f32[136,128]{1,0:T(8,128)S(1)} %get-tuple-element.68.refs_0_, f32[136,128]{1,0:T(8,128)S(1)} %collective-permute-done.15.refs_1_, f32[136,128]{1,0:T(8,128)S(1)} %collective-permute-done.16.refs_2_, f32[136,128]{1,0:T(8,128)S(1)} %collective-permute-done.17.refs_3_), custom_call_target="tpu_custom_call" | custom-call | flops 1 | bytes 1 | tf_op jit(solution)/shard_map/mixing/pallas_call | solution.py:304
  70.0 1.5 %collective-permute-start.18 = (f32[136,128]{1,0:T(8,128)S(1)}, f32[136,128]{1,0:T(8,128)S(1)}, u32[]{:S(2)}, u32[]{:S(2)}) collective-permute-start(f32[136,128]{1,0:T(8,128)S(1)} %mixing.1.refs_0_), channel_id=1, source_target_pairs={{2,0},{3,1},{0,2},{1,3},{6,4},{7,5},{4,6},{5,7},{10,8},{11,9},{8,1... | collective-permute-start | bytes 208904 | tf_op jit(solution)/shard_map/ppermute | solution.py:49
  71.5 0.4 collective-permute-start.19
  71.9 1.7 %collective-permute-start.20 = (f32[136,128]{1,0:T(8,128)S(1)}, f32[136,128]{1,0:T(8,128)S(1)}, u32[]{:S(2)}, u32[]{:S(2)}) collective-permute-start(f32[136,128]{1,0:T(8,128)S(1)} %mixing.1.refs_0_), channel_id=1, source_target_pairs={{6,0},{7,1},{4,2},{5,3},{2,4},{3,5},{0,6},{1,7},{14,8},{15,9},{12,... | collective-permute-start | bytes 208904 | tf_op jit(solution)/shard_map/ppermute | solution.py:49
  73.6 0.0 collective-permute-done.24.refs_0_
  73.6 0.1 relay_step.15.refs_13_
  73.7 1.3 %collective-permute-start.25 = (bf16[128,1280]{1,0:T(8,128)(2,1)S(1)}, bf16[128,1280]{1,0:T(8,128)(2,1)S(1)}, u32[]{:S(2)}, u32[]{:S(2)}) collective-permute-start(bf16[128,1280]{1,0:T(8,128)(2,1)S(1)} %relay_step.15.refs_13_), channel_id=1, source_target_pairs={{8,0},{16,8},{24,16},{9,1},{17,9},{25,17},{10,2},{18,10},{26,18},{... | collective-permute-start | bytes 983048 | tf_op jit(solution)/shard_map/ppermute | solution.py:97
  75.0 1.3 %collective-permute-done.19.refs_2_ = f32[136,128]{1,0:T(8,128)S(1)} collective-permute-done((f32[136,128]{1,0:T(8,128)S(1)}, f32[136,128]{1,0:T(8,128)S(1)}, u32[]{:S(2)}, u32[]{:S(2)}) %collective-permute-start.19) | collective-permute-done | bytes 69664 | tf_op jit(solution)/shard_map/ppermute | solution.py:49
  76.3 0.8 collective-permute-done.20.refs_3_
  77.2 0.1 collective-permute-start.23
  77.2 1.3 %collective-permute-done.21.refs_0_ = bf16[128,1280]{1,0:T(8,128)(2,1)S(1)} collective-permute-done((bf16[128,1280]{1,0:T(8,128)(2,1)S(1)}, bf16[128,1280]{1,0:T(8,128)(2,1)S(1)}, u32[]{:S(2)}, u32[]{:S(2)}) %collective-permute-start.21) | collective-permute-done | bytes 327712 | tf_op jit(solution)/shard_map/ppermute | solution.py:97
  78.5 0.3 collective-permute-done.23.refs_5_
  78.8 1.0 %collective-permute-done.22.refs_4_ = f32[136,128]{1,0:T(8,128)S(1)} collective-permute-done((f32[136,128]{1,0:T(8,128)S(1)}, f32[136,128]{1,0:T(8,128)S(1)}, u32[]{:S(2)}, u32[]{:S(2)}) %collective-permute-start.22) | collective-permute-done | bytes 69664 | tf_op jit(solution)/shard_map/ppermute | solution.py:49
  79.8 4.9 %apply_mixing.1 = (bf16[640,2048]{1,0:T(8,128)(2,1)}, bf16[128,5120]{1,0:T(8,128)(2,1)}) custom-call(f32[136,128]{1,0:T(8,128)S(1)} %mixing.1.refs_0_, f32[136,128]{1,0:T(8,128)S(1)} %collective-permute-done.18.refs_1_, f32[136,128]{1,0:T(8,128)S(1)} %collective-permute-done.19.refs_2_, f32[136,128]{1,0:T(8,128)S(1)} %collective-permute-done.20.refs_3_, ...), custom_call_target="tpu_custom_call" | custom-call | flops 1 | bytes 1 | tf_op jit(solution)/shard_map/apply_mixing/pallas_call | solution.py:379
  84.7 0.6 collective-permute-done.25.refs_1_
  85.3 0.9 %last_step.1 = bf16[128,5120]{1,0:T(8,128)(2,1)} custom-call(bf16[128,1280]{1,0:T(8,128)(2,1)S(1)} %collective-permute-done.21.refs_0_, bf16[128,1280]{1,0:T(8,128)(2,1)S(1)} %collective-permute-done.25.refs_1_, f32[128,1280]{1,0:T(8,128)S(1)} %get-tuple-element.47.refs_3_.refs_2_, ...), custom_call_target="tpu_custom_call", output_to_operand_aliasing={{}: (4, {})} | custom-call | flops 1 | bytes 1 | tf_op jit(solution)/shard_map/last_step/pallas_call | solution.py:492
  (30 shorter events, 0.1 us)
Async XLA Ops:
  0.6 16.0 %collective-permute-start = (bf16[128,2048]{1,0:T(8,128)(2,1)}, bf16[128,2048]{1,0:T(8,128)(2,1)}, u32[]{:S(2)}, u32[]{:S(2)}) collective-permute-start(bf16[128,2048]{1,0:T(8,128)(2,1)} %bitcast.6), channel_id=1, source_target_pairs={{2,0},{5,1},{0,2},{7,3},{6,4},{1,5},{4,6},{3,7},{10,8},{13,9},{8,1... | collective-permute-start | bytes 1572872 | tf_op jit(solution)/shard_map/ppermute | solution.py:49
  3.6 13.3 %collective-permute-start.3 = (bf16[128,2048]{1,0:T(8,128)(2,1)}, bf16[128,2048]{1,0:T(8,128)(2,1)}, u32[]{:S(2)}, u32[]{:S(2)}) collective-permute-start(bf16[128,2048]{1,0:T(8,128)(2,1)} %bitcast.7), channel_id=1, source_target_pairs={{1,0},{0,1},{3,2},{2,3},{5,4},{4,5},{7,6},{6,7},{9,8},{8,9},{11,10... | collective-permute-start | bytes 1572872 | tf_op jit(solution)/shard_map/ppermute | solution.py:49
  6.2 4.4 %copy-start.1 = (bf16[1,128,2048]{2,1,0:T(8,128)(2,1)S(1)}, bf16[1,128,2048]{2,1,0:T(8,128)(2,1)}, u32[]{:S(2)}) copy-start(bf16[1,128,2048]{2,1,0:T(8,128)(2,1)} %param.7) | copy-start | bytes 1572868
  6.2 36.5 %all-to-all-start = ((bf16[8,640,128]{2,1,0:T(8,128)(2,1)}), bf16[8,640,128]{2,1,0:T(8,128)(2,1)}, u32[]{:S(2)}, u32[]{:S(2)}) async-start(bf16[8,640,128]{2,1,0:T(8,128)(2,1)} %split_columns.1), calls=%async_computation | async-start | bytes 2621440 | tf_op jit(solution)/shard_map/all_to_all | solution.py:543
  10.7 22.8 %collective-permute-start.1 = (bf16[128,2048]{1,0:T(8,128)(2,1)S(1)}, bf16[128,2048]{1,0:T(8,128)(2,1)S(1)}, u32[]{:S(2)}, u32[]{:S(2)}) collective-permute-start(bf16[128,2048]{1,0:T(8,128)(2,1)S(1)} %bitcast.9), channel_id=1, source_target_pairs={{4,0},{3,1},{6,2},{1,3},{0,4},{7,5},{2,6},{5,7},{12,8},{11,9},{14,... | collective-permute-start | bytes 1572872 | tf_op jit(solution)/shard_map/ppermute | solution.py:49
  12.6 4.3 %copy-start = (bf16[128,5120]{1,0:T(8,128)(2,1)S(1)}, bf16[128,5120]{1,0:T(8,128)(2,1)}, u32[]{:S(2)}) copy-start(bf16[128,5120]{1,0:T(8,128)(2,1)} %refs_1_.3) | copy-start | bytes 3932164
  16.6 22.4 %collective-permute-start.2 = (bf16[128,2048]{1,0:T(8,128)(2,1)}, bf16[128,2048]{1,0:T(8,128)(2,1)S(1)}, u32[]{:S(2)}, u32[]{:S(2)}) collective-permute-start(bf16[128,2048]{1,0:T(8,128)(2,1)} %collective-permute-done.refs_2_), channel_id=1, source_target_pairs={{4,0},{3,1},{6,2},{1,3},{0,4},{7,5},{2,6},{5,7},{12,8},{11,9},{14,... | collective-permute-start | bytes 1572872 | tf_op jit(solution)/shard_map/ppermute | solution.py:49
  16.9 23.6 %collective-permute-start.4 = (bf16[128,2048]{1,0:T(8,128)(2,1)}, bf16[128,2048]{1,0:T(8,128)(2,1)S(1)}, u32[]{:S(2)}, u32[]{:S(2)}) collective-permute-start(bf16[128,2048]{1,0:T(8,128)(2,1)} %collective-permute-done.refs_2_), channel_id=1, source_target_pairs={{1,0},{0,1},{3,2},{2,3},{5,4},{4,5},{7,6},{6,7},{9,8},{8,9},{11,10... | collective-permute-start | bytes 1572872 | tf_op jit(solution)/shard_map/ppermute | solution.py:49
  16.9 16.5 %collective-permute-start.5 = (bf16[128,1280]{1,0:T(8,128)(2,1)S(1)}, bf16[128,1280]{1,0:T(8,128)(2,1)S(1)}, u32[]{:S(2)}, u32[]{:S(2)}) collective-permute-start(bf16[128,1280]{1,0:T(8,128)(2,1)S(1)} %relay_step.8.refs_6_), channel_id=1, source_target_pairs={{8,0},{16,8},{24,16},{9,1},{17,9},{25,17},{10,2},{18,10},{26,18},{... | collective-permute-start | bytes 983048 | tf_op jit(solution)/shard_map/ppermute | solution.py:97
  22.2 7.5 %copy-start.4 = (bf16[128,1280]{1,0:T(8,128)(2,1)}, bf16[128,1280]{1,0:T(8,128)(2,1)S(1)}, u32[]{:S(2)}) copy-start(bf16[128,1280]{1,0:T(8,128)(2,1)S(1)} %relay_step.9.refs_7_) | copy-start | bytes 983044
  22.2 17.9 %collective-permute-start.10 = (bf16[128,1280]{1,0:T(8,128)(2,1)S(1)}, bf16[128,1280]{1,0:T(8,128)(2,1)S(1)}, u32[]{:S(2)}, u32[]{:S(2)}) collective-permute-start(bf16[128,1280]{1,0:T(8,128)(2,1)S(1)} %relay_step.9.refs_7_), channel_id=1, source_target_pairs={{8,0},{16,8},{24,16},{9,1},{17,9},{25,17},{10,2},{18,10},{26,18},{... | collective-permute-start | bytes 983048 | tf_op jit(solution)/shard_map/ppermute | solution.py:97
  33.4 0.8 copy-start.2
  34.2 7.2 %copy-start.6 = (bf16[128,1280]{1,0:T(8,128)(2,1)}, bf16[128,1280]{1,0:T(8,128)(2,1)S(1)}, u32[]{:S(2)}) copy-start(bf16[128,1280]{1,0:T(8,128)(2,1)S(1)} %relay_step.10.refs_8_) | copy-start | bytes 983044
  34.3 7.1 %collective-permute-start.6 = (bf16[64,2048]{1,0:T(8,128)(2,1)S(1)}, bf16[64,2048]{1,0:T(8,128)(2,1)S(1)}, u32[]{:S(2)}, u32[]{:S(2)}) collective-permute-start(bf16[64,2048]{1,0:T(8,128)(2,1)S(1)} %get-tuple-element.49), channel_id=1, source_target_pairs={{1,0},{0,1},{3,2},{2,3},{5,4},{4,5},{7,6},{6,7},{9,8},{8,9},{11,10... | collective-permute-start | bytes 786440 | tf_op jit(solution)/shard_map/ppermute | solution.py:49
  34.5 15.7 %collective-permute-start.12 = (bf16[128,1280]{1,0:T(8,128)(2,1)S(1)}, bf16[128,1280]{1,0:T(8,128)(2,1)}, u32[]{:S(2)}, u32[]{:S(2)}) collective-permute-start(bf16[128,1280]{1,0:T(8,128)(2,1)S(1)} %relay_step.10.refs_8_), channel_id=1, source_target_pairs={{8,0},{16,8},{24,16},{9,1},{17,9},{25,17},{10,2},{18,10},{26,18},{... | collective-permute-start | bytes 983048 | tf_op jit(solution)/shard_map/ppermute | solution.py:97
  39.0 2.3 %copy-start.3 = (bf16[128,2048]{1,0:T(8,128)(2,1)}, bf16[128,2048]{1,0:T(8,128)(2,1)S(1)}, u32[]{:S(2)}) copy-start(bf16[128,2048]{1,0:T(8,128)(2,1)S(1)} %collective-permute-done.2.in_ref.refs_4_) | copy-start | bytes 1572868
  39.0 3.7 %collective-permute-start.7 = (bf16[64,2048]{1,0:T(8,128)(2,1)S(1)}, bf16[64,2048]{1,0:T(8,128)(2,1)}, u32[]{:S(2)}, u32[]{:S(2)}) collective-permute-start(bf16[64,2048]{1,0:T(8,128)(2,1)S(1)} %get-tuple-element.50), channel_id=1, source_target_pairs={{1,0},{0,1},{3,2},{2,3},{5,4},{4,5},{7,6},{6,7},{9,8},{8,9},{11,10... | collective-permute-start | bytes 786440 | tf_op jit(solution)/shard_map/ppermute | solution.py:49
  40.1 2.7 %collective-permute-start.8 = (bf16[64,2048]{1,0:T(8,128)(2,1)}, bf16[64,2048]{1,0:T(8,128)(2,1)}, u32[]{:S(2)}, u32[]{:S(2)}) collective-permute-start(bf16[64,2048]{1,0:T(8,128)(2,1)} %get-tuple-element.52), channel_id=1, source_target_pairs={{1,0},{0,1},{3,2},{2,3},{5,4},{4,5},{7,6},{6,7},{9,8},{8,9},{11,10... | collective-permute-start | bytes 786440 | tf_op jit(solution)/shard_map/ppermute | solution.py:49
  40.5 0.9 %copy-start.8 = (bf16[128,2048]{1,0:T(8,128)(2,1)}, bf16[128,2048]{1,0:T(8,128)(2,1)S(1)}, u32[]{:S(2)}) copy-start(bf16[128,2048]{1,0:T(8,128)(2,1)S(1)} %collective-permute-done.4.refs_6_) | copy-start | bytes 1572868
  40.5 2.3 %collective-permute-start.9 = (bf16[64,2048]{1,0:T(8,128)(2,1)}, bf16[64,2048]{1,0:T(8,128)(2,1)}, u32[]{:S(2)}, u32[]{:S(2)}) collective-permute-start(bf16[64,2048]{1,0:T(8,128)(2,1)} %get-tuple-element.53), channel_id=1, source_target_pairs={{1,0},{0,1},{3,2},{2,3},{5,4},{4,5},{7,6},{6,7},{9,8},{8,9},{11,10... | collective-permute-start | bytes 786440 | tf_op jit(solution)/shard_map/ppermute | solution.py:49
  41.4 1.4 %copy-start.9 = (bf16[64,2048]{1,0:T(8,128)(2,1)}, bf16[64,2048]{1,0:T(8,128)(2,1)S(1)}, u32[]{:S(2)}) copy-start(bf16[64,2048]{1,0:T(8,128)(2,1)S(1)} %collective-permute-done.6.refs_7_) | copy-start | bytes 786436
  41.4 12.2 %collective-permute-start.11 = (bf16[128,1280]{1,0:T(8,128)(2,1)}, bf16[128,1280]{1,0:T(8,128)(2,1)}, u32[]{:S(2)}, u32[]{:S(2)}) collective-permute-start(bf16[128,1280]{1,0:T(8,128)(2,1)} %relay_step.11.refs_9_), channel_id=1, source_target_pairs={{8,0},{16,8},{24,16},{9,1},{17,9},{25,17},{10,2},{18,10},{26,18},{... | collective-permute-start | bytes 983048 | tf_op jit(solution)/shard_map/ppermute | solution.py:97
  51.2 4.6 %collective-permute-start.13 = (f32[5,136,128]{2,1,0:T(8,128)S(1)}, f32[5,136,128]{2,1,0:T(8,128)S(1)}, u32[]{:S(2)}, u32[]{:S(2)}) collective-permute-start(f32[5,136,128]{2,1,0:T(8,128)S(1)} %get-tuple-element.62), channel_id=1, source_target_pairs={{1,0},{0,1},{3,2},{2,3},{5,4},{4,5},{7,6},{6,7},{9,8},{8,9},{11,10... | collective-permute-start | bytes 1044488 | tf_op jit(solution)/shard_map/ppermute | solution.py:49
  51.5 12.9 %collective-permute-start.14 = (bf16[128,1280]{1,0:T(8,128)(2,1)S(1)}, bf16[128,1280]{1,0:T(8,128)(2,1)S(1)}, u32[]{:S(2)}, u32[]{:S(2)}) collective-permute-start(bf16[128,1280]{1,0:T(8,128)(2,1)S(1)} %relay_step.12.refs_10_), channel_id=1, source_target_pairs={{8,0},{16,8},{24,16},{9,1},{17,9},{25,17},{10,2},{18,10},{26,18},{... | collective-permute-start | bytes 983048 | tf_op jit(solution)/shard_map/ppermute | solution.py:97
  54.5 19.0 %collective-permute-start.24 = (bf16[128,1280]{1,0:T(8,128)(2,1)S(1)}, bf16[128,1280]{1,0:T(8,128)(2,1)S(1)}, u32[]{:S(2)}, u32[]{:S(2)}) collective-permute-start(bf16[128,1280]{1,0:T(8,128)(2,1)S(1)} %relay_step.13.refs_11_), channel_id=1, source_target_pairs={{8,0},{16,8},{24,16},{9,1},{17,9},{25,17},{10,2},{18,10},{26,18},{... | collective-permute-start | bytes 983048 | tf_op jit(solution)/shard_map/ppermute | solution.py:97
  55.9 8.6 %collective-permute-start.15 = (f32[136,128]{1,0:T(8,128)S(1)}, f32[136,128]{1,0:T(8,128)S(1)}, u32[]{:S(2)}, u32[]{:S(2)}) collective-permute-start(f32[136,128]{1,0:T(8,128)S(1)} %get-tuple-element.64), channel_id=1, source_target_pairs={{2,0},{3,1},{0,2},{1,3},{6,4},{7,5},{4,6},{5,7},{10,8},{11,9},{8,1... | collective-permute-start | bytes 208904 | tf_op jit(solution)/shard_map/ppermute | solution.py:49
  57.4 7.1 %collective-permute-start.16 = (f32[136,128]{1,0:T(8,128)S(1)}, f32[136,128]{1,0:T(8,128)S(1)}, u32[]{:S(2)}, u32[]{:S(2)}) collective-permute-start(f32[136,128]{1,0:T(8,128)S(1)} %get-tuple-element.65), channel_id=1, source_target_pairs={{4,0},{5,1},{6,2},{7,3},{0,4},{1,5},{2,6},{3,7},{12,8},{13,9},{14,... | collective-permute-start | bytes 208904 | tf_op jit(solution)/shard_map/ppermute | solution.py:49
  57.8 6.7 %collective-permute-start.17 = (f32[136,128]{1,0:T(8,128)S(1)}, f32[136,128]{1,0:T(8,128)S(1)}, u32[]{:S(2)}, u32[]{:S(2)}) collective-permute-start(f32[136,128]{1,0:T(8,128)S(1)} %get-tuple-element.66), channel_id=1, source_target_pairs={{6,0},{7,1},{4,2},{5,3},{2,4},{3,5},{0,6},{1,7},{14,8},{15,9},{12,... | collective-permute-start | bytes 208904 | tf_op jit(solution)/shard_map/ppermute | solution.py:49
  64.6 14.0 %collective-permute-start.21 = (bf16[128,1280]{1,0:T(8,128)(2,1)S(1)}, bf16[128,1280]{1,0:T(8,128)(2,1)S(1)}, u32[]{:S(2)}, u32[]{:S(2)}) collective-permute-start(bf16[128,1280]{1,0:T(8,128)(2,1)S(1)} %relay_step.14.refs_12_), channel_id=1, source_target_pairs={{8,0},{16,8},{24,16},{9,1},{17,9},{25,17},{10,2},{18,10},{26,18},{... | collective-permute-start | bytes 983048 | tf_op jit(solution)/shard_map/ppermute | solution.py:97
  70.0 9.8 %copy-start.5 = (bf16[128,1280]{1,0:T(8,128)(2,1)S(1)}, bf16[128,1280]{1,0:T(8,128)(2,1)}, u32[]{:S(2)}) copy-start(bf16[128,1280]{1,0:T(8,128)(2,1)} %copy-done.4) | copy-start | bytes 983044
  70.0 9.8 %copy-start.7 = (bf16[128,1280]{1,0:T(8,128)(2,1)S(1)}, bf16[128,1280]{1,0:T(8,128)(2,1)}, u32[]{:S(2)}) copy-start(bf16[128,1280]{1,0:T(8,128)(2,1)} %copy-done.6) | copy-start | bytes 983044
  70.0 4.9 %collective-permute-start.18 = (f32[136,128]{1,0:T(8,128)S(1)}, f32[136,128]{1,0:T(8,128)S(1)}, u32[]{:S(2)}, u32[]{:S(2)}) collective-permute-start(f32[136,128]{1,0:T(8,128)S(1)} %mixing.1.refs_0_), channel_id=1, source_target_pairs={{2,0},{3,1},{0,2},{1,3},{6,4},{7,5},{4,6},{5,7},{10,8},{11,9},{8,1... | collective-permute-start | bytes 208904 | tf_op jit(solution)/shard_map/ppermute | solution.py:49
  71.5 4.8 %collective-permute-start.19 = (f32[136,128]{1,0:T(8,128)S(1)}, f32[136,128]{1,0:T(8,128)S(1)}, u32[]{:S(2)}, u32[]{:S(2)}) collective-permute-start(f32[136,128]{1,0:T(8,128)S(1)} %mixing.1.refs_0_), channel_id=1, source_target_pairs={{4,0},{5,1},{6,2},{7,3},{0,4},{1,5},{2,6},{3,7},{12,8},{13,9},{14,... | collective-permute-start | bytes 208904 | tf_op jit(solution)/shard_map/ppermute | solution.py:49
  71.9 5.2 %collective-permute-start.20 = (f32[136,128]{1,0:T(8,128)S(1)}, f32[136,128]{1,0:T(8,128)S(1)}, u32[]{:S(2)}, u32[]{:S(2)}) collective-permute-start(f32[136,128]{1,0:T(8,128)S(1)} %mixing.1.refs_0_), channel_id=1, source_target_pairs={{6,0},{7,1},{4,2},{5,3},{2,4},{3,5},{0,6},{1,7},{14,8},{15,9},{12,... | collective-permute-start | bytes 208904 | tf_op jit(solution)/shard_map/ppermute | solution.py:49
  73.7 11.7 %collective-permute-start.25 = (bf16[128,1280]{1,0:T(8,128)(2,1)S(1)}, bf16[128,1280]{1,0:T(8,128)(2,1)S(1)}, u32[]{:S(2)}, u32[]{:S(2)}) collective-permute-start(bf16[128,1280]{1,0:T(8,128)(2,1)S(1)} %relay_step.15.refs_13_), channel_id=1, source_target_pairs={{8,0},{16,8},{24,16},{9,1},{17,9},{25,17},{10,2},{18,10},{26,18},{... | collective-permute-start | bytes 983048 | tf_op jit(solution)/shard_map/ppermute | solution.py:97
  77.2 1.6 %collective-permute-start.23 = (f32[4,136,128]{2,1,0:T(8,128)S(1)}, f32[4,136,128]{2,1,0:T(8,128)S(1)}, u32[]{:S(2)}, u32[]{:S(2)}) collective-permute-start(f32[4,136,128]{2,1,0:T(8,128)S(1)} %join.1), channel_id=1, source_target_pairs={{1,0},{0,1},{3,2},{2,3},{5,4},{4,5},{7,6},{6,7},{9,8},{8,9},{11,10... | collective-permute-start | bytes 835592 | tf_op jit(solution)/shard_map/ppermute | solution.py:49
  78.5 1.3 %collective-permute-start.22 = (f32[136,128]{1,0:T(8,128)S(1)}, f32[136,128]{1,0:T(8,128)S(1)}, u32[]{:S(2)}, u32[]{:S(2)}) collective-permute-start(f32[136,128]{1,0:T(8,128)S(1)} %mixing.1.refs_0_), channel_id=1, source_target_pairs={{1,0},{0,1},{3,2},{2,3},{5,4},{4,5},{7,6},{6,7},{9,8},{8,9},{11,10... | collective-permute-start | bytes 208904 | tf_op jit(solution)/shard_map/ppermute | solution.py:49
